TPU v7x, 256 devices: a whole 4x4x8 slice. The times are simulated.
256 devices in a mesh: seq: 64 (over y, x_hi, z), head: 4 (over x_lo, core).
Axes of the slice: x: 4 (x_hi: 2, x_lo: 2; x = x_hi * 2 + x_lo), y: 4, z: 8, core: 2. Of those that a mesh axis runs over, the one named last changes fastest.
Arguments:
- queries: bfloat16 [65536, 2048], P('seq', 'head'), may hold values from -11 to 11
- keys_values: bfloat16 [65536, 2, 2048], P('seq', None, 'head'), may hold values from -6 to 6
- rand_blocks: int32 [1024, 2], P('seq'), may hold values from 0 to 1023, as said below
- w_out: bfloat16 [2048, 4096], P('head'), may hold values from -1 to 1
Outputs:
- mixed: bfloat16 [65536, 4096], P(('seq', 'head'))
Inputs may be any that keep to these rules, and one draw needn't show every extreme that they name: `rand_blocks`: of the 32 entries in the rows of one index of seq, at most 1 name blocks o * 16 to o * 16 + 15 of any one index o; in every draw the blocks of some index o are named exactly 1 times from the rows of every index.
All inputs are finite; a program needn't handle non-finite values.
Results may differ from a plain program's by a relative error of at most 0.013.
Values may be sent and summed in bfloat16 or wider, within the bound.
No kernel may reach another device: no remote copies, remote signals or barrier semaphores. Data moves between devices by JAX's collectives and lax.ppermute only.
A program may use at most 128 MiB of HBM per device.

v0:
```python
from functools import reduce

import jax
import jax.numpy as jnp
from jax import lax
from jax.sharding import PartitionSpec as P

HEAD_DIM = 128
BLOCK = 64


def with_halo(cells, sides, width):
    for axis, dim in sides:
        count = lax.axis_size(axis)
        ends = count - 1
        head = lax.slice_in_dim(cells, 0, width, axis=dim)
        tail = lax.slice_in_dim(cells, cells.shape[dim] - width, cells.shape[dim], axis=dim)
        cells = jnp.concatenate(
            [
                lax.ppermute(tail, axis, [(i, (i + 1) % count) for i in range(ends)]),
                cells,
                lax.ppermute(head, axis, [((i + 1) % count, i) for i in range(ends)]),
            ],
            axis=dim,
        )
    return cells


def spread(array, axis, root):
    mine = lax.axis_index(axis) == root
    return lax.psum(jnp.where(mine, array, jnp.zeros_like(array)), axis)


def fetch_random(keys_values, rand_blocks, blocks_dev, seq_count):
    entries = rand_blocks.shape[0] * rand_blocks.shape[1]
    feat_dev = keys_values.shape[2]
    slots = max(1, entries // seq_count)
    flat = rand_blocks.reshape(entries)
    owner = flat // blocks_dev
    offset = flat % blocks_dev
    earlier = jnp.arange(entries)[:, None] > jnp.arange(entries)[None, :]
    rank = jnp.sum((owner[:, None] == owner[None, :]) & earlier, axis=1)
    slot = owner * slots + rank
    placed = slot[:, None] == jnp.arange(seq_count * slots)[None, :]
    outgoing = jnp.sum(jnp.where(placed, offset[:, None], 0), axis=0)
    wanted = lax.all_to_all(
        outgoing.reshape(seq_count, slots), "seq", split_axis=0, concat_axis=0, tiled=True
    )
    local_blocks = keys_values.reshape(blocks_dev, BLOCK, 2, feat_dev)
    answers = local_blocks[wanted]
    returned = lax.all_to_all(answers, "seq", split_axis=0, concat_axis=0, tiled=True)
    picked = returned.reshape(seq_count * slots, BLOCK, 2, feat_dev)[slot]
    return picked.reshape(blocks_dev, entries // blocks_dev * BLOCK, 2, feat_dev)


def body(queries, keys_values, rand_blocks, w_out):
    tok_rows, feat_dev = queries.shape
    heads_dev = feat_dev // HEAD_DIM
    blocks_dev = tok_rows // BLOCK
    seq_count = lax.axis_size("seq")
    all_blocks = blocks_dev * seq_count
    position = lax.axis_index("seq")
    scale = HEAD_DIM ** (-0.5)
    padded = with_halo(keys_values, (("seq", 0),), BLOCK)
    padded = padded.reshape(blocks_dev + 2, BLOCK, 2, heads_dev, HEAD_DIM)
    window = jnp.concatenate([padded[:-2], padded[1:-1], padded[2:]], axis=1)
    first = spread(keys_values[:BLOCK], "seq", 0)
    final = spread(keys_values[-BLOCK:], "seq", seq_count - 1)
    ends = jnp.concatenate([first, final], axis=0)
    ends = ends.reshape(2 * BLOCK, 2, heads_dev, HEAD_DIM)
    random_kv = fetch_random(keys_values, rand_blocks, blocks_dev, seq_count)
    random_kv = random_kv.reshape(blocks_dev, -1, 2, heads_dev, HEAD_DIM)
    block_ids = position * blocks_dev + jnp.arange(blocks_dev, dtype=jnp.int32)
    near_ok = jnp.stack([block_ids >= 1, block_ids >= 0, block_ids <= all_blocks - 2], axis=1)
    ends_ok = jnp.stack([block_ids >= 2, block_ids <= all_blocks - 3], axis=1)
    taken = [
        block_ids - 1,
        block_ids,
        block_ids + 1,
        jnp.zeros_like(block_ids),
        jnp.zeros_like(block_ids) + (all_blocks - 1),
    ]
    rand_flags = []
    for column in range(rand_blocks.shape[1]):
        chosen = rand_blocks[:, column]
        clash = reduce(jnp.logical_or, [chosen == other for other in taken])
        rand_flags.append(jnp.logical_not(clash))
        taken.append(chosen)
    rand_ok = jnp.stack(rand_flags, axis=1)
    near_mask = jnp.repeat(near_ok, BLOCK, axis=1)[:, None, None, :]
    ends_mask = jnp.repeat(ends_ok, BLOCK, axis=1)[:, None, None, :]
    rand_mask = jnp.repeat(rand_ok, BLOCK, axis=1)[:, None, None, :]
    query_heads = queries.reshape(blocks_dev, BLOCK, heads_dev, HEAD_DIM)
    near_scores = (
        jnp.einsum(
            "jqhd,jkhd->jhqk", query_heads, window[:, :, 0], preferred_element_type=jnp.float32
        )
        * scale
    )
    ends_scores = (
        jnp.einsum("jqhd,khd->jhqk", query_heads, ends[:, 0], preferred_element_type=jnp.float32)
        * scale
    )
    rand_scores = (
        jnp.einsum(
            "jqhd,jkhd->jhqk", query_heads, random_kv[:, :, 0], preferred_element_type=jnp.float32
        )
        * scale
    )
    near_scores = jnp.where(near_mask, near_scores, -1e30)
    ends_scores = jnp.where(ends_mask, ends_scores, -1e30)
    rand_scores = jnp.where(rand_mask, rand_scores, -1e30)
    peak = jnp.maximum(
        jnp.max(near_scores, axis=-1, keepdims=True), jnp.max(ends_scores, axis=-1, keepdims=True)
    )
    peak = jnp.maximum(peak, jnp.max(rand_scores, axis=-1, keepdims=True))
    near_raw = jnp.where(near_mask, jnp.exp(near_scores - peak), 0.0)
    ends_raw = jnp.where(ends_mask, jnp.exp(ends_scores - peak), 0.0)
    rand_raw = jnp.where(rand_mask, jnp.exp(rand_scores - peak), 0.0)
    total = jnp.sum(near_raw, axis=-1) + jnp.sum(ends_raw, axis=-1) + jnp.sum(rand_raw, axis=-1)
    mixture = jnp.einsum(
        "jhqk,jkhd->jqhd",
        near_raw.astype(jnp.bfloat16),
        window[:, :, 1],
        preferred_element_type=jnp.float32,
    )
    mixture = mixture + jnp.einsum(
        "jhqk,khd->jqhd",
        ends_raw.astype(jnp.bfloat16),
        ends[:, 1],
        preferred_element_type=jnp.float32,
    )
    mixture = mixture + jnp.einsum(
        "jhqk,jkhd->jqhd",
        rand_raw.astype(jnp.bfloat16),
        random_kv[:, :, 1],
        preferred_element_type=jnp.float32,
    )
    attended = (mixture / jnp.transpose(total, (0, 2, 1))[..., None]).astype(jnp.bfloat16)
    attended = attended.reshape(tok_rows, feat_dev)
    return lax.psum_scatter(
        jnp.dot(attended, w_out, preferred_element_type=jnp.float32).astype(jnp.bfloat16),
        "head",
        scatter_dimension=0,
        tiled=True,
    )


def solution(mesh):
    in_specs = (P("seq", "head"), P("seq", None, "head"), P("seq", None), P("head", None))
    out_specs = P(("seq", "head"), None)
    return jax.shard_map(body, mesh=mesh, in_specs=in_specs, out_specs=out_specs, check_vma=False)
```

profile of v0, /device:TPU:1, one launch (start us, length us, event | category | flops | bytes accessed | tf_op | source)
XLA Modules:
  0.0 896.9 jit_solution(1453318806021883987)
XLA Ops:
  6.5 0.8 copy.286
  7.7 0.7 copy.287
  8.4 15.1 %all-to-all-start = ((s32[64,1,1]{2,1,0:T(1,128)}), s32[64,1,1]{2,1,0:T(1,128)S(1)}, u32[]{:S(2)}, u32[]{:S(2)}) async-start(s32[64,1,1]{2,1,0:T(1,128)} %copy.287), calls=%async_computation | async-start | bytes 65536 | tf_op jit(solution)/shard_map/all_to_all | solution.py:46
  23.5 2.0 copy.288
  25.6 8.6 all-to-all-done
  34.2 1.2 fusion.38
  35.4 5.4 gather_fusion
  40.9 5.9 all-to-all-start.1
  46.8 0.2 fusion.53
  47.0 0.2 copy.316
  47.2 1.3 collective-permute-start.1
  48.5 0.9 copy.315
  49.4 4.7 collective-permute-start
  54.1 0.7 broadcast_select_fusion
  54.8 0.7 broadcast_select_fusion.1
  55.6 0.2 reduce-scatter.2.cloned.1.call-start
  56.0 2.6 reshape.267
  58.7 1.1 reshape.240
  59.8 1.5 copy.282
  62.1 172.0 %collective-permute-done.1 = bf16[64,2,512]{0,2,1:T(8,128)(2,1)} collective-permute-done((bf16[64,2,512]{0,2,1:T(8,128)(2,1)S(1)}, bf16[64,2,512]{0,2,1:T(8,128)(2,1)}, u32[]{:S(2)}, u32[]{:S(2)}) %collective-permute-start.1) | collective-permute-done | bytes 131104 | tf_op jit(solution)/shard_map/ppermute | solution.py:22
  234.1 1.1 copy.273
  235.3 1.1 copy.269
  236.4 6.5 pad_maximum_fusion
  242.8 4.5 reshape.266
  247.4 2.6 reshape.268
  250.0 2.3 copy_dynamic-update-slice_fusion.2
  252.3 0.7 copy_dynamic-update-slice_fusion.1
  253.0 0.9 copy-done.3
  253.9 0.7 copy_dynamic-update-slice_fusion
  254.6 2.6 copy-done.8
  257.3 4.2 bitcast_reduce_fusion
  261.4 463.1 %all-reduce.3.cloned.1.call-done = (bf16[64,2,512]{0,2,1:T(8,128)(2,1)}, bf16[64,2,512]{0,2,1:T(8,128)(2,1)}) async-done(((bf16[64,2,512]{0,2,1:T(8,128)(2,1)}, bf16[64,2,512]{0,2,1:T(8,128)(2,1)}), (bf16[64,2,512]{0,2,1:T(8,128)(2,1)}, bf16[64,2,512]{0,2,1:T(8,128)(2,1)})) %all-reduce.3.cloned.1.call-update) | async-done | bytes 262160 | tf_op jit(solution)/shard_map/psum | solution.py:31
  724.6 1.2 pad_maximum_fusion.2
  725.7 0.4 fusion.34
  726.2 0.6 fusion.21
  726.8 6.2 gather_fusion.1
  733.0 4.6 copy.291
  737.6 6.9 reshape_reshape.3
  744.5 3.2 fusion.52
  747.7 1.6 bitcast_reduce_fusion.1
  749.4 2.7 fusion.22
  752.2 0.4 fusion.29
  752.6 1.9 fusion.4
  754.5 0.7 fusion.10
  755.2 2.2 fusion.12
  757.4 0.9 copy.302
  758.3 6.8 convolution_convert_fusion
  765.2 124.9 %reduce-scatter.2.cloned.1.call-done = bf16[256,4096]{1,0:T(8,128)(2,1)} async-done(((bf16[1024,4096]{1,0:T(8,128)(2,1)}), bf16[256,4096]{1,0:T(8,128)(2,1)}) %reduce-scatter.2.cloned.1.call-update) | async-done | bytes 2097168 | tf_op jit(solution)/shard_map/reduce_scatter | solution.py:141
  (58 shorter events, 1.6 us)
Async XLA Ops:
  8.4 25.8 %all-to-all-start = ((s32[64,1,1]{2,1,0:T(1,128)}), s32[64,1,1]{2,1,0:T(1,128)S(1)}, u32[]{:S(2)}, u32[]{:S(2)}) async-start(s32[64,1,1]{2,1,0:T(1,128)} %copy.287), calls=%async_computation | async-start | bytes 65536 | tf_op jit(solution)/shard_map/all_to_all | solution.py:46
  40.9 6.0 copy-start
  40.9 685.9 %all-to-all-start.1 = ((bf16[64,1,64,2,512]{4,2,3,1,0:T(8,128)(2,1)}), bf16[64,1,64,2,512]{4,2,3,1,0:T(8,128)(2,1)}, u32[]{:S(2)}, u32[]{:S(2)}) async-start(bf16[64,1,64,2,512]{4,2,3,1,0:T(8,128)(2,1)} %bitcast.106), calls=%async_computation.1 | async-start | bytes 16777216 | tf_op jit(solution)/shard_map/all_to_all | solution.py:51
  46.8 9.1 %copy-start.9 = (s32[16,2]{0,1:T(2,128)S(1)}, s32[16,2]{0,1:T(2,128)}, u32[]{:S(2)}) copy-start(s32[16,2]{0,1:T(2,128)} %param.6) | copy-start | bytes 388
  46.8 677.8 %all-reduce.3.cloned.1.call-start = ((), (), s32[]{:S(2)}) async-start(), calls=%async_computation.4 | async-start | bytes 1048576 | tf_op jit(solution)/shard_map/psum | solution.py:31
  47.2 186.9 %collective-permute-start.1 = (bf16[64,2,512]{0,2,1:T(8,128)(2,1)S(1)}, bf16[64,2,512]{0,2,1:T(8,128)(2,1)}, u32[]{:S(2)}, u32[]{:S(2)}) collective-permute-start(bf16[64,2,512]{0,2,1:T(8,128)(2,1)S(1)} %copy.316), channel_id=1, source_target_pairs={{4,0},{8,4},{12,8},{16,12},{20,16},{24,20},{28,24},{32,28},{36,32}... | collective-permute-start | bytes 393224 | tf_op jit(solution)/shard_map/ppermute | solution.py:22
  49.4 185.8 %collective-permute-start = (bf16[64,2,512]{0,2,1:T(8,128)(2,1)}, bf16[64,2,512]{0,2,1:T(8,128)(2,1)}, u32[]{:S(2)}, u32[]{:S(2)}) collective-permute-start(bf16[64,2,512]{0,2,1:T(8,128)(2,1)} %copy.315), channel_id=1, source_target_pairs={{0,4},{4,8},{8,12},{12,16},{16,20},{20,24},{24,28},{28,32},{32,36}... | collective-permute-start | bytes 393224 | tf_op jit(solution)/shard_map/ppermute | solution.py:20
  55.6 834.5 %reduce-scatter.2.cloned.1.call-start = ((), (), s32[]{:S(2)}) async-start(), calls=%async_computation.3 | async-start | bytes 10485760 | tf_op jit(solution)/shard_map/reduce_scatter | solution.py:141
  56.0 2.6 copy-start.7
  242.8 4.5 copy-start.1
  250.0 2.3 copy-start.2
  252.3 1.6 copy-start.3
  253.9 3.4 copy-start.5
  254.6 2.7 copy-start.8
  744.5 3.2 copy-start.6
  749.4 3.2 copy-start.4
  752.1 3.1 slice-start
  752.6 2.6 slice-start.1
  755.2 3.1 copy-start.10
Sparse Core Ops, SparseCore 0:
  55.7 668.8 all-reduce.2
  765.3 124.7 reduce-scatter.1
where the time goes:
time: 898 us; the launch traced here: 897 us
  waiting for transfers between devices  769 us (86%)
  local copies, waits for them, and re-layouts  54.8 us (6%)
  starting transfers between devices  27.3 us (3%)
  matrix products  16.3 us (2%)
  other arithmetic  15.9 us (2%)
  between operations  13.8 us (2%)
    psum x1, waiting for transfers between devices, spread(): return lax.psum(jnp.where(mine, array, jnp.zeros_like(array)), axis)  463 us
    ppermute x1, waiting for transfers between devices, with_halo(): lax.ppermute(head, axis, [((i + 1) % count, i) for i in range(ends)])  172 us
    reduce_scatter x1, waiting for transfers between devices, body(): lax.psum_scatter(jnp.dot(attended, w_out, preferred_element_type=jnp.floa...  125 us
  transfers between devices with their start and end apart: 6, of which 4 were waited for; matrix products, arithmetic and copies ran while one was open for 4% of the time, Pallas kernels for 0%

commit v1 on v0

v1 whole, which is shorter than its diff:
```python
from functools import reduce

import jax
import jax.numpy as jnp
from jax import lax
from jax.experimental import pallas as pl
from jax.experimental.pallas import tpu as pltpu
from jax.sharding import Mesh, PartitionSpec as P

HEAD_DIM = 128
BLOCK = 64
NEG = -1e30
SEQ = ("y", "xh", "z")
LANE = ("y", "xh")
HEAD = ("xl", "core")
XRING = ("xh", "xl")
NY, NXH, NZ, NXL, NC = 4, 2, 8, 2, 2
LANES = NY * NXH
SCALE = HEAD_DIM ** (-0.5)
F32 = jnp.float32
BF16 = jnp.bfloat16
VMEM_LIMIT = 48 * 1024 * 1024


def dot_nt(a, b):
    return lax.dot_general(a, b, (((1,), (1,)), ((), ())), preferred_element_type=F32)


def local_kernel(all_blocks, id_ref, q_ref, kv_ref, ends_ref, o_ref, st_ref):
    feat = q_ref.shape[1]
    heads = feat // HEAD_DIM
    blocks = q_ref.shape[0] // BLOCK
    col = lax.broadcasted_iota(jnp.int32, (BLOCK, 3 * BLOCK), 1)
    shift = jnp.where(col < BLOCK, -1, jnp.where(col < 2 * BLOCK, 0, 1))
    end_col = lax.broadcasted_iota(jnp.int32, (BLOCK, 2 * BLOCK), 1)

    def step(j, carry):
        block = id_ref[0] + j
        near = block + shift
        near_ok = jnp.logical_and(near >= 0, near < all_blocks)
        ends_ok = jnp.where(end_col < BLOCK, block, all_blocks - 1 - block) >= 2
        rows = pl.ds(pl.multiple_of(j * BLOCK, BLOCK), BLOCK)
        wrows = pl.ds(pl.multiple_of(j * BLOCK, BLOCK), 3 * BLOCK)
        for h in range(heads):
            kcol = pl.ds(h * HEAD_DIM, HEAD_DIM)
            vcol = pl.ds(feat + h * HEAD_DIM, HEAD_DIM)
            q = q_ref[rows, kcol]
            sw = jnp.where(near_ok, dot_nt(q, kv_ref[wrows, kcol]) * SCALE, NEG)
            se = jnp.where(ends_ok, dot_nt(q, ends_ref[:, kcol]) * SCALE, NEG)
            peak = jnp.maximum(
                jnp.max(sw, axis=1, keepdims=True), jnp.max(se, axis=1, keepdims=True)
            )
            pw = jnp.exp(sw - peak)
            pe = jnp.exp(se - peak)
            total = jnp.sum(pw, axis=1, keepdims=True) + jnp.sum(pe, axis=1, keepdims=True)
            out = jnp.dot(pw.astype(BF16), kv_ref[wrows, vcol], preferred_element_type=F32)
            out += jnp.dot(pe.astype(BF16), ends_ref[:, vcol], preferred_element_type=F32)
            o_ref[rows, kcol] = out
            st_ref[rows, pl.ds(h, 1)] = peak
            st_ref[rows, pl.ds(heads + h, 1)] = total
        return carry

    lax.fori_loop(0, blocks, step, 0)


def add_slots(where_ref, base, slots_ref, q_ref, o_ref, st_ref):
    feat = q_ref.shape[1]
    heads = feat // HEAD_DIM

    def step(s, carry):
        j = where_ref[base + s]

        @pl.when(j >= 0)
        def _():
            rows = pl.ds(pl.multiple_of(j * BLOCK, BLOCK), BLOCK)
            for h in range(heads):
                kcol = pl.ds(h * HEAD_DIM, HEAD_DIM)
                vcol = pl.ds(feat + h * HEAD_DIM, HEAD_DIM)
                sc = dot_nt(q_ref[rows, kcol], slots_ref[s, :, kcol]) * SCALE
                old = st_ref[rows, pl.ds(h, 1)]
                peak = jnp.maximum(old, jnp.max(sc, axis=1, keepdims=True))
                fade = jnp.exp(old - peak)
                p = jnp.exp(sc - peak)
                total = st_ref[rows, pl.ds(heads + h, 1)] * fade + jnp.sum(p, axis=1, keepdims=True)
                out = jnp.dot(p.astype(BF16), slots_ref[s, :, vcol], preferred_element_type=F32)
                o_ref[rows, kcol] = o_ref[rows, kcol] * fade + out
                st_ref[rows, pl.ds(h, 1)] = peak
                st_ref[rows, pl.ds(heads + h, 1)] = total

        return carry

    lax.fori_loop(0, slots_ref.shape[0], step, 0)


def more_kernel(count, where_ref, q_ref, oin_ref, stin_ref, *refs):
    slots, (o_ref, st_ref) = refs[:count], refs[count:]
    o_ref[...] = oin_ref[...]
    st_ref[...] = stin_ref[...]
    base = 0
    for ref in slots:
        add_slots(where_ref, base, ref, q_ref, o_ref, st_ref)
        base += ref.shape[0]


def final_kernel(count, where_ref, q_ref, oin_ref, stin_ref, *refs):
    slots, (att_ref, o_ref, st_ref) = refs[:count], refs[count:]
    o_ref[...] = oin_ref[...]
    st_ref[...] = stin_ref[...]
    base = 0
    for ref in slots:
        add_slots(where_ref, base, ref, q_ref, o_ref, st_ref)
        base += ref.shape[0]
    heads = q_ref.shape[1] // HEAD_DIM

    def step(j, carry):
        rows = pl.ds(pl.multiple_of(j * BLOCK, BLOCK), BLOCK)
        for h in range(heads):
            kcol = pl.ds(h * HEAD_DIM, HEAD_DIM)
            att_ref[rows, kcol] = (
                o_ref[rows, kcol] / st_ref[rows, pl.ds(heads + h, 1)]
            ).astype(BF16)
        return carry

    lax.fori_loop(0, q_ref.shape[0] // BLOCK, step, 0)


VM = pl.BlockSpec(memory_space=pltpu.VMEM)
SM = pl.BlockSpec(memory_space=pltpu.SMEM)


def local_part(first_id, all_blocks, q, kv_pad, ends):
    tok, feat = q.shape
    return pl.pallas_call(
        lambda *refs: local_kernel(all_blocks, *refs),
        out_shape=(
            jax.ShapeDtypeStruct((tok, feat), F32),
            jax.ShapeDtypeStruct((tok, 128), F32),
        ),
        in_specs=[SM, VM, VM, VM],
        out_specs=(VM, VM),
        compiler_params=pltpu.CompilerParams(vmem_limit_bytes=VMEM_LIMIT),
        cost_estimate=pl.CostEstimate(
            flops=4 * tok * feat * 5 * BLOCK, bytes_accessed=8 * 2**20, transcendentals=0
        ),
        name="local_part",
    )(first_id, q, kv_pad, ends)


def more_part(where, q, o, st, slots):
    tok, feat = q.shape
    return pl.pallas_call(
        lambda *refs: more_kernel(len(slots), *refs),
        out_shape=(
            jax.ShapeDtypeStruct((tok, feat), F32),
            jax.ShapeDtypeStruct((tok, 128), F32),
        ),
        in_specs=[SM] + [VM] * (3 + len(slots)),
        out_specs=(VM, VM),
        compiler_params=pltpu.CompilerParams(vmem_limit_bytes=VMEM_LIMIT),
        cost_estimate=pl.CostEstimate(
            flops=2 * tok * feat * BLOCK, bytes_accessed=8 * 2**20, transcendentals=0
        ),
        name="more_part",
    )(where, q, o, st, *slots)


def final_part(where, q, o, st, slots):
    tok, feat = q.shape
    return pl.pallas_call(
        lambda *refs: final_kernel(len(slots), *refs),
        out_shape=jax.ShapeDtypeStruct((tok, feat), BF16),
        in_specs=[SM] + [VM] * (3 + len(slots)),
        out_specs=VM,
        scratch_shapes=[pltpu.VMEM((tok, feat), F32), pltpu.VMEM((tok, 128), F32)],
        compiler_params=pltpu.CompilerParams(vmem_limit_bytes=VMEM_LIMIT),
        name="final_part",
    )(where, q, o, st, *slots)


def project_kernel(me_ref, a_ref, own_ref, core_ref, lo_ref, hi_ref, clo_ref, chi_ref, out_ref):
    me = me_ref[0]
    half = lo_ref.shape[0]

    def mul(a, w_ref):
        return jnp.dot(a, w_ref[...], preferred_element_type=F32)

    acc = mul(a_ref[me], own_ref)
    acc += mul(a_ref[me ^ 1], core_ref)
    acc += mul(a_ref[me ^ 2, :, :half], lo_ref)
    acc += mul(a_ref[me ^ 2, :, half:], hi_ref)
    acc += mul(a_ref[me ^ 3, :, :half], clo_ref)
    acc += mul(a_ref[me ^ 3, :, half:], chi_ref)
    out_ref[...] = acc.astype(BF16)


def project(me, a, weights, tile=512):
    _, rows, feat = a.shape
    cols = weights[0].shape[1]
    return pl.pallas_call(
        project_kernel,
        out_shape=jax.ShapeDtypeStruct((rows, cols), BF16),
        grid_spec=pltpu.PrefetchScalarGridSpec(
            num_scalar_prefetch=1,
            grid=(cols // tile,),
            in_specs=[pl.BlockSpec(a.shape, lambda n, me: (0, 0, 0))]
            + [pl.BlockSpec((w.shape[0], tile), lambda n, me: (0, n)) for w in weights],
            out_specs=pl.BlockSpec((rows, tile), lambda n, me: (0, n)),
        ),
        compiler_params=pltpu.CompilerParams(vmem_limit_bytes=VMEM_LIMIT),
        name="project",
    )(me, a, *weights)


def z_shift(x, by):
    return lax.ppermute(x, "z", [(i, (i + by) % NZ) for i in range(NZ)])


def lane_exchange(x):
    return lax.all_to_all(x, LANE, split_axis=0, concat_axis=0, tiled=True)


def wanted_blocks(rand_blocks, block_ids, all_blocks, blocks_dev):
    taken = [
        block_ids - 1,
        block_ids,
        block_ids + 1,
        jnp.zeros_like(block_ids),
        jnp.zeros_like(block_ids) + (all_blocks - 1),
    ]
    fresh = []
    for column in range(rand_blocks.shape[1]):
        chosen = rand_blocks[:, column]
        clash = reduce(jnp.logical_or, [chosen == other for other in taken])
        fresh.append(jnp.logical_not(clash))
        taken.append(chosen)
    fresh = jnp.stack(fresh, axis=1).reshape(-1)
    flat = rand_blocks.reshape(-1)
    entries = flat.shape[0]
    query = jnp.arange(entries, dtype=jnp.int32) // rand_blocks.shape[1]
    owners = jnp.arange(all_blocks // blocks_dev, dtype=jnp.int32)
    named = (flat // blocks_dev)[:, None] == owners[None, :]
    offset = jnp.sum(jnp.where(named, (flat % blocks_dev)[:, None], 0), axis=0)
    used = jnp.logical_and(named, fresh[:, None])
    where = jnp.sum(jnp.where(used, query[:, None] + 1, 0), axis=0) - 1
    return offset.astype(jnp.int32), where.astype(jnp.int32)


def body(queries, keys_values, rand_blocks, w_out):
    tok, feat = queries.shape
    blocks_dev = tok // BLOCK
    all_blocks = blocks_dev * LANES * NZ
    z = lax.axis_index("z")
    seq = lax.axis_index(SEQ)
    me = lax.axis_index(HEAD)
    first_id = seq * blocks_dev

    kv = keys_values.reshape(blocks_dev, BLOCK, 2 * feat)

    block_ids = first_id + jnp.arange(blocks_dev, dtype=jnp.int32)
    offset, where = wanted_blocks(rand_blocks, block_ids, all_blocks, blocks_dev)
    asked = jnp.broadcast_to(offset.reshape(LANES, 1, NZ), (LANES, NZ, NZ)).reshape(-1, NZ)
    asked = lax.all_to_all(asked, SEQ, split_axis=0, concat_axis=0, tiled=True)
    asked = asked.reshape(LANES, NZ, NZ)

    def asks(plane, owner):
        part = lax.dynamic_index_in_dim(asked, plane % NZ, axis=1, keepdims=False)
        return lax.dynamic_index_in_dim(part, owner % NZ, axis=1, keepdims=False)

    def for_query(owner):
        return lax.dynamic_index_in_dim(
            where.reshape(LANES, NZ), owner % NZ, axis=1, keepdims=False
        )

    up1, down1 = z_shift(kv, 1), z_shift(kv, -1)
    edge = jnp.where(z == 0, kv[0], kv[blocks_dev - 1])
    turns = [(NZ * i + NZ - 1, NZ * i + NZ) for i in range(LANES - 1)]
    crossed = lax.ppermute(edge, SEQ, turns + [(b, a) for a, b in turns])
    up2, down2 = z_shift(up1, 1), z_shift(down1, -1)
    half = LANES // 2
    up4 = z_shift(up2[asks(z + 2, z - 2)[:half]], 1)
    down4 = z_shift(down2[asks(z - 2, z + 2)[half:]], -1)
    up3 = z_shift(up2[asks(z + 1, z - 2)], 1)
    down3 = z_shift(down2[asks(z - 1, z + 2)], -1)
    far = jnp.concatenate([z_shift(up4, 1), z_shift(down4, -1)], axis=0)

    r0 = lane_exchange(kv[asks(z, z)])
    r1u = lane_exchange(up1[asks(z, z - 1)])
    r1d = lane_exchange(down1[asks(z, z + 1)])
    r2u = lane_exchange(up2[asks(z, z - 2)])
    r2d = lane_exchange(down2[asks(z, z + 2)])
    r3u = lane_exchange(up3)
    r3d = lane_exchange(down3)
    r4 = lane_exchange(far)

    plane_ends = lane_exchange(jnp.broadcast_to(edge[None], (LANES,) + edge.shape))
    held = jnp.where(z == 0, plane_ends[0], plane_ends[LANES - 1])
    got = lax.ppermute(held, "z", [(0, 4), (7, 3)])
    held = jnp.where(jnp.logical_or(z == 4, z == 3), got, held)
    got = lax.ppermute(held, "z", [(0, 2), (4, 6), (7, 5), (3, 1)])
    fresh = reduce(jnp.logical_or, [z == 2, z == 6, z == 5, z == 1])
    held = jnp.where(fresh, got, held)
    got = lax.ppermute(held, "z", [(i, i ^ 1) for i in range(NZ)])
    even = z % 2 == 0
    ends = jnp.concatenate([jnp.where(even, held, got), jnp.where(even, got, held)], axis=0)

    rows = w_out.shape[0] // 2
    ring = NXH * NXL
    lo = lax.ppermute(w_out[:rows], XRING, [(i, (i + 1) % ring) for i in range(ring)])
    hi = lax.ppermute(w_out[rows:], XRING, [(i, (i - 1) % ring) for i in range(ring)])
    swap = [(0, 1), (1, 0)]
    weights = [w_out, lax.ppermute(w_out, "core", swap), lo, hi]
    weights += [lax.ppermute(lo, "core", swap), lax.ppermute(hi, "core", swap)]

    before = jnp.where(z == 0, crossed, up1[blocks_dev - 1])
    after = jnp.where(z == NZ - 1, crossed, down1[0])
    kv_pad = jnp.concatenate([before, kv.reshape(tok, 2 * feat), after], axis=0)
    o, st = local_part(first_id.reshape(1), all_blocks, queries, kv_pad, ends)
    at = [for_query(z), for_query(z - 1), for_query(z + 1)]
    o, st = more_part(jnp.concatenate(at), queries, o, st, [r0, r1u, r1d])
    at = [for_query(z - 2), for_query(z + 2)]
    o, st = more_part(jnp.concatenate(at), queries, o, st, [r2u, r2d])
    at = [for_query(z - 3), for_query(z + 3)]
    o, st = more_part(jnp.concatenate(at), queries, o, st, [r3u, r3d])
    attended = final_part(for_query(z + 4), queries, o, st, [r4])

    heads = NXL * NC
    a = lax.all_to_all(
        attended.reshape(heads, tok // heads, feat), HEAD, split_axis=0, concat_axis=0, tiled=True
    )
    return project(me.reshape(1), a, weights)


def solution(mesh):
    fine = Mesh(mesh.devices.reshape(NY, NXH, NZ, NXL, NC), ("y", "xh", "z", "xl", "core"))
    in_specs = (P(SEQ, HEAD), P(SEQ, None, HEAD), P(SEQ, None), P(HEAD, None))
    out_specs = P(SEQ + HEAD, None)
    return jax.shard_map(body, mesh=fine, in_specs=in_specs, out_specs=out_specs, check_vma=False)
```

time: 898 us -> 390 us (0.43)
  waiting for transfers between devices: 769 us -> 131 us
  Pallas kernels: 0 us -> 91.4 us
  starting transfers between devices: 27.3 us -> 106 us
  matrix products: 16.3 us -> 0 us
  between operations: 13.8 us -> 0.33 us
    psum x1 -> x0, waiting for transfers between devices: 463 us -> none  [spread(): return lax.psum(jnp.where(mine, array, jnp.zeros_like(array)), axis)]
    ppermute x2 -> x19, waiting for transfers between devices: 172 us -> 36.8 us  [the longest x10 27.2 us: z_shift(): return lax.ppermute(x, 'z', [(i, (i + by) % NZ) for i in range(NZ)])]
    reduce_scatter x1 -> x0, waiting for transfers between devices: 125 us -> none  [body(): lax.psum_scatter(jnp.dot(attended, w_out, preferred_element_type=jnp.floa...]
    pallas_call x0 -> x6, Pallas kernels: none -> 91.4 us  [the longest x3 50.7 us: more_part(): pl.pallas_call(lambda *refs: more_kernel(len(slots), *refs), out_shape=(j...]
    all_to_all x2 -> x11, waiting for transfers between devices: 8.64 us -> 94.6 us  [the longest x9 43.8 us: lane_exchange(): return lax.all_to_all(x, LANE, split_axis=0, concat_axis=0, tiled=True)]
    all_to_all x2 -> x11, starting transfers between devices: 21 us -> 64.9 us  [the longest x9 45.6 us: lane_exchange(): return lax.all_to_all(x, LANE, split_axis=0, concat_axis=0, tiled=True)]
    ppermute x2 -> x19, starting transfers between devices: 5.99 us -> 41.4 us  [the longest x10 21.3 us: z_shift(): return lax.ppermute(x, 'z', [(i, (i + by) % NZ) for i in range(NZ)])]
    dot_general x6 -> x0, matrix products: 15.9 us -> none  [the longest x1 6.84 us: body(): jnp.dot(attended, w_out, preferred_element_type=jnp.float32)]
  transfers between devices with their start and end apart: 6 -> 30, of which waited for: 4 -> 13; matrix products, arithmetic and copies ran while one was open for 4% -> 13% of each run, Pallas kernels for 0% -> 21%
where the time goes in v1:
time: 390 us; the launch traced here: 389 us
  waiting for transfers between devices  131 us (34%)
  starting transfers between devices  106 us (27%)
  Pallas kernels  91.4 us (23%)
  local copies, waits for them, and re-layouts  47.6 us (12%)
  other arithmetic  11.5 us (3%)
    pallas_call x3, Pallas kernels, more_part(): pl.pallas_call(lambda *refs: more_kernel(len(slots), *refs), out_shape=(j...  50.7 us
    all_to_all x9, starting transfers between devices, lane_exchange(): return lax.all_to_all(x, LANE, split_axis=0, concat_axis=0, tiled=True)  45.6 us
    all_to_all x9, waiting for transfers between devices, lane_exchange(): return lax.all_to_all(x, LANE, split_axis=0, concat_axis=0, tiled=True)  43.8 us
    all_to_all x1, waiting for transfers between devices, body(): asked = lax.all_to_all(asked, SEQ, split_axis=0, concat_axis=0, tiled=True)  37.2 us
    ppermute x10, waiting for transfers between devices, z_shift(): return lax.ppermute(x, 'z', [(i, (i + by) % NZ) for i in range(NZ)])  27.2 us
    ppermute x10, starting transfers between devices, z_shift(): return lax.ppermute(x, 'z', [(i, (i + by) % NZ) for i in range(NZ)])  21.3 us
    pallas_call x1, Pallas kernels, local_part(): pl.pallas_call(lambda *refs: local_kernel(all_blocks, *refs), out_shape=(...  21 us
    all_to_all x1, waiting for transfers between devices, body(): lax.all_to_all(attended.reshape(heads, tok // heads, feat), HEAD, split_a...  13.6 us
  transfers between devices with their start and end apart: 30, of which 13 were waited for; matrix products, arithmetic and copies ran while one was open for 13% of the time, Pallas kernels for 21%

profile of v1, /device:TPU:1, one launch (start us, length us, event | category | flops | bytes accessed | tf_op | source)
XLA Modules:
  0.0 388.5 jit_solution(8224635270968804624)
XLA Ops:
  0.0 4.4 %reshape.407 = bf16[16,64,1024]{2,1,0:T(8,128)(2,1)} reshape(bf16[1024,2,512]{2,1,0:T(2,128)(2,1)} %param.5) | data formatting | bytes 4194304 | tf_op jit(solution)/shard_map/reshape | solution.py:257
  4.4 6.4 %collective-permute-start.2 = (bf16[16,64,1024]{2,1,0:T(8,128)(2,1)}, bf16[16,64,1024]{2,1,0:T(8,128)(2,1)}, u32[]{:S(2)}, u32[]{:S(2)}) collective-permute-start(bf16[16,64,1024]{2,1,0:T(8,128)(2,1)} %reshape.407), channel_id=1, source_target_pairs={{0,28},{4,0},{8,4},{12,8},{16,12},{20,16},{24,20},{28,24},{1,29},{... | collective-permute-start | bytes 6291464 | tf_op jit(solution)/shard_map/ppermute | solution.py:215
  12.6 9.0 %all-to-all-start.1 = ((s32[64,1,8]{2,1,0:T(1,128)}), s32[64,1,8]{2,1,0:T(1,128)S(1)}, u32[]{:S(2)}, u32[]{:S(2)}) async-start(s32[64,1,8]{2,1,0:T(1,128)} %bitcast.5), calls=%async_computation.1 | async-start | bytes 65536 | tf_op jit(solution)/shard_map/all_to_all | solution.py:262
  22.7 37.2 %all-to-all-done.1 = s32[64,1,8]{2,1,0:T(1,128)S(1)} async-done(((s32[64,1,8]{2,1,0:T(1,128)}), s32[64,1,8]{2,1,0:T(1,128)S(1)}, u32[]{:S(2)}, u32[]{:S(2)}) %all-to-all-start.1) | async-done | bytes 2080 | tf_op jit(solution)/shard_map/all_to_all | solution.py:262
  61.1 3.6 all-to-all-start
  64.7 3.9 collective-permute-start.1
  68.8 3.2 gather_fusion
  72.0 7.8 %all-to-all-done = bf16[8,64,1024]{2,1,0:T(8,128)(2,1)S(1)} async-done(((bf16[8,64,1024]{2,1,0:T(8,128)(2,1)}), bf16[8,64,1024]{2,1,0:T(8,128)(2,1)S(1)}, u32[]{:S(2)}, u32[]{:S(2)}) %all-to-all-start) | async-done | bytes 1048608 | tf_op jit(solution)/shard_map/all_to_all | solution.py:219
  80.8 4.1 %all-to-all-start.2 = ((bf16[8,64,1024]{2,1,0:T(8,128)(2,1)}), bf16[8,64,1024]{2,1,0:T(8,128)(2,1)S(1)}, u32[]{:S(2)}, u32[]{:S(2)}) async-start(bf16[8,64,1024]{2,1,0:T(8,128)(2,1)} %gather_fusion), calls=%async_computation.2 | async-start | bytes 2097152 | tf_op jit(solution)/shard_map/all_to_all | solution.py:219
  85.0 4.2 %collective-permute-start.7 = (bf16[16,64,1024]{2,1,0:T(8,128)(2,1)}, bf16[16,64,1024]{2,1,0:T(8,128)(2,1)}, u32[]{:S(2)}, u32[]{:S(2)}) collective-permute-start(bf16[16,64,1024]{2,1,0:T(8,128)(2,1)} %collective-permute-done.2), channel_id=1, source_target_pairs={{0,28},{4,0},{8,4},{12,8},{16,12},{20,16},{24,20},{28,24},{1,29},{... | collective-permute-start | bytes 6291464 | tf_op jit(solution)/shard_map/ppermute | solution.py:215
  89.2 3.2 gather_fusion.2
  92.5 7.4 %all-to-all-done.2.refs_4_ = bf16[8,64,1024]{2,1,0:T(8,128)(2,1)S(1)} async-done(((bf16[8,64,1024]{2,1,0:T(8,128)(2,1)}), bf16[8,64,1024]{2,1,0:T(8,128)(2,1)S(1)}, u32[]{:S(2)}, u32[]{:S(2)}) %all-to-all-start.2) | async-done | bytes 1048608 | tf_op jit(solution)/shard_map/all_to_all | solution.py:219
  99.8 3.6 all-to-all-start.4
  103.5 9.9 %collective-permute-done.1 = bf16[16,64,1024]{2,1,0:T(8,128)(2,1)} collective-permute-done((bf16[16,64,1024]{2,1,0:T(8,128)(2,1)}, bf16[16,64,1024]{2,1,0:T(8,128)(2,1)}, u32[]{:S(2)}, u32[]{:S(2)}) %collective-permute-start.1) | collective-permute-done | bytes 2097184 | tf_op jit(solution)/shard_map/ppermute | solution.py:215
  113.9 3.2 gather_fusion.1
  117.3 6.0 %all-to-all-start.3 = ((bf16[8,64,1024]{2,1,0:T(8,128)(2,1)}), bf16[8,64,1024]{2,1,0:T(8,128)(2,1)S(1)}, u32[]{:S(2)}, u32[]{:S(2)}) async-start(bf16[8,64,1024]{2,1,0:T(8,128)(2,1)} %gather_fusion.1), calls=%async_computation.3 | async-start | bytes 2097152 | tf_op jit(solution)/shard_map/all_to_all | solution.py:219
  123.4 8.6 %collective-permute-done.7 = bf16[16,64,1024]{2,1,0:T(8,128)(2,1)} collective-permute-done((bf16[16,64,1024]{2,1,0:T(8,128)(2,1)}, bf16[16,64,1024]{2,1,0:T(8,128)(2,1)}, u32[]{:S(2)}, u32[]{:S(2)}) %collective-permute-start.7) | collective-permute-done | bytes 2097184 | tf_op jit(solution)/shard_map/ppermute | solution.py:215
  132.0 3.2 gather_fusion.4
  136.4 5.2 %all-to-all-start.6 = ((bf16[8,64,1024]{2,1,0:T(8,128)(2,1)}), bf16[8,64,1024]{2,1,0:T(8,128)(2,1)}, u32[]{:S(2)}, u32[]{:S(2)}) async-start(bf16[8,64,1024]{2,1,0:T(8,128)(2,1)} %gather_fusion.4), calls=%async_computation.6 | async-start | bytes 2097152 | tf_op jit(solution)/shard_map/all_to_all | solution.py:219
  141.6 4.2 %collective-permute-start.14 = (bf16[512,4096]{1,0:T(8,128)(2,1)}, bf16[512,4096]{1,0:T(8,128)(2,1)}, u32[]{:S(2)}, u32[]{:S(2)}) collective-permute-start(bf16[512,4096]{1,0:T(8,128)(2,1)} %own_ref.1), channel_id=1, source_target_pairs={{0,1},{1,0},{2,3},{3,2},{4,5},{5,4},{6,7},{7,6},{8,9},{9,8},{10,11... | collective-permute-start | bytes 12582920 | tf_op jit(solution)/shard_map/ppermute | solution.py:311
  146.1 3.2 gather_fusion.6
  149.3 3.1 collective-permute-start.9
  152.4 7.2 %collective-permute-done.6 = bf16[16,64,1024]{2,1,0:T(8,128)(2,1)} collective-permute-done((bf16[16,64,1024]{2,1,0:T(8,128)(2,1)}, bf16[16,64,1024]{2,1,0:T(8,128)(2,1)}, u32[]{:S(2)}, u32[]{:S(2)}) %collective-permute-start.6) | collective-permute-done | bytes 2097184 | tf_op jit(solution)/shard_map/ppermute | solution.py:215
  159.6 3.2 gather_fusion.3
  162.8 5.9 %all-to-all-start.5 = ((bf16[8,64,1024]{2,1,0:T(8,128)(2,1)}), bf16[8,64,1024]{2,1,0:T(8,128)(2,1)S(1)}, u32[]{:S(2)}, u32[]{:S(2)}) async-start(bf16[8,64,1024]{2,1,0:T(8,128)(2,1)} %gather_fusion.3), calls=%async_computation.5 | async-start | bytes 2097152 | tf_op jit(solution)/shard_map/all_to_all | solution.py:219
  168.7 4.7 %fusion.16 = (bf16[256,4096]{1,0:T(8,128)(2,1)}, bf16[256,4096]{1,0:T(8,128)(2,1)}) fusion(bf16[512,4096]{1,0:T(8,128)(2,1)} %own_ref.1), kind=kLoop, calls=%fused_computation.90 | loop fusion | bytes 8388608 | tf_op jit(solution)/shard_map/slice | solution.py:309
  173.4 2.7 collective-permute-start.16
  176.5 3.2 gather_fusion.5
  180.7 5.2 %collective-permute-start.3 = (bf16[64,1024]{1,0:T(8,128)(2,1)S(1)}, bf16[64,1024]{1,0:T(8,128)(2,1)}, u32[]{:S(2)}, u32[]{:S(2)}) collective-permute-start(bf16[64,1024]{1,0:T(8,128)(2,1)S(1)} %fusion), channel_id=1, source_target_pairs={{0,16},{28,12},{1,17},{29,13},{2,18},{30,14},{3,19},{31,15},{32,48... | collective-permute-start | bytes 393224 | tf_op jit(solution)/shard_map/ppermute | solution.py:297
  186.0 5.4 %all-to-all-start.8 = ((bf16[8,64,1024]{2,1,0:T(8,128)(2,1)}), bf16[8,64,1024]{2,1,0:T(8,128)(2,1)}, u32[]{:S(2)}, u32[]{:S(2)}) async-start(bf16[8,64,1024]{2,1,0:T(8,128)(2,1)} %collective-permute-done.9), calls=%async_computation.8 | async-start | bytes 2097152 | tf_op jit(solution)/shard_map/all_to_all | solution.py:219
  191.4 9.6 %collective-permute-done.3 = bf16[64,1024]{1,0:T(8,128)(2,1)} collective-permute-done((bf16[64,1024]{1,0:T(8,128)(2,1)S(1)}, bf16[64,1024]{1,0:T(8,128)(2,1)}, u32[]{:S(2)}, u32[]{:S(2)}) %collective-permute-start.3) | collective-permute-done | bytes 131104 | tf_op jit(solution)/shard_map/ppermute | solution.py:297
  203.3 3.0 gather_fusion.8
  206.3 3.0 gather_fusion.7
  211.0 27.1 %all-to-all-done.8.refs_5_ = bf16[8,64,1024]{2,1,0:T(8,128)(2,1)} async-done(((bf16[8,64,1024]{2,1,0:T(8,128)(2,1)}), bf16[8,64,1024]{2,1,0:T(8,128)(2,1)}, u32[]{:S(2)}, u32[]{:S(2)}) %all-to-all-start.8) | async-done | bytes 1048608 | tf_op jit(solution)/shard_map/all_to_all | solution.py:219
  238.0 3.6 all-to-all-start.7
  241.7 3.5 copy.32
  247.3 5.8 %collective-permute-start.18 = (bf16[256,4096]{1,0:T(8,128)(2,1)}, bf16[256,4096]{1,0:T(8,128)(2,1)}, u32[]{:S(2)}, u32[]{:S(2)}) collective-permute-start(bf16[256,4096]{1,0:T(8,128)(2,1)} %collective-permute-done.16.hi_ref), channel_id=1, source_target_pairs={{0,1},{1,0},{2,3},{3,2},{4,5},{5,4},{6,7},{7,6},{8,9},{9,8},{10,11... | collective-permute-start | bytes 6291464 | tf_op jit(solution)/shard_map/ppermute | solution.py:312
  256.7 8.3 %all-to-all-start.9 = ((bf16[8,64,1024]{2,1,0:T(8,128)(2,1)}), bf16[8,64,1024]{2,1,0:T(8,128)(2,1)}, u32[]{:S(2)}, u32[]{:S(2)}) async-start(bf16[8,64,1024]{2,1,0:T(8,128)(2,1)} %pad_maximum_fusion.1), calls=%async_computation.9 | async-start | bytes 2097152 | tf_op jit(solution)/shard_map/all_to_all | solution.py:219
  267.0 3.3 pad_maximum_fusion.refs_2_
  270.3 21.0 %local_part.1 = (f32[1024,512]{1,0:T(8,128)S(1)}, f32[1024,128]{1,0:T(8,128)S(1)}) custom-call(s32[1]{0:T(128)} %bitcast.1.refs_0_, bf16[1024,512]{1,0:T(8,128)(2,1)S(1)} %copy-done, bf16[1152,1024]{1,0:T(8,128)(2,1)} %pad_maximum_fusion.refs_2_, bf16[128,1024]{1,0:T(8,128)(2,1)S(1)} %pad_maximum_fusion.2.refs_3_), custom_call_target="tpu_custom_call" | custom-call | flops 671088640 | bytes 8388608 | tf_op jit(solution)/shard_map/local_part/pallas_call | solution.py:133
  292.7 21.4 %more_part.3 = (f32[1024,512]{1,0:T(8,128)}, f32[1024,128]{1,0:T(8,128)S(1)}) custom-call(s32[24]{0:T(128)S(1)} %pad_add_fusion.3.refs_0_, bf16[1024,512]{1,0:T(8,128)(2,1)S(1)} %copy-done, f32[1024,512]{1,0:T(8,128)} %copy-done.8, f32[1024,128]{1,0:T(8,128)S(1)} %get-tuple-element.14.refs_3_, bf16[8,64,1024]{2,1,0:T(8,128)(2,1)S(1)} %all-to-all-done.2.refs_4_, ...), custom_call_target="tpu_custom_call" | custom-call | flops 67108864 | bytes 8388608 | tf_op jit(solution)/shard_map/more_part/pallas_call | solution.py:151
  314.1 13.3 %more_part.4 = (f32[1024,512]{1,0:T(8,128)}, f32[1024,128]{1,0:T(8,128)S(1)}) custom-call(s32[16]{0:T(128)S(1)} %pad_add_fusion.2.refs_0_, bf16[1024,512]{1,0:T(8,128)(2,1)S(1)} %copy-done, f32[1024,512]{1,0:T(8,128)} %get-tuple-element.15.refs_2_, f32[1024,128]{1,0:T(8,128)S(1)} %get-tuple-element.16.refs_3_, bf16[8,64,1024]{2,1,0:T(8,128)(2,1)S(1)} %copy-done.4, ...), custom_call_target="tpu_custom_call" | custom-call | flops 67108864 | bytes 8388608 | tf_op jit(solution)/shard_map/more_part/pallas_call | solution.py:151
  327.4 16.0 %more_part.5 = (f32[1024,512]{1,0:T(8,128)}, f32[1024,128]{1,0:T(8,128)S(1)}) custom-call(s32[16]{0:T(128)S(1)} %pad_add_fusion.1.refs_0_, bf16[1024,512]{1,0:T(8,128)(2,1)S(1)} %copy-done, f32[1024,512]{1,0:T(8,128)} %get-tuple-element.17.refs_2_, f32[1024,128]{1,0:T(8,128)S(1)} %get-tuple-element.18.refs_3_, bf16[8,64,1024]{2,1,0:T(8,128)(2,1)S(1)} %copy-done.6, ...), custom_call_target="tpu_custom_call" | custom-call | flops 67108864 | bytes 8388608 | tf_op jit(solution)/shard_map/more_part/pallas_call | solution.py:151
  343.4 1.6 copy-done.7
  345.0 8.4 %final_part.1 = bf16[1024,512]{1,0:T(8,128)(2,1)} custom-call(s32[8]{0:T(128)S(1)} %get-tuple-element.28.refs_0_, bf16[1024,512]{1,0:T(8,128)(2,1)S(1)} %copy-done, f32[1024,512]{1,0:T(8,128)S(1)} %copy-done.7, f32[1024,128]{1,0:T(8,128)S(1)} %get-tuple-element.20.refs_3_, bf16[8,64,1024]{2,1,0:T(8,128)(2,1)} %all-to-all-done.9.refs_4_), custom_call_target="tpu_custom_call" | custom-call | tf_op jit(solution)/shard_map/final_part/pallas_call | solution.py:169
  353.5 10.3 %all-to-all-start.10 = ((bf16[4,256,512]{2,1,0:T(8,128)(2,1)}), bf16[4,256,512]{2,1,0:T(8,128)(2,1)S(1)}, u32[]{:S(2)}, u32[]{:S(2)}) async-start(bf16[4,256,512]{2,1,0:T(8,128)(2,1)} %bitcast.16), calls=%async_computation.10 | async-start | bytes 2097152 | tf_op jit(solution)/shard_map/all_to_all | solution.py:327
  363.8 13.6 %all-to-all-done.10.a_ref = bf16[4,256,512]{2,1,0:T(8,128)(2,1)S(1)} async-done(((bf16[4,256,512]{2,1,0:T(8,128)(2,1)}), bf16[4,256,512]{2,1,0:T(8,128)(2,1)S(1)}, u32[]{:S(2)}, u32[]{:S(2)}) %all-to-all-start.10) | async-done | bytes 1048608 | tf_op jit(solution)/shard_map/all_to_all | solution.py:327
  377.4 11.1 %project.1 = bf16[256,4096]{1,0:T(8,128)(2,1)} custom-call(s32[1]{0:T(128)} %bitcast.me_ref, bf16[4,256,512]{2,1,0:T(8,128)(2,1)S(1)} %all-to-all-done.10.a_ref, bf16[512,4096]{1,0:T(8,128)(2,1)} %own_ref.1, bf16[512,4096]{1,0:T(8,128)(2,1)} %collective-permute-done.14.core_ref, bf16[256,4096]{1,0:T(8,128)(2,1)} %collective-permute-done.15.lo_ref, ...), custom_call_target="tpu_custom_call" | custom-call | tf_op jit(solution)/shard_map/project/pallas_call | solution.py:199
  (112 shorter events, 22.3 us)
Async XLA Ops:
  0.0 10.8 %copy-start.11 = (s32[16,2]{0,1:T(2,128)S(1)}, s32[16,2]{0,1:T(2,128)}, u32[]{:S(2)}) copy-start(s32[16,2]{0,1:T(2,128)} %param.6) | copy-start | bytes 388
  4.4 80.6 %collective-permute-start.2 = (bf16[16,64,1024]{2,1,0:T(8,128)(2,1)}, bf16[16,64,1024]{2,1,0:T(8,128)(2,1)}, u32[]{:S(2)}, u32[]{:S(2)}) collective-permute-start(bf16[16,64,1024]{2,1,0:T(8,128)(2,1)} %reshape.407), channel_id=1, source_target_pairs={{0,28},{4,0},{8,4},{12,8},{16,12},{20,16},{24,20},{28,24},{1,29},{... | collective-permute-start | bytes 6291464 | tf_op jit(solution)/shard_map/ppermute | solution.py:215
  12.6 47.4 %all-to-all-start.1 = ((s32[64,1,8]{2,1,0:T(1,128)}), s32[64,1,8]{2,1,0:T(1,128)S(1)}, u32[]{:S(2)}, u32[]{:S(2)}) async-start(s32[64,1,8]{2,1,0:T(1,128)} %bitcast.5), calls=%async_computation.1 | async-start | bytes 65536 | tf_op jit(solution)/shard_map/all_to_all | solution.py:262
  61.1 18.7 %all-to-all-start = ((bf16[8,64,1024]{2,1,0:T(8,128)(2,1)}), bf16[8,64,1024]{2,1,0:T(8,128)(2,1)S(1)}, u32[]{:S(2)}, u32[]{:S(2)}) async-start(bf16[8,64,1024]{2,1,0:T(8,128)(2,1)} %broadcast_in_dim.26), calls=%async_computation | async-start | bytes 2097152 | tf_op jit(solution)/shard_map/all_to_all | solution.py:219
  64.7 48.8 %collective-permute-start.1 = (bf16[16,64,1024]{2,1,0:T(8,128)(2,1)}, bf16[16,64,1024]{2,1,0:T(8,128)(2,1)}, u32[]{:S(2)}, u32[]{:S(2)}) collective-permute-start(bf16[16,64,1024]{2,1,0:T(8,128)(2,1)} %reshape.407), channel_id=1, source_target_pairs={{0,4},{4,8},{8,12},{12,16},{16,20},{20,24},{24,28},{28,0},{1,5},{5... | collective-permute-start | bytes 6291464 | tf_op jit(solution)/shard_map/ppermute | solution.py:215
  79.8 1.0 copy-start.9
  80.8 19.0 %all-to-all-start.2 = ((bf16[8,64,1024]{2,1,0:T(8,128)(2,1)}), bf16[8,64,1024]{2,1,0:T(8,128)(2,1)S(1)}, u32[]{:S(2)}, u32[]{:S(2)}) async-start(bf16[8,64,1024]{2,1,0:T(8,128)(2,1)} %gather_fusion), calls=%async_computation.2 | async-start | bytes 2097152 | tf_op jit(solution)/shard_map/all_to_all | solution.py:219
  85.0 47.0 %collective-permute-start.7 = (bf16[16,64,1024]{2,1,0:T(8,128)(2,1)}, bf16[16,64,1024]{2,1,0:T(8,128)(2,1)}, u32[]{:S(2)}, u32[]{:S(2)}) collective-permute-start(bf16[16,64,1024]{2,1,0:T(8,128)(2,1)} %collective-permute-done.2), channel_id=1, source_target_pairs={{0,28},{4,0},{8,4},{12,8},{16,12},{20,16},{24,20},{28,24},{1,29},{... | collective-permute-start | bytes 6291464 | tf_op jit(solution)/shard_map/ppermute | solution.py:215
  99.8 17.5 %all-to-all-start.4 = ((bf16[8,64,1024]{2,1,0:T(8,128)(2,1)}), bf16[8,64,1024]{2,1,0:T(8,128)(2,1)S(1)}, u32[]{:S(2)}, u32[]{:S(2)}) async-start(bf16[8,64,1024]{2,1,0:T(8,128)(2,1)} %gather_fusion.2), calls=%async_computation.4 | async-start | bytes 2097152 | tf_op jit(solution)/shard_map/all_to_all | solution.py:219
  113.4 46.2 %collective-permute-start.6 = (bf16[16,64,1024]{2,1,0:T(8,128)(2,1)}, bf16[16,64,1024]{2,1,0:T(8,128)(2,1)}, u32[]{:S(2)}, u32[]{:S(2)}) collective-permute-start(bf16[16,64,1024]{2,1,0:T(8,128)(2,1)} %collective-permute-done.1), channel_id=1, source_target_pairs={{0,4},{4,8},{8,12},{12,16},{16,20},{20,24},{24,28},{28,0},{1,5},{5... | collective-permute-start | bytes 6291464 | tf_op jit(solution)/shard_map/ppermute | solution.py:215
  117.3 19.1 %all-to-all-start.3 = ((bf16[8,64,1024]{2,1,0:T(8,128)(2,1)}), bf16[8,64,1024]{2,1,0:T(8,128)(2,1)S(1)}, u32[]{:S(2)}, u32[]{:S(2)}) async-start(bf16[8,64,1024]{2,1,0:T(8,128)(2,1)} %gather_fusion.1), calls=%async_computation.3 | async-start | bytes 2097152 | tf_op jit(solution)/shard_map/all_to_all | solution.py:219
  136.4 12.8 %copy-start.1 = (bf16[8,64,1024]{2,1,0:T(8,128)(2,1)}, bf16[8,64,1024]{2,1,0:T(8,128)(2,1)S(1)}, u32[]{:S(2)}) copy-start(bf16[8,64,1024]{2,1,0:T(8,128)(2,1)S(1)} %all-to-all-done.3.refs_5_) | copy-start | bytes 3145732
  136.4 26.3 %all-to-all-start.6 = ((bf16[8,64,1024]{2,1,0:T(8,128)(2,1)}), bf16[8,64,1024]{2,1,0:T(8,128)(2,1)}, u32[]{:S(2)}, u32[]{:S(2)}) async-start(bf16[8,64,1024]{2,1,0:T(8,128)(2,1)} %gather_fusion.4), calls=%async_computation.6 | async-start | bytes 2097152 | tf_op jit(solution)/shard_map/all_to_all | solution.py:219
  141.6 222.1 %collective-permute-start.14 = (bf16[512,4096]{1,0:T(8,128)(2,1)}, bf16[512,4096]{1,0:T(8,128)(2,1)}, u32[]{:S(2)}, u32[]{:S(2)}) collective-permute-start(bf16[512,4096]{1,0:T(8,128)(2,1)} %own_ref.1), channel_id=1, source_target_pairs={{0,1},{1,0},{2,3},{3,2},{4,5},{5,4},{6,7},{7,6},{8,9},{9,8},{10,11... | collective-permute-start | bytes 12582920 | tf_op jit(solution)/shard_map/ppermute | solution.py:311
  149.3 31.5 %collective-permute-start.9 = (bf16[8,64,1024]{2,1,0:T(8,128)(2,1)}, bf16[8,64,1024]{2,1,0:T(8,128)(2,1)}, u32[]{:S(2)}, u32[]{:S(2)}) collective-permute-start(bf16[8,64,1024]{2,1,0:T(8,128)(2,1)} %gather_fusion.6), channel_id=1, source_target_pairs={{0,28},{4,0},{8,4},{12,8},{16,12},{20,16},{24,20},{28,24},{1,29},{... | collective-permute-start | bytes 3145736 | tf_op jit(solution)/shard_map/ppermute | solution.py:215
  162.8 23.2 %all-to-all-start.5 = ((bf16[8,64,1024]{2,1,0:T(8,128)(2,1)}), bf16[8,64,1024]{2,1,0:T(8,128)(2,1)S(1)}, u32[]{:S(2)}, u32[]{:S(2)}) async-start(bf16[8,64,1024]{2,1,0:T(8,128)(2,1)} %gather_fusion.3), calls=%async_computation.5 | async-start | bytes 2097152 | tf_op jit(solution)/shard_map/all_to_all | solution.py:219
  173.4 73.9 %collective-permute-start.16 = (bf16[256,4096]{1,0:T(8,128)(2,1)}, bf16[256,4096]{1,0:T(8,128)(2,1)}, u32[]{:S(2)}, u32[]{:S(2)}) collective-permute-start(bf16[256,4096]{1,0:T(8,128)(2,1)} %get-tuple-element.31), channel_id=1, source_target_pairs={{0,34},{2,0},{32,2},{34,32},{1,35},{3,1},{33,3},{35,33},{4,38},{6,... | collective-permute-start | bytes 6291464 | tf_op jit(solution)/shard_map/ppermute | solution.py:309
  176.1 77.0 %collective-permute-start.15 = (bf16[256,4096]{1,0:T(8,128)(2,1)}, bf16[256,4096]{1,0:T(8,128)(2,1)}, u32[]{:S(2)}, u32[]{:S(2)}) collective-permute-start(bf16[256,4096]{1,0:T(8,128)(2,1)} %get-tuple-element.32), channel_id=1, source_target_pairs={{0,2},{2,32},{32,34},{34,0},{1,3},{3,33},{33,35},{35,1},{4,6},{6,3... | collective-permute-start | bytes 6291464 | tf_op jit(solution)/shard_map/ppermute | solution.py:308
  179.7 29.8 %collective-permute-start.8 = (bf16[8,64,1024]{2,1,0:T(8,128)(2,1)}, bf16[8,64,1024]{2,1,0:T(8,128)(2,1)}, u32[]{:S(2)}, u32[]{:S(2)}) collective-permute-start(bf16[8,64,1024]{2,1,0:T(8,128)(2,1)} %gather_fusion.5), channel_id=1, source_target_pairs={{0,4},{4,8},{8,12},{12,16},{16,20},{20,24},{24,28},{28,0},{1,5},{5... | collective-permute-start | bytes 3145736 | tf_op jit(solution)/shard_map/ppermute | solution.py:215
  180.7 20.2 %collective-permute-start.3 = (bf16[64,1024]{1,0:T(8,128)(2,1)S(1)}, bf16[64,1024]{1,0:T(8,128)(2,1)}, u32[]{:S(2)}, u32[]{:S(2)}) collective-permute-start(bf16[64,1024]{1,0:T(8,128)(2,1)S(1)} %fusion), channel_id=1, source_target_pairs={{0,16},{28,12},{1,17},{29,13},{2,18},{30,14},{3,19},{31,15},{32,48... | collective-permute-start | bytes 393224 | tf_op jit(solution)/shard_map/ppermute | solution.py:297
  185.9 23.3 %copy-start.3 = (bf16[8,64,1024]{2,1,0:T(8,128)(2,1)}, bf16[8,64,1024]{2,1,0:T(8,128)(2,1)S(1)}, u32[]{:S(2)}) copy-start(bf16[8,64,1024]{2,1,0:T(8,128)(2,1)S(1)} %all-to-all-done.5.refs_4_) | copy-start | bytes 3145732
  186.0 52.1 %all-to-all-start.8 = ((bf16[8,64,1024]{2,1,0:T(8,128)(2,1)}), bf16[8,64,1024]{2,1,0:T(8,128)(2,1)}, u32[]{:S(2)}, u32[]{:S(2)}) async-start(bf16[8,64,1024]{2,1,0:T(8,128)(2,1)} %collective-permute-done.9), calls=%async_computation.8 | async-start | bytes 2097152 | tf_op jit(solution)/shard_map/all_to_all | solution.py:219
  201.9 7.3 %collective-permute-start.4 = (bf16[64,1024]{1,0:T(8,128)(2,1)S(1)}, bf16[64,1024]{1,0:T(8,128)(2,1)S(1)}, u32[]{:S(2)}, u32[]{:S(2)}) collective-permute-start(bf16[64,1024]{1,0:T(8,128)(2,1)S(1)} %broadcast_select_fusion.1), channel_id=1, source_target_pairs={{0,8},{16,24},{28,20},{12,4},{1,9},{17,25},{29,21},{13,5},{2,10},{... | collective-permute-start | bytes 393224 | tf_op jit(solution)/shard_map/ppermute | solution.py:299
  203.3 38.3 %copy-start.12 = (s32[64]{0:T(128)S(1)}, s32[64]{0:T(128)}, u32[]{:S(2)}) copy-start(s32[64]{0:T(128)} %get-tuple-element.30) | copy-start | bytes 772
  209.3 35.9 %copy-start.10 = (bf16[64,1024]{1,0:T(8,128)(2,1)}, bf16[64,1024]{1,0:T(8,128)(2,1)S(1)}, u32[]{:S(2)}) copy-start(bf16[64,1024]{1,0:T(8,128)(2,1)S(1)} %collective-permute-done.4) | copy-start | bytes 393220
  209.3 36.2 %collective-permute-start.12 = (bf16[4,64,1024]{2,1,0:T(8,128)(2,1)}, bf16[4,64,1024]{2,1,0:T(8,128)(2,1)}, u32[]{:S(2)}, u32[]{:S(2)}) collective-permute-start(bf16[4,64,1024]{2,1,0:T(8,128)(2,1)} %gather_fusion.8), channel_id=1, source_target_pairs={{0,28},{4,0},{8,4},{12,8},{16,12},{20,16},{24,20},{28,24},{1,29},{... | collective-permute-start | bytes 1572872 | tf_op jit(solution)/shard_map/ppermute | solution.py:215
  209.5 36.0 %collective-permute-start.10 = (bf16[4,64,1024]{2,1,0:T(8,128)(2,1)}, bf16[4,64,1024]{2,1,0:T(8,128)(2,1)}, u32[]{:S(2)}, u32[]{:S(2)}) collective-permute-start(bf16[4,64,1024]{2,1,0:T(8,128)(2,1)} %gather_fusion.7), channel_id=1, source_target_pairs={{0,4},{4,8},{8,12},{12,16},{16,20},{20,24},{24,28},{28,0},{1,5},{5... | collective-permute-start | bytes 1572872 | tf_op jit(solution)/shard_map/ppermute | solution.py:215
  238.0 18.6 %all-to-all-start.7 = ((bf16[8,64,1024]{2,1,0:T(8,128)(2,1)}), bf16[8,64,1024]{2,1,0:T(8,128)(2,1)S(1)}, u32[]{:S(2)}, u32[]{:S(2)}) async-start(bf16[8,64,1024]{2,1,0:T(8,128)(2,1)} %collective-permute-done.8), calls=%async_computation.7 | async-start | bytes 2097152 | tf_op jit(solution)/shard_map/all_to_all | solution.py:219
  245.5 8.6 %collective-permute-start.13 = (bf16[4,64,1024]{2,1,0:T(8,128)(2,1)}, bf16[4,64,1024]{2,1,0:T(8,128)(2,1)S(1)}, u32[]{:S(2)}, u32[]{:S(2)}) collective-permute-start(bf16[4,64,1024]{2,1,0:T(8,128)(2,1)} %collective-permute-done.12), channel_id=1, source_target_pairs={{0,28},{4,0},{8,4},{12,8},{16,12},{20,16},{24,20},{28,24},{1,29},{... | collective-permute-start | bytes 1572872 | tf_op jit(solution)/shard_map/ppermute | solution.py:215
  245.6 9.8 %collective-permute-start.11 = (bf16[4,64,1024]{2,1,0:T(8,128)(2,1)}, bf16[4,64,1024]{2,1,0:T(8,128)(2,1)S(1)}, u32[]{:S(2)}, u32[]{:S(2)}) collective-permute-start(bf16[4,64,1024]{2,1,0:T(8,128)(2,1)} %collective-permute-done.10), channel_id=1, source_target_pairs={{0,4},{4,8},{8,12},{12,16},{16,20},{20,24},{24,28},{28,0},{1,5},{5... | collective-permute-start | bytes 1572872 | tf_op jit(solution)/shard_map/ppermute | solution.py:215
  247.3 116.5 %collective-permute-start.18 = (bf16[256,4096]{1,0:T(8,128)(2,1)}, bf16[256,4096]{1,0:T(8,128)(2,1)}, u32[]{:S(2)}, u32[]{:S(2)}) collective-permute-start(bf16[256,4096]{1,0:T(8,128)(2,1)} %collective-permute-done.16.hi_ref), channel_id=1, source_target_pairs={{0,1},{1,0},{2,3},{3,2},{4,5},{5,4},{6,7},{7,6},{8,9},{9,8},{10,11... | collective-permute-start | bytes 6291464 | tf_op jit(solution)/shard_map/ppermute | solution.py:312
  253.1 110.7 %collective-permute-start.17 = (bf16[256,4096]{1,0:T(8,128)(2,1)}, bf16[256,4096]{1,0:T(8,128)(2,1)}, u32[]{:S(2)}, u32[]{:S(2)}) collective-permute-start(bf16[256,4096]{1,0:T(8,128)(2,1)} %collective-permute-done.15.lo_ref), channel_id=1, source_target_pairs={{0,1},{1,0},{2,3},{3,2},{4,5},{5,4},{6,7},{7,6},{8,9},{9,8},{10,11... | collective-permute-start | bytes 6291464 | tf_op jit(solution)/shard_map/ppermute | solution.py:312
  254.1 11.8 %collective-permute-start = (bf16[64,1024]{1,0:T(8,128)(2,1)S(1)}, bf16[64,1024]{1,0:T(8,128)(2,1)S(1)}, u32[]{:S(2)}, u32[]{:S(2)}) collective-permute-start(bf16[64,1024]{1,0:T(8,128)(2,1)S(1)} %bitcast.71), channel_id=1, source_target_pairs={{28,32},{60,64},{92,96},{124,128},{156,160},{188,192},{220,224},{3... | collective-permute-start | bytes 393224 | tf_op jit(solution)/shard_map/ppermute | solution.py:277
  255.4 9.6 %collective-permute-start.5 = (bf16[64,1024]{1,0:T(8,128)(2,1)S(1)}, bf16[64,1024]{1,0:T(8,128)(2,1)}, u32[]{:S(2)}, u32[]{:S(2)}) collective-permute-start(bf16[64,1024]{1,0:T(8,128)(2,1)S(1)} %broadcast_select_fusion.2), channel_id=1, source_target_pairs={{0,4},{4,0},{8,12},{12,8},{16,20},{20,16},{24,28},{28,24},{1,5},{5... | collective-permute-start | bytes 393224 | tf_op jit(solution)/shard_map/ppermute | solution.py:302
  256.7 10.3 %copy-start.5 = (bf16[8,64,1024]{2,1,0:T(8,128)(2,1)}, bf16[8,64,1024]{2,1,0:T(8,128)(2,1)S(1)}, u32[]{:S(2)}) copy-start(bf16[8,64,1024]{2,1,0:T(8,128)(2,1)S(1)} %all-to-all-done.7.refs_4_) | copy-start | bytes 3145732
  256.7 86.8 %all-to-all-start.9 = ((bf16[8,64,1024]{2,1,0:T(8,128)(2,1)}), bf16[8,64,1024]{2,1,0:T(8,128)(2,1)}, u32[]{:S(2)}, u32[]{:S(2)}) async-start(bf16[8,64,1024]{2,1,0:T(8,128)(2,1)} %pad_maximum_fusion.1), calls=%async_computation.9 | async-start | bytes 2097152 | tf_op jit(solution)/shard_map/all_to_all | solution.py:219
  267.0 3.3 copy-start
  270.3 22.4 %copy-start.2 = (bf16[8,64,1024]{2,1,0:T(8,128)(2,1)S(1)}, bf16[8,64,1024]{2,1,0:T(8,128)(2,1)}, u32[]{:S(2)}) copy-start(bf16[8,64,1024]{2,1,0:T(8,128)(2,1)} %copy-done.1) | copy-start | bytes 3145732
  291.4 1.3 copy-start.8
  292.7 21.5 %copy-start.4 = (bf16[8,64,1024]{2,1,0:T(8,128)(2,1)S(1)}, bf16[8,64,1024]{2,1,0:T(8,128)(2,1)}, u32[]{:S(2)}) copy-start(bf16[8,64,1024]{2,1,0:T(8,128)(2,1)} %copy-done.3) | copy-start | bytes 3145732
  314.1 13.3 %copy-start.6 = (bf16[8,64,1024]{2,1,0:T(8,128)(2,1)S(1)}, bf16[8,64,1024]{2,1,0:T(8,128)(2,1)}, u32[]{:S(2)}) copy-start(bf16[8,64,1024]{2,1,0:T(8,128)(2,1)} %copy-done.5) | copy-start | bytes 3145732
  343.4 1.6 copy-start.7
  353.5 23.9 %all-to-all-start.10 = ((bf16[4,256,512]{2,1,0:T(8,128)(2,1)}), bf16[4,256,512]{2,1,0:T(8,128)(2,1)S(1)}, u32[]{:S(2)}, u32[]{:S(2)}) async-start(bf16[4,256,512]{2,1,0:T(8,128)(2,1)} %bitcast.16), calls=%async_computation.10 | async-start | bytes 2097152 | tf_op jit(solution)/shard_map/all_to_all | solution.py:327

commit v2 on v1

v2 whole, which is shorter than its diff:
```python
from functools import reduce

import jax
import jax.numpy as jnp
from jax import lax
from jax.experimental import pallas as pl
from jax.experimental.pallas import tpu as pltpu
from jax.sharding import Mesh, PartitionSpec as P

HEAD_DIM = 128
BLOCK = 64
NEG = -1e30
SEQ = ("y", "xh", "z")
LANE = ("y", "xh")
HEAD = ("xl", "core")
XRING = ("xh", "xl")
NY, NXH, NZ, NXL, NC = 4, 2, 8, 2, 2
LANES = NY * NXH
SCALE = HEAD_DIM ** (-0.5)
F32 = jnp.float32
BF16 = jnp.bfloat16
VMEM_LIMIT = 24 * 1024 * 1024
VM = pl.BlockSpec(memory_space=pltpu.VMEM)
SM = pl.BlockSpec(memory_space=pltpu.SMEM)
HB = pl.BlockSpec(memory_space=pltpu.HBM)


def dot_nt(a, b):
    return lax.dot_general(a, b, (((1,), (1,)), ((), ())), preferred_element_type=F32)


def dot_nn(a, b):
    return jnp.dot(a, b, preferred_element_type=F32)


def row_max(a):
    return jnp.max(a, axis=1, keepdims=True)


def row_sum(a):
    return jnp.sum(a, axis=1, keepdims=True)


def local_kernel(all_blocks, deltas, z_ref, where_ref, id_ref, *refs):
    q_ref, kv_ref, ends_ref, slots_ref, o_ref, st_ref = refs
    feat = q_ref.shape[1]
    heads = range(feat // HEAD_DIM)
    blocks = q_ref.shape[0] // BLOCK
    col = lax.broadcasted_iota(jnp.int32, (BLOCK, 3 * BLOCK), 1)
    shift = jnp.where(col < BLOCK, -1, jnp.where(col < 2 * BLOCK, 0, 1))
    end_col = lax.broadcasted_iota(jnp.int32, (BLOCK, 2 * BLOCK), 1)
    kcol = [pl.ds(h * HEAD_DIM, HEAD_DIM) for h in heads]
    vcol = [pl.ds(feat + h * HEAD_DIM, HEAD_DIM) for h in heads]

    def step(j, carry):
        block = id_ref[0] + j
        near = block + shift
        near_ok = jnp.logical_and(near >= 0, near < all_blocks)
        ends_ok = jnp.where(end_col < BLOCK, block, all_blocks - 1 - block) >= 2
        rows = pl.ds(pl.multiple_of(j * BLOCK, BLOCK), BLOCK)
        wrows = pl.ds(pl.multiple_of(j * BLOCK, BLOCK), 3 * BLOCK)
        q = [q_ref[rows, kcol[h]] for h in heads]
        sw = [dot_nt(q[h], kv_ref[wrows, kcol[h]]) for h in heads]
        se = [dot_nt(q[h], ends_ref[:, kcol[h]]) for h in heads]
        sw = [jnp.where(near_ok, x * SCALE, NEG) for x in sw]
        se = [jnp.where(ends_ok, x * SCALE, NEG) for x in se]
        peak = [jnp.maximum(row_max(sw[h]), row_max(se[h])) for h in heads]
        pw = [jnp.exp(sw[h] - peak[h]) for h in heads]
        pe = [jnp.exp(se[h] - peak[h]) for h in heads]
        total = [row_sum(pw[h]) + row_sum(pe[h]) for h in heads]
        out = [
            dot_nn(pw[h].astype(BF16), kv_ref[wrows, vcol[h]])
            + dot_nn(pe[h].astype(BF16), ends_ref[:, vcol[h]])
            for h in heads
        ]
        for h in heads:
            o_ref[rows, kcol[h]] = out[h]
            st_ref[rows, pl.ds(h, 1)] = peak[h]
            st_ref[rows, pl.ds(len(heads) + h, 1)] = total[h]
        return carry

    lax.fori_loop(0, blocks, step, 0)
    add_slots(deltas, z_ref, where_ref, slots_ref, q_ref, o_ref, st_ref)


def add_slots(deltas, z_ref, where_ref, slots_ref, q_ref, o_ref, st_ref):
    feat = q_ref.shape[1]
    heads = range(feat // HEAD_DIM)
    kcol = [pl.ds(h * HEAD_DIM, HEAD_DIM) for h in heads]
    vcol = [pl.ds(feat + h * HEAD_DIM, HEAD_DIM) for h in heads]

    def step(lane, carry):
        for s, delta in enumerate(deltas):
            j = where_ref[lane * NZ + lax.rem(z_ref[0] + (delta + NZ), NZ)]

            @pl.when(j >= 0)
            def _():
                rows = pl.ds(pl.multiple_of(j * BLOCK, BLOCK), BLOCK)
                sc = [
                    dot_nt(q_ref[rows, kcol[h]], slots_ref[lane, s, :, kcol[h]]) * SCALE
                    for h in heads
                ]
                old = [st_ref[rows, pl.ds(h, 1)] for h in heads]
                tot = [st_ref[rows, pl.ds(len(heads) + h, 1)] for h in heads]
                acc = [o_ref[rows, kcol[h]] for h in heads]
                peak = [jnp.maximum(old[h], row_max(sc[h])) for h in heads]
                fade = [jnp.exp(old[h] - peak[h]) for h in heads]
                p = [jnp.exp(sc[h] - peak[h]) for h in heads]
                tot = [tot[h] * fade[h] + row_sum(p[h]) for h in heads]
                out = [dot_nn(p[h].astype(BF16), slots_ref[lane, s, :, vcol[h]]) for h in heads]
                for h in heads:
                    o_ref[rows, kcol[h]] = acc[h] * fade[h] + out[h]
                    st_ref[rows, pl.ds(h, 1)] = peak[h]
                    st_ref[rows, pl.ds(len(heads) + h, 1)] = tot[h]

        return carry

    lax.fori_loop(0, LANES, step, 0)


def more_kernel(deltas, z_ref, where_ref, q_ref, oin_ref, stin_ref, *refs):
    slots, (o_ref, st_ref) = refs[: len(deltas)], refs[len(deltas) :]
    o_ref[...] = oin_ref[...]
    st_ref[...] = stin_ref[...]
    for which, ref in zip(deltas, slots):
        add_slots(which, z_ref, where_ref, ref, q_ref, o_ref, st_ref)


def final_kernel(deltas, z_ref, where_ref, q_ref, oin_ref, stin_ref, *refs):
    slots, (att_ref, o_ref, st_ref) = refs[: len(deltas)], refs[len(deltas) :]
    more_kernel(deltas, z_ref, where_ref, q_ref, oin_ref, stin_ref, *slots, o_ref, st_ref)
    heads = range(q_ref.shape[1] // HEAD_DIM)

    def step(j, carry):
        rows = pl.ds(pl.multiple_of(j * BLOCK, BLOCK), BLOCK)
        for h in heads:
            kcol = pl.ds(h * HEAD_DIM, HEAD_DIM)
            total = st_ref[rows, pl.ds(len(heads) + h, 1)]
            att_ref[rows, kcol] = (o_ref[rows, kcol] / total).astype(BF16)
        return carry

    lax.fori_loop(0, q_ref.shape[0] // BLOCK, step, 0)


def cost(us):
    return pl.CostEstimate(flops=int(us * 1e9), bytes_accessed=4 * 2**20, transcendentals=0)


def local_part(z, where, first_id, all_blocks, q, kv_pad, ends, deltas, slots):
    tok, feat = q.shape
    return pl.pallas_call(
        lambda *refs: local_kernel(all_blocks, deltas, *refs),
        out_shape=(
            jax.ShapeDtypeStruct((tok, feat), F32),
            jax.ShapeDtypeStruct((tok, 128), F32),
        ),
        in_specs=[SM, SM, SM, VM, VM, VM, VM],
        out_specs=(VM, VM),
        compiler_params=pltpu.CompilerParams(vmem_limit_bytes=VMEM_LIMIT),
        cost_estimate=cost(25),
        name="local_part",
    )(z, where, first_id, q, kv_pad, ends, slots)


def more_part(z, where, q, o, st, deltas, slots):
    tok, feat = q.shape
    return pl.pallas_call(
        lambda *refs: more_kernel(deltas, *refs),
        out_shape=(
            jax.ShapeDtypeStruct((tok, feat), F32),
            jax.ShapeDtypeStruct((tok, 128), F32),
        ),
        in_specs=[SM, SM] + [VM] * (3 + len(slots)),
        out_specs=(VM, VM),
        compiler_params=pltpu.CompilerParams(vmem_limit_bytes=VMEM_LIMIT),
        cost_estimate=cost(12),
        name="more_part",
    )(z, where, q, o, st, *slots)


def final_part(z, where, q, o, st, deltas, slots):
    tok, feat = q.shape
    return pl.pallas_call(
        lambda *refs: final_kernel(deltas, *refs),
        out_shape=jax.ShapeDtypeStruct((tok, feat), BF16),
        in_specs=[SM, SM] + [VM] * (3 + len(slots)),
        out_specs=VM,
        scratch_shapes=[pltpu.VMEM((tok, feat), F32), pltpu.VMEM((tok, 128), F32)],
        compiler_params=pltpu.CompilerParams(vmem_limit_bytes=VMEM_LIMIT),
        cost_estimate=cost(6),
        name="final_part",
    )(z, where, q, o, st, *slots)


def pick(z, asked, sources, plan, shapes):
    def kernel(z_ref, asked_ref, *refs):
        src, out = refs[: len(sources)], refs[len(sources) : -1]
        sems = refs[-1]
        copies = []
        for n, (o, position, s, lane, plane, owner) in enumerate(plan):
            row = lane * NZ + lax.rem(z_ref[0] + (plane + NZ), NZ)
            block = asked_ref[row, lax.rem(z_ref[0] + (owner + NZ), NZ)]
            copies.append(
                pltpu.make_async_copy(src[s].at[block], out[o].at[position], sems.at[n])
            )
            copies[-1].start()
        for copy in copies:
            copy.wait()

    block_shape = sources[0].shape[1:]
    return pl.pallas_call(
        kernel,
        out_shape=tuple(pltpu.HBM(shape + block_shape, BF16) for shape in shapes),
        in_specs=[SM, SM] + [HB] * len(sources),
        out_specs=tuple(HB for _ in shapes),
        scratch_shapes=[pltpu.SemaphoreType.DMA((len(plan),))],
        compiler_params=pltpu.CompilerParams(vmem_limit_bytes=2 * 1024 * 1024),
        cost_estimate=cost(3),
        name="pick",
    )(z, asked, *sources)


def project_kernel(me_ref, a_ref, own_ref, core_ref, lo_ref, hi_ref, clo_ref, chi_ref, out_ref):
    me = me_ref[0]
    half = lo_ref.shape[0]

    def mul(a, w_ref):
        return jnp.dot(a, w_ref[...], preferred_element_type=F32)

    acc = mul(a_ref[me], own_ref)
    acc += mul(a_ref[me ^ 1], core_ref)
    acc += mul(a_ref[me ^ 2, :, :half], lo_ref)
    acc += mul(a_ref[me ^ 2, :, half:], hi_ref)
    acc += mul(a_ref[me ^ 3, :, :half], clo_ref)
    acc += mul(a_ref[me ^ 3, :, half:], chi_ref)
    out_ref[...] = acc.astype(BF16)


def project(me, a, weights, tile=512):
    _, rows, feat = a.shape
    cols = weights[0].shape[1]
    return pl.pallas_call(
        project_kernel,
        out_shape=jax.ShapeDtypeStruct((rows, cols), BF16),
        grid_spec=pltpu.PrefetchScalarGridSpec(
            num_scalar_prefetch=1,
            grid=(cols // tile,),
            in_specs=[pl.BlockSpec(a.shape, lambda n, me: (0, 0, 0))]
            + [pl.BlockSpec((w.shape[0], tile), lambda n, me: (0, n)) for w in weights],
            out_specs=pl.BlockSpec((rows, tile), lambda n, me: (0, n)),
        ),
        compiler_params=pltpu.CompilerParams(vmem_limit_bytes=VMEM_LIMIT),
        name="project",
    )(me, a, *weights)


def z_shift(x, by):
    return lax.ppermute(x, "z", [(i, (i + by) % NZ) for i in range(NZ)])


def lane_exchange(x):
    return lax.all_to_all(x, LANE, split_axis=0, concat_axis=0, tiled=True)


def wanted_blocks(rand_blocks, block_ids, all_blocks, blocks_dev):
    taken = [
        block_ids - 1,
        block_ids,
        block_ids + 1,
        jnp.zeros_like(block_ids),
        jnp.zeros_like(block_ids) + (all_blocks - 1),
    ]
    fresh = []
    for column in range(rand_blocks.shape[1]):
        chosen = rand_blocks[:, column]
        clash = reduce(jnp.logical_or, [chosen == other for other in taken])
        fresh.append(jnp.logical_not(clash))
        taken.append(chosen)
    fresh = jnp.stack(fresh, axis=1).reshape(-1)
    flat = rand_blocks.reshape(-1)
    entries = flat.shape[0]
    query = jnp.arange(entries, dtype=jnp.int32) // rand_blocks.shape[1]
    owners = jnp.arange(all_blocks // blocks_dev, dtype=jnp.int32)
    named = (flat // blocks_dev)[:, None] == owners[None, :]
    offset = jnp.sum(jnp.where(named, (flat % blocks_dev)[:, None], 0), axis=0)
    used = jnp.logical_and(named, fresh[:, None])
    where = jnp.sum(jnp.where(used, query[:, None] + 1, 0), axis=0) - 1
    return offset.astype(jnp.int32), where.astype(jnp.int32)


def tie(*arrays):
    return lax.optimization_barrier(arrays)


def body(queries, keys_values, rand_blocks, w_out):
    tok, feat = queries.shape
    blocks_dev = tok // BLOCK
    all_blocks = blocks_dev * LANES * NZ
    lanes = range(LANES)
    half = LANES // 2
    z = lax.axis_index("z")
    zs = z.reshape(1)
    first_id = lax.axis_index(SEQ) * blocks_dev

    kv = keys_values.reshape(blocks_dev, BLOCK, 2 * feat)

    block_ids = first_id + jnp.arange(blocks_dev, dtype=jnp.int32)
    offset, where = wanted_blocks(rand_blocks, block_ids, all_blocks, blocks_dev)
    asked = jnp.broadcast_to(offset.reshape(LANES, 1, NZ), (LANES, NZ, NZ)).reshape(-1, NZ)
    edge = jnp.where(z == 0, kv[0], kv[blocks_dev - 1])
    rows = w_out.shape[0] // 2
    low, high = w_out[:rows], w_out[rows:]
    asked = lax.all_to_all(asked, SEQ, split_axis=0, concat_axis=0, tiled=True)
    up1, down1 = z_shift(kv, 1), z_shift(kv, -1)
    ring = NXH * NXL
    low = lax.ppermute(low, XRING, [(i, (i + 1) % ring) for i in range(ring)])
    high = lax.ppermute(high, XRING, [(i, (i - 1) % ring) for i in range(ring)])
    turns = [(NZ * i + NZ - 1, NZ * i + NZ) for i in range(LANES - 1)]
    crossed = lax.ppermute(edge, SEQ, turns + [(b, a) for a, b in turns])
    plane_ends = lane_exchange(jnp.broadcast_to(edge[None], (LANES,) + edge.shape))
    up1, down1, asked, low, high, crossed, plane_ends = tie(
        up1, down1, asked, low, high, crossed, plane_ends
    )

    up2, down2 = z_shift(up1, 1), z_shift(down1, -1)
    plan = [(0, (lane, 0), 0, lane, 0, 0) for lane in lanes]
    plan += [(0, (lane, 1), 1, lane, 0, -1) for lane in lanes]
    plan += [(0, (lane, 2), 2, lane, 0, 1) for lane in lanes]
    (c1,) = pick(zs, asked, [kv, up1, down1], plan, [(LANES, 3)])
    r1 = lane_exchange(c1)
    swap = [(0, 1), (1, 0)]
    weights = [w_out, lax.ppermute(w_out, "core", swap), low, high]
    weights += [lax.ppermute(low, "core", swap), lax.ppermute(high, "core", swap)]
    held = jnp.where(z == 0, plane_ends[0], plane_ends[LANES - 1])
    got = lax.ppermute(held, "z", [(0, 4), (7, 3)])
    held = jnp.where(jnp.logical_or(z == 4, z == 3), got, held)
    got = lax.ppermute(held, "z", [(0, 2), (4, 6), (7, 5), (3, 1)])
    fresh = reduce(jnp.logical_or, [z == 2, z == 6, z == 5, z == 1])
    held = jnp.where(fresh, got, held)
    got = lax.ppermute(held, "z", [(i, i ^ 1) for i in range(NZ)])
    even = z % 2 == 0
    ends = jnp.concatenate([jnp.where(even, held, got), jnp.where(even, got, held)], axis=0)
    before = jnp.where(z == 0, crossed, up1[blocks_dev - 1])
    after = jnp.where(z == NZ - 1, crossed, down1[0])
    kv_pad = jnp.concatenate([before, kv.reshape(tok, 2 * feat), after], axis=0)
    up2, down2, r1, ends, kv_pad = tie(up2, down2, r1, ends, kv_pad)

    plan = [(0, lane, 0, lane, 1, -2) for lane in lanes]
    plan += [(1, lane, 1, lane, -1, 2) for lane in lanes]
    plan += [(2, lane, 0, lane, 2, -2) for lane in lanes[:half]]
    plan += [(3, lane - half, 1, lane, -2, 2) for lane in lanes[half:]]
    plan += [(4, (lane, 0), 0, lane, 0, -2) for lane in lanes]
    plan += [(4, (lane, 1), 1, lane, 0, 2) for lane in lanes]
    c3u, c3d, fu, fd, c2 = pick(
        zs, asked, [up2, down2], plan, [(LANES,), (LANES,), (half,), (half,), (LANES, 2)]
    )
    fu, fd = z_shift(fu, 1), z_shift(fd, -1)
    c3u = lane_exchange(c3u)
    c3d, c3u, fu, fd = tie(c3d, c3u, fu, fd)
    r3u = z_shift(c3u, 1)
    fu, fd = z_shift(fu, 1), z_shift(fd, -1)
    c3d = lane_exchange(c3d)
    c2, c3d, fu, fd = tie(c2, c3d, fu, fd)
    r3d = z_shift(c3d, -1)
    r2 = lane_exchange(c2)
    far = jnp.concatenate([fu, fd], axis=0)
    far, r2 = tie(far, r2)
    r4 = lane_exchange(far)

    def slots(x):
        return x.reshape(LANES, 1, BLOCK, 2 * feat)

    o, st = local_part(
        zs, where, first_id.reshape(1), all_blocks, queries, kv_pad, ends, (0, -1, 1), r1
    )
    o, st = more_part(
        zs, where, queries, o, st, [(-3,), (3,), (-2, 2)], [slots(r3u), slots(r3d), r2]
    )
    attended = final_part(zs, where, queries, o, st, [(4,)], [slots(r4)])

    heads = NXL * NC
    a = lax.all_to_all(
        attended.reshape(heads, tok // heads, feat), HEAD, split_axis=0, concat_axis=0, tiled=True
    )
    return project(lax.axis_index(HEAD).reshape(1), a, weights)


def solution(mesh):
    fine = Mesh(mesh.devices.reshape(NY, NXH, NZ, NXL, NC), ("y", "xh", "z", "xl", "core"))
    in_specs = (P(SEQ, HEAD), P(SEQ, None, HEAD), P(SEQ, None), P(HEAD, None))
    out_specs = P(SEQ + HEAD, None)
    return jax.shard_map(body, mesh=fine, in_specs=in_specs, out_specs=out_specs, check_vma=False)
```

time: 390 us -> 520 us (1.33)
  Pallas kernels: 91.4 us -> 270 us
  waiting for transfers between devices: 131 us -> 108 us
  local copies, waits for them, and re-layouts: 47.6 us -> 26.3 us
    pallas_call x5, Pallas kernels: 80.2 us -> 259 us  [the longest x2 227 us: pick(): pl.pallas_call(kernel, out_shape=tuple((pltpu.HBM(shape + block_shape, BF...]
    gather x9 -> x0, local copies, waits for them, and re-layouts: 28.3 us -> none  [the longest x1 3.21 us: body(): up3 = z_shift(up2[asks(z + 1, z - 2)], 1)]
    all_to_all x9 -> x6, waiting for transfers between devices: 43.8 us -> 16.7 us  [lane_exchange(): return lax.all_to_all(x, LANE, split_axis=0, concat_axis=0, tiled=True)]
    ppermute x1, waiting for transfers between devices: 9.58 us -> 32.7 us  [body(): got = lax.ppermute(held, 'z', [(0, 4), (7, 3)])]
    ppermute x10, waiting for transfers between devices: 27.2 us -> 6.9 us  [z_shift(): return lax.ppermute(x, 'z', [(i, (i + by) % NZ) for i in range(NZ)])]
    all_to_all x9 -> x6, starting transfers between devices: 45.6 us -> 32.9 us  [lane_exchange(): return lax.all_to_all(x, LANE, split_axis=0, concat_axis=0, tiled=True)]
    unnamed x29 -> x27, local copies, waits for them, and re-layouts: 7.48 us -> 16.3 us
    ppermute x1, starting transfers between devices: 0.16 us -> 7.12 us  [body(): got = lax.ppermute(held, 'z', [(i, i ^ 1) for i in range(NZ)])]
  transfers between devices with their start and end apart: 30 -> 27, of which waited for: 13 -> 7; matrix products, arithmetic and copies ran while one was open for 13% -> 4% of each run, Pallas kernels for 21% -> 6%
where the time goes in v2:
time: 520 us; the launch traced here: 517 us
  Pallas kernels  270 us (52%)
  waiting for transfers between devices  108 us (21%)
  starting transfers between devices  102 us (20%)
  local copies, waits for them, and re-layouts  26.3 us (5%)
  other arithmetic  9.89 us (2%)
    pallas_call x2, Pallas kernels, pick(): pl.pallas_call(kernel, out_shape=tuple((pltpu.HBM(shape + block_shape, BF...  227 us
    all_to_all x1, waiting for transfers between devices, body(): asked = lax.all_to_all(asked, SEQ, split_axis=0, concat_axis=0, tiled=True)  36.1 us
    all_to_all x6, starting transfers between devices, lane_exchange(): return lax.all_to_all(x, LANE, split_axis=0, concat_axis=0, tiled=True)  32.9 us
    ppermute x1, waiting for transfers between devices, body(): got = lax.ppermute(held, 'z', [(0, 4), (7, 3)])  32.7 us
    ppermute x10, starting transfers between devices, z_shift(): return lax.ppermute(x, 'z', [(i, (i + by) % NZ) for i in range(NZ)])  17.9 us
    all_to_all x6, waiting for transfers between devices, lane_exchange(): return lax.all_to_all(x, LANE, split_axis=0, concat_axis=0, tiled=True)  16.7 us
    unnamed x27, local copies, waits for them, and re-layouts  16.3 us
    pallas_call x1, Pallas kernels, local_part(): pl.pallas_call(lambda *refs: local_kernel(all_blocks, deltas, *refs), out...  15.5 us
  transfers between devices with their start and end apart: 27, of which 7 were waited for; matrix products, arithmetic and copies ran while one was open for 4% of the time, Pallas kernels for 6%

profile of v2, /device:TPU:1, one launch (start us, length us, event | category | flops | bytes accessed | tf_op | source)
XLA Modules:
  0.0 516.5 jit_solution(7670265910659656539)
XLA Ops:
  0.0 3.2 reshape.133.refs_0_
  3.2 2.5 collective-permute-start
  5.8 4.0 collective-permute-start.1
  9.8 4.8 fusion.4
  14.6 1.2 collective-permute-start.2
  15.8 1.5 collective-permute-start.3
  18.5 10.1 %all-to-all-start = ((s32[64,1,8]{2,1,0:T(1,128)}), s32[64,1,8]{2,1,0:T(1,128)S(1)}, u32[]{:S(2)}, u32[]{:S(2)}) async-start(s32[64,1,8]{2,1,0:T(1,128)} %bitcast.3), calls=%async_computation | async-start | bytes 65536 | tf_op jit(solution)/shard_map/all_to_all | solution.py:313
  28.6 1.1 broadcast_select_fusion
  29.7 36.1 %all-to-all-done = s32[64,1,8]{2,1,0:T(1,128)S(1)} async-done(((s32[64,1,8]{2,1,0:T(1,128)}), s32[64,1,8]{2,1,0:T(1,128)S(1)}, u32[]{:S(2)}, u32[]{:S(2)}) %all-to-all-start) | async-done | bytes 2080 | tf_op jit(solution)/shard_map/all_to_all | solution.py:313
  65.8 1.1 broadcast_in_dim.40
  66.9 3.6 all-to-all-start.1
  71.1 14.3 %all-to-all-done.1 = bf16[8,64,1024]{2,1,0:T(8,128)(2,1)S(1)} async-done(((bf16[8,64,1024]{2,1,0:T(8,128)(2,1)}), bf16[8,64,1024]{2,1,0:T(8,128)(2,1)S(1)}, u32[]{:S(2)}, u32[]{:S(2)}) %all-to-all-start.1) | async-done | bytes 1048608 | tf_op jit(solution)/shard_map/all_to_all | solution.py:262
  86.5 66.0 %pick.2 = bf16[8,3,64,1024]{3,2,1,0:T(8,128)(2,1)} custom-call(s32[1]{0:T(128)} %bitcast.1.z_ref.refs_0_, s32[64,8]{1,0:T(8,128)S(1)} %bitcast.22, bf16[16,64,1024]{2,1,0:T(8,128)(2,1)S(1)} %reshape.133.refs_0_, bf16[16,64,1024]{2,1,0:T(8,128)(2,1)} %collective-permute-done.refs_1_, bf16[16,64,1024]{2,1,0:T(8,128)(2,1)} %collective-permute-done.1.refs_2_), custom_call_target="tpu_custom_call" | custom-call | flops 3000000000 | bytes 4194304 | tf_op jit(solution)/shard_map/pick/pallas_call | solution.py:211
  152.4 4.7 all-to-all-start.2
  157.1 2.8 collective-permute-start.6
  160.8 4.9 collective-permute-start.7
  165.7 3.5 copy.14
  169.2 32.7 %collective-permute-done.7 = bf16[64,1024]{1,0:T(8,128)(2,1)} collective-permute-done((bf16[64,1024]{1,0:T(8,128)(2,1)S(1)}, bf16[64,1024]{1,0:T(8,128)(2,1)}, u32[]{:S(2)}, u32[]{:S(2)}) %collective-permute-start.7) | collective-permute-done | bytes 131104 | tf_op jit(solution)/shard_map/ppermute | solution.py:335
  202.9 1.3 collective-permute-start.8
  204.2 1.0 bitcast_select_fusion.1
  205.2 1.8 collective-permute-done.8
  207.0 7.1 %collective-permute-start.9 = (bf16[64,1024]{1,0:T(8,128)(2,1)S(1)}, bf16[64,1024]{1,0:T(8,128)(2,1)S(1)}, u32[]{:S(2)}, u32[]{:S(2)}) collective-permute-start(bf16[64,1024]{1,0:T(8,128)(2,1)S(1)} %broadcast_select_fusion.2), channel_id=1, source_target_pairs={{0,4},{4,0},{8,12},{12,8},{16,20},{20,16},{24,28},{28,24},{1,5},{5... | collective-permute-start | bytes 393224 | tf_op jit(solution)/shard_map/ppermute | solution.py:340
  214.1 3.2 pad_maximum_fusion.refs_4_
  217.4 161.4 %pick.3 = (bf16[8,64,1024]{2,1,0:T(8,128)(2,1)}, bf16[8,64,1024]{2,1,0:T(8,128)(2,1)}, bf16[4,64,1024]{2,1,0:T(8,128)(2,1)}, bf16[4,64,1024]{2,1,0:T(8,128)(2,1)}, bf16[8,2,64,1024]{3,2,1,0:T(8,128)(2,1)}) custom-call(s32[1]{0:T(128)} %bitcast.1.z_ref.refs_0_, s32[64,8]{1,0:T(8,128)S(1)} %bitcast.23, bf16[16,64,1024]{2,1,0:T(8,128)(2,1)} %collective-permute-done.5.refs_0_, ...), custom_call_target="tpu_custom_call" | custom-call | flops 3000000000 | bytes 4194304 | tf_op jit(solution)/shard_map/pick/pallas_call | solution.py:211
  378.8 6.2 %all-to-all-start.3 = ((bf16[8,64,1024]{2,1,0:T(8,128)(2,1)}), bf16[8,64,1024]{2,1,0:T(8,128)(2,1)}, u32[]{:S(2)}, u32[]{:S(2)}) async-start(bf16[8,64,1024]{2,1,0:T(8,128)(2,1)} %get-tuple-element.49), calls=%async_computation.3 | async-start | bytes 2097152 | tf_op jit(solution)/shard_map/all_to_all | solution.py:262
  385.6 2.1 collective-permute-start.11
  387.7 6.9 %collective-permute-done.10 = bf16[4,64,1024]{2,1,0:T(8,128)(2,1)} collective-permute-done((bf16[4,64,1024]{2,1,0:T(8,128)(2,1)}, bf16[4,64,1024]{2,1,0:T(8,128)(2,1)}, u32[]{:S(2)}, u32[]{:S(2)}) %collective-permute-start.10) | collective-permute-done | bytes 524320 | tf_op jit(solution)/shard_map/ppermute | solution.py:258
  394.6 2.4 all-to-all-done.3
  397.0 4.3 all-to-all-start.4
  401.9 2.6 collective-permute-start.14
  404.4 10.3 %collective-permute-start.16 = (bf16[512,4096]{1,0:T(8,128)(2,1)}, bf16[512,4096]{1,0:T(8,128)(2,1)}, u32[]{:S(2)}, u32[]{:S(2)}) collective-permute-start(bf16[512,4096]{1,0:T(8,128)(2,1)} %own_ref.1), channel_id=1, source_target_pairs={{0,1},{1,0},{2,3},{3,2},{4,5},{5,4},{6,7},{7,6},{8,9},{9,8},{10,11... | collective-permute-start | bytes 12582920 | tf_op jit(solution)/shard_map/ppermute | solution.py:332
  415.2 6.9 %all-to-all-start.5 = ((bf16[8,2,64,1024]{3,2,1,0:T(8,128)(2,1)}), bf16[8,2,64,1024]{3,2,1,0:T(8,128)(2,1)}, u32[]{:S(2)}, u32[]{:S(2)}) async-start(bf16[8,2,64,1024]{3,2,1,0:T(8,128)(2,1)} %get-tuple-element.60), calls=%async_computation.5 | async-start | bytes 4194304 | tf_op jit(solution)/shard_map/all_to_all | solution.py:262
  422.2 2.7 collective-permute-start.15
  424.8 1.7 copy-done.1
  426.5 1.2 copy-done.2
  427.7 15.5 %local_part.1 = (f32[1024,512]{1,0:T(8,128)S(1)}, f32[1024,128]{1,0:T(8,128)S(1)}) custom-call(s32[1]{0:T(128)} %bitcast.1.z_ref.refs_0_, s32[64]{0:T(128)S(1)} %broadcast_add_fusion.refs_1_, s32[1]{0:T(128)} %bitcast.2.refs_2_, bf16[1024,512]{1,0:T(8,128)(2,1)S(1)} %copy-done.2, bf16[1152,1024]{1,0:T(8,128)(2,1)S(1)} %copy-done.1, ...), custom_call_target="tpu_custom_call" | custom-call | flops 24999999488 | bytes 4194304 | tf_op jit(solution)/shard_map/local_part/pallas_call | solution.py:151
  443.2 1.3 copy-done.6
  445.4 2.4 pad_maximum_fusion.1
  447.7 7.3 %all-to-all-start.6 = ((bf16[8,64,1024]{2,1,0:T(8,128)(2,1)}), bf16[8,64,1024]{2,1,0:T(8,128)(2,1)S(1)}, u32[]{:S(2)}, u32[]{:S(2)}) async-start(bf16[8,64,1024]{2,1,0:T(8,128)(2,1)} %pad_maximum_fusion.1), calls=%async_computation.6 | async-start | bytes 2097152 | tf_op jit(solution)/shard_map/all_to_all | solution.py:262
  455.0 1.6 copy-done.7
  456.6 11.6 %more_part.1 = (f32[1024,512]{1,0:T(8,128)S(1)}, f32[1024,128]{1,0:T(8,128)S(1)}) custom-call(s32[1]{0:T(128)} %bitcast.1.z_ref.refs_0_, s32[64]{0:T(128)S(1)} %broadcast_add_fusion.refs_1_, bf16[1024,512]{1,0:T(8,128)(2,1)S(1)} %copy-done.3, f32[1024,512]{1,0:T(8,128)S(1)} %copy-done.7, f32[1024,128]{1,0:T(8,128)S(1)} %copy-done.9, ...), custom_call_target="tpu_custom_call" | custom-call | flops 12000000000 | bytes 4194304 | tf_op jit(solution)/shard_map/more_part/pallas_call | solution.py:167
  468.2 1.3 copy-done.4
  469.5 1.6 copy-done.5
  471.1 5.1 final_part.1
  476.2 14.1 %all-to-all-start.7 = ((bf16[4,256,512]{2,1,0:T(8,128)(2,1)}), bf16[4,256,512]{2,1,0:T(8,128)(2,1)S(1)}, u32[]{:S(2)}, u32[]{:S(2)}) async-start(bf16[4,256,512]{2,1,0:T(8,128)(2,1)} %bitcast.11), calls=%async_computation.7 | async-start | bytes 2097152 | tf_op jit(solution)/shard_map/all_to_all | solution.py:382
  490.3 13.6 %all-to-all-done.7.a_ref = bf16[4,256,512]{2,1,0:T(8,128)(2,1)S(1)} async-done(((bf16[4,256,512]{2,1,0:T(8,128)(2,1)}), bf16[4,256,512]{2,1,0:T(8,128)(2,1)S(1)}, u32[]{:S(2)}, u32[]{:S(2)}) %all-to-all-start.7) | async-done | bytes 1048608 | tf_op jit(solution)/shard_map/all_to_all | solution.py:382
  503.9 2.2 copy-done
  506.1 10.4 %project.1 = bf16[256,4096]{1,0:T(8,128)(2,1)} custom-call(s32[1]{0:T(128)} %bitcast.me_ref, bf16[4,256,512]{2,1,0:T(8,128)(2,1)S(1)} %all-to-all-done.7.a_ref, bf16[512,4096]{1,0:T(8,128)(2,1)S(1)} %copy-done, bf16[512,4096]{1,0:T(8,128)(2,1)} %collective-permute-done.16.core_ref, bf16[256,4096]{1,0:T(8,128)(2,1)} %collective-permute-done.2.lo_ref, ...), custom_call_target="tpu_custom_call" | custom-call | tf_op jit(solution)/shard_map/project/pallas_call | solution.py:242
  (61 shorter events, 7.5 us)
Async XLA Ops:
  3.2 14.0 %copy-start.11 = (s32[16,2]{0,1:T(2,128)S(1)}, s32[16,2]{0,1:T(2,128)}, u32[]{:S(2)}) copy-start(s32[16,2]{0,1:T(2,128)} %param.6) | copy-start | bytes 388
  3.2 82.2 %collective-permute-start = (bf16[16,64,1024]{2,1,0:T(8,128)(2,1)S(1)}, bf16[16,64,1024]{2,1,0:T(8,128)(2,1)}, u32[]{:S(2)}, u32[]{:S(2)}) collective-permute-start(bf16[16,64,1024]{2,1,0:T(8,128)(2,1)S(1)} %reshape.133.refs_0_), channel_id=1, source_target_pairs={{0,4},{4,8},{8,12},{12,16},{16,20},{20,24},{24,28},{28,0},{1,5},{5... | collective-permute-start | bytes 6291464 | tf_op jit(solution)/shard_map/ppermute | solution.py:258
  5.8 79.7 %collective-permute-start.1 = (bf16[16,64,1024]{2,1,0:T(8,128)(2,1)S(1)}, bf16[16,64,1024]{2,1,0:T(8,128)(2,1)}, u32[]{:S(2)}, u32[]{:S(2)}) collective-permute-start(bf16[16,64,1024]{2,1,0:T(8,128)(2,1)S(1)} %reshape.133.refs_0_), channel_id=1, source_target_pairs={{0,28},{4,0},{8,4},{12,8},{16,12},{20,16},{24,20},{28,24},{1,29},{... | collective-permute-start | bytes 6291464 | tf_op jit(solution)/shard_map/ppermute | solution.py:258
  14.6 71.9 %collective-permute-start.2 = (bf16[256,4096]{1,0:T(8,128)(2,1)}, bf16[256,4096]{1,0:T(8,128)(2,1)}, u32[]{:S(2)}, u32[]{:S(2)}) collective-permute-start(bf16[256,4096]{1,0:T(8,128)(2,1)} %get-tuple-element.70), channel_id=1, source_target_pairs={{0,2},{2,32},{32,34},{34,0},{1,3},{3,33},{33,35},{35,1},{4,6},{6,3... | collective-permute-start | bytes 6291464 | tf_op jit(solution)/shard_map/ppermute | solution.py:316
  15.8 70.7 %collective-permute-start.3 = (bf16[256,4096]{1,0:T(8,128)(2,1)}, bf16[256,4096]{1,0:T(8,128)(2,1)}, u32[]{:S(2)}, u32[]{:S(2)}) collective-permute-start(bf16[256,4096]{1,0:T(8,128)(2,1)} %get-tuple-element.69), channel_id=1, source_target_pairs={{0,34},{2,0},{32,2},{34,32},{1,35},{3,1},{33,3},{35,33},{4,38},{6,... | collective-permute-start | bytes 6291464 | tf_op jit(solution)/shard_map/ppermute | solution.py:317
  18.5 47.3 %all-to-all-start = ((s32[64,1,8]{2,1,0:T(1,128)}), s32[64,1,8]{2,1,0:T(1,128)S(1)}, u32[]{:S(2)}, u32[]{:S(2)}) async-start(s32[64,1,8]{2,1,0:T(1,128)} %bitcast.3), calls=%async_computation | async-start | bytes 65536 | tf_op jit(solution)/shard_map/all_to_all | solution.py:313
  66.9 18.6 %all-to-all-start.1 = ((bf16[8,64,1024]{2,1,0:T(8,128)(2,1)}), bf16[8,64,1024]{2,1,0:T(8,128)(2,1)S(1)}, u32[]{:S(2)}, u32[]{:S(2)}) async-start(bf16[8,64,1024]{2,1,0:T(8,128)(2,1)} %broadcast_in_dim.40), calls=%async_computation.1 | async-start | bytes 2097152 | tf_op jit(solution)/shard_map/all_to_all | solution.py:262
  70.5 0.7 collective-permute-start.4
  85.5 1.0 copy-start.10
  152.4 65.0 %all-to-all-start.2 = ((bf16[8,3,64,1024]{3,2,1,0:T(8,128)(2,1)}), bf16[8,3,64,1024]{3,2,1,0:T(8,128)(2,1)S(1)}, u32[]{:S(2)}, u32[]{:S(2)}) async-start(bf16[8,3,64,1024]{3,2,1,0:T(8,128)(2,1)} %pick.2), calls=%async_computation.2 | async-start | bytes 6291456 | tf_op jit(solution)/shard_map/all_to_all | solution.py:262
  157.1 60.3 %collective-permute-start.5 = (bf16[16,64,1024]{2,1,0:T(8,128)(2,1)}, bf16[16,64,1024]{2,1,0:T(8,128)(2,1)}, u32[]{:S(2)}, u32[]{:S(2)}) collective-permute-start(bf16[16,64,1024]{2,1,0:T(8,128)(2,1)} %collective-permute-done.refs_1_), channel_id=1, source_target_pairs={{0,4},{4,8},{8,12},{12,16},{16,20},{20,24},{24,28},{28,0},{1,5},{5... | collective-permute-start | bytes 6291464 | tf_op jit(solution)/shard_map/ppermute | solution.py:258
  157.1 60.3 %collective-permute-start.6 = (bf16[16,64,1024]{2,1,0:T(8,128)(2,1)}, bf16[16,64,1024]{2,1,0:T(8,128)(2,1)}, u32[]{:S(2)}, u32[]{:S(2)}) collective-permute-start(bf16[16,64,1024]{2,1,0:T(8,128)(2,1)} %collective-permute-done.1.refs_2_), channel_id=1, source_target_pairs={{0,28},{4,0},{8,4},{12,8},{16,12},{20,16},{24,20},{28,24},{1,29},{... | collective-permute-start | bytes 6291464 | tf_op jit(solution)/shard_map/ppermute | solution.py:258
  160.8 41.1 %collective-permute-start.7 = (bf16[64,1024]{1,0:T(8,128)(2,1)S(1)}, bf16[64,1024]{1,0:T(8,128)(2,1)}, u32[]{:S(2)}, u32[]{:S(2)}) collective-permute-start(bf16[64,1024]{1,0:T(8,128)(2,1)S(1)} %select_bitcast_fusion), channel_id=1, source_target_pairs={{0,16},{28,12},{1,17},{29,13},{2,18},{30,14},{3,19},{31,15},{32,48... | collective-permute-start | bytes 393224 | tf_op jit(solution)/shard_map/ppermute | solution.py:335
  202.9 4.1 collective-permute-start.8
  207.0 10.4 %collective-permute-start.9 = (bf16[64,1024]{1,0:T(8,128)(2,1)S(1)}, bf16[64,1024]{1,0:T(8,128)(2,1)S(1)}, u32[]{:S(2)}, u32[]{:S(2)}) collective-permute-start(bf16[64,1024]{1,0:T(8,128)(2,1)S(1)} %broadcast_select_fusion.2), channel_id=1, source_target_pairs={{0,4},{4,0},{8,12},{12,8},{16,20},{20,16},{24,28},{28,24},{1,5},{5... | collective-permute-start | bytes 393224 | tf_op jit(solution)/shard_map/ppermute | solution.py:340
  378.8 18.2 %all-to-all-start.3 = ((bf16[8,64,1024]{2,1,0:T(8,128)(2,1)}), bf16[8,64,1024]{2,1,0:T(8,128)(2,1)}, u32[]{:S(2)}, u32[]{:S(2)}) async-start(bf16[8,64,1024]{2,1,0:T(8,128)(2,1)} %get-tuple-element.49), calls=%async_computation.3 | async-start | bytes 2097152 | tf_op jit(solution)/shard_map/all_to_all | solution.py:262
  385.0 9.6 %collective-permute-start.10 = (bf16[4,64,1024]{2,1,0:T(8,128)(2,1)}, bf16[4,64,1024]{2,1,0:T(8,128)(2,1)}, u32[]{:S(2)}, u32[]{:S(2)}) collective-permute-start(bf16[4,64,1024]{2,1,0:T(8,128)(2,1)} %get-tuple-element.50), channel_id=1, source_target_pairs={{0,4},{4,8},{8,12},{12,16},{16,20},{20,24},{24,28},{28,0},{1,5},{5... | collective-permute-start | bytes 1572872 | tf_op jit(solution)/shard_map/ppermute | solution.py:258
  385.6 9.0 %collective-permute-start.11 = (bf16[4,64,1024]{2,1,0:T(8,128)(2,1)}, bf16[4,64,1024]{2,1,0:T(8,128)(2,1)}, u32[]{:S(2)}, u32[]{:S(2)}) collective-permute-start(bf16[4,64,1024]{2,1,0:T(8,128)(2,1)} %get-tuple-element.51), channel_id=1, source_target_pairs={{0,28},{4,0},{8,4},{12,8},{16,12},{20,16},{24,20},{28,24},{1,29},{... | collective-permute-start | bytes 1572872 | tf_op jit(solution)/shard_map/ppermute | solution.py:258
  397.0 18.2 %all-to-all-start.4 = ((bf16[8,64,1024]{2,1,0:T(8,128)(2,1)}), bf16[8,64,1024]{2,1,0:T(8,128)(2,1)}, u32[]{:S(2)}, u32[]{:S(2)}) async-start(bf16[8,64,1024]{2,1,0:T(8,128)(2,1)} %get-tuple-element.54), calls=%async_computation.4 | async-start | bytes 2097152 | tf_op jit(solution)/shard_map/all_to_all | solution.py:262
  401.2 14.0 %collective-permute-start.13 = (bf16[4,64,1024]{2,1,0:T(8,128)(2,1)}, bf16[4,64,1024]{2,1,0:T(8,128)(2,1)}, u32[]{:S(2)}, u32[]{:S(2)}) collective-permute-start(bf16[4,64,1024]{2,1,0:T(8,128)(2,1)} %collective-permute-done.10), channel_id=1, source_target_pairs={{0,4},{4,8},{8,12},{12,16},{16,20},{20,24},{24,28},{28,0},{1,5},{5... | collective-permute-start | bytes 1572872 | tf_op jit(solution)/shard_map/ppermute | solution.py:258
  401.9 13.3 %collective-permute-start.14 = (bf16[4,64,1024]{2,1,0:T(8,128)(2,1)}, bf16[4,64,1024]{2,1,0:T(8,128)(2,1)}, u32[]{:S(2)}, u32[]{:S(2)}) collective-permute-start(bf16[4,64,1024]{2,1,0:T(8,128)(2,1)} %collective-permute-done.11), channel_id=1, source_target_pairs={{0,28},{4,0},{8,4},{12,8},{16,12},{20,16},{24,20},{28,24},{1,29},{... | collective-permute-start | bytes 1572872 | tf_op jit(solution)/shard_map/ppermute | solution.py:258
  404.4 85.9 %collective-permute-start.16 = (bf16[512,4096]{1,0:T(8,128)(2,1)}, bf16[512,4096]{1,0:T(8,128)(2,1)}, u32[]{:S(2)}, u32[]{:S(2)}) collective-permute-start(bf16[512,4096]{1,0:T(8,128)(2,1)} %own_ref.1), channel_id=1, source_target_pairs={{0,1},{1,0},{2,3},{3,2},{4,5},{5,4},{6,7},{7,6},{8,9},{9,8},{10,11... | collective-permute-start | bytes 12582920 | tf_op jit(solution)/shard_map/ppermute | solution.py:332
  414.7 75.6 %collective-permute-start.17 = (bf16[256,4096]{1,0:T(8,128)(2,1)}, bf16[256,4096]{1,0:T(8,128)(2,1)}, u32[]{:S(2)}, u32[]{:S(2)}) collective-permute-start(bf16[256,4096]{1,0:T(8,128)(2,1)} %collective-permute-done.2.lo_ref), channel_id=1, source_target_pairs={{0,1},{1,0},{2,3},{3,2},{4,5},{5,4},{6,7},{7,6},{8,9},{9,8},{10,11... | collective-permute-start | bytes 6291464 | tf_op jit(solution)/shard_map/ppermute | solution.py:333
  414.7 75.6 %collective-permute-start.18 = (bf16[256,4096]{1,0:T(8,128)(2,1)}, bf16[256,4096]{1,0:T(8,128)(2,1)}, u32[]{:S(2)}, u32[]{:S(2)}) collective-permute-start(bf16[256,4096]{1,0:T(8,128)(2,1)} %collective-permute-done.3.hi_ref), channel_id=1, source_target_pairs={{0,1},{1,0},{2,3},{3,2},{4,5},{5,4},{6,7},{7,6},{8,9},{9,8},{10,11... | collective-permute-start | bytes 6291464 | tf_op jit(solution)/shard_map/ppermute | solution.py:333
  415.2 39.8 %collective-permute-start.12 = (bf16[8,64,1024]{2,1,0:T(8,128)(2,1)}, bf16[8,64,1024]{2,1,0:T(8,128)(2,1)}, u32[]{:S(2)}, u32[]{:S(2)}) collective-permute-start(bf16[8,64,1024]{2,1,0:T(8,128)(2,1)} %all-to-all-done.3), channel_id=1, source_target_pairs={{0,4},{4,8},{8,12},{12,16},{16,20},{20,24},{24,28},{28,0},{1,5},{5... | collective-permute-start | bytes 3145736 | tf_op jit(solution)/shard_map/ppermute | solution.py:258
  415.2 32.5 %all-to-all-start.5 = ((bf16[8,2,64,1024]{3,2,1,0:T(8,128)(2,1)}), bf16[8,2,64,1024]{3,2,1,0:T(8,128)(2,1)}, u32[]{:S(2)}, u32[]{:S(2)}) async-start(bf16[8,2,64,1024]{3,2,1,0:T(8,128)(2,1)} %get-tuple-element.60), calls=%async_computation.5 | async-start | bytes 4194304 | tf_op jit(solution)/shard_map/all_to_all | solution.py:262
  422.2 32.8 %collective-permute-start.15 = (bf16[8,64,1024]{2,1,0:T(8,128)(2,1)}, bf16[8,64,1024]{2,1,0:T(8,128)(2,1)}, u32[]{:S(2)}, u32[]{:S(2)}) collective-permute-start(bf16[8,64,1024]{2,1,0:T(8,128)(2,1)} %all-to-all-done.4), channel_id=1, source_target_pairs={{0,28},{4,0},{8,4},{12,8},{16,12},{20,16},{24,20},{28,24},{1,29},{... | collective-permute-start | bytes 3145736 | tf_op jit(solution)/shard_map/ppermute | solution.py:258
  424.8 1.7 copy-start.1
  426.5 1.2 copy-start.2
  443.2 1.3 copy-start.6
  444.5 0.8 copy-start.8
  445.4 9.7 %copy-start.3 = (bf16[1024,512]{1,0:T(8,128)(2,1)S(1)}, bf16[1024,512]{1,0:T(8,128)(2,1)}, u32[]{:S(2)}) copy-start(bf16[1024,512]{1,0:T(8,128)(2,1)} %refs_2_.3) | copy-start | bytes 3145732
  447.7 7.3 %copy-start.9 = (f32[1024,128]{1,0:T(8,128)S(1)}, f32[1024,128]{1,0:T(8,128)}, u32[]{:S(2)}) copy-start(f32[1024,128]{1,0:T(8,128)} %copy-done.8) | copy-start | bytes 1572868
  447.7 21.8 %all-to-all-start.6 = ((bf16[8,64,1024]{2,1,0:T(8,128)(2,1)}), bf16[8,64,1024]{2,1,0:T(8,128)(2,1)S(1)}, u32[]{:S(2)}, u32[]{:S(2)}) async-start(bf16[8,64,1024]{2,1,0:T(8,128)(2,1)} %pad_maximum_fusion.1), calls=%async_computation.6 | async-start | bytes 2097152 | tf_op jit(solution)/shard_map/all_to_all | solution.py:262
  455.0 1.6 copy-start.7
  468.2 1.3 copy-start.4
  469.5 1.6 copy-start.5
  476.2 27.7 %all-to-all-start.7 = ((bf16[4,256,512]{2,1,0:T(8,128)(2,1)}), bf16[4,256,512]{2,1,0:T(8,128)(2,1)S(1)}, u32[]{:S(2)}, u32[]{:S(2)}) async-start(bf16[4,256,512]{2,1,0:T(8,128)(2,1)} %bitcast.11), calls=%async_computation.7 | async-start | bytes 2097152 | tf_op jit(solution)/shard_map/all_to_all | solution.py:382
  503.9 2.2 copy-start

commit v3 on v2

--- a/solution.py
+++ b/solution.py
@@ -194,18 +194,20 @@
 
 def pick(z, asked, sources, plan, shapes):
     def kernel(z_ref, asked_ref, *refs):
-        src, out = refs[: len(sources)], refs[len(sources) : -1]
-        sems = refs[-1]
-        copies = []
+        src, out = refs[: len(sources)], refs[len(sources) : -3]
+        held, in_sems, out_sems = refs[-3:]
+        loads, stores = [], []
         for n, (o, position, s, lane, plane, owner) in enumerate(plan):
             row = lane * NZ + lax.rem(z_ref[0] + (plane + NZ), NZ)
             block = asked_ref[row, lax.rem(z_ref[0] + (owner + NZ), NZ)]
-            copies.append(
-                pltpu.make_async_copy(src[s].at[block], out[o].at[position], sems.at[n])
-            )
-            copies[-1].start()
-        for copy in copies:
-            copy.wait()
+            loads.append(pltpu.make_async_copy(src[s].at[block], held.at[n], in_sems.at[n]))
+            stores.append(pltpu.make_async_copy(held.at[n], out[o].at[position], out_sems.at[n]))
+            loads[-1].start()
+        for load, store in zip(loads, stores):
+            load.wait()
+            store.start()
+        for store in stores:
+            store.wait()
 
     block_shape = sources[0].shape[1:]
     return pl.pallas_call(
@@ -213,42 +215,57 @@
         out_shape=tuple(pltpu.HBM(shape + block_shape, BF16) for shape in shapes),
         in_specs=[SM, SM] + [HB] * len(sources),
         out_specs=tuple(HB for _ in shapes),
-        scratch_shapes=[pltpu.SemaphoreType.DMA((len(plan),))],
-        compiler_params=pltpu.CompilerParams(vmem_limit_bytes=2 * 1024 * 1024),
+        scratch_shapes=[
+            pltpu.VMEM((len(plan),) + block_shape, BF16),
+            pltpu.SemaphoreType.DMA((len(plan),)),
+            pltpu.SemaphoreType.DMA((len(plan),)),
+        ],
+        compiler_params=pltpu.CompilerParams(vmem_limit_bytes=8 * 1024 * 1024),
         cost_estimate=cost(3),
         name="pick",
     )(z, asked, *sources)
 
 
-def project_kernel(me_ref, a_ref, own_ref, core_ref, lo_ref, hi_ref, clo_ref, chi_ref, out_ref):
+def project_kernel(tile, me_ref, a_ref, *refs):
+    weights, (out_ref, w_ref, acat_ref, sems) = refs[:-4], refs[-4:]
+    rows, feat = a_ref.shape[1:]
+    cols = out_ref.shape[1]
+    copies = []
+    for n in range(cols // tile):
+        top = 0
+        span = pl.ds(n * tile, tile)
+        for k, weight in enumerate(weights):
+            part = pl.ds(top, weight.shape[0])
+            copies.append(
+                pltpu.make_async_copy(
+                    weight.at[:, span], w_ref.at[part, span], sems.at[n * len(weights) + k]
+                )
+            )
+            copies[-1].start()
+            top += weight.shape[0]
     me = me_ref[0]
-    half = lo_ref.shape[0]
-
-    def mul(a, w_ref):
-        return jnp.dot(a, w_ref[...], preferred_element_type=F32)
-
-    acc = mul(a_ref[me], own_ref)
-    acc += mul(a_ref[me ^ 1], core_ref)
-    acc += mul(a_ref[me ^ 2, :, :half], lo_ref)
-    acc += mul(a_ref[me ^ 2, :, half:], hi_ref)
-    acc += mul(a_ref[me ^ 3, :, :half], clo_ref)
-    acc += mul(a_ref[me ^ 3, :, half:], chi_ref)
-    out_ref[...] = acc.astype(BF16)
+    for g in range(a_ref.shape[0]):
+        acat_ref[:, pl.ds(g * feat, feat)] = a_ref[me ^ g]
+    for n in range(cols // tile):
+        for k in range(len(weights)):
+            copies[n * len(weights) + k].wait()
+        span = pl.ds(n * tile, tile)
+        out_ref[:, span] = dot_nn(acat_ref[...], w_ref[:, span]).astype(BF16)
 
 
 def project(me, a, weights, tile=512):
-    _, rows, feat = a.shape
+    groups, rows, feat = a.shape
     cols = weights[0].shape[1]
     return pl.pallas_call(
-        project_kernel,
+        lambda *refs: project_kernel(tile, *refs),
         out_shape=jax.ShapeDtypeStruct((rows, cols), BF16),
-        grid_spec=pltpu.PrefetchScalarGridSpec(
-            num_scalar_prefetch=1,
-            grid=(cols // tile,),
-            in_specs=[pl.BlockSpec(a.shape, lambda n, me: (0, 0, 0))]
-            + [pl.BlockSpec((w.shape[0], tile), lambda n, me: (0, n)) for w in weights],
-            out_specs=pl.BlockSpec((rows, tile), lambda n, me: (0, n)),
-        ),
+        in_specs=[SM, VM] + [HB] * len(weights),
+        out_specs=VM,
+        scratch_shapes=[
+            pltpu.VMEM((groups * feat, cols), BF16),
+            pltpu.VMEM((rows, groups * feat), BF16),
+            pltpu.SemaphoreType.DMA((cols // tile * len(weights),)),
+        ],
         compiler_params=pltpu.CompilerParams(vmem_limit_bytes=VMEM_LIMIT),
         name="project",
     )(me, a, *weights)
@@ -317,9 +334,8 @@
     high = lax.ppermute(high, XRING, [(i, (i - 1) % ring) for i in range(ring)])
     turns = [(NZ * i + NZ - 1, NZ * i + NZ) for i in range(LANES - 1)]
     crossed = lax.ppermute(edge, SEQ, turns + [(b, a) for a, b in turns])
-    plane_ends = lane_exchange(jnp.broadcast_to(edge[None], (LANES,) + edge.shape))
-    up1, down1, asked, low, high, crossed, plane_ends = tie(
-        up1, down1, asked, low, high, crossed, plane_ends
+    up1, down1, asked, low, high, crossed, edge = tie(
+        up1, down1, asked, low, high, crossed, edge
     )
 
     up2, down2 = z_shift(up1, 1), z_shift(down1, -1)
@@ -331,6 +347,13 @@
     swap = [(0, 1), (1, 0)]
     weights = [w_out, lax.ppermute(w_out, "core", swap), low, high]
     weights += [lax.ppermute(low, "core", swap), lax.ppermute(high, "core", swap)]
+    edge, r1 = tie(edge, r1)
+    plane_ends = lane_exchange(jnp.broadcast_to(edge[None], (LANES,) + edge.shape))
+    before = jnp.where(z == 0, crossed, up1[blocks_dev - 1])
+    after = jnp.where(z == NZ - 1, crossed, down1[0])
+    kv_pad = jnp.concatenate([before, kv.reshape(tok, 2 * feat), after], axis=0)
+    up2, down2, r1, plane_ends, kv_pad = tie(up2, down2, r1, plane_ends, kv_pad)
+
     held = jnp.where(z == 0, plane_ends[0], plane_ends[LANES - 1])
     got = lax.ppermute(held, "z", [(0, 4), (7, 3)])
     held = jnp.where(jnp.logical_or(z == 4, z == 3), got, held)
@@ -340,10 +363,6 @@
     got = lax.ppermute(held, "z", [(i, i ^ 1) for i in range(NZ)])
     even = z % 2 == 0
     ends = jnp.concatenate([jnp.where(even, held, got), jnp.where(even, got, held)], axis=0)
-    before = jnp.where(z == 0, crossed, up1[blocks_dev - 1])
-    after = jnp.where(z == NZ - 1, crossed, down1[0])
-    kv_pad = jnp.concatenate([before, kv.reshape(tok, 2 * feat), after], axis=0)
-    up2, down2, r1, ends, kv_pad = tie(up2, down2, r1, ends, kv_pad)
 
     plan = [(0, lane, 0, lane, 1, -2) for lane in lanes]
     plan += [(1, lane, 1, lane, -1, 2) for lane in lanes]

time: 520 us -> 287 us (0.55)
  Pallas kernels: 270 us -> 53.9 us
  blocking collectives: 0 us -> 48.9 us
  waiting for transfers between devices: 108 us -> 75.8 us
  starting transfers between devices: 102 us -> 74.2 us
    pallas_call x2, Pallas kernels: 227 us -> 12.9 us  [pick(): pl.pallas_call(kernel, out_shape=tuple((pltpu.HBM(shape + block_shape, BF...]
    all_to_all x0 -> x1, blocking collectives: none -> 48.9 us  [body(): asked = lax.all_to_all(asked, SEQ, split_axis=0, concat_axis=0, tiled=True)]
    all_to_all x1 -> x0, waiting for transfers between devices: 36.1 us -> none  [body(): asked = lax.all_to_all(asked, SEQ, split_axis=0, concat_axis=0, tiled=True)]
    all_to_all x6, waiting for transfers between devices: 16.7 us -> 50.5 us  [lane_exchange(): return lax.all_to_all(x, LANE, split_axis=0, concat_axis=0, tiled=True)]
    ppermute x1, waiting for transfers between devices: 32.7 us -> 5.54 us  [body(): got = lax.ppermute(held, 'z', [(0, 4), (7, 3)])]
    all_to_all x1 -> x0, starting transfers between devices: 10.1 us -> none  [body(): asked = lax.all_to_all(asked, SEQ, split_axis=0, concat_axis=0, tiled=True)]
    all_to_all x1, starting transfers between devices: 14.1 us -> 6.29 us  [body(): lax.all_to_all(attended.reshape(heads, tok // heads, feat), HEAD, split_a...]
    ppermute x1, starting transfers between devices: 7.12 us -> 0.09 us  [body(): got = lax.ppermute(held, 'z', [(i, i ^ 1) for i in range(NZ)])]
  transfers between devices with their start and end apart: 27 -> 26, of which waited for: 7 -> 9; matrix products, arithmetic and copies ran while one was open for 4% -> 6% of each run, Pallas kernels for 6% -> 11%
where the time goes in v3:
time: 287 us; the launch traced here: 285 us
  waiting for transfers between devices  75.8 us (26%)
  starting transfers between devices  74.2 us (26%)
  Pallas kernels  53.9 us (19%)
  blocking collectives  48.9 us (17%)
  local copies, waits for them, and re-layouts  23.4 us (8%)
  other arithmetic  8.3 us (3%)
    all_to_all x6, waiting for transfers between devices, lane_exchange(): return lax.all_to_all(x, LANE, split_axis=0, concat_axis=0, tiled=True)  50.5 us
    all_to_all x1, blocking collectives, body(): asked = lax.all_to_all(asked, SEQ, split_axis=0, concat_axis=0, tiled=True)  48.9 us
    all_to_all x6, starting transfers between devices, lane_exchange(): return lax.all_to_all(x, LANE, split_axis=0, concat_axis=0, tiled=True)  30 us
    ppermute x10, starting transfers between devices, z_shift(): return lax.ppermute(x, 'z', [(i, (i + by) % NZ) for i in range(NZ)])  21.8 us
    pallas_call x1, Pallas kernels, local_part(): pl.pallas_call(lambda *refs: local_kernel(all_blocks, deltas, *refs), out...  15.5 us
    unnamed x25, local copies, waits for them, and re-layouts  13.9 us
    all_to_all x1, waiting for transfers between devices, body(): lax.all_to_all(attended.reshape(heads, tok // heads, feat), HEAD, split_a...  13.6 us
    pallas_call x2, Pallas kernels, pick(): pl.pallas_call(kernel, out_shape=tuple((pltpu.HBM(shape + block_shape, BF...  12.9 us
  transfers between devices with their start and end apart: 26, of which 9 were waited for; matrix products, arithmetic and copies ran while one was open for 6% of the time, Pallas kernels for 11%

profile of v3, /device:TPU:1, one launch (start us, length us, event | category | flops | bytes accessed | tf_op | source)
XLA Modules:
  0.0 285.0 jit_solution(4496146601750373423)
XLA Ops:
  0.0 3.2 %reshape.125.refs_0_ = bf16[16,64,1024]{2,1,0:T(8,128)(2,1)S(1)} reshape(bf16[1024,2,512]{2,1,0:T(2,128)(2,1)} %param.5) | data formatting | bytes 4194304 | tf_op jit(solution)/shard_map/reshape | solution.py:322
  3.2 2.5 collective-permute-start
  5.8 4.0 %collective-permute-start.1 = (bf16[16,64,1024]{2,1,0:T(8,128)(2,1)S(1)}, bf16[16,64,1024]{2,1,0:T(8,128)(2,1)}, u32[]{:S(2)}, u32[]{:S(2)}) collective-permute-start(bf16[16,64,1024]{2,1,0:T(8,128)(2,1)S(1)} %reshape.125.refs_0_), channel_id=1, source_target_pairs={{0,28},{4,0},{8,4},{12,8},{16,12},{20,16},{24,20},{28,24},{1,29},{... | collective-permute-start | bytes 6291464 | tf_op jit(solution)/shard_map/ppermute | solution.py:275
  9.8 4.8 %fusion.4 = (bf16[256,4096]{1,0:T(8,128)(2,1)}, bf16[256,4096]{1,0:T(8,128)(2,1)}) fusion(bf16[512,4096]{1,0:T(8,128)(2,1)} %refs_2_.5), kind=kLoop, calls=%fused_computation.32 | loop fusion | bytes 8388608 | tf_op jit(solution)/shard_map/slice | solution.py:329
  14.6 1.2 collective-permute-start.2
  15.8 1.5 collective-permute-start.3
  17.3 1.1 broadcast_select_fusion
  19.7 48.9 %all_to_all.47 = s32[64,1,8]{2,1,0:T(1,128)S(1)} all-to-all(s32[64,1,8]{2,1,0:T(1,128)S(1)} %bitcast.29), channel_id=1, replica_groups=mesh['y'=4,'xh'=2,'z'=8,'xl'=2,'core'=2] {'y','xh','z'}, dimensions={0} | all-to-all | bytes 4096 | tf_op jit(solution)/shard_map/all_to_all | solution.py:330
  68.6 6.1 %pick.2 = bf16[8,3,64,1024]{3,2,1,0:T(8,128)(2,1)} custom-call(s32[1]{0:T(128)} %bitcast.1.z_ref.refs_0_, s32[64,8]{1,0:T(8,128)S(1)} %bitcast.22, bf16[16,64,1024]{2,1,0:T(8,128)(2,1)S(1)} %reshape.125.refs_0_, bf16[16,64,1024]{2,1,0:T(8,128)(2,1)} %collective-permute-done.refs_1_, bf16[16,64,1024]{2,1,0:T(8,128)(2,1)} %collective-permute-done.1.refs_2_), custom_call_target="tpu_custom_call" | custom-call | flops 3000000000 | bytes 4194304 | tf_op jit(solution)/shard_map/pick/pallas_call | solution.py:213
  74.8 3.7 %all-to-all-start.1 = ((bf16[8,3,64,1024]{3,2,1,0:T(8,128)(2,1)}), bf16[8,3,64,1024]{3,2,1,0:T(8,128)(2,1)S(1)}, u32[]{:S(2)}, u32[]{:S(2)}) async-start(bf16[8,3,64,1024]{3,2,1,0:T(8,128)(2,1)} %pick.2), calls=%async_computation.1 | async-start | bytes 6291456 | tf_op jit(solution)/shard_map/all_to_all | solution.py:279
  78.6 2.7 collective-permute-start.6
  81.2 34.7 %all-to-all-done.1.refs_6_ = bf16[8,3,64,1024]{3,2,1,0:T(8,128)(2,1)S(1)} async-done(((bf16[8,3,64,1024]{3,2,1,0:T(8,128)(2,1)}), bf16[8,3,64,1024]{3,2,1,0:T(8,128)(2,1)S(1)}, u32[]{:S(2)}, u32[]{:S(2)}) %all-to-all-start.1) | async-done | bytes 3145760 | tf_op jit(solution)/shard_map/all_to_all | solution.py:279
  115.9 1.1 broadcast_in_dim.40
  117.0 5.0 %all-to-all-start.2 = ((bf16[8,64,1024]{2,1,0:T(8,128)(2,1)}), bf16[8,64,1024]{2,1,0:T(8,128)(2,1)}, u32[]{:S(2)}, u32[]{:S(2)}) async-start(bf16[8,64,1024]{2,1,0:T(8,128)(2,1)} %broadcast_in_dim.40), calls=%async_computation.2 | async-start | bytes 2097152 | tf_op jit(solution)/shard_map/all_to_all | solution.py:279
  122.1 2.1 copy.14
  124.2 1.0 bitcast_select_fusion.1
  125.2 1.6 pad_maximum_fusion.refs_4_
  126.9 10.3 %all-to-all-done.2 = bf16[8,64,1024]{2,1,0:T(8,128)(2,1)} async-done(((bf16[8,64,1024]{2,1,0:T(8,128)(2,1)}), bf16[8,64,1024]{2,1,0:T(8,128)(2,1)}, u32[]{:S(2)}, u32[]{:S(2)}) %all-to-all-start.2) | async-done | bytes 1048608 | tf_op jit(solution)/shard_map/all_to_all | solution.py:279
  137.1 6.7 %pick.3 = (bf16[8,64,1024]{2,1,0:T(8,128)(2,1)}, bf16[8,64,1024]{2,1,0:T(8,128)(2,1)}, bf16[4,64,1024]{2,1,0:T(8,128)(2,1)}, bf16[4,64,1024]{2,1,0:T(8,128)(2,1)}, bf16[8,2,64,1024]{3,2,1,0:T(8,128)(2,1)}) custom-call(s32[1]{0:T(128)} %bitcast.1.z_ref.refs_0_, s32[64,8]{1,0:T(8,128)S(1)} %bitcast.23, bf16[16,64,1024]{2,1,0:T(8,128)(2,1)} %collective-permute-done.5.refs_0_, ...), custom_call_target="tpu_custom_call" | custom-call | flops 3000000000 | bytes 4194304 | tf_op jit(solution)/shard_map/pick/pallas_call | solution.py:213
  143.9 4.3 %all-to-all-start.3 = ((bf16[8,64,1024]{2,1,0:T(8,128)(2,1)}), bf16[8,64,1024]{2,1,0:T(8,128)(2,1)}, u32[]{:S(2)}, u32[]{:S(2)}) async-start(bf16[8,64,1024]{2,1,0:T(8,128)(2,1)} %get-tuple-element.53), calls=%async_computation.3 | async-start | bytes 2097152 | tf_op jit(solution)/shard_map/all_to_all | solution.py:279
  148.2 2.7 collective-permute-start.11
  151.9 2.1 collective-permute-start.7
  154.0 5.5 %collective-permute-done.7 = bf16[64,1024]{1,0:T(8,128)(2,1)S(1)} collective-permute-done((bf16[64,1024]{1,0:T(8,128)(2,1)S(1)}, bf16[64,1024]{1,0:T(8,128)(2,1)S(1)}, u32[]{:S(2)}, u32[]{:S(2)}) %collective-permute-start.7) | collective-permute-done | bytes 131104 | tf_op jit(solution)/shard_map/ppermute | solution.py:358
  160.6 1.3 collective-permute-start.8
  162.2 5.9 %all-to-all-start.4 = ((bf16[8,64,1024]{2,1,0:T(8,128)(2,1)}), bf16[8,64,1024]{2,1,0:T(8,128)(2,1)}, u32[]{:S(2)}, u32[]{:S(2)}) async-start(bf16[8,64,1024]{2,1,0:T(8,128)(2,1)} %get-tuple-element.58), calls=%async_computation.4 | async-start | bytes 2097152 | tf_op jit(solution)/shard_map/all_to_all | solution.py:279
  168.1 5.3 %collective-permute-start.16 = (bf16[512,4096]{1,0:T(8,128)(2,1)}, bf16[512,4096]{1,0:T(8,128)(2,1)}, u32[]{:S(2)}, u32[]{:S(2)}) collective-permute-start(bf16[512,4096]{1,0:T(8,128)(2,1)} %refs_2_.5), channel_id=1, source_target_pairs={{0,1},{1,0},{2,3},{3,2},{4,5},{5,4},{6,7},{7,6},{8,9},{9,8},{10,11... | collective-permute-start | bytes 12582920 | tf_op jit(solution)/shard_map/ppermute | solution.py:348
  173.5 1.5 collective-permute-start.13
  174.9 2.2 collective-permute-start.14
  177.2 3.3 %collective-permute-start.17 = (bf16[256,4096]{1,0:T(8,128)(2,1)}, bf16[256,4096]{1,0:T(8,128)(2,1)}, u32[]{:S(2)}, u32[]{:S(2)}) collective-permute-start(bf16[256,4096]{1,0:T(8,128)(2,1)} %collective-permute-done.2.refs_4_), channel_id=1, source_target_pairs={{0,1},{1,0},{2,3},{3,2},{4,5},{5,4},{6,7},{7,6},{8,9},{9,8},{10,11... | collective-permute-start | bytes 6291464 | tf_op jit(solution)/shard_map/ppermute | solution.py:349
  181.2 5.3 %collective-permute-done.13 = bf16[4,64,1024]{2,1,0:T(8,128)(2,1)} collective-permute-done((bf16[4,64,1024]{2,1,0:T(8,128)(2,1)}, bf16[4,64,1024]{2,1,0:T(8,128)(2,1)}, u32[]{:S(2)}, u32[]{:S(2)}) %collective-permute-start.13) | collective-permute-done | bytes 524320 | tf_op jit(solution)/shard_map/ppermute | solution.py:275
  186.5 5.8 %collective-permute-start.12 = (bf16[8,64,1024]{2,1,0:T(8,128)(2,1)}, bf16[8,64,1024]{2,1,0:T(8,128)(2,1)}, u32[]{:S(2)}, u32[]{:S(2)}) collective-permute-start(bf16[8,64,1024]{2,1,0:T(8,128)(2,1)} %all-to-all-done.3), channel_id=1, source_target_pairs={{0,4},{4,8},{8,12},{12,16},{16,20},{20,24},{24,28},{28,0},{1,5},{5... | collective-permute-start | bytes 3145736 | tf_op jit(solution)/shard_map/ppermute | solution.py:275
  193.3 7.0 %all-to-all-start.5 = ((bf16[8,2,64,1024]{3,2,1,0:T(8,128)(2,1)}), bf16[8,2,64,1024]{3,2,1,0:T(8,128)(2,1)}, u32[]{:S(2)}, u32[]{:S(2)}) async-start(bf16[8,2,64,1024]{3,2,1,0:T(8,128)(2,1)} %get-tuple-element.64), calls=%async_computation.5 | async-start | bytes 4194304 | tf_op jit(solution)/shard_map/all_to_all | solution.py:279
  200.3 1.7 copy-done.1
  201.9 1.2 copy-done.2
  203.2 15.5 %local_part.1 = (f32[1024,512]{1,0:T(8,128)S(1)}, f32[1024,128]{1,0:T(8,128)S(1)}) custom-call(s32[1]{0:T(128)} %bitcast.1.z_ref.refs_0_, s32[64]{0:T(128)S(1)} %broadcast_add_fusion.refs_1_, s32[1]{0:T(128)} %bitcast.2.refs_2_, bf16[1024,512]{1,0:T(8,128)(2,1)S(1)} %copy-done.2, bf16[1152,1024]{1,0:T(8,128)(2,1)S(1)} %copy-done.1, ...), custom_call_target="tpu_custom_call" | custom-call | flops 24999999488 | bytes 4194304 | tf_op jit(solution)/shard_map/local_part/pallas_call | solution.py:151
  218.6 1.3 copy-done.6
  220.8 2.4 pad_maximum_fusion.1
  223.1 4.4 %all-to-all-done.5.refs_7_ = bf16[8,2,64,1024]{3,2,1,0:T(8,128)(2,1)} async-done(((bf16[8,2,64,1024]{3,2,1,0:T(8,128)(2,1)}), bf16[8,2,64,1024]{3,2,1,0:T(8,128)(2,1)}, u32[]{:S(2)}, u32[]{:S(2)}) %all-to-all-start.5) | async-done | bytes 2097184 | tf_op jit(solution)/shard_map/all_to_all | solution.py:279
  227.5 4.2 %all-to-all-start.6 = ((bf16[8,64,1024]{2,1,0:T(8,128)(2,1)}), bf16[8,64,1024]{2,1,0:T(8,128)(2,1)S(1)}, u32[]{:S(2)}, u32[]{:S(2)}) async-start(bf16[8,64,1024]{2,1,0:T(8,128)(2,1)} %pad_maximum_fusion.1), calls=%async_computation.6 | async-start | bytes 2097152 | tf_op jit(solution)/shard_map/all_to_all | solution.py:279
  231.8 1.6 copy-done.7
  233.4 11.6 %more_part.1 = (f32[1024,512]{1,0:T(8,128)S(1)}, f32[1024,128]{1,0:T(8,128)S(1)}) custom-call(s32[1]{0:T(128)} %bitcast.1.z_ref.refs_0_, s32[64]{0:T(128)S(1)} %broadcast_add_fusion.refs_1_, bf16[1024,512]{1,0:T(8,128)(2,1)S(1)} %copy-done.3, f32[1024,512]{1,0:T(8,128)S(1)} %copy-done.7, f32[1024,128]{1,0:T(8,128)S(1)} %copy-done.9, ...), custom_call_target="tpu_custom_call" | custom-call | flops 12000000000 | bytes 4194304 | tf_op jit(solution)/shard_map/more_part/pallas_call | solution.py:167
  244.9 1.3 copy-done.4
  247.1 1.6 copy-done.5
  248.7 5.1 %final_part.1 = bf16[1024,512]{1,0:T(8,128)(2,1)} custom-call(s32[1]{0:T(128)} %bitcast.1.z_ref.refs_0_, s32[64]{0:T(128)S(1)} %broadcast_add_fusion.refs_1_, bf16[1024,512]{1,0:T(8,128)(2,1)S(1)} %copy-done.3, f32[1024,512]{1,0:T(8,128)S(1)} %copy-done.5, f32[1024,128]{1,0:T(8,128)S(1)} %get-tuple-element.67.refs_4_, bf16[8,1,64,1024]{3,2,1,0:T(8,128)(2,1)S(1)} %bitcast.21), custom_call_target="tpu_custom_call" | custom-call | flops 6000000000 | bytes 4194304 | tf_op jit(solution)/shard_map/final_part/pallas_call | solution.py:183
  253.8 6.3 %all-to-all-start.7 = ((bf16[4,256,512]{2,1,0:T(8,128)(2,1)}), bf16[4,256,512]{2,1,0:T(8,128)(2,1)S(1)}, u32[]{:S(2)}, u32[]{:S(2)}) async-start(bf16[4,256,512]{2,1,0:T(8,128)(2,1)} %bitcast.11), calls=%async_computation.7 | async-start | bytes 2097152 | tf_op jit(solution)/shard_map/all_to_all | solution.py:401
  260.1 13.6 %all-to-all-done.7.refs_1_ = bf16[4,256,512]{2,1,0:T(8,128)(2,1)S(1)} async-done(((bf16[4,256,512]{2,1,0:T(8,128)(2,1)}), bf16[4,256,512]{2,1,0:T(8,128)(2,1)S(1)}, u32[]{:S(2)}, u32[]{:S(2)}) %all-to-all-start.7) | async-done | bytes 1048608 | tf_op jit(solution)/shard_map/all_to_all | solution.py:401
  273.6 2.2 copy-done
  275.8 9.0 %project.1 = bf16[256,4096]{1,0:T(8,128)(2,1)} custom-call(s32[1]{0:T(128)} %bitcast.refs_0_, bf16[4,256,512]{2,1,0:T(8,128)(2,1)S(1)} %all-to-all-done.7.refs_1_, bf16[512,4096]{1,0:T(8,128)(2,1)S(1)} %copy-done, bf16[512,4096]{1,0:T(8,128)(2,1)} %collective-permute-done.16.refs_3_, bf16[256,4096]{1,0:T(8,128)(2,1)} %collective-permute-done.2.refs_4_, ...), custom_call_target="tpu_custom_call" | custom-call | tf_op jit(solution)/shard_map/project/pallas_call | solution.py:259
  (58 shorter events, 7.3 us)
Async XLA Ops:
  3.2 15.8 %copy-start.10 = (s32[16,2]{0,1:T(2,128)S(1)}, s32[16,2]{0,1:T(2,128)}, u32[]{:S(2)}) copy-start(s32[16,2]{0,1:T(2,128)} %param.6) | copy-start | bytes 388
  3.2 65.4 %collective-permute-start = (bf16[16,64,1024]{2,1,0:T(8,128)(2,1)S(1)}, bf16[16,64,1024]{2,1,0:T(8,128)(2,1)}, u32[]{:S(2)}, u32[]{:S(2)}) collective-permute-start(bf16[16,64,1024]{2,1,0:T(8,128)(2,1)S(1)} %reshape.125.refs_0_), channel_id=1, source_target_pairs={{0,4},{4,8},{8,12},{12,16},{16,20},{20,24},{24,28},{28,0},{1,5},{5... | collective-permute-start | bytes 6291464 | tf_op jit(solution)/shard_map/ppermute | solution.py:275
  5.8 62.8 %collective-permute-start.1 = (bf16[16,64,1024]{2,1,0:T(8,128)(2,1)S(1)}, bf16[16,64,1024]{2,1,0:T(8,128)(2,1)}, u32[]{:S(2)}, u32[]{:S(2)}) collective-permute-start(bf16[16,64,1024]{2,1,0:T(8,128)(2,1)S(1)} %reshape.125.refs_0_), channel_id=1, source_target_pairs={{0,28},{4,0},{8,4},{12,8},{16,12},{20,16},{24,20},{28,24},{1,29},{... | collective-permute-start | bytes 6291464 | tf_op jit(solution)/shard_map/ppermute | solution.py:275
  14.6 54.0 %collective-permute-start.2 = (bf16[256,4096]{1,0:T(8,128)(2,1)}, bf16[256,4096]{1,0:T(8,128)(2,1)}, u32[]{:S(2)}, u32[]{:S(2)}) collective-permute-start(bf16[256,4096]{1,0:T(8,128)(2,1)} %get-tuple-element.74), channel_id=1, source_target_pairs={{0,2},{2,32},{32,34},{34,0},{1,3},{3,33},{33,35},{35,1},{4,6},{6,3... | collective-permute-start | bytes 6291464 | tf_op jit(solution)/shard_map/ppermute | solution.py:333
  15.8 52.8 %collective-permute-start.3 = (bf16[256,4096]{1,0:T(8,128)(2,1)}, bf16[256,4096]{1,0:T(8,128)(2,1)}, u32[]{:S(2)}, u32[]{:S(2)}) collective-permute-start(bf16[256,4096]{1,0:T(8,128)(2,1)} %get-tuple-element.73), channel_id=1, source_target_pairs={{0,34},{2,0},{32,2},{34,32},{1,35},{3,1},{33,3},{35,33},{4,38},{6,... | collective-permute-start | bytes 6291464 | tf_op jit(solution)/shard_map/ppermute | solution.py:334
  18.4 50.2 %collective-permute-start.4 = (bf16[64,1024]{1,0:T(8,128)(2,1)S(1)}, bf16[64,1024]{1,0:T(8,128)(2,1)S(1)}, u32[]{:S(2)}, u32[]{:S(2)}) collective-permute-start(bf16[64,1024]{1,0:T(8,128)(2,1)S(1)} %bitcast.26), channel_id=1, source_target_pairs={{28,32},{60,64},{92,96},{124,128},{156,160},{188,192},{220,224},{3... | collective-permute-start | bytes 393224 | tf_op jit(solution)/shard_map/ppermute | solution.py:336
  74.8 41.1 %all-to-all-start.1 = ((bf16[8,3,64,1024]{3,2,1,0:T(8,128)(2,1)}), bf16[8,3,64,1024]{3,2,1,0:T(8,128)(2,1)S(1)}, u32[]{:S(2)}, u32[]{:S(2)}) async-start(bf16[8,3,64,1024]{3,2,1,0:T(8,128)(2,1)} %pick.2), calls=%async_computation.1 | async-start | bytes 6291456 | tf_op jit(solution)/shard_map/all_to_all | solution.py:279
  78.5 48.4 %collective-permute-start.5 = (bf16[16,64,1024]{2,1,0:T(8,128)(2,1)}, bf16[16,64,1024]{2,1,0:T(8,128)(2,1)}, u32[]{:S(2)}, u32[]{:S(2)}) collective-permute-start(bf16[16,64,1024]{2,1,0:T(8,128)(2,1)} %collective-permute-done.refs_1_), channel_id=1, source_target_pairs={{0,4},{4,8},{8,12},{12,16},{16,20},{20,24},{24,28},{28,0},{1,5},{5... | collective-permute-start | bytes 6291464 | tf_op jit(solution)/shard_map/ppermute | solution.py:275
  78.6 48.3 %collective-permute-start.6 = (bf16[16,64,1024]{2,1,0:T(8,128)(2,1)}, bf16[16,64,1024]{2,1,0:T(8,128)(2,1)}, u32[]{:S(2)}, u32[]{:S(2)}) collective-permute-start(bf16[16,64,1024]{2,1,0:T(8,128)(2,1)} %collective-permute-done.1.refs_2_), channel_id=1, source_target_pairs={{0,28},{4,0},{8,4},{12,8},{16,12},{20,16},{24,20},{28,24},{1,29},{... | collective-permute-start | bytes 6291464 | tf_op jit(solution)/shard_map/ppermute | solution.py:275
  117.0 20.1 %all-to-all-start.2 = ((bf16[8,64,1024]{2,1,0:T(8,128)(2,1)}), bf16[8,64,1024]{2,1,0:T(8,128)(2,1)}, u32[]{:S(2)}, u32[]{:S(2)}) async-start(bf16[8,64,1024]{2,1,0:T(8,128)(2,1)} %broadcast_in_dim.40), calls=%async_computation.2 | async-start | bytes 2097152 | tf_op jit(solution)/shard_map/all_to_all | solution.py:279
  143.9 18.3 %all-to-all-start.3 = ((bf16[8,64,1024]{2,1,0:T(8,128)(2,1)}), bf16[8,64,1024]{2,1,0:T(8,128)(2,1)}, u32[]{:S(2)}, u32[]{:S(2)}) async-start(bf16[8,64,1024]{2,1,0:T(8,128)(2,1)} %get-tuple-element.53), calls=%async_computation.3 | async-start | bytes 2097152 | tf_op jit(solution)/shard_map/all_to_all | solution.py:279
  148.1 13.7 %collective-permute-start.10 = (bf16[4,64,1024]{2,1,0:T(8,128)(2,1)}, bf16[4,64,1024]{2,1,0:T(8,128)(2,1)}, u32[]{:S(2)}, u32[]{:S(2)}) collective-permute-start(bf16[4,64,1024]{2,1,0:T(8,128)(2,1)} %get-tuple-element.54), channel_id=1, source_target_pairs={{0,4},{4,8},{8,12},{12,16},{16,20},{20,24},{24,28},{28,0},{1,5},{5... | collective-permute-start | bytes 1572872 | tf_op jit(solution)/shard_map/ppermute | solution.py:275
  148.2 13.6 %collective-permute-start.11 = (bf16[4,64,1024]{2,1,0:T(8,128)(2,1)}, bf16[4,64,1024]{2,1,0:T(8,128)(2,1)}, u32[]{:S(2)}, u32[]{:S(2)}) collective-permute-start(bf16[4,64,1024]{2,1,0:T(8,128)(2,1)} %get-tuple-element.55), channel_id=1, source_target_pairs={{0,28},{4,0},{8,4},{12,8},{16,12},{20,16},{24,20},{28,24},{1,29},{... | collective-permute-start | bytes 1572872 | tf_op jit(solution)/shard_map/ppermute | solution.py:275
  151.9 7.7 %collective-permute-start.7 = (bf16[64,1024]{1,0:T(8,128)(2,1)S(1)}, bf16[64,1024]{1,0:T(8,128)(2,1)S(1)}, u32[]{:S(2)}, u32[]{:S(2)}) collective-permute-start(bf16[64,1024]{1,0:T(8,128)(2,1)S(1)} %select_bitcast_fusion), channel_id=1, source_target_pairs={{0,16},{28,12},{1,17},{29,13},{2,18},{30,14},{3,19},{31,15},{32,48... | collective-permute-start | bytes 393224 | tf_op jit(solution)/shard_map/ppermute | solution.py:358
  160.6 12.8 %collective-permute-start.8 = (bf16[64,1024]{1,0:T(8,128)(2,1)S(1)}, bf16[64,1024]{1,0:T(8,128)(2,1)S(1)}, u32[]{:S(2)}, u32[]{:S(2)}) collective-permute-start(bf16[64,1024]{1,0:T(8,128)(2,1)S(1)} %broadcast_select_fusion.1), channel_id=1, source_target_pairs={{0,8},{16,24},{28,20},{12,4},{1,9},{17,25},{29,21},{13,5},{2,10},{... | collective-permute-start | bytes 393224 | tf_op jit(solution)/shard_map/ppermute | solution.py:360
  162.2 30.9 %all-to-all-start.4 = ((bf16[8,64,1024]{2,1,0:T(8,128)(2,1)}), bf16[8,64,1024]{2,1,0:T(8,128)(2,1)}, u32[]{:S(2)}, u32[]{:S(2)}) async-start(bf16[8,64,1024]{2,1,0:T(8,128)(2,1)} %get-tuple-element.58), calls=%async_computation.4 | async-start | bytes 2097152 | tf_op jit(solution)/shard_map/all_to_all | solution.py:279
  168.1 92.0 %collective-permute-start.16 = (bf16[512,4096]{1,0:T(8,128)(2,1)}, bf16[512,4096]{1,0:T(8,128)(2,1)}, u32[]{:S(2)}, u32[]{:S(2)}) collective-permute-start(bf16[512,4096]{1,0:T(8,128)(2,1)} %refs_2_.5), channel_id=1, source_target_pairs={{0,1},{1,0},{2,3},{3,2},{4,5},{5,4},{6,7},{7,6},{8,9},{9,8},{10,11... | collective-permute-start | bytes 12582920 | tf_op jit(solution)/shard_map/ppermute | solution.py:348
  173.4 7.1 %collective-permute-start.9 = (bf16[64,1024]{1,0:T(8,128)(2,1)S(1)}, bf16[64,1024]{1,0:T(8,128)(2,1)S(1)}, u32[]{:S(2)}, u32[]{:S(2)}) collective-permute-start(bf16[64,1024]{1,0:T(8,128)(2,1)S(1)} %broadcast_select_fusion.2), channel_id=1, source_target_pairs={{0,4},{4,0},{8,12},{12,8},{16,20},{20,16},{24,28},{28,24},{1,5},{5... | collective-permute-start | bytes 393224 | tf_op jit(solution)/shard_map/ppermute | solution.py:363
  173.5 13.1 %collective-permute-start.13 = (bf16[4,64,1024]{2,1,0:T(8,128)(2,1)}, bf16[4,64,1024]{2,1,0:T(8,128)(2,1)}, u32[]{:S(2)}, u32[]{:S(2)}) collective-permute-start(bf16[4,64,1024]{2,1,0:T(8,128)(2,1)} %collective-permute-done.10), channel_id=1, source_target_pairs={{0,4},{4,8},{8,12},{12,16},{16,20},{20,24},{24,28},{28,0},{1,5},{5... | collective-permute-start | bytes 1572872 | tf_op jit(solution)/shard_map/ppermute | solution.py:275
  174.9 18.2 %collective-permute-start.14 = (bf16[4,64,1024]{2,1,0:T(8,128)(2,1)}, bf16[4,64,1024]{2,1,0:T(8,128)(2,1)}, u32[]{:S(2)}, u32[]{:S(2)}) collective-permute-start(bf16[4,64,1024]{2,1,0:T(8,128)(2,1)} %collective-permute-done.11), channel_id=1, source_target_pairs={{0,28},{4,0},{8,4},{12,8},{16,12},{20,16},{24,20},{28,24},{1,29},{... | collective-permute-start | bytes 1572872 | tf_op jit(solution)/shard_map/ppermute | solution.py:275
  177.2 82.9 %collective-permute-start.17 = (bf16[256,4096]{1,0:T(8,128)(2,1)}, bf16[256,4096]{1,0:T(8,128)(2,1)}, u32[]{:S(2)}, u32[]{:S(2)}) collective-permute-start(bf16[256,4096]{1,0:T(8,128)(2,1)} %collective-permute-done.2.refs_4_), channel_id=1, source_target_pairs={{0,1},{1,0},{2,3},{3,2},{4,5},{5,4},{6,7},{7,6},{8,9},{9,8},{10,11... | collective-permute-start | bytes 6291464 | tf_op jit(solution)/shard_map/ppermute | solution.py:349
  180.4 79.6 %collective-permute-start.18 = (bf16[256,4096]{1,0:T(8,128)(2,1)}, bf16[256,4096]{1,0:T(8,128)(2,1)}, u32[]{:S(2)}, u32[]{:S(2)}) collective-permute-start(bf16[256,4096]{1,0:T(8,128)(2,1)} %collective-permute-done.3.refs_5_), channel_id=1, source_target_pairs={{0,1},{1,0},{2,3},{3,2},{4,5},{5,4},{6,7},{7,6},{8,9},{9,8},{10,11... | collective-permute-start | bytes 6291464 | tf_op jit(solution)/shard_map/ppermute | solution.py:349
  186.5 45.2 %collective-permute-start.12 = (bf16[8,64,1024]{2,1,0:T(8,128)(2,1)}, bf16[8,64,1024]{2,1,0:T(8,128)(2,1)}, u32[]{:S(2)}, u32[]{:S(2)}) collective-permute-start(bf16[8,64,1024]{2,1,0:T(8,128)(2,1)} %all-to-all-done.3), channel_id=1, source_target_pairs={{0,4},{4,8},{8,12},{12,16},{16,20},{20,24},{24,28},{28,0},{1,5},{5... | collective-permute-start | bytes 3145736 | tf_op jit(solution)/shard_map/ppermute | solution.py:275
  193.1 38.6 %collective-permute-start.15 = (bf16[8,64,1024]{2,1,0:T(8,128)(2,1)}, bf16[8,64,1024]{2,1,0:T(8,128)(2,1)}, u32[]{:S(2)}, u32[]{:S(2)}) collective-permute-start(bf16[8,64,1024]{2,1,0:T(8,128)(2,1)} %all-to-all-done.4), channel_id=1, source_target_pairs={{0,28},{4,0},{8,4},{12,8},{16,12},{20,16},{24,20},{28,24},{1,29},{... | collective-permute-start | bytes 3145736 | tf_op jit(solution)/shard_map/ppermute | solution.py:275
  193.3 34.2 %all-to-all-start.5 = ((bf16[8,2,64,1024]{3,2,1,0:T(8,128)(2,1)}), bf16[8,2,64,1024]{3,2,1,0:T(8,128)(2,1)}, u32[]{:S(2)}, u32[]{:S(2)}) async-start(bf16[8,2,64,1024]{3,2,1,0:T(8,128)(2,1)} %get-tuple-element.64), calls=%async_computation.5 | async-start | bytes 4194304 | tf_op jit(solution)/shard_map/all_to_all | solution.py:279
  200.3 1.7 copy-start.1
  201.9 1.2 copy-start.2
  218.6 1.3 copy-start.6
  219.9 0.8 copy-start.8
  220.7 11.0 %copy-start.3 = (bf16[1024,512]{1,0:T(8,128)(2,1)S(1)}, bf16[1024,512]{1,0:T(8,128)(2,1)}, u32[]{:S(2)}) copy-start(bf16[1024,512]{1,0:T(8,128)(2,1)} %refs_2_.4) | copy-start | bytes 3145732
  223.1 8.6 %copy-start.9 = (f32[1024,128]{1,0:T(8,128)S(1)}, f32[1024,128]{1,0:T(8,128)}, u32[]{:S(2)}) copy-start(f32[1024,128]{1,0:T(8,128)} %copy-done.8) | copy-start | bytes 1572868
  227.5 19.6 %all-to-all-start.6 = ((bf16[8,64,1024]{2,1,0:T(8,128)(2,1)}), bf16[8,64,1024]{2,1,0:T(8,128)(2,1)S(1)}, u32[]{:S(2)}, u32[]{:S(2)}) async-start(bf16[8,64,1024]{2,1,0:T(8,128)(2,1)} %pad_maximum_fusion.1), calls=%async_computation.6 | async-start | bytes 2097152 | tf_op jit(solution)/shard_map/all_to_all | solution.py:279
  231.8 1.6 copy-start.7
  244.9 1.3 copy-start.4
  247.1 1.6 copy-start.5
  253.8 19.9 %all-to-all-start.7 = ((bf16[4,256,512]{2,1,0:T(8,128)(2,1)}), bf16[4,256,512]{2,1,0:T(8,128)(2,1)S(1)}, u32[]{:S(2)}, u32[]{:S(2)}) async-start(bf16[4,256,512]{2,1,0:T(8,128)(2,1)} %bitcast.11), calls=%async_computation.7 | async-start | bytes 2097152 | tf_op jit(solution)/shard_map/all_to_all | solution.py:401
  273.6 2.2 copy-start

commit v4 on v3

--- a/solution.py
+++ b/solution.py
@@ -42,7 +42,8 @@
 
 
 def local_kernel(all_blocks, deltas, z_ref, where_ref, id_ref, *refs):
-    q_ref, kv_ref, ends_ref, slots_ref, o_ref, st_ref = refs
+    q_ref, kv_ref, ends_ref = refs[:3]
+    slots, (o_ref, st_ref) = refs[3:-2], refs[-2:]
     feat = q_ref.shape[1]
     heads = range(feat // HEAD_DIM)
     blocks = q_ref.shape[0] // BLOCK
@@ -80,7 +81,8 @@
         return carry
 
     lax.fori_loop(0, blocks, step, 0)
-    add_slots(deltas, z_ref, where_ref, slots_ref, q_ref, o_ref, st_ref)
+    for which, ref in zip(deltas, slots):
+        add_slots(which, z_ref, where_ref, ref, q_ref, o_ref, st_ref)
 
 
 def add_slots(deltas, z_ref, where_ref, slots_ref, q_ref, o_ref, st_ref):
@@ -154,12 +156,12 @@
             jax.ShapeDtypeStruct((tok, feat), F32),
             jax.ShapeDtypeStruct((tok, 128), F32),
         ),
-        in_specs=[SM, SM, SM, VM, VM, VM, VM],
+        in_specs=[SM, SM, SM] + [VM] * (3 + len(slots)),
         out_specs=(VM, VM),
         compiler_params=pltpu.CompilerParams(vmem_limit_bytes=VMEM_LIMIT),
         cost_estimate=cost(25),
         name="local_part",
-    )(z, where, first_id, q, kv_pad, ends, slots)
+    )(z, where, first_id, q, kv_pad, ends, *slots)
 
 
 def more_part(z, where, q, o, st, deltas, slots):
@@ -198,8 +200,13 @@
         held, in_sems, out_sems = refs[-3:]
         loads, stores = [], []
         for n, (o, position, s, lane, plane, owner) in enumerate(plan):
-            row = lane * NZ + lax.rem(z_ref[0] + (plane + NZ), NZ)
-            block = asked_ref[row, lax.rem(z_ref[0] + (owner + NZ), NZ)]
+            if lane is None:
+                block = jnp.where(z_ref[0] == 0, 0, sources[s].shape[0] - 1)
+            else:
+                row = lane
+                if asked.shape[0] > LANES:
+                    row = lax.rem(z_ref[0] + (plane + NZ), NZ) * LANES + lane
+                block = asked_ref[row, lax.rem(z_ref[0] + (owner + NZ), NZ)]
             loads.append(pltpu.make_async_copy(src[s].at[block], held.at[n], in_sems.at[n]))
             stores.append(pltpu.make_async_copy(held.at[n], out[o].at[position], out_sems.at[n]))
             loads[-1].start()
@@ -321,79 +328,82 @@
 
     kv = keys_values.reshape(blocks_dev, BLOCK, 2 * feat)
 
+    up1, down1 = z_shift(kv, 1), z_shift(kv, -1)
     block_ids = first_id + jnp.arange(blocks_dev, dtype=jnp.int32)
     offset, where = wanted_blocks(rand_blocks, block_ids, all_blocks, blocks_dev)
-    asked = jnp.broadcast_to(offset.reshape(LANES, 1, NZ), (LANES, NZ, NZ)).reshape(-1, NZ)
+    mine = lane_exchange(offset.reshape(LANES, NZ))
+    rows = w_out.shape[0] // 2
+    own = [w_out[:rows], w_out[rows:]]
+    ring = NXH * NXL
+    low = lax.ppermute(own[0], XRING, [(i, (i + 1) % ring) for i in range(ring)])
+    high = lax.ppermute(own[1], XRING, [(i, (i - 1) % ring) for i in range(ring)])
     edge = jnp.where(z == 0, kv[0], kv[blocks_dev - 1])
-    rows = w_out.shape[0] // 2
-    low, high = w_out[:rows], w_out[rows:]
-    asked = lax.all_to_all(asked, SEQ, split_axis=0, concat_axis=0, tiled=True)
-    up1, down1 = z_shift(kv, 1), z_shift(kv, -1)
-    ring = NXH * NXL
-    low = lax.ppermute(low, XRING, [(i, (i + 1) % ring) for i in range(ring)])
-    high = lax.ppermute(high, XRING, [(i, (i - 1) % ring) for i in range(ring)])
     turns = [(NZ * i + NZ - 1, NZ * i + NZ) for i in range(LANES - 1)]
     crossed = lax.ppermute(edge, SEQ, turns + [(b, a) for a, b in turns])
-    up1, down1, asked, low, high, crossed, edge = tie(
-        up1, down1, asked, low, high, crossed, edge
+    plan = [(0, (lane, 0), 0, lane, 0, 0) for lane in lanes]
+    plan += [(0, (lane, 1), 0, None, 0, 0) for lane in lanes]
+    (c0,) = pick(zs, mine, [kv], plan, [(LANES, 2)])
+    r0 = lane_exchange(c0)
+    table, r0 = tie(mine, r0)
+    table = jnp.broadcast_to(table[None], (NZ, LANES, NZ))
+    asked = lax.all_to_all(table, "z", split_axis=0, concat_axis=0, tiled=True)
+    asked = asked.reshape(NZ * LANES, NZ)
+    up1, down1, asked, low, high, crossed, r0 = tie(up1, down1, asked, low, high, crossed, r0)
+
+    plan = [(0, lane, 0, lane, 3, -1) for lane in lanes[:half]]
+    plan += [(1, lane - half, 1, lane, -3, 1) for lane in lanes[half:]]
+    plan += [(2, lane, 0, lane, 2, -1) for lane in lanes]
+    plan += [(3, lane, 1, lane, -2, 1) for lane in lanes]
+    fu, fd, c3u, c3d = pick(
+        zs, asked, [up1, down1], plan, [(half,), (half,), (LANES,), (LANES,)]
     )
-
-    up2, down2 = z_shift(up1, 1), z_shift(down1, -1)
-    plan = [(0, (lane, 0), 0, lane, 0, 0) for lane in lanes]
-    plan += [(0, (lane, 1), 1, lane, 0, -1) for lane in lanes]
-    plan += [(0, (lane, 2), 2, lane, 0, 1) for lane in lanes]
-    (c1,) = pick(zs, asked, [kv, up1, down1], plan, [(LANES, 3)])
-    r1 = lane_exchange(c1)
+    fu, fd = z_shift(fu, 1), z_shift(fd, -1)
+    c3u, c3d = z_shift(c3u, 1), z_shift(c3d, -1)
+    plan = [(0, (lane, 0), 0, lane, 1, -1) for lane in lanes]
+    plan += [(0, (lane, 1), 1, lane, -1, 1) for lane in lanes]
+    plan += [(1, (lane, 0), 0, lane, 0, -1) for lane in lanes]
+    plan += [(1, (lane, 1), 1, lane, 0, 1) for lane in lanes]
+    c2, c1 = pick(zs, asked, [up1, down1], plan, [(LANES, 2), (LANES, 2)])
+    c2 = lane_exchange(c2)
     swap = [(0, 1), (1, 0)]
-    weights = [w_out, lax.ppermute(w_out, "core", swap), low, high]
+    weights = own + [lax.ppermute(w_out, "core", swap), low, high]
     weights += [lax.ppermute(low, "core", swap), lax.ppermute(high, "core", swap)]
-    edge, r1 = tie(edge, r1)
-    plane_ends = lane_exchange(jnp.broadcast_to(edge[None], (LANES,) + edge.shape))
     before = jnp.where(z == 0, crossed, up1[blocks_dev - 1])
     after = jnp.where(z == NZ - 1, crossed, down1[0])
     kv_pad = jnp.concatenate([before, kv.reshape(tok, 2 * feat), after], axis=0)
-    up2, down2, r1, plane_ends, kv_pad = tie(up2, down2, r1, plane_ends, kv_pad)
-
-    held = jnp.where(z == 0, plane_ends[0], plane_ends[LANES - 1])
+    held = jnp.where(z == 0, r0[0, 1], r0[LANES - 1, 1])
     got = lax.ppermute(held, "z", [(0, 4), (7, 3)])
     held = jnp.where(jnp.logical_or(z == 4, z == 3), got, held)
+    fu, fd, c3u, c3d, c2, c1, kv_pad, held = tie(fu, fd, c3u, c3d, c2, c1, kv_pad, held)
+
+    fu, fd = z_shift(fu, 1), z_shift(fd, -1)
+    r1 = lane_exchange(c1)
+    r2u, r2d = z_shift(c2[:, 0], 1), z_shift(c2[:, 1], -1)
     got = lax.ppermute(held, "z", [(0, 2), (4, 6), (7, 5), (3, 1)])
     fresh = reduce(jnp.logical_or, [z == 2, z == 6, z == 5, z == 1])
     held = jnp.where(fresh, got, held)
+    c3u, r1, fu, fd = tie(c3u, r1, fu, fd)
+    fu, fd = z_shift(fu, 1), z_shift(fd, -1)
     got = lax.ppermute(held, "z", [(i, i ^ 1) for i in range(NZ)])
     even = z % 2 == 0
     ends = jnp.concatenate([jnp.where(even, held, got), jnp.where(even, got, held)], axis=0)
-
-    plan = [(0, lane, 0, lane, 1, -2) for lane in lanes]
-    plan += [(1, lane, 1, lane, -1, 2) for lane in lanes]
-    plan += [(2, lane, 0, lane, 2, -2) for lane in lanes[:half]]
-    plan += [(3, lane - half, 1, lane, -2, 2) for lane in lanes[half:]]
-    plan += [(4, (lane, 0), 0, lane, 0, -2) for lane in lanes]
-    plan += [(4, (lane, 1), 1, lane, 0, 2) for lane in lanes]
-    c3u, c3d, fu, fd, c2 = pick(
-        zs, asked, [up2, down2], plan, [(LANES,), (LANES,), (half,), (half,), (LANES, 2)]
-    )
-    fu, fd = z_shift(fu, 1), z_shift(fd, -1)
     c3u = lane_exchange(c3u)
-    c3d, c3u, fu, fd = tie(c3d, c3u, fu, fd)
+    c3d, c3u = tie(c3d, c3u)
     r3u = z_shift(c3u, 1)
-    fu, fd = z_shift(fu, 1), z_shift(fd, -1)
     c3d = lane_exchange(c3d)
-    c2, c3d, fu, fd = tie(c2, c3d, fu, fd)
+    far = jnp.concatenate([fu, fd], axis=0)
+    far, c3d = tie(far, c3d)
     r3d = z_shift(c3d, -1)
-    r2 = lane_exchange(c2)
-    far = jnp.concatenate([fu, fd], axis=0)
-    far, r2 = tie(far, r2)
     r4 = lane_exchange(far)
 
     def slots(x):
         return x.reshape(LANES, 1, BLOCK, 2 * feat)
 
     o, st = local_part(
-        zs, where, first_id.reshape(1), all_blocks, queries, kv_pad, ends, (0, -1, 1), r1
+        zs, where, first_id.reshape(1), all_blocks, queries, kv_pad, ends, [(0,), (-1, 1)], [r0, r1]
     )
     o, st = more_part(
-        zs, where, queries, o, st, [(-3,), (3,), (-2, 2)], [slots(r3u), slots(r3d), r2]
+        zs, where, queries, o, st, [(-2,), (2,), (-3,), (3,)], [slots(x) for x in (r2u, r2d, r3u, r3d)]
     )
     attended = final_part(zs, where, queries, o, st, [(4,)], [slots(r4)])
 

time: 287 us -> 327 us (1.14)
  blocking collectives: 48.9 us -> 0 us
  waiting for transfers between devices: 75.8 us -> 124 us
  starting transfers between devices: 74.2 us -> 102 us
  local copies, waits for them, and re-layouts: 23.4 us -> 31.3 us
  Pallas kernels: 53.9 us -> 58.1 us
    all_to_all x1 -> x0, blocking collectives: 48.9 us -> none  [body(): asked = lax.all_to_all(asked, SEQ, split_axis=0, concat_axis=0, tiled=True)]
    all_to_all x6 -> x7, waiting for transfers between devices: 50.5 us -> 77.3 us  [lane_exchange(): return lax.all_to_all(x, LANE, split_axis=0, concat_axis=0, tiled=True)]
    ppermute x1, starting transfers between devices: 3.28 us -> 15.6 us  [body(): lax.ppermute(low, 'core', swap)]
    ppermute x1, waiting for transfers between devices: 5.54 us -> 16.5 us  [body(): got = lax.ppermute(held, 'z', [(0, 4), (7, 3)])]
    all_to_all x6 -> x7, starting transfers between devices: 30 us -> 40.3 us  [lane_exchange(): return lax.all_to_all(x, LANE, split_axis=0, concat_axis=0, tiled=True)]
    all_to_all x0 -> x1, waiting for transfers between devices: none -> 6.87 us  [body(): asked = lax.all_to_all(table, 'z', split_axis=0, concat_axis=0, tiled=True)]
    all_to_all x0 -> x1, starting transfers between devices: none -> 5.27 us  [body(): asked = lax.all_to_all(table, 'z', split_axis=0, concat_axis=0, tiled=True)]
    unnamed x25 -> x31, local copies, waits for them, and re-layouts: 13.9 us -> 18.2 us
  transfers between devices with their start and end apart: 26 -> 32, of which waited for: 9 -> 9; matrix products, arithmetic and copies ran while one was open for 6% -> 6% of each run, Pallas kernels for 11% -> 13%
where the time goes in v4:
time: 327 us; the launch traced here: 324 us
  waiting for transfers between devices  124 us (38%)
  starting transfers between devices  102 us (31%)
  Pallas kernels  58.1 us (18%)
  local copies, waits for them, and re-layouts  31.3 us (10%)
  other arithmetic  8.59 us (3%)
    all_to_all x7, waiting for transfers between devices, lane_exchange(): return lax.all_to_all(x, LANE, split_axis=0, concat_axis=0, tiled=True)  77.3 us
    all_to_all x7, starting transfers between devices, lane_exchange(): return lax.all_to_all(x, LANE, split_axis=0, concat_axis=0, tiled=True)  40.3 us
    ppermute x14, starting transfers between devices, z_shift(): return lax.ppermute(x, 'z', [(i, (i + by) % NZ) for i in range(NZ)])  21.4 us
    unnamed x31, local copies, waits for them, and re-layouts  18.2 us
    pallas_call x1, Pallas kernels, local_part(): pl.pallas_call(lambda *refs: local_kernel(all_blocks, deltas, *refs), out...  17.8 us
    ppermute x1, waiting for transfers between devices, body(): got = lax.ppermute(held, 'z', [(0, 4), (7, 3)])  16.5 us
    pallas_call x3, Pallas kernels, pick(): pl.pallas_call(kernel, out_shape=tuple((pltpu.HBM(shape + block_shape, BF...  16.1 us
    ppermute x1, starting transfers between devices, body(): lax.ppermute(low, 'core', swap)  15.6 us
  transfers between devices with their start and end apart: 32, of which 9 were waited for; matrix products, arithmetic and copies ran while one was open for 6% of the time, Pallas kernels for 13%

profile of v4, /device:TPU:1, one launch (start us, length us, event | category | flops | bytes accessed | tf_op | source)
XLA Modules:
  0.0 324.2 jit_solution(7699538098547032408)
XLA Ops:
  0.0 4.4 %reshape.132.refs_0_ = bf16[16,64,1024]{2,1,0:T(8,128)(2,1)} reshape(bf16[1024,2,512]{2,1,0:T(2,128)(2,1)} %param.5) | data formatting | bytes 4194304 | tf_op jit(solution)/shard_map/reshape | solution.py:329
  4.4 2.5 collective-permute-start
  6.9 3.9 %collective-permute-start.1 = (bf16[16,64,1024]{2,1,0:T(8,128)(2,1)}, bf16[16,64,1024]{2,1,0:T(8,128)(2,1)}, u32[]{:S(2)}, u32[]{:S(2)}) collective-permute-start(bf16[16,64,1024]{2,1,0:T(8,128)(2,1)} %reshape.132.refs_0_), channel_id=1, source_target_pairs={{0,28},{4,0},{8,4},{12,8},{16,12},{20,16},{24,20},{28,24},{1,29},{... | collective-permute-start | bytes 6291464 | tf_op jit(solution)/shard_map/ppermute | solution.py:282
  12.1 6.7 %all-to-all-start = ((s32[8,1,8]{2,1,0:T(1,128)}), s32[8,1,8]{2,1,0:T(1,128)S(1)}, u32[]{:S(2)}, u32[]{:S(2)}) async-start(s32[8,1,8]{2,1,0:T(1,128)} %bitcast.3), calls=%async_computation | async-start | bytes 8192 | tf_op jit(solution)/shard_map/all_to_all | solution.py:286
  18.7 4.0 %fusion.4 = (bf16[256,4096]{1,0:T(8,128)(2,1)S(1)}, bf16[256,4096]{1,0:T(8,128)(2,1)}) fusion(bf16[512,4096]{1,0:T(8,128)(2,1)} %param.7), kind=kLoop, calls=%fused_computation.34 | loop fusion | bytes 8388608 | tf_op jit(solution)/shard_map/slice | solution.py:336
  23.0 2.4 collective-permute-start.3
  25.4 4.4 %pick.3 = bf16[8,2,64,1024]{3,2,1,0:T(8,128)(2,1)} custom-call(s32[1]{0:T(128)} %bitcast.1.z_ref.refs_0_, s32[8,8]{1,0:T(8,128)S(1)} %bitcast.32, bf16[16,64,1024]{2,1,0:T(8,128)(2,1)} %reshape.132.refs_0_), custom_call_target="tpu_custom_call" | custom-call | flops 3000000000 | bytes 4194304 | tf_op jit(solution)/shard_map/pick/pallas_call | solution.py:220
  29.8 5.5 %all-to-all-start.1 = ((bf16[8,2,64,1024]{3,2,1,0:T(8,128)(2,1)}), bf16[8,2,64,1024]{3,2,1,0:T(8,128)(2,1)}, u32[]{:S(2)}, u32[]{:S(2)}) async-start(bf16[8,2,64,1024]{3,2,1,0:T(8,128)(2,1)} %pick.3), calls=%async_computation.1 | async-start | bytes 4194304 | tf_op jit(solution)/shard_map/all_to_all | solution.py:286
  37.2 58.5 %all-to-all-done.1.refs_6_ = bf16[8,2,64,1024]{3,2,1,0:T(8,128)(2,1)} async-done(((bf16[8,2,64,1024]{3,2,1,0:T(8,128)(2,1)}), bf16[8,2,64,1024]{3,2,1,0:T(8,128)(2,1)}, u32[]{:S(2)}, u32[]{:S(2)}) %all-to-all-start.1) | async-done | bytes 2097184 | tf_op jit(solution)/shard_map/all_to_all | solution.py:286
  96.3 5.3 %all-to-all-start.2 = ((s32[8,8,8]{2,1,0:T(8,128)}), s32[8,8,8]{2,1,0:T(8,128)S(1)}, u32[]{:S(2)}, u32[]{:S(2)}) async-start(s32[8,8,8]{2,1,0:T(8,128)} %broadcast_in_dim.31), calls=%async_computation.2 | async-start | bytes 65536 | tf_op jit(solution)/shard_map/all_to_all | solution.py:349
  101.5 6.9 %all-to-all-done.2 = s32[8,8,8]{2,1,0:T(8,128)S(1)} async-done(((s32[8,8,8]{2,1,0:T(8,128)}), s32[8,8,8]{2,1,0:T(8,128)S(1)}, u32[]{:S(2)}, u32[]{:S(2)}) %all-to-all-start.2) | async-done | bytes 2080 | tf_op jit(solution)/shard_map/all_to_all | solution.py:349
  108.4 6.3 %pick.5 = (bf16[8,2,64,1024]{3,2,1,0:T(8,128)(2,1)}, bf16[8,2,64,1024]{3,2,1,0:T(8,128)(2,1)}) custom-call(s32[1]{0:T(128)} %bitcast.1.z_ref.refs_0_, s32[64,8]{1,0:T(8,128)S(1)} %bitcast.30, bf16[16,64,1024]{2,1,0:T(8,128)(2,1)} %collective-permute-done.refs_0_, bf16[16,64,1024]{2,1,0:T(8,128)(2,1)} %collective-permute-done.1.refs_1_), custom_call_target="tpu_custom_call" | custom-call | flops 3000000000 | bytes 4194304 | tf_op jit(solution)/shard_map/pick/pallas_call | solution.py:220
  114.7 4.4 %all-to-all-start.3 = ((bf16[8,2,64,1024]{3,2,1,0:T(8,128)(2,1)}), bf16[8,2,64,1024]{3,2,1,0:T(8,128)(2,1)}, u32[]{:S(2)}, u32[]{:S(2)}) async-start(bf16[8,2,64,1024]{3,2,1,0:T(8,128)(2,1)} %get-tuple-element.49), calls=%async_computation.3 | async-start | bytes 4194304 | tf_op jit(solution)/shard_map/all_to_all | solution.py:286
  119.1 5.5 %pick.4 = (bf16[4,64,1024]{2,1,0:T(8,128)(2,1)}, bf16[4,64,1024]{2,1,0:T(8,128)(2,1)}, bf16[8,64,1024]{2,1,0:T(8,128)(2,1)}, bf16[8,64,1024]{2,1,0:T(8,128)(2,1)}) custom-call(s32[1]{0:T(128)} %bitcast.1.z_ref.refs_0_, s32[64,8]{1,0:T(8,128)S(1)} %bitcast.31, bf16[16,64,1024]{2,1,0:T(8,128)(2,1)} %collective-permute-done.refs_0_, ...), custom_call_target="tpu_custom_call" | custom-call | flops 3000000000 | bytes 4194304 | tf_op jit(solution)/shard_map/pick/pallas_call | solution.py:220
  124.6 2.7 collective-permute-start.8
  127.3 3.5 %copy.24 = bf16[128,8,2,512]{3,1,2,0:T(8,128)(2,1)} copy(bf16[128,8,2,512]{3,2,1,0:T(2,128)(2,1)} %bitcast.34) | data formatting | bytes 4194304
  130.8 2.7 collective-permute-start.6
  134.5 2.3 collective-permute-start.9
  137.7 3.2 %pad_maximum_fusion.refs_4_ = bf16[1152,1024]{1,0:T(8,128)(2,1)} fusion(bf16[64,1024]{1,0:T(8,128)(2,1)S(1)} %get-tuple-element.84, bf16[1024,1024]{1,0:T(8,128)(2,1)} %bitcast.35, bf16[64,1024]{1,0:T(8,128)(2,1)S(1)} %get-tuple-element.83), kind=kLoop, calls=%fused_computation | loop fusion | flops 7077888 | bytes 4718592 | tf_op jit(solution)/shard_map/concatenate | solution.py:373
  141.0 16.5 %collective-permute-done.9 = bf16[64,1024]{1,0:T(8,128)(2,1)S(1)} collective-permute-done((bf16[64,1024]{1,0:T(8,128)(2,1)S(1)}, bf16[64,1024]{1,0:T(8,128)(2,1)S(1)}, u32[]{:S(2)}, u32[]{:S(2)}) %collective-permute-start.9) | collective-permute-done | bytes 131104 | tf_op jit(solution)/shard_map/ppermute | solution.py:375
  158.5 6.5 %all-to-all-start.4 = ((bf16[8,2,64,1024]{3,2,1,0:T(8,128)(2,1)}), bf16[8,2,64,1024]{3,2,1,0:T(8,128)(2,1)}, u32[]{:S(2)}, u32[]{:S(2)}) async-start(bf16[8,2,64,1024]{3,2,1,0:T(8,128)(2,1)} %get-tuple-element.56), calls=%async_computation.4 | async-start | bytes 4194304 | tf_op jit(solution)/shard_map/all_to_all | solution.py:286
  165.0 2.7 collective-permute-start.13
  167.7 6.7 %collective-permute-done.12 = bf16[4,64,1024]{2,1,0:T(8,128)(2,1)} collective-permute-done((bf16[4,64,1024]{2,1,0:T(8,128)(2,1)S(1)}, bf16[4,64,1024]{2,1,0:T(8,128)(2,1)}, u32[]{:S(2)}, u32[]{:S(2)}) %collective-permute-start.12) | collective-permute-done | bytes 524320 | tf_op jit(solution)/shard_map/ppermute | solution.py:282
  174.3 13.9 %all-to-all-done.4.refs_7_ = bf16[8,2,64,1024]{3,2,1,0:T(8,128)(2,1)} async-done(((bf16[8,2,64,1024]{3,2,1,0:T(8,128)(2,1)}), bf16[8,2,64,1024]{3,2,1,0:T(8,128)(2,1)}, u32[]{:S(2)}, u32[]{:S(2)}) %all-to-all-start.4) | async-done | bytes 2097184 | tf_op jit(solution)/shard_map/all_to_all | solution.py:286
  188.2 5.0 %all-to-all-start.5 = ((bf16[8,64,1024]{2,1,0:T(8,128)(2,1)}), bf16[8,64,1024]{2,1,0:T(8,128)(2,1)}, u32[]{:S(2)}, u32[]{:S(2)}) async-start(bf16[8,64,1024]{2,1,0:T(8,128)(2,1)} %collective-permute-done.7), calls=%async_computation.5 | async-start | bytes 2097152 | tf_op jit(solution)/shard_map/all_to_all | solution.py:286
  193.3 5.8 %collective-permute-start.20 = (bf16[512,4096]{1,0:T(8,128)(2,1)}, bf16[512,4096]{1,0:T(8,128)(2,1)}, u32[]{:S(2)}, u32[]{:S(2)}) collective-permute-start(bf16[512,4096]{1,0:T(8,128)(2,1)} %param.7), channel_id=1, source_target_pairs={{0,1},{1,0},{2,3},{3,2},{4,5},{5,4},{6,7},{7,6},{8,9},{9,8},{10,11... | collective-permute-start | bytes 12582920 | tf_op jit(solution)/shard_map/ppermute | solution.py:369
  199.1 1.3 collective-permute-start.10
  200.4 4.9 %all-to-all-done.5 = bf16[8,64,1024]{2,1,0:T(8,128)(2,1)} async-done(((bf16[8,64,1024]{2,1,0:T(8,128)(2,1)}), bf16[8,64,1024]{2,1,0:T(8,128)(2,1)}, u32[]{:S(2)}, u32[]{:S(2)}) %all-to-all-start.5) | async-done | bytes 1048608 | tf_op jit(solution)/shard_map/all_to_all | solution.py:286
  205.3 4.2 %all-to-all-start.6 = ((bf16[8,64,1024]{2,1,0:T(8,128)(2,1)}), bf16[8,64,1024]{2,1,0:T(8,128)(2,1)}, u32[]{:S(2)}, u32[]{:S(2)}) async-start(bf16[8,64,1024]{2,1,0:T(8,128)(2,1)} %collective-permute-done.8), calls=%async_computation.6 | async-start | bytes 2097152 | tf_op jit(solution)/shard_map/all_to_all | solution.py:286
  211.9 3.1 slice_bitcast_fusion
  215.0 2.7 collective-permute-start.14
  217.8 1.7 collective-permute-done.18
  219.5 1.3 collective-permute-done.17
  222.9 1.8 collective-permute-start.19
  224.6 1.7 copy-done
  226.3 17.8 %local_part.1 = (f32[1024,512]{1,0:T(8,128)S(1)}, f32[1024,128]{1,0:T(8,128)S(1)}) custom-call(s32[1]{0:T(128)} %bitcast.1.z_ref.refs_0_, s32[64]{0:T(128)S(1)} %broadcast_add_fusion.refs_1_, s32[1]{0:T(128)} %bitcast.2.refs_2_, bf16[1024,512]{1,0:T(8,128)(2,1)S(1)} %copy-done.2, bf16[1152,1024]{1,0:T(8,128)(2,1)S(1)} %copy-done, ...), custom_call_target="tpu_custom_call" | custom-call | flops 24999999488 | bytes 4194304 | tf_op jit(solution)/shard_map/local_part/pallas_call | solution.py:153
  244.1 1.3 copy-done.9
  246.3 7.9 %all-to-all-start.7 = ((bf16[8,64,1024]{2,1,0:T(8,128)(2,1)}), bf16[8,64,1024]{2,1,0:T(8,128)(2,1)S(1)}, u32[]{:S(2)}, u32[]{:S(2)}) async-start(bf16[8,64,1024]{2,1,0:T(8,128)(2,1)} %pad_maximum_fusion.1), calls=%async_computation.7 | async-start | bytes 2097152 | tf_op jit(solution)/shard_map/all_to_all | solution.py:286
  254.2 15.6 %collective-permute-start.21 = (bf16[256,4096]{1,0:T(8,128)(2,1)}, bf16[256,4096]{1,0:T(8,128)(2,1)}, u32[]{:S(2)}, u32[]{:S(2)}) collective-permute-start(bf16[256,4096]{1,0:T(8,128)(2,1)} %collective-permute-done.2.refs_5_), channel_id=1, source_target_pairs={{0,1},{1,0},{2,3},{3,2},{4,5},{5,4},{6,7},{7,6},{8,9},{9,8},{10,11... | collective-permute-start | bytes 6291464 | tf_op jit(solution)/shard_map/ppermute | solution.py:370
  271.2 1.6 copy-done.10
  273.8 9.6 %more_part.1 = (f32[1024,512]{1,0:T(8,128)S(1)}, f32[1024,128]{1,0:T(8,128)S(1)}) custom-call(s32[1]{0:T(128)} %bitcast.1.z_ref.refs_0_, s32[64]{0:T(128)S(1)} %broadcast_add_fusion.refs_1_, bf16[1024,512]{1,0:T(8,128)(2,1)S(1)} %copy-done.3, f32[1024,512]{1,0:T(8,128)S(1)} %copy-done.10, f32[1024,128]{1,0:T(8,128)S(1)} %copy-done.12, ...), custom_call_target="tpu_custom_call" | custom-call | flops 12000000000 | bytes 4194304 | tf_op jit(solution)/shard_map/more_part/pallas_call | solution.py:169
  283.4 1.3 copy-done.5
  285.6 1.2 copy-done.4
  286.8 1.6 copy-done.6
  289.4 5.5 %final_part.1 = bf16[1024,512]{1,0:T(8,128)(2,1)S(1)} custom-call(s32[1]{0:T(128)} %bitcast.1.z_ref.refs_0_, s32[64]{0:T(128)S(1)} %broadcast_add_fusion.refs_1_, bf16[1024,512]{1,0:T(8,128)(2,1)S(1)} %copy-done.4, f32[1024,512]{1,0:T(8,128)S(1)} %copy-done.6, f32[1024,128]{1,0:T(8,128)S(1)} %copy-done.8, bf16[8,1,64,1024]{3,2,1,0:T(8,128)(2,1)S(1)} %bitcast.28), custom_call_target="tpu_custom_call" | custom-call | flops 6000000000 | bytes 4194304 | tf_op jit(solution)/shard_map/final_part/pallas_call | solution.py:185
  295.9 5.5 %all-to-all-start.8 = ((bf16[4,256,512]{2,1,0:T(8,128)(2,1)}), bf16[4,256,512]{2,1,0:T(8,128)(2,1)S(1)}, u32[]{:S(2)}, u32[]{:S(2)}) async-start(bf16[4,256,512]{2,1,0:T(8,128)(2,1)} %bitcast.29), calls=%async_computation.8 | async-start | bytes 2097152 | tf_op jit(solution)/shard_map/all_to_all | solution.py:411
  301.4 13.6 %all-to-all-done.8.refs_1_ = bf16[4,256,512]{2,1,0:T(8,128)(2,1)S(1)} async-done(((bf16[4,256,512]{2,1,0:T(8,128)(2,1)}), bf16[4,256,512]{2,1,0:T(8,128)(2,1)S(1)}, u32[]{:S(2)}, u32[]{:S(2)}) %all-to-all-start.8) | async-done | bytes 1048608 | tf_op jit(solution)/shard_map/all_to_all | solution.py:411
  315.0 9.0 %project.1 = bf16[256,4096]{1,0:T(8,128)(2,1)} custom-call(s32[1]{0:T(128)} %bitcast.refs_0_, bf16[4,256,512]{2,1,0:T(8,128)(2,1)S(1)} %all-to-all-done.8.refs_1_, bf16[256,4096]{1,0:T(8,128)(2,1)} %get-tuple-element.78.refs_2_, bf16[256,4096]{1,0:T(8,128)(2,1)S(1)} %get-tuple-element.77.refs_3_, bf16[512,4096]{1,0:T(8,128)(2,1)} %collective-permute-done.20.refs_4_, ...), custom_call_target="tpu_custom_call" | custom-call | tf_op jit(solution)/shard_map/project/pallas_call | solution.py:266
  (76 shorter events, 17.4 us)
Async XLA Ops:
  0.0 10.9 %copy-start.13 = (s32[16,2]{0,1:T(2,128)S(1)}, s32[16,2]{0,1:T(2,128)}, u32[]{:S(2)}) copy-start(s32[16,2]{0,1:T(2,128)} %param.6) | copy-start | bytes 388
  4.4 104.0 %collective-permute-start = (bf16[16,64,1024]{2,1,0:T(8,128)(2,1)}, bf16[16,64,1024]{2,1,0:T(8,128)(2,1)}, u32[]{:S(2)}, u32[]{:S(2)}) collective-permute-start(bf16[16,64,1024]{2,1,0:T(8,128)(2,1)} %reshape.132.refs_0_), channel_id=1, source_target_pairs={{0,4},{4,8},{8,12},{12,16},{16,20},{20,24},{24,28},{28,0},{1,5},{5... | collective-permute-start | bytes 6291464 | tf_op jit(solution)/shard_map/ppermute | solution.py:282
  6.9 101.5 %collective-permute-start.1 = (bf16[16,64,1024]{2,1,0:T(8,128)(2,1)}, bf16[16,64,1024]{2,1,0:T(8,128)(2,1)}, u32[]{:S(2)}, u32[]{:S(2)}) collective-permute-start(bf16[16,64,1024]{2,1,0:T(8,128)(2,1)} %reshape.132.refs_0_), channel_id=1, source_target_pairs={{0,28},{4,0},{8,4},{12,8},{16,12},{20,16},{24,20},{28,24},{1,29},{... | collective-permute-start | bytes 6291464 | tf_op jit(solution)/shard_map/ppermute | solution.py:282
  12.1 13.4 %all-to-all-start = ((s32[8,1,8]{2,1,0:T(1,128)}), s32[8,1,8]{2,1,0:T(1,128)S(1)}, u32[]{:S(2)}, u32[]{:S(2)}) async-start(s32[8,1,8]{2,1,0:T(1,128)} %bitcast.3), calls=%async_computation | async-start | bytes 8192 | tf_op jit(solution)/shard_map/all_to_all | solution.py:286
  22.7 85.7 %collective-permute-start.2 = (bf16[256,4096]{1,0:T(8,128)(2,1)}, bf16[256,4096]{1,0:T(8,128)(2,1)}, u32[]{:S(2)}, u32[]{:S(2)}) collective-permute-start(bf16[256,4096]{1,0:T(8,128)(2,1)} %get-tuple-element.78.refs_2_), channel_id=1, source_target_pairs={{0,2},{2,32},{32,34},{34,0},{1,3},{3,33},{33,35},{35,1},{4,6},{6,3... | collective-permute-start | bytes 6291464 | tf_op jit(solution)/shard_map/ppermute | solution.py:338
  23.0 85.4 %collective-permute-start.3 = (bf16[256,4096]{1,0:T(8,128)(2,1)S(1)}, bf16[256,4096]{1,0:T(8,128)(2,1)}, u32[]{:S(2)}, u32[]{:S(2)}) collective-permute-start(bf16[256,4096]{1,0:T(8,128)(2,1)S(1)} %get-tuple-element.77.refs_3_), channel_id=1, source_target_pairs={{0,34},{2,0},{32,2},{34,32},{1,35},{3,1},{33,3},{35,33},{4,38},{6,... | collective-permute-start | bytes 6291464 | tf_op jit(solution)/shard_map/ppermute | solution.py:339
  29.8 65.8 %all-to-all-start.1 = ((bf16[8,2,64,1024]{3,2,1,0:T(8,128)(2,1)}), bf16[8,2,64,1024]{3,2,1,0:T(8,128)(2,1)}, u32[]{:S(2)}, u32[]{:S(2)}) async-start(bf16[8,2,64,1024]{3,2,1,0:T(8,128)(2,1)} %pick.3), calls=%async_computation.1 | async-start | bytes 4194304 | tf_op jit(solution)/shard_map/all_to_all | solution.py:286
  36.5 65.1 %collective-permute-start.4 = (bf16[64,1024]{1,0:T(8,128)(2,1)S(1)}, bf16[64,1024]{1,0:T(8,128)(2,1)S(1)}, u32[]{:S(2)}, u32[]{:S(2)}) collective-permute-start(bf16[64,1024]{1,0:T(8,128)(2,1)S(1)} %bitcast.37), channel_id=1, source_target_pairs={{28,32},{60,64},{92,96},{124,128},{156,160},{188,192},{220,224},{3... | collective-permute-start | bytes 393224 | tf_op jit(solution)/shard_map/ppermute | solution.py:342
  96.3 12.1 %all-to-all-start.2 = ((s32[8,8,8]{2,1,0:T(8,128)}), s32[8,8,8]{2,1,0:T(8,128)S(1)}, u32[]{:S(2)}, u32[]{:S(2)}) async-start(s32[8,8,8]{2,1,0:T(8,128)} %broadcast_in_dim.31), calls=%async_computation.2 | async-start | bytes 65536 | tf_op jit(solution)/shard_map/all_to_all | solution.py:349
  114.7 43.8 %all-to-all-start.3 = ((bf16[8,2,64,1024]{3,2,1,0:T(8,128)(2,1)}), bf16[8,2,64,1024]{3,2,1,0:T(8,128)(2,1)}, u32[]{:S(2)}, u32[]{:S(2)}) async-start(bf16[8,2,64,1024]{3,2,1,0:T(8,128)(2,1)} %get-tuple-element.49), calls=%async_computation.3 | async-start | bytes 4194304 | tf_op jit(solution)/shard_map/all_to_all | solution.py:286
  124.6 33.9 %collective-permute-start.7 = (bf16[8,64,1024]{2,1,0:T(8,128)(2,1)}, bf16[8,64,1024]{2,1,0:T(8,128)(2,1)}, u32[]{:S(2)}, u32[]{:S(2)}) collective-permute-start(bf16[8,64,1024]{2,1,0:T(8,128)(2,1)} %get-tuple-element.47), channel_id=1, source_target_pairs={{0,4},{4,8},{8,12},{12,16},{16,20},{20,24},{24,28},{28,0},{1,5},{5... | collective-permute-start | bytes 3145736 | tf_op jit(solution)/shard_map/ppermute | solution.py:282
  124.6 33.9 %collective-permute-start.8 = (bf16[8,64,1024]{2,1,0:T(8,128)(2,1)}, bf16[8,64,1024]{2,1,0:T(8,128)(2,1)}, u32[]{:S(2)}, u32[]{:S(2)}) collective-permute-start(bf16[8,64,1024]{2,1,0:T(8,128)(2,1)} %get-tuple-element.48), channel_id=1, source_target_pairs={{0,28},{4,0},{8,4},{12,8},{16,12},{20,16},{24,20},{28,24},{1,29},{... | collective-permute-start | bytes 3145736 | tf_op jit(solution)/shard_map/ppermute | solution.py:282
  130.8 27.7 %collective-permute-start.5 = (bf16[4,64,1024]{2,1,0:T(8,128)(2,1)}, bf16[4,64,1024]{2,1,0:T(8,128)(2,1)S(1)}, u32[]{:S(2)}, u32[]{:S(2)}) collective-permute-start(bf16[4,64,1024]{2,1,0:T(8,128)(2,1)} %get-tuple-element.45), channel_id=1, source_target_pairs={{0,4},{4,8},{8,12},{12,16},{16,20},{20,24},{24,28},{28,0},{1,5},{5... | collective-permute-start | bytes 1572872 | tf_op jit(solution)/shard_map/ppermute | solution.py:282
  130.8 27.7 %collective-permute-start.6 = (bf16[4,64,1024]{2,1,0:T(8,128)(2,1)}, bf16[4,64,1024]{2,1,0:T(8,128)(2,1)S(1)}, u32[]{:S(2)}, u32[]{:S(2)}) collective-permute-start(bf16[4,64,1024]{2,1,0:T(8,128)(2,1)} %get-tuple-element.46), channel_id=1, source_target_pairs={{0,28},{4,0},{8,4},{12,8},{16,12},{20,16},{24,20},{28,24},{1,29},{... | collective-permute-start | bytes 1572872 | tf_op jit(solution)/shard_map/ppermute | solution.py:282
  134.5 23.0 %collective-permute-start.9 = (bf16[64,1024]{1,0:T(8,128)(2,1)S(1)}, bf16[64,1024]{1,0:T(8,128)(2,1)S(1)}, u32[]{:S(2)}, u32[]{:S(2)}) collective-permute-start(bf16[64,1024]{1,0:T(8,128)(2,1)S(1)} %select_bitcast_fusion), channel_id=1, source_target_pairs={{0,16},{28,12},{1,17},{29,13},{2,18},{30,14},{3,19},{31,15},{32,48... | collective-permute-start | bytes 393224 | tf_op jit(solution)/shard_map/ppermute | solution.py:375
  158.5 29.7 %all-to-all-start.4 = ((bf16[8,2,64,1024]{3,2,1,0:T(8,128)(2,1)}), bf16[8,2,64,1024]{3,2,1,0:T(8,128)(2,1)}, u32[]{:S(2)}, u32[]{:S(2)}) async-start(bf16[8,2,64,1024]{3,2,1,0:T(8,128)(2,1)} %get-tuple-element.56), calls=%async_computation.4 | async-start | bytes 4194304 | tf_op jit(solution)/shard_map/all_to_all | solution.py:286
  165.0 9.3 %collective-permute-start.12 = (bf16[4,64,1024]{2,1,0:T(8,128)(2,1)S(1)}, bf16[4,64,1024]{2,1,0:T(8,128)(2,1)}, u32[]{:S(2)}, u32[]{:S(2)}) collective-permute-start(bf16[4,64,1024]{2,1,0:T(8,128)(2,1)S(1)} %collective-permute-done.5), channel_id=1, source_target_pairs={{0,4},{4,8},{8,12},{12,16},{16,20},{20,24},{24,28},{28,0},{1,5},{5... | collective-permute-start | bytes 1572872 | tf_op jit(solution)/shard_map/ppermute | solution.py:282
  165.0 9.3 %collective-permute-start.13 = (bf16[4,64,1024]{2,1,0:T(8,128)(2,1)S(1)}, bf16[4,64,1024]{2,1,0:T(8,128)(2,1)}, u32[]{:S(2)}, u32[]{:S(2)}) collective-permute-start(bf16[4,64,1024]{2,1,0:T(8,128)(2,1)S(1)} %collective-permute-done.6), channel_id=1, source_target_pairs={{0,28},{4,0},{8,4},{12,8},{16,12},{20,16},{24,20},{28,24},{1,29},{... | collective-permute-start | bytes 1572872 | tf_op jit(solution)/shard_map/ppermute | solution.py:282
  188.2 17.1 %all-to-all-start.5 = ((bf16[8,64,1024]{2,1,0:T(8,128)(2,1)}), bf16[8,64,1024]{2,1,0:T(8,128)(2,1)}, u32[]{:S(2)}, u32[]{:S(2)}) async-start(bf16[8,64,1024]{2,1,0:T(8,128)(2,1)} %collective-permute-done.7), calls=%async_computation.5 | async-start | bytes 2097152 | tf_op jit(solution)/shard_map/all_to_all | solution.py:286
  193.3 108.2 %collective-permute-start.20 = (bf16[512,4096]{1,0:T(8,128)(2,1)}, bf16[512,4096]{1,0:T(8,128)(2,1)}, u32[]{:S(2)}, u32[]{:S(2)}) collective-permute-start(bf16[512,4096]{1,0:T(8,128)(2,1)} %param.7), channel_id=1, source_target_pairs={{0,1},{1,0},{2,3},{3,2},{4,5},{5,4},{6,7},{7,6},{8,9},{9,8},{10,11... | collective-permute-start | bytes 12582920 | tf_op jit(solution)/shard_map/ppermute | solution.py:369
  199.1 10.5 %collective-permute-start.10 = (bf16[64,1024]{1,0:T(8,128)(2,1)S(1)}, bf16[64,1024]{1,0:T(8,128)(2,1)S(1)}, u32[]{:S(2)}, u32[]{:S(2)}) collective-permute-start(bf16[64,1024]{1,0:T(8,128)(2,1)S(1)} %broadcast_select_fusion.4), channel_id=1, source_target_pairs={{0,8},{16,24},{28,20},{12,4},{1,9},{17,25},{29,21},{13,5},{2,10},{... | collective-permute-start | bytes 393224 | tf_op jit(solution)/shard_map/ppermute | solution.py:382
  205.3 17.5 %all-to-all-start.6 = ((bf16[8,64,1024]{2,1,0:T(8,128)(2,1)}), bf16[8,64,1024]{2,1,0:T(8,128)(2,1)}, u32[]{:S(2)}, u32[]{:S(2)}) async-start(bf16[8,64,1024]{2,1,0:T(8,128)(2,1)} %collective-permute-done.8), calls=%async_computation.6 | async-start | bytes 2097152 | tf_op jit(solution)/shard_map/all_to_all | solution.py:286
  209.6 8.1 %collective-permute-start.11 = (bf16[64,1024]{1,0:T(8,128)(2,1)S(1)}, bf16[64,1024]{1,0:T(8,128)(2,1)S(1)}, u32[]{:S(2)}, u32[]{:S(2)}) collective-permute-start(bf16[64,1024]{1,0:T(8,128)(2,1)S(1)} %broadcast_select_fusion.1), channel_id=1, source_target_pairs={{0,4},{4,0},{8,12},{12,8},{16,20},{20,16},{24,28},{28,24},{1,5},{5... | collective-permute-start | bytes 393224 | tf_op jit(solution)/shard_map/ppermute | solution.py:387
  210.4 9.1 %collective-permute-start.18 = (bf16[4,64,1024]{2,1,0:T(8,128)(2,1)}, bf16[4,64,1024]{2,1,0:T(8,128)(2,1)S(1)}, u32[]{:S(2)}, u32[]{:S(2)}) collective-permute-start(bf16[4,64,1024]{2,1,0:T(8,128)(2,1)} %collective-permute-done.13), channel_id=1, source_target_pairs={{0,28},{4,0},{8,4},{12,8},{16,12},{20,16},{24,20},{28,24},{1,29},{... | collective-permute-start | bytes 1572872 | tf_op jit(solution)/shard_map/ppermute | solution.py:282
  211.0 9.9 %collective-permute-start.17 = (bf16[4,64,1024]{2,1,0:T(8,128)(2,1)}, bf16[4,64,1024]{2,1,0:T(8,128)(2,1)S(1)}, u32[]{:S(2)}, u32[]{:S(2)}) collective-permute-start(bf16[4,64,1024]{2,1,0:T(8,128)(2,1)} %collective-permute-done.12), channel_id=1, source_target_pairs={{0,4},{4,8},{8,12},{12,16},{16,20},{20,24},{24,28},{28,0},{1,5},{5... | collective-permute-start | bytes 1572872 | tf_op jit(solution)/shard_map/ppermute | solution.py:282
  215.0 9.6 %copy-start.2 = (bf16[1024,512]{1,0:T(8,128)(2,1)S(1)}, bf16[1024,512]{1,0:T(8,128)(2,1)}, u32[]{:S(2)}) copy-start(bf16[1024,512]{1,0:T(8,128)(2,1)} %refs_2_.3) | copy-start | bytes 3145732
  215.0 39.2 %collective-permute-start.14 = (bf16[8,64,1024]{2,1,0:T(8,128)(2,1)}, bf16[8,64,1024]{2,1,0:T(8,128)(2,1)}, u32[]{:S(2)}, u32[]{:S(2)}) collective-permute-start(bf16[8,64,1024]{2,1,0:T(8,128)(2,1)} %get-tuple-element.80), channel_id=1, source_target_pairs={{0,4},{4,8},{8,12},{12,16},{16,20},{20,24},{24,28},{28,0},{1,5},{5... | collective-permute-start | bytes 3145736 | tf_op jit(solution)/shard_map/ppermute | solution.py:282
  217.7 52.1 %collective-permute-start.15 = (bf16[8,64,1024]{2,1,0:T(8,128)(2,1)}, bf16[8,64,1024]{2,1,0:T(8,128)(2,1)}, u32[]{:S(2)}, u32[]{:S(2)}) collective-permute-start(bf16[8,64,1024]{2,1,0:T(8,128)(2,1)} %get-tuple-element.79), channel_id=1, source_target_pairs={{0,28},{4,0},{8,4},{12,8},{16,12},{20,16},{24,20},{28,24},{1,29},{... | collective-permute-start | bytes 3145736 | tf_op jit(solution)/shard_map/ppermute | solution.py:282
  221.9 48.0 %collective-permute-start.16 = (bf16[8,64,1024]{2,1,0:T(8,128)(2,1)}, bf16[8,64,1024]{2,1,0:T(8,128)(2,1)}, u32[]{:S(2)}, u32[]{:S(2)}) collective-permute-start(bf16[8,64,1024]{2,1,0:T(8,128)(2,1)} %all-to-all-done.5), channel_id=1, source_target_pairs={{0,4},{4,8},{8,12},{12,16},{16,20},{20,24},{24,28},{28,0},{1,5},{5... | collective-permute-start | bytes 3145736 | tf_op jit(solution)/shard_map/ppermute | solution.py:282
  222.9 47.1 %collective-permute-start.19 = (bf16[8,64,1024]{2,1,0:T(8,128)(2,1)}, bf16[8,64,1024]{2,1,0:T(8,128)(2,1)}, u32[]{:S(2)}, u32[]{:S(2)}) collective-permute-start(bf16[8,64,1024]{2,1,0:T(8,128)(2,1)} %all-to-all-done.6), channel_id=1, source_target_pairs={{0,28},{4,0},{8,4},{12,8},{16,12},{20,16},{24,20},{28,24},{1,29},{... | collective-permute-start | bytes 3145736 | tf_op jit(solution)/shard_map/ppermute | solution.py:282
  224.6 1.7 copy-start
  244.1 1.3 copy-start.9
  245.4 0.8 copy-start.11
  246.3 39.3 %all-to-all-start.7 = ((bf16[8,64,1024]{2,1,0:T(8,128)(2,1)}), bf16[8,64,1024]{2,1,0:T(8,128)(2,1)S(1)}, u32[]{:S(2)}, u32[]{:S(2)}) async-start(bf16[8,64,1024]{2,1,0:T(8,128)(2,1)} %pad_maximum_fusion.1), calls=%async_computation.7 | async-start | bytes 2097152 | tf_op jit(solution)/shard_map/all_to_all | solution.py:286
  254.2 47.2 %collective-permute-start.21 = (bf16[256,4096]{1,0:T(8,128)(2,1)}, bf16[256,4096]{1,0:T(8,128)(2,1)}, u32[]{:S(2)}, u32[]{:S(2)}) collective-permute-start(bf16[256,4096]{1,0:T(8,128)(2,1)} %collective-permute-done.2.refs_5_), channel_id=1, source_target_pairs={{0,1},{1,0},{2,3},{3,2},{4,5},{5,4},{6,7},{7,6},{8,9},{9,8},{10,11... | collective-permute-start | bytes 6291464 | tf_op jit(solution)/shard_map/ppermute | solution.py:370
  269.8 31.6 %collective-permute-start.22 = (bf16[256,4096]{1,0:T(8,128)(2,1)}, bf16[256,4096]{1,0:T(8,128)(2,1)}, u32[]{:S(2)}, u32[]{:S(2)}) collective-permute-start(bf16[256,4096]{1,0:T(8,128)(2,1)} %collective-permute-done.3.refs_6_), channel_id=1, source_target_pairs={{0,1},{1,0},{2,3},{3,2},{4,5},{5,4},{6,7},{7,6},{8,9},{9,8},{10,11... | collective-permute-start | bytes 6291464 | tf_op jit(solution)/shard_map/ppermute | solution.py:370
  269.9 1.2 copy-start.3
  271.1 1.6 copy-start.10
  272.7 1.0 copy-start.12
  283.4 1.3 copy-start.5
  284.8 0.8 copy-start.7
  285.6 1.2 copy-start.4
  286.8 1.6 copy-start.6
  288.4 1.0 copy-start.8
  295.0 1.0 copy-start.1
  295.9 19.1 %all-to-all-start.8 = ((bf16[4,256,512]{2,1,0:T(8,128)(2,1)}), bf16[4,256,512]{2,1,0:T(8,128)(2,1)S(1)}, u32[]{:S(2)}, u32[]{:S(2)}) async-start(bf16[4,256,512]{2,1,0:T(8,128)(2,1)} %bitcast.29), calls=%async_computation.8 | async-start | bytes 2097152 | tf_op jit(solution)/shard_map/all_to_all | solution.py:411

commit v5 on v3

--- a/solution.py
+++ b/solution.py
@@ -198,8 +198,11 @@
         held, in_sems, out_sems = refs[-3:]
         loads, stores = [], []
         for n, (o, position, s, lane, plane, owner) in enumerate(plan):
-            row = lane * NZ + lax.rem(z_ref[0] + (plane + NZ), NZ)
-            block = asked_ref[row, lax.rem(z_ref[0] + (owner + NZ), NZ)]
+            if lane is None:
+                block = jnp.where(z_ref[0] == 0, 0, sources[s].shape[0] - 1)
+            else:
+                row = lane * NZ + lax.rem(z_ref[0] + (plane + NZ), NZ)
+                block = asked_ref[row, lax.rem(z_ref[0] + (owner + NZ), NZ)]
             loads.append(pltpu.make_async_copy(src[s].at[block], held.at[n], in_sems.at[n]))
             stores.append(pltpu.make_async_copy(held.at[n], out[o].at[position], out_sems.at[n]))
             loads[-1].start()
@@ -253,7 +256,7 @@
         out_ref[:, span] = dot_nn(acat_ref[...], w_ref[:, span]).astype(BF16)
 
 
-def project(me, a, weights, tile=512):
+def project(me, a, weights, tile=1024):
     groups, rows, feat = a.shape
     cols = weights[0].shape[1]
     return pl.pallas_call(
@@ -321,67 +324,62 @@
 
     kv = keys_values.reshape(blocks_dev, BLOCK, 2 * feat)
 
+    up1, down1 = z_shift(kv, 1), z_shift(kv, -1)
     block_ids = first_id + jnp.arange(blocks_dev, dtype=jnp.int32)
     offset, where = wanted_blocks(rand_blocks, block_ids, all_blocks, blocks_dev)
     asked = jnp.broadcast_to(offset.reshape(LANES, 1, NZ), (LANES, NZ, NZ)).reshape(-1, NZ)
+    asked = lax.all_to_all(asked, SEQ, split_axis=0, concat_axis=0, tiled=True)
+    rows = w_out.shape[0] // 2
+    own = [w_out[:rows], w_out[rows:]]
+    ring = NXH * NXL
+    low = lax.ppermute(own[0], XRING, [(i, (i + 1) % ring) for i in range(ring)])
+    high = lax.ppermute(own[1], XRING, [(i, (i - 1) % ring) for i in range(ring)])
     edge = jnp.where(z == 0, kv[0], kv[blocks_dev - 1])
-    rows = w_out.shape[0] // 2
-    low, high = w_out[:rows], w_out[rows:]
-    asked = lax.all_to_all(asked, SEQ, split_axis=0, concat_axis=0, tiled=True)
-    up1, down1 = z_shift(kv, 1), z_shift(kv, -1)
-    ring = NXH * NXL
-    low = lax.ppermute(low, XRING, [(i, (i + 1) % ring) for i in range(ring)])
-    high = lax.ppermute(high, XRING, [(i, (i - 1) % ring) for i in range(ring)])
     turns = [(NZ * i + NZ - 1, NZ * i + NZ) for i in range(LANES - 1)]
     crossed = lax.ppermute(edge, SEQ, turns + [(b, a) for a, b in turns])
-    up1, down1, asked, low, high, crossed, edge = tie(
-        up1, down1, asked, low, high, crossed, edge
+    up1, down1, asked, low, high, crossed, w_core = tie(
+        up1, down1, asked, low, high, crossed, w_out
     )
 
     up2, down2 = z_shift(up1, 1), z_shift(down1, -1)
     plan = [(0, (lane, 0), 0, lane, 0, 0) for lane in lanes]
     plan += [(0, (lane, 1), 1, lane, 0, -1) for lane in lanes]
     plan += [(0, (lane, 2), 2, lane, 0, 1) for lane in lanes]
-    (c1,) = pick(zs, asked, [kv, up1, down1], plan, [(LANES, 3)])
+    plan += [(0, (lane, 3), 0, None, 0, 0) for lane in lanes]
+    (c1,) = pick(zs, asked, [kv, up1, down1], plan, [(LANES, 4)])
     r1 = lane_exchange(c1)
     swap = [(0, 1), (1, 0)]
-    weights = [w_out, lax.ppermute(w_out, "core", swap), low, high]
-    weights += [lax.ppermute(low, "core", swap), lax.ppermute(high, "core", swap)]
-    edge, r1 = tie(edge, r1)
-    plane_ends = lane_exchange(jnp.broadcast_to(edge[None], (LANES,) + edge.shape))
+    others = [lax.ppermute(x, "core", swap) for x in (w_core, low, high)]
     before = jnp.where(z == 0, crossed, up1[blocks_dev - 1])
     after = jnp.where(z == NZ - 1, crossed, down1[0])
     kv_pad = jnp.concatenate([before, kv.reshape(tok, 2 * feat), after], axis=0)
-    up2, down2, r1, plane_ends, kv_pad = tie(up2, down2, r1, plane_ends, kv_pad)
-
-    held = jnp.where(z == 0, plane_ends[0], plane_ends[LANES - 1])
+    up2, down2, r1, kv_pad, *others = tie(up2, down2, r1, kv_pad, *others)
+    weights = own + [others[0], low, high] + others[1:]
+
+    plan = [(0, (lane, 0), 0, lane, 1, -2) for lane in lanes]
+    plan += [(0, (lane, 1), 1, lane, -1, 2) for lane in lanes]
+    plan += [(1, lane, 0, lane, 2, -2) for lane in lanes[:half]]
+    plan += [(2, lane - half, 1, lane, -2, 2) for lane in lanes[half:]]
+    plan += [(3, (lane, 0), 0, lane, 0, -2) for lane in lanes]
+    plan += [(3, (lane, 1), 1, lane, 0, 2) for lane in lanes]
+    c3, fu, fd, c2 = pick(
+        zs, asked, [up2, down2], plan, [(LANES, 2), (half,), (half,), (LANES, 2)]
+    )
+    fu, fd = z_shift(fu, 1), z_shift(fd, -1)
+    c3 = lane_exchange(c3)
+    held = jnp.where(z == 0, r1[0, 3], r1[LANES - 1, 3])
     got = lax.ppermute(held, "z", [(0, 4), (7, 3)])
     held = jnp.where(jnp.logical_or(z == 4, z == 3), got, held)
+    c2, c3, fu, fd = tie(c2, c3, fu, fd)
+    r2 = lane_exchange(c2)
+    fu, fd = z_shift(fu, 1), z_shift(fd, -1)
+    r3u, r3d = z_shift(c3[:, 0], 1), z_shift(c3[:, 1], -1)
     got = lax.ppermute(held, "z", [(0, 2), (4, 6), (7, 5), (3, 1)])
     fresh = reduce(jnp.logical_or, [z == 2, z == 6, z == 5, z == 1])
     held = jnp.where(fresh, got, held)
     got = lax.ppermute(held, "z", [(i, i ^ 1) for i in range(NZ)])
     even = z % 2 == 0
     ends = jnp.concatenate([jnp.where(even, held, got), jnp.where(even, got, held)], axis=0)
-
-    plan = [(0, lane, 0, lane, 1, -2) for lane in lanes]
-    plan += [(1, lane, 1, lane, -1, 2) for lane in lanes]
-    plan += [(2, lane, 0, lane, 2, -2) for lane in lanes[:half]]
-    plan += [(3, lane - half, 1, lane, -2, 2) for lane in lanes[half:]]
-    plan += [(4, (lane, 0), 0, lane, 0, -2) for lane in lanes]
-    plan += [(4, (lane, 1), 1, lane, 0, 2) for lane in lanes]
-    c3u, c3d, fu, fd, c2 = pick(
-        zs, asked, [up2, down2], plan, [(LANES,), (LANES,), (half,), (half,), (LANES, 2)]
-    )
-    fu, fd = z_shift(fu, 1), z_shift(fd, -1)
-    c3u = lane_exchange(c3u)
-    c3d, c3u, fu, fd = tie(c3d, c3u, fu, fd)
-    r3u = z_shift(c3u, 1)
-    fu, fd = z_shift(fu, 1), z_shift(fd, -1)
-    c3d = lane_exchange(c3d)
-    c2, c3d, fu, fd = tie(c2, c3d, fu, fd)
-    r3d = z_shift(c3d, -1)
-    r2 = lane_exchange(c2)
     far = jnp.concatenate([fu, fd], axis=0)
     far, r2 = tie(far, r2)
     r4 = lane_exchange(far)

time: 287 us -> 275 us (0.958)
  starting transfers between devices: 74.2 us -> 59.1 us
  local copies, waits for them, and re-layouts: 23.4 us -> 29.5 us
  waiting for transfers between devices: 75.8 us -> 71.6 us
    all_to_all x6 -> x4, waiting for transfers between devices: 50.5 us -> 6.52 us  [lane_exchange(): return lax.all_to_all(x, LANE, split_axis=0, concat_axis=0, tiled=True)]
    ppermute x10, waiting for transfers between devices: 6.09 us -> 43.3 us  [z_shift(): return lax.ppermute(x, 'z', [(i, (i + by) % NZ) for i in range(NZ)])]
    all_to_all x6 -> x4, starting transfers between devices: 30 us -> 20.2 us  [lane_exchange(): return lax.all_to_all(x, LANE, split_axis=0, concat_axis=0, tiled=True)]
    ppermute x5, starting transfers between devices: 11.9 us -> 5.63 us  [the longest x3 3.15 us: body(): others = [lax.ppermute(x, 'core', swap) for x in (w_core, low, high)]]
    ppermute x1, waiting for transfers between devices: 0.01 us -> 6.18 us  [body(): got = lax.ppermute(held, 'z', [(i, i ^ 1) for i in range(NZ)])]
    ppermute x1, starting transfers between devices: 0.09 us -> 5.93 us  [body(): got = lax.ppermute(held, 'z', [(i, i ^ 1) for i in range(NZ)])]
    ppermute x10, starting transfers between devices: 21.8 us -> 16.1 us  [z_shift(): return lax.ppermute(x, 'z', [(i, (i + by) % NZ) for i in range(NZ)])]
    unnamed x25 -> x37, local copies, waits for them, and re-layouts: 13.9 us -> 17.6 us
  transfers between devices with their start and end apart: 26 -> 24, of which waited for: 9 -> 8; matrix products, arithmetic and copies ran while one was open for 6% -> 5% of each run, Pallas kernels for 11% -> 13%
where the time goes in v5:
time: 275 us; the launch traced here: 273 us
  waiting for transfers between devices  71.6 us (26%)
  starting transfers between devices  59.1 us (21%)
  Pallas kernels  55.6 us (20%)
  blocking collectives  49.3 us (18%)
  local copies, waits for them, and re-layouts  29.5 us (11%)
  other arithmetic  6.96 us (3%)
    all_to_all x1, blocking collectives, body(): asked = lax.all_to_all(asked, SEQ, split_axis=0, concat_axis=0, tiled=True)  49.3 us
    ppermute x10, waiting for transfers between devices, z_shift(): return lax.ppermute(x, 'z', [(i, (i + by) % NZ) for i in range(NZ)])  43.3 us
    all_to_all x4, starting transfers between devices, lane_exchange(): return lax.all_to_all(x, LANE, split_axis=0, concat_axis=0, tiled=True)  20.2 us
    unnamed x37, local copies, waits for them, and re-layouts  17.6 us
    pallas_call x1, Pallas kernels, local_part(): pl.pallas_call(lambda *refs: local_kernel(all_blocks, deltas, *refs), out...  17.3 us
    ppermute x10, starting transfers between devices, z_shift(): return lax.ppermute(x, 'z', [(i, (i + by) % NZ) for i in range(NZ)])  16.1 us
    pallas_call x2, Pallas kernels, pick(): pl.pallas_call(kernel, out_shape=tuple((pltpu.HBM(shape + block_shape, BF...  14 us
    all_to_all x1, waiting for transfers between devices, body(): lax.all_to_all(attended.reshape(heads, tok // heads, feat), HEAD, split_a...  13.6 us
  transfers between devices with their start and end apart: 24, of which 8 were waited for; matrix products, arithmetic and copies ran while one was open for 5% of the time, Pallas kernels for 13%

profile of v5, /device:TPU:1, one launch (start us, length us, event | category | flops | bytes accessed | tf_op | source)
XLA Modules:
  0.0 272.7 jit_solution(8106697486847545551)
XLA Ops:
  0.0 4.4 %reshape.124.refs_0_ = bf16[16,64,1024]{2,1,0:T(8,128)(2,1)} reshape(bf16[1024,2,512]{2,1,0:T(2,128)(2,1)} %param.5) | data formatting | bytes 4194304 | tf_op jit(solution)/shard_map/reshape | solution.py:325
  4.4 6.4 %collective-permute-start.1 = (bf16[16,64,1024]{2,1,0:T(8,128)(2,1)}, bf16[16,64,1024]{2,1,0:T(8,128)(2,1)}, u32[]{:S(2)}, u32[]{:S(2)}) collective-permute-start(bf16[16,64,1024]{2,1,0:T(8,128)(2,1)} %reshape.124.refs_0_), channel_id=1, source_target_pairs={{0,28},{4,0},{8,4},{12,8},{16,12},{20,16},{24,20},{28,24},{1,29},{... | collective-permute-start | bytes 6291464 | tf_op jit(solution)/shard_map/ppermute | solution.py:278
  10.8 4.0 %fusion.4 = (bf16[256,4096]{1,0:T(8,128)(2,1)S(1)}, bf16[256,4096]{1,0:T(8,128)(2,1)}) fusion(bf16[512,4096]{1,0:T(8,128)(2,1)} %param.7), kind=kLoop, calls=%fused_computation.34 | loop fusion | bytes 8388608 | tf_op jit(solution)/shard_map/slice | solution.py:333
  14.9 2.5 collective-permute-start.3
  17.3 1.1 broadcast_select_fusion
  19.8 49.3 %all_to_all.37 = s32[64,1,8]{2,1,0:T(1,128)S(1)} all-to-all(s32[64,1,8]{2,1,0:T(1,128)S(1)} %bitcast.33), channel_id=1, replica_groups=mesh['y'=4,'xh'=2,'z'=8,'xl'=2,'core'=2] {'y','xh','z'}, dimensions={0} | all-to-all | bytes 4096 | tf_op jit(solution)/shard_map/all_to_all | solution.py:331
  69.2 2.6 collective-permute-start.7
  71.7 6.3 %pick.2 = bf16[8,4,64,1024]{3,2,1,0:T(8,128)(2,1)} custom-call(s32[1]{0:T(128)} %bitcast.1.z_ref.refs_0_, s32[64,8]{1,0:T(8,128)S(1)} %bitcast.27, bf16[16,64,1024]{2,1,0:T(8,128)(2,1)} %reshape.124.refs_0_, bf16[16,64,1024]{2,1,0:T(8,128)(2,1)} %collective-permute-done.refs_1_, bf16[16,64,1024]{2,1,0:T(8,128)(2,1)} %collective-permute-done.1.refs_2_), custom_call_target="tpu_custom_call" | custom-call | flops 3000000000 | bytes 4194304 | tf_op jit(solution)/shard_map/pick/pallas_call | solution.py:216
  78.1 4.6 %all-to-all-start.1 = ((bf16[8,4,64,1024]{3,2,1,0:T(8,128)(2,1)}), bf16[8,4,64,1024]{3,2,1,0:T(8,128)(2,1)}, u32[]{:S(2)}, u32[]{:S(2)}) async-start(bf16[8,4,64,1024]{3,2,1,0:T(8,128)(2,1)} %pick.2), calls=%async_computation.1 | async-start | bytes 8388608 | tf_op jit(solution)/shard_map/all_to_all | solution.py:282
  83.2 2.7 collective-permute-start.6
  85.9 2.1 copy.22
  88.1 1.0 bitcast_select_fusion.1
  89.1 1.6 pad_maximum_fusion.refs_4_
  90.7 41.3 %collective-permute-done.5.refs_0_ = bf16[16,64,1024]{2,1,0:T(8,128)(2,1)} collective-permute-done((bf16[16,64,1024]{2,1,0:T(8,128)(2,1)}, bf16[16,64,1024]{2,1,0:T(8,128)(2,1)}, u32[]{:S(2)}, u32[]{:S(2)}) %collective-permute-start.5) | collective-permute-done | bytes 2097184 | tf_op jit(solution)/shard_map/ppermute | solution.py:278
  132.0 1.8 all-to-all-done.1.refs_6_
  133.7 7.7 %pick.3 = (bf16[8,2,64,1024]{3,2,1,0:T(8,128)(2,1)}, bf16[4,64,1024]{2,1,0:T(8,128)(2,1)}, bf16[4,64,1024]{2,1,0:T(8,128)(2,1)}, bf16[8,2,64,1024]{3,2,1,0:T(8,128)(2,1)}) custom-call(s32[1]{0:T(128)} %bitcast.1.z_ref.refs_0_, s32[64,8]{1,0:T(8,128)S(1)} %bitcast.28, bf16[16,64,1024]{2,1,0:T(8,128)(2,1)} %collective-permute-done.5.refs_0_, ...), custom_call_target="tpu_custom_call" | custom-call | flops 3000000000 | bytes 4194304 | tf_op jit(solution)/shard_map/pick/pallas_call | solution.py:216
  141.4 4.5 %all-to-all-start.2 = ((bf16[8,2,64,1024]{3,2,1,0:T(8,128)(2,1)}), bf16[8,2,64,1024]{3,2,1,0:T(8,128)(2,1)}, u32[]{:S(2)}, u32[]{:S(2)}) async-start(bf16[8,2,64,1024]{3,2,1,0:T(8,128)(2,1)} %get-tuple-element.47), calls=%async_computation.2 | async-start | bytes 4194304 | tf_op jit(solution)/shard_map/all_to_all | solution.py:282
  145.9 1.0 select_bitcast_fusion
  146.9 1.3 collective-permute-start.10
  148.3 1.9 collective-permute-done.10
  150.2 1.0 broadcast_select_fusion.1
  151.2 1.3 collective-permute-start.11
  152.6 2.7 collective-permute-start.14
  155.3 5.9 %collective-permute-start.12 = (bf16[64,1024]{1,0:T(8,128)(2,1)S(1)}, bf16[64,1024]{1,0:T(8,128)(2,1)S(1)}, u32[]{:S(2)}, u32[]{:S(2)}) collective-permute-start(bf16[64,1024]{1,0:T(8,128)(2,1)S(1)} %broadcast_select_fusion.2), channel_id=1, source_target_pairs={{0,4},{4,0},{8,12},{12,8},{16,20},{20,16},{24,28},{28,24},{1,5},{5... | collective-permute-start | bytes 393224 | tf_op jit(solution)/shard_map/ppermute | solution.py:380
  161.2 6.2 %collective-permute-done.12 = bf16[64,1024]{1,0:T(8,128)(2,1)S(1)} collective-permute-done((bf16[64,1024]{1,0:T(8,128)(2,1)S(1)}, bf16[64,1024]{1,0:T(8,128)(2,1)S(1)}, u32[]{:S(2)}, u32[]{:S(2)}) %collective-permute-start.12) | collective-permute-done | bytes 131104 | tf_op jit(solution)/shard_map/ppermute | solution.py:380
  168.3 4.8 %all-to-all-done.2 = bf16[8,2,64,1024]{3,2,1,0:T(8,128)(2,1)} async-done(((bf16[8,2,64,1024]{3,2,1,0:T(8,128)(2,1)}), bf16[8,2,64,1024]{3,2,1,0:T(8,128)(2,1)}, u32[]{:S(2)}, u32[]{:S(2)}) %all-to-all-start.2) | async-done | bytes 2097184 | tf_op jit(solution)/shard_map/all_to_all | solution.py:282
  173.0 3.1 %slice_bitcast_fusion = (bf16[8,64,1024]{2,1,0:T(8,128)(2,1)}, bf16[8,64,1024]{2,1,0:T(8,128)(2,1)}) fusion(bf16[8,2,64,1024]{3,2,1,0:T(8,128)(2,1)} %all-to-all-done.2), kind=kLoop, calls=%fused_computation.1 | loop fusion | bytes 4194304 | tf_op jit(solution)/shard_map/squeeze | solution.py:376
  176.1 4.5 %all-to-all-start.3 = ((bf16[8,2,64,1024]{3,2,1,0:T(8,128)(2,1)}), bf16[8,2,64,1024]{3,2,1,0:T(8,128)(2,1)}, u32[]{:S(2)}, u32[]{:S(2)}) async-start(bf16[8,2,64,1024]{3,2,1,0:T(8,128)(2,1)} %get-tuple-element.53), calls=%async_computation.3 | async-start | bytes 4194304 | tf_op jit(solution)/shard_map/all_to_all | solution.py:282
  181.2 2.1 collective-permute-start.18
  184.8 1.7 copy-done
  186.5 17.3 %local_part.1 = (f32[1024,512]{1,0:T(8,128)S(1)}, f32[1024,128]{1,0:T(8,128)S(1)}) custom-call(s32[1]{0:T(128)} %bitcast.1.z_ref.refs_0_, s32[64]{0:T(128)S(1)} %broadcast_add_fusion.refs_1_, s32[1]{0:T(128)} %bitcast.2.refs_2_, bf16[1024,512]{1,0:T(8,128)(2,1)S(1)} %copy-done.2, bf16[1152,1024]{1,0:T(8,128)(2,1)S(1)} %copy-done, ...), custom_call_target="tpu_custom_call" | custom-call | flops 24999999488 | bytes 4194304 | tf_op jit(solution)/shard_map/local_part/pallas_call | solution.py:151
  203.8 1.3 copy-done.9
  205.9 1.1 pad_maximum_fusion.1
  207.0 6.7 %all-to-all-start.4 = ((bf16[8,64,1024]{2,1,0:T(8,128)(2,1)}), bf16[8,64,1024]{2,1,0:T(8,128)(2,1)S(1)}, u32[]{:S(2)}, u32[]{:S(2)}) async-start(bf16[8,64,1024]{2,1,0:T(8,128)(2,1)} %pad_maximum_fusion.1), calls=%async_computation.4 | async-start | bytes 2097152 | tf_op jit(solution)/shard_map/all_to_all | solution.py:282
  213.7 1.9 collective-permute-done.16
  215.7 1.2 copy-done.3
  216.9 1.6 copy-done.10
  218.5 1.0 copy-done.12
  219.6 11.2 %more_part.1 = (f32[1024,512]{1,0:T(8,128)S(1)}, f32[1024,128]{1,0:T(8,128)S(1)}) custom-call(s32[1]{0:T(128)} %bitcast.1.z_ref.refs_0_, s32[64]{0:T(128)S(1)} %broadcast_add_fusion.refs_1_, bf16[1024,512]{1,0:T(8,128)(2,1)S(1)} %copy-done.3, f32[1024,512]{1,0:T(8,128)S(1)} %copy-done.10, f32[1024,128]{1,0:T(8,128)S(1)} %copy-done.12, ...), custom_call_target="tpu_custom_call" | custom-call | flops 12000000000 | bytes 4194304 | tf_op jit(solution)/shard_map/more_part/pallas_call | solution.py:167
  230.8 1.3 copy-done.5
  232.9 1.2 copy-done.4
  234.1 1.6 copy-done.6
  235.7 1.0 copy-done.8
  236.7 4.6 %final_part.1 = bf16[1024,512]{1,0:T(8,128)(2,1)S(1)} custom-call(s32[1]{0:T(128)} %bitcast.1.z_ref.refs_0_, s32[64]{0:T(128)S(1)} %broadcast_add_fusion.refs_1_, bf16[1024,512]{1,0:T(8,128)(2,1)S(1)} %copy-done.4, f32[1024,512]{1,0:T(8,128)S(1)} %copy-done.6, f32[1024,128]{1,0:T(8,128)S(1)} %copy-done.8, bf16[8,1,64,1024]{3,2,1,0:T(8,128)(2,1)S(1)} %bitcast.25), custom_call_target="tpu_custom_call" | custom-call | flops 6000000000 | bytes 4194304 | tf_op jit(solution)/shard_map/final_part/pallas_call | solution.py:183
  241.3 1.0 copy-done.1
  242.3 8.0 %all-to-all-start.5 = ((bf16[4,256,512]{2,1,0:T(8,128)(2,1)}), bf16[4,256,512]{2,1,0:T(8,128)(2,1)S(1)}, u32[]{:S(2)}, u32[]{:S(2)}) async-start(bf16[4,256,512]{2,1,0:T(8,128)(2,1)} %bitcast.26), calls=%async_computation.5 | async-start | bytes 2097152 | tf_op jit(solution)/shard_map/all_to_all | solution.py:399
  250.3 13.6 %all-to-all-done.5.refs_1_ = bf16[4,256,512]{2,1,0:T(8,128)(2,1)S(1)} async-done(((bf16[4,256,512]{2,1,0:T(8,128)(2,1)}), bf16[4,256,512]{2,1,0:T(8,128)(2,1)S(1)}, u32[]{:S(2)}, u32[]{:S(2)}) %all-to-all-start.5) | async-done | bytes 1048608 | tf_op jit(solution)/shard_map/all_to_all | solution.py:399
  263.9 8.6 %project.1 = bf16[256,4096]{1,0:T(8,128)(2,1)} custom-call(s32[1]{0:T(128)} %bitcast.refs_0_, bf16[4,256,512]{2,1,0:T(8,128)(2,1)S(1)} %all-to-all-done.5.refs_1_, bf16[256,4096]{1,0:T(8,128)(2,1)} %get-tuple-element.64.refs_2_, bf16[256,4096]{1,0:T(8,128)(2,1)S(1)} %get-tuple-element.63.refs_3_, bf16[512,4096]{1,0:T(8,128)(2,1)} %collective-permute-done.7.refs_4_, ...), custom_call_target="tpu_custom_call" | custom-call | tf_op jit(solution)/shard_map/project/pallas_call | solution.py:262
  (66 shorter events, 6.8 us)
Async XLA Ops:
  4.4 14.7 %copy-start.13 = (s32[16,2]{0,1:T(2,128)S(1)}, s32[16,2]{0,1:T(2,128)}, u32[]{:S(2)}) copy-start(s32[16,2]{0,1:T(2,128)} %param.6) | copy-start | bytes 388
  4.4 64.7 %collective-permute-start.1 = (bf16[16,64,1024]{2,1,0:T(8,128)(2,1)}, bf16[16,64,1024]{2,1,0:T(8,128)(2,1)}, u32[]{:S(2)}, u32[]{:S(2)}) collective-permute-start(bf16[16,64,1024]{2,1,0:T(8,128)(2,1)} %reshape.124.refs_0_), channel_id=1, source_target_pairs={{0,28},{4,0},{8,4},{12,8},{16,12},{20,16},{24,20},{28,24},{1,29},{... | collective-permute-start | bytes 6291464 | tf_op jit(solution)/shard_map/ppermute | solution.py:278
  10.8 58.3 %collective-permute-start = (bf16[16,64,1024]{2,1,0:T(8,128)(2,1)}, bf16[16,64,1024]{2,1,0:T(8,128)(2,1)}, u32[]{:S(2)}, u32[]{:S(2)}) collective-permute-start(bf16[16,64,1024]{2,1,0:T(8,128)(2,1)} %reshape.124.refs_0_), channel_id=1, source_target_pairs={{0,4},{4,8},{8,12},{12,16},{16,20},{20,24},{24,28},{28,0},{1,5},{5... | collective-permute-start | bytes 6291464 | tf_op jit(solution)/shard_map/ppermute | solution.py:278
  14.9 54.3 %collective-permute-start.3 = (bf16[256,4096]{1,0:T(8,128)(2,1)S(1)}, bf16[256,4096]{1,0:T(8,128)(2,1)}, u32[]{:S(2)}, u32[]{:S(2)}) collective-permute-start(bf16[256,4096]{1,0:T(8,128)(2,1)S(1)} %get-tuple-element.63.refs_3_), channel_id=1, source_target_pairs={{0,34},{2,0},{32,2},{34,32},{1,35},{3,1},{33,3},{35,33},{4,38},{6,... | collective-permute-start | bytes 6291464 | tf_op jit(solution)/shard_map/ppermute | solution.py:336
  17.3 51.8 %collective-permute-start.2 = (bf16[256,4096]{1,0:T(8,128)(2,1)}, bf16[256,4096]{1,0:T(8,128)(2,1)}, u32[]{:S(2)}, u32[]{:S(2)}) collective-permute-start(bf16[256,4096]{1,0:T(8,128)(2,1)} %get-tuple-element.64.refs_2_), channel_id=1, source_target_pairs={{0,2},{2,32},{32,34},{34,0},{1,3},{3,33},{33,35},{35,1},{4,6},{6,3... | collective-permute-start | bytes 6291464 | tf_op jit(solution)/shard_map/ppermute | solution.py:335
  18.5 50.7 %collective-permute-start.4 = (bf16[64,1024]{1,0:T(8,128)(2,1)S(1)}, bf16[64,1024]{1,0:T(8,128)(2,1)S(1)}, u32[]{:S(2)}, u32[]{:S(2)}) collective-permute-start(bf16[64,1024]{1,0:T(8,128)(2,1)S(1)} %bitcast.32), channel_id=1, source_target_pairs={{28,32},{60,64},{92,96},{124,128},{156,160},{188,192},{220,224},{3... | collective-permute-start | bytes 393224 | tf_op jit(solution)/shard_map/ppermute | solution.py:339
  69.2 64.5 %collective-permute-start.7 = (bf16[512,4096]{1,0:T(8,128)(2,1)}, bf16[512,4096]{1,0:T(8,128)(2,1)}, u32[]{:S(2)}, u32[]{:S(2)}) collective-permute-start(bf16[512,4096]{1,0:T(8,128)(2,1)} %param.7), channel_id=1, source_target_pairs={{0,1},{1,0},{2,3},{3,2},{4,5},{5,4},{6,7},{7,6},{8,9},{9,8},{10,11... | collective-permute-start | bytes 12582920 | tf_op jit(solution)/shard_map/ppermute | solution.py:352
  78.1 55.7 %all-to-all-start.1 = ((bf16[8,4,64,1024]{3,2,1,0:T(8,128)(2,1)}), bf16[8,4,64,1024]{3,2,1,0:T(8,128)(2,1)}, u32[]{:S(2)}, u32[]{:S(2)}) async-start(bf16[8,4,64,1024]{3,2,1,0:T(8,128)(2,1)} %pick.2), calls=%async_computation.1 | async-start | bytes 8388608 | tf_op jit(solution)/shard_map/all_to_all | solution.py:282
  82.6 8.1 %collective-permute-start.8 = (bf16[256,4096]{1,0:T(8,128)(2,1)}, bf16[256,4096]{1,0:T(8,128)(2,1)}, u32[]{:S(2)}, u32[]{:S(2)}) collective-permute-start(bf16[256,4096]{1,0:T(8,128)(2,1)} %collective-permute-done.2.refs_5_), channel_id=1, source_target_pairs={{0,1},{1,0},{2,3},{3,2},{4,5},{5,4},{6,7},{7,6},{8,9},{9,8},{10,11... | collective-permute-start | bytes 6291464 | tf_op jit(solution)/shard_map/ppermute | solution.py:352
  82.8 7.9 %collective-permute-start.9 = (bf16[256,4096]{1,0:T(8,128)(2,1)}, bf16[256,4096]{1,0:T(8,128)(2,1)}, u32[]{:S(2)}, u32[]{:S(2)}) collective-permute-start(bf16[256,4096]{1,0:T(8,128)(2,1)} %collective-permute-done.3.refs_6_), channel_id=1, source_target_pairs={{0,1},{1,0},{2,3},{3,2},{4,5},{5,4},{6,7},{7,6},{8,9},{9,8},{10,11... | collective-permute-start | bytes 6291464 | tf_op jit(solution)/shard_map/ppermute | solution.py:352
  83.2 48.7 %collective-permute-start.5 = (bf16[16,64,1024]{2,1,0:T(8,128)(2,1)}, bf16[16,64,1024]{2,1,0:T(8,128)(2,1)}, u32[]{:S(2)}, u32[]{:S(2)}) collective-permute-start(bf16[16,64,1024]{2,1,0:T(8,128)(2,1)} %collective-permute-done.refs_1_), channel_id=1, source_target_pairs={{0,4},{4,8},{8,12},{12,16},{16,20},{20,24},{24,28},{28,0},{1,5},{5... | collective-permute-start | bytes 6291464 | tf_op jit(solution)/shard_map/ppermute | solution.py:278
  83.2 48.7 %collective-permute-start.6 = (bf16[16,64,1024]{2,1,0:T(8,128)(2,1)}, bf16[16,64,1024]{2,1,0:T(8,128)(2,1)}, u32[]{:S(2)}, u32[]{:S(2)}) collective-permute-start(bf16[16,64,1024]{2,1,0:T(8,128)(2,1)} %collective-permute-done.1.refs_2_), channel_id=1, source_target_pairs={{0,28},{4,0},{8,4},{12,8},{16,12},{20,16},{24,20},{28,24},{1,29},{... | collective-permute-start | bytes 6291464 | tf_op jit(solution)/shard_map/ppermute | solution.py:278
  141.4 11.1 %copy-start.15 = (bf16[4,64,1024]{2,1,0:T(8,128)(2,1)S(1)}, bf16[4,64,1024]{2,1,0:T(8,128)(2,1)}, u32[]{:S(2)}) copy-start(bf16[4,64,1024]{2,1,0:T(8,128)(2,1)} %get-tuple-element.48) | copy-start | bytes 1572868
  141.4 11.2 %copy-start.14 = (bf16[4,64,1024]{2,1,0:T(8,128)(2,1)S(1)}, bf16[4,64,1024]{2,1,0:T(8,128)(2,1)}, u32[]{:S(2)}) copy-start(bf16[4,64,1024]{2,1,0:T(8,128)(2,1)} %get-tuple-element.49) | copy-start | bytes 1572868
  141.4 31.6 %all-to-all-start.2 = ((bf16[8,2,64,1024]{3,2,1,0:T(8,128)(2,1)}), bf16[8,2,64,1024]{3,2,1,0:T(8,128)(2,1)}, u32[]{:S(2)}, u32[]{:S(2)}) async-start(bf16[8,2,64,1024]{3,2,1,0:T(8,128)(2,1)} %get-tuple-element.47), calls=%async_computation.2 | async-start | bytes 4194304 | tf_op jit(solution)/shard_map/all_to_all | solution.py:282
  146.9 3.2 %collective-permute-start.10 = (bf16[64,1024]{1,0:T(8,128)(2,1)S(1)}, bf16[64,1024]{1,0:T(8,128)(2,1)S(1)}, u32[]{:S(2)}, u32[]{:S(2)}) collective-permute-start(bf16[64,1024]{1,0:T(8,128)(2,1)S(1)} %select_bitcast_fusion), channel_id=1, source_target_pairs={{0,16},{28,12},{1,17},{29,13},{2,18},{30,14},{3,19},{31,15},{32,48... | collective-permute-start | bytes 393224 | tf_op jit(solution)/shard_map/ppermute | solution.py:371
  151.2 4.1 %collective-permute-start.11 = (bf16[64,1024]{1,0:T(8,128)(2,1)S(1)}, bf16[64,1024]{1,0:T(8,128)(2,1)S(1)}, u32[]{:S(2)}, u32[]{:S(2)}) collective-permute-start(bf16[64,1024]{1,0:T(8,128)(2,1)S(1)} %broadcast_select_fusion.1), channel_id=1, source_target_pairs={{0,8},{16,24},{28,20},{12,4},{1,9},{17,25},{29,21},{13,5},{2,10},{... | collective-permute-start | bytes 393224 | tf_op jit(solution)/shard_map/ppermute | solution.py:377
  152.5 15.0 %collective-permute-start.13 = (bf16[4,64,1024]{2,1,0:T(8,128)(2,1)S(1)}, bf16[4,64,1024]{2,1,0:T(8,128)(2,1)S(1)}, u32[]{:S(2)}, u32[]{:S(2)}) collective-permute-start(bf16[4,64,1024]{2,1,0:T(8,128)(2,1)S(1)} %copy-done.15), channel_id=1, source_target_pairs={{0,4},{4,8},{8,12},{12,16},{16,20},{20,24},{24,28},{28,0},{1,5},{5... | collective-permute-start | bytes 1572872 | tf_op jit(solution)/shard_map/ppermute | solution.py:278
  152.6 15.6 %collective-permute-start.14 = (bf16[4,64,1024]{2,1,0:T(8,128)(2,1)S(1)}, bf16[4,64,1024]{2,1,0:T(8,128)(2,1)}, u32[]{:S(2)}, u32[]{:S(2)}) collective-permute-start(bf16[4,64,1024]{2,1,0:T(8,128)(2,1)S(1)} %copy-done.14), channel_id=1, source_target_pairs={{0,28},{4,0},{8,4},{12,8},{16,12},{20,16},{24,20},{28,24},{1,29},{... | collective-permute-start | bytes 1572872 | tf_op jit(solution)/shard_map/ppermute | solution.py:278
  155.3 12.1 %collective-permute-start.12 = (bf16[64,1024]{1,0:T(8,128)(2,1)S(1)}, bf16[64,1024]{1,0:T(8,128)(2,1)S(1)}, u32[]{:S(2)}, u32[]{:S(2)}) collective-permute-start(bf16[64,1024]{1,0:T(8,128)(2,1)S(1)} %broadcast_select_fusion.2), channel_id=1, source_target_pairs={{0,4},{4,0},{8,12},{12,8},{16,20},{20,16},{24,28},{28,24},{1,5},{5... | collective-permute-start | bytes 393224 | tf_op jit(solution)/shard_map/ppermute | solution.py:380
  167.5 0.8 copy-start.16
  176.1 8.7 %copy-start.2 = (bf16[1024,512]{1,0:T(8,128)(2,1)S(1)}, bf16[1024,512]{1,0:T(8,128)(2,1)}, u32[]{:S(2)}) copy-start(bf16[1024,512]{1,0:T(8,128)(2,1)} %refs_2_.3) | copy-start | bytes 3145732
  176.1 30.9 %all-to-all-start.3 = ((bf16[8,2,64,1024]{3,2,1,0:T(8,128)(2,1)}), bf16[8,2,64,1024]{3,2,1,0:T(8,128)(2,1)}, u32[]{:S(2)}, u32[]{:S(2)}) async-start(bf16[8,2,64,1024]{3,2,1,0:T(8,128)(2,1)} %get-tuple-element.53), calls=%async_computation.3 | async-start | bytes 4194304 | tf_op jit(solution)/shard_map/all_to_all | solution.py:282
  180.6 25.3 %collective-permute-start.17 = (bf16[4,64,1024]{2,1,0:T(8,128)(2,1)}, bf16[4,64,1024]{2,1,0:T(8,128)(2,1)S(1)}, u32[]{:S(2)}, u32[]{:S(2)}) collective-permute-start(bf16[4,64,1024]{2,1,0:T(8,128)(2,1)} %copy-done.16), channel_id=1, source_target_pairs={{0,4},{4,8},{8,12},{12,16},{16,20},{20,24},{24,28},{28,0},{1,5},{5... | collective-permute-start | bytes 1572872 | tf_op jit(solution)/shard_map/ppermute | solution.py:278
  181.2 24.7 %collective-permute-start.18 = (bf16[4,64,1024]{2,1,0:T(8,128)(2,1)}, bf16[4,64,1024]{2,1,0:T(8,128)(2,1)S(1)}, u32[]{:S(2)}, u32[]{:S(2)}) collective-permute-start(bf16[4,64,1024]{2,1,0:T(8,128)(2,1)} %collective-permute-done.14), channel_id=1, source_target_pairs={{0,28},{4,0},{8,4},{12,8},{16,12},{20,16},{24,20},{28,24},{1,29},{... | collective-permute-start | bytes 1572872 | tf_op jit(solution)/shard_map/ppermute | solution.py:278
  183.4 32.2 %collective-permute-start.16 = (bf16[8,64,1024]{2,1,0:T(8,128)(2,1)}, bf16[8,64,1024]{2,1,0:T(8,128)(2,1)}, u32[]{:S(2)}, u32[]{:S(2)}) collective-permute-start(bf16[8,64,1024]{2,1,0:T(8,128)(2,1)} %get-tuple-element.65), channel_id=1, source_target_pairs={{0,28},{4,0},{8,4},{12,8},{16,12},{20,16},{24,20},{28,24},{1,29},{... | collective-permute-start | bytes 3145736 | tf_op jit(solution)/shard_map/ppermute | solution.py:278
  184.2 31.5 %collective-permute-start.15 = (bf16[8,64,1024]{2,1,0:T(8,128)(2,1)}, bf16[8,64,1024]{2,1,0:T(8,128)(2,1)}, u32[]{:S(2)}, u32[]{:S(2)}) collective-permute-start(bf16[8,64,1024]{2,1,0:T(8,128)(2,1)} %get-tuple-element.66), channel_id=1, source_target_pairs={{0,4},{4,8},{8,12},{12,16},{16,20},{20,24},{24,28},{28,0},{1,5},{5... | collective-permute-start | bytes 3145736 | tf_op jit(solution)/shard_map/ppermute | solution.py:278
  184.8 1.7 copy-start
  203.8 1.3 copy-start.9
  205.1 0.8 copy-start.11
  207.0 25.9 %all-to-all-start.4 = ((bf16[8,64,1024]{2,1,0:T(8,128)(2,1)}), bf16[8,64,1024]{2,1,0:T(8,128)(2,1)S(1)}, u32[]{:S(2)}, u32[]{:S(2)}) async-start(bf16[8,64,1024]{2,1,0:T(8,128)(2,1)} %pad_maximum_fusion.1), calls=%async_computation.4 | async-start | bytes 2097152 | tf_op jit(solution)/shard_map/all_to_all | solution.py:282
  215.7 1.2 copy-start.3
  216.9 1.6 copy-start.10
  218.5 1.0 copy-start.12
  230.7 1.3 copy-start.5
  232.1 0.8 copy-start.7
  232.9 1.2 copy-start.4
  234.1 1.6 copy-start.6
  235.7 1.0 copy-start.8
  241.3 1.0 copy-start.1
  242.3 21.6 %all-to-all-start.5 = ((bf16[4,256,512]{2,1,0:T(8,128)(2,1)}), bf16[4,256,512]{2,1,0:T(8,128)(2,1)S(1)}, u32[]{:S(2)}, u32[]{:S(2)}) async-start(bf16[4,256,512]{2,1,0:T(8,128)(2,1)} %bitcast.26), calls=%async_computation.5 | async-start | bytes 2097152 | tf_op jit(solution)/shard_map/all_to_all | solution.py:399

commit v6 on v5

--- a/solution.py
+++ b/solution.py
@@ -126,20 +126,26 @@
         add_slots(which, z_ref, where_ref, ref, q_ref, o_ref, st_ref)
 
 
-def final_kernel(deltas, z_ref, where_ref, q_ref, oin_ref, stin_ref, *refs):
-    slots, (att_ref, o_ref, st_ref) = refs[: len(deltas)], refs[len(deltas) :]
+def final_kernel(deltas, me_ref, z_ref, where_ref, q_ref, oin_ref, stin_ref, *refs):
+    groups = NXL * NC
+    slots, outs = refs[: len(deltas)], refs[len(deltas) : len(deltas) + groups]
+    o_ref, st_ref = refs[-2:]
     more_kernel(deltas, z_ref, where_ref, q_ref, oin_ref, stin_ref, *slots, o_ref, st_ref)
     heads = range(q_ref.shape[1] // HEAD_DIM)
-
-    def step(j, carry):
-        rows = pl.ds(pl.multiple_of(j * BLOCK, BLOCK), BLOCK)
-        for h in heads:
-            kcol = pl.ds(h * HEAD_DIM, HEAD_DIM)
-            total = st_ref[rows, pl.ds(len(heads) + h, 1)]
-            att_ref[rows, kcol] = (o_ref[rows, kcol] / total).astype(BF16)
+    share = q_ref.shape[0] // groups
+
+    def step(i, carry):
+        to = pl.ds(pl.multiple_of(i * BLOCK, BLOCK), BLOCK)
+        for k, out_ref in enumerate(outs):
+            start = (me_ref[0] ^ k) * share + i * BLOCK
+            rows = pl.ds(pl.multiple_of(start, BLOCK), BLOCK)
+            for h in heads:
+                kcol = pl.ds(h * HEAD_DIM, HEAD_DIM)
+                total = st_ref[rows, pl.ds(len(heads) + h, 1)]
+                out_ref[to, kcol] = (o_ref[rows, kcol] / total).astype(BF16)
         return carry
 
-    lax.fori_loop(0, q_ref.shape[0] // BLOCK, step, 0)
+    lax.fori_loop(0, share // BLOCK, step, 0)
 
 
 def cost(us):
@@ -178,21 +184,22 @@
     )(z, where, q, o, st, *slots)
 
 
-def final_part(z, where, q, o, st, deltas, slots):
+def final_part(me, z, where, q, o, st, deltas, slots):
     tok, feat = q.shape
+    groups = NXL * NC
     return pl.pallas_call(
         lambda *refs: final_kernel(deltas, *refs),
-        out_shape=jax.ShapeDtypeStruct((tok, feat), BF16),
-        in_specs=[SM, SM] + [VM] * (3 + len(slots)),
-        out_specs=VM,
+        out_shape=tuple(jax.ShapeDtypeStruct((tok // groups, feat), BF16) for _ in range(groups)),
+        in_specs=[SM, SM, SM] + [VM] * (3 + len(slots)),
+        out_specs=tuple(VM for _ in range(groups)),
         scratch_shapes=[pltpu.VMEM((tok, feat), F32), pltpu.VMEM((tok, 128), F32)],
         compiler_params=pltpu.CompilerParams(vmem_limit_bytes=VMEM_LIMIT),
         cost_estimate=cost(6),
         name="final_part",
-    )(z, where, q, o, st, *slots)
-
-
-def pick(z, asked, sources, plan, shapes):
+    )(me, z, where, q, o, st, *slots)
+
+
+def pick(z, asked, sources, plan, shapes, us=3):
     def kernel(z_ref, asked_ref, *refs):
         src, out = refs[: len(sources)], refs[len(sources) : -3]
         held, in_sems, out_sems = refs[-3:]
@@ -224,14 +231,15 @@
             pltpu.SemaphoreType.DMA((len(plan),)),
         ],
         compiler_params=pltpu.CompilerParams(vmem_limit_bytes=8 * 1024 * 1024),
-        cost_estimate=cost(3),
+        cost_estimate=cost(us),
         name="pick",
     )(z, asked, *sources)
 
 
-def project_kernel(tile, me_ref, a_ref, *refs):
-    weights, (out_ref, w_ref, acat_ref, sems) = refs[:-4], refs[-4:]
-    rows, feat = a_ref.shape[1:]
+def project_kernel(tile, count, base, *refs):
+    parts, weights = refs[:count], refs[count : -4 - base]
+    out_ref, w_ref, a_ref, sems = refs[-4:]
+    feat = parts[0].shape[1]
     cols = out_ref.shape[1]
     copies = []
     for n in range(cols // tile):
@@ -246,32 +254,36 @@
             )
             copies[-1].start()
             top += weight.shape[0]
-    me = me_ref[0]
-    for g in range(a_ref.shape[0]):
-        acat_ref[:, pl.ds(g * feat, feat)] = a_ref[me ^ g]
+    for g, part in enumerate(parts):
+        a_ref[:, pl.ds(g * feat, feat)] = part[...]
     for n in range(cols // tile):
         for k in range(len(weights)):
             copies[n * len(weights) + k].wait()
         span = pl.ds(n * tile, tile)
-        out_ref[:, span] = dot_nn(acat_ref[...], w_ref[:, span]).astype(BF16)
-
-
-def project(me, a, weights, tile=1024):
-    groups, rows, feat = a.shape
+        value = dot_nn(a_ref[...], w_ref[:, span])
+        if base:
+            value += refs[-5][:, span]
+        out_ref[:, span] = value.astype(out_ref.dtype)
+
+
+def project(parts, weights, base=None, tile=1024):
+    rows, feat = parts[0].shape
     cols = weights[0].shape[1]
+    bases = [] if base is None else [base]
     return pl.pallas_call(
-        lambda *refs: project_kernel(tile, *refs),
-        out_shape=jax.ShapeDtypeStruct((rows, cols), BF16),
-        in_specs=[SM, VM] + [HB] * len(weights),
+        lambda *refs: project_kernel(tile, len(parts), len(bases), *refs),
+        out_shape=jax.ShapeDtypeStruct((rows, cols), F32 if base is None else BF16),
+        in_specs=[VM] * len(parts) + [HB] * len(weights) + [VM] * len(bases),
         out_specs=VM,
         scratch_shapes=[
-            pltpu.VMEM((groups * feat, cols), BF16),
-            pltpu.VMEM((rows, groups * feat), BF16),
+            pltpu.VMEM((len(parts) * feat, cols), BF16),
+            pltpu.VMEM((rows, len(parts) * feat), BF16),
             pltpu.SemaphoreType.DMA((cols // tile * len(weights),)),
         ],
         compiler_params=pltpu.CompilerParams(vmem_limit_bytes=VMEM_LIMIT),
+        cost_estimate=cost(6),
         name="project",
-    )(me, a, *weights)
+    )(*parts, *weights, *bases)
 
 
 def z_shift(x, by):
@@ -353,7 +365,7 @@
     before = jnp.where(z == 0, crossed, up1[blocks_dev - 1])
     after = jnp.where(z == NZ - 1, crossed, down1[0])
     kv_pad = jnp.concatenate([before, kv.reshape(tok, 2 * feat), after], axis=0)
-    up2, down2, r1, kv_pad, *others = tie(up2, down2, r1, kv_pad, *others)
+    up2, down2, kv_pad, *others = tie(up2, down2, kv_pad, *others)
     weights = own + [others[0], low, high] + others[1:]
 
     plan = [(0, (lane, 0), 0, lane, 1, -2) for lane in lanes]
@@ -363,8 +375,9 @@
     plan += [(3, (lane, 0), 0, lane, 0, -2) for lane in lanes]
     plan += [(3, (lane, 1), 1, lane, 0, 2) for lane in lanes]
     c3, fu, fd, c2 = pick(
-        zs, asked, [up2, down2], plan, [(LANES, 2), (half,), (half,), (LANES, 2)]
+        zs, asked, [up2, down2], plan, [(LANES, 2), (half,), (half,), (LANES, 2)], 60
     )
+    c3, r1 = tie(c3, r1)
     fu, fd = z_shift(fu, 1), z_shift(fd, -1)
     c3 = lane_exchange(c3)
     held = jnp.where(z == 0, r1[0, 3], r1[LANES - 1, 3])
@@ -393,13 +406,14 @@
     o, st = more_part(
         zs, where, queries, o, st, [(-3,), (3,), (-2, 2)], [slots(r3u), slots(r3d), r2]
     )
-    attended = final_part(zs, where, queries, o, st, [(4,)], [slots(r4)])
-
-    heads = NXL * NC
-    a = lax.all_to_all(
-        attended.reshape(heads, tok // heads, feat), HEAD, split_axis=0, concat_axis=0, tiled=True
-    )
-    return project(lax.axis_index(HEAD).reshape(1), a, weights)
+    me = lax.axis_index(HEAD).reshape(1)
+    mine, *away = final_part(me, zs, where, queries, o, st, [(4,)], [slots(r4)])
+
+    heads = range(NXL * NC)
+    far_x, far_xc = [lax.ppermute(away[k - 1], HEAD, [(h, h ^ k) for h in heads]) for k in (2, 3)]
+    near = lax.ppermute(away[0], HEAD, [(h, h ^ 1) for h in heads])
+    partial = project([mine, near], weights[:3])
+    return project([far_x, far_xc], weights[3:], partial)
 
 
 def solution(mesh):

time: 275 us -> 260 us (0.945)
  waiting for transfers between devices: 71.6 us -> 60.8 us
  local copies, waits for them, and re-layouts: 29.5 us -> 21.7 us
    ppermute x10, waiting for transfers between devices: 43.3 us -> 27.8 us  [z_shift(): return lax.ppermute(x, 'z', [(i, (i + by) % NZ) for i in range(NZ)])]
    all_to_all x1 -> x0, waiting for transfers between devices: 13.6 us -> none  [body(): lax.all_to_all(attended.reshape(heads, tok // heads, feat), HEAD, split_a...]
    all_to_all x4, waiting for transfers between devices: 6.52 us -> 14.8 us  [lane_exchange(): return lax.all_to_all(x, LANE, split_axis=0, concat_axis=0, tiled=True)]
    all_to_all x1 -> x0, starting transfers between devices: 8.01 us -> none  [body(): lax.all_to_all(attended.reshape(heads, tok // heads, feat), HEAD, split_a...]
    unnamed x37 -> x23, local copies, waits for them, and re-layouts: 17.6 us -> 10.2 us
    ppermute x0 -> x3, waiting for transfers between devices: none -> 7.37 us  [the longest x2 7.37 us: body(): lax.ppermute(away[k - 1], HEAD, [(h, h ^ k) for h in heads])]
    ppermute x0 -> x3, starting transfers between devices: none -> 5.92 us  [the longest x1 4.19 us: body(): near = lax.ppermute(away[0], HEAD, [(h, h ^ 1) for h in heads])]
    ppermute x1, starting transfers between devices: 1.3 us -> 4.8 us  [body(): got = lax.ppermute(held, 'z', [(0, 4), (7, 3)])]
  transfers between devices with their start and end apart: 24 -> 26, of which waited for: 8 -> 7; matrix products, arithmetic and copies ran while one was open for 5% -> 7% of each run, Pallas kernels for 13% -> 19%
where the time goes in v6:
time: 260 us; the launch traced here: 256 us
  waiting for transfers between devices  60.8 us (23%)
  starting transfers between devices  59.4 us (23%)
  Pallas kernels  56.3 us (22%)
  blocking collectives  49.1 us (19%)
  local copies, waits for them, and re-layouts  21.7 us (8%)
  other arithmetic  8.33 us (3%)
    all_to_all x1, blocking collectives, body(): asked = lax.all_to_all(asked, SEQ, split_axis=0, concat_axis=0, tiled=True)  49.1 us
    ppermute x10, waiting for transfers between devices, z_shift(): return lax.ppermute(x, 'z', [(i, (i + by) % NZ) for i in range(NZ)])  27.8 us
    all_to_all x4, starting transfers between devices, lane_exchange(): return lax.all_to_all(x, LANE, split_axis=0, concat_axis=0, tiled=True)  19.3 us
    pallas_call x1, Pallas kernels, local_part(): pl.pallas_call(lambda *refs: local_kernel(all_blocks, deltas, *refs), out...  18.1 us
    ppermute x10, starting transfers between devices, z_shift(): return lax.ppermute(x, 'z', [(i, (i + by) % NZ) for i in range(NZ)])  17.9 us
    all_to_all x4, waiting for transfers between devices, lane_exchange(): return lax.all_to_all(x, LANE, split_axis=0, concat_axis=0, tiled=True)  14.8 us
    pallas_call x2, Pallas kernels, pick(): pl.pallas_call(kernel, out_shape=tuple((pltpu.HBM(shape + block_shape, BF...  14 us
    pallas_call x1, Pallas kernels, more_part(): pl.pallas_call(lambda *refs: more_kernel(deltas, *refs), out_shape=(jax.S...  11.1 us
  transfers between devices with their start and end apart: 26, of which 7 were waited for; matrix products, arithmetic and copies ran while one was open for 7% of the time, Pallas kernels for 19%

profile of v6, /device:TPU:1, one launch (start us, length us, event | category | flops | bytes accessed | tf_op | source)
XLA Modules:
  0.0 256.3 jit_solution(14743387368248891274)
XLA Ops:
  0.0 4.7 %fusion.4 = (bf16[256,4096]{1,0:T(8,128)(2,1)}, bf16[256,4096]{1,0:T(8,128)(2,1)}) fusion(bf16[512,4096]{1,0:T(8,128)(2,1)} %param.7), kind=kLoop, calls=%fused_computation.34 | loop fusion | bytes 8388608 | tf_op jit(solution)/shard_map/slice | solution.py:345
  4.7 2.0 collective-permute-start.2
  6.7 1.3 collective-permute-start.3
  8.0 3.2 %reshape.121.refs_0_ = bf16[16,64,1024]{2,1,0:T(8,128)(2,1)S(1)} reshape(bf16[1024,2,512]{2,1,0:T(2,128)(2,1)} %param.5) | data formatting | bytes 4194304 | tf_op jit(solution)/shard_map/reshape | solution.py:337
  11.2 1.9 collective-permute-start
  13.2 4.0 %collective-permute-start.1 = (bf16[16,64,1024]{2,1,0:T(8,128)(2,1)S(1)}, bf16[16,64,1024]{2,1,0:T(8,128)(2,1)}, u32[]{:S(2)}, u32[]{:S(2)}) collective-permute-start(bf16[16,64,1024]{2,1,0:T(8,128)(2,1)S(1)} %reshape.121.refs_0_), channel_id=1, source_target_pairs={{0,28},{4,0},{8,4},{12,8},{16,12},{20,16},{24,20},{28,24},{1,29},{... | collective-permute-start | bytes 6291464 | tf_op jit(solution)/shard_map/ppermute | solution.py:290
  17.2 1.1 broadcast_select_fusion
  19.6 49.1 %all_to_all.32 = s32[64,1,8]{2,1,0:T(1,128)S(1)} all-to-all(s32[64,1,8]{2,1,0:T(1,128)S(1)} %bitcast.31), channel_id=1, replica_groups=mesh['y'=4,'xh'=2,'z'=8,'xl'=2,'core'=2] {'y','xh','z'}, dimensions={0} | all-to-all | bytes 4096 | tf_op jit(solution)/shard_map/all_to_all | solution.py:343
  68.8 2.4 collective-permute-start.7
  71.1 1.4 collective-permute-start.5
  72.5 1.4 collective-permute-start.6
  74.5 3.5 %copy.22 = bf16[128,8,2,512]{3,1,2,0:T(8,128)(2,1)} copy(bf16[128,8,2,512]{3,2,1,0:T(2,128)(2,1)} %bitcast.27) | data formatting | bytes 4194304
  78.0 7.0 %pick.3 = bf16[8,4,64,1024]{3,2,1,0:T(8,128)(2,1)} custom-call(s32[1]{0:T(128)} %bitcast.1.z_ref.refs_0_.refs_1_, s32[64,8]{1,0:T(8,128)S(1)} %bitcast.25, bf16[16,64,1024]{2,1,0:T(8,128)(2,1)S(1)} %reshape.121.refs_0_, bf16[16,64,1024]{2,1,0:T(8,128)(2,1)} %collective-permute-done.refs_1_, bf16[16,64,1024]{2,1,0:T(8,128)(2,1)} %collective-permute-done.1.refs_2_), custom_call_target="tpu_custom_call" | custom-call | flops 3000000000 | bytes 4194304 | tf_op jit(solution)/shard_map/pick/pallas_call | solution.py:223
  84.9 4.6 %all-to-all-start.1 = ((bf16[8,4,64,1024]{3,2,1,0:T(8,128)(2,1)}), bf16[8,4,64,1024]{3,2,1,0:T(8,128)(2,1)}, u32[]{:S(2)}, u32[]{:S(2)}) async-start(bf16[8,4,64,1024]{3,2,1,0:T(8,128)(2,1)} %pick.3), calls=%async_computation.1 | async-start | bytes 8388608 | tf_op jit(solution)/shard_map/all_to_all | solution.py:294
  89.5 1.0 bitcast_select_fusion.1
  90.5 1.8 pad_maximum_fusion.refs_4_
  92.3 27.7 %collective-permute-done.5.refs_0_ = bf16[16,64,1024]{2,1,0:T(8,128)(2,1)} collective-permute-done((bf16[16,64,1024]{2,1,0:T(8,128)(2,1)}, bf16[16,64,1024]{2,1,0:T(8,128)(2,1)}, u32[]{:S(2)}, u32[]{:S(2)}) %collective-permute-start.5) | collective-permute-done | bytes 2097184 | tf_op jit(solution)/shard_map/ppermute | solution.py:290
  120.1 7.0 %pick.2 = (bf16[8,2,64,1024]{3,2,1,0:T(8,128)(2,1)}, bf16[4,64,1024]{2,1,0:T(8,128)(2,1)}, bf16[4,64,1024]{2,1,0:T(8,128)(2,1)}, bf16[8,2,64,1024]{3,2,1,0:T(8,128)(2,1)}) custom-call(s32[1]{0:T(128)} %bitcast.1.z_ref.refs_0_.refs_1_, s32[64,8]{1,0:T(8,128)S(1)} %bitcast.26, bf16[16,64,1024]{2,1,0:T(8,128)(2,1)} %collective-permute-done.5.refs_0_, ...), custom_call_target="tpu_custom_call" | custom-call | flops 60000002048 | bytes 4194304 | tf_op jit(solution)/shard_map/pick/pallas_call | solution.py:223
  127.1 12.9 %all-to-all-done.1.refs_6_ = bf16[8,4,64,1024]{3,2,1,0:T(8,128)(2,1)} async-done(((bf16[8,4,64,1024]{3,2,1,0:T(8,128)(2,1)}), bf16[8,4,64,1024]{3,2,1,0:T(8,128)(2,1)}, u32[]{:S(2)}, u32[]{:S(2)}) %all-to-all-start.1) | async-done | bytes 4194336 | tf_op jit(solution)/shard_map/all_to_all | solution.py:294
  140.0 4.5 %all-to-all-start.2 = ((bf16[8,2,64,1024]{3,2,1,0:T(8,128)(2,1)}), bf16[8,2,64,1024]{3,2,1,0:T(8,128)(2,1)}, u32[]{:S(2)}, u32[]{:S(2)}) async-start(bf16[8,2,64,1024]{3,2,1,0:T(8,128)(2,1)} %get-tuple-element.53), calls=%async_computation.2 | async-start | bytes 4194304 | tf_op jit(solution)/shard_map/all_to_all | solution.py:294
  145.5 4.8 %collective-permute-start.10 = (bf16[64,1024]{1,0:T(8,128)(2,1)S(1)}, bf16[64,1024]{1,0:T(8,128)(2,1)S(1)}, u32[]{:S(2)}, u32[]{:S(2)}) collective-permute-start(bf16[64,1024]{1,0:T(8,128)(2,1)S(1)} %select_bitcast_fusion), channel_id=1, source_target_pairs={{0,16},{28,12},{1,17},{29,13},{2,18},{30,14},{3,19},{31,15},{32,48... | collective-permute-start | bytes 393224 | tf_op jit(solution)/shard_map/ppermute | solution.py:384
  150.3 1.9 collective-permute-done.10
  152.2 1.0 broadcast_select_fusion.1
  153.2 1.3 collective-permute-start.11
  154.7 2.7 %collective-permute-start.14 = (bf16[4,64,1024]{2,1,0:T(8,128)(2,1)S(1)}, bf16[4,64,1024]{2,1,0:T(8,128)(2,1)}, u32[]{:S(2)}, u32[]{:S(2)}) collective-permute-start(bf16[4,64,1024]{2,1,0:T(8,128)(2,1)S(1)} %copy-done.9), channel_id=1, source_target_pairs={{0,28},{4,0},{8,4},{12,8},{16,12},{20,16},{24,20},{28,24},{1,29},{... | collective-permute-start | bytes 1572872 | tf_op jit(solution)/shard_map/ppermute | solution.py:290
  157.3 3.3 %collective-permute-start.12 = (bf16[64,1024]{1,0:T(8,128)(2,1)S(1)}, bf16[64,1024]{1,0:T(8,128)(2,1)S(1)}, u32[]{:S(2)}, u32[]{:S(2)}) collective-permute-start(bf16[64,1024]{1,0:T(8,128)(2,1)S(1)} %broadcast_select_fusion.2), channel_id=1, source_target_pairs={{0,4},{4,0},{8,12},{12,8},{16,20},{20,16},{24,28},{28,24},{1,5},{5... | collective-permute-start | bytes 393224 | tf_op jit(solution)/shard_map/ppermute | solution.py:393
  160.7 9.0 %collective-permute-done.12 = bf16[64,1024]{1,0:T(8,128)(2,1)S(1)} collective-permute-done((bf16[64,1024]{1,0:T(8,128)(2,1)S(1)}, bf16[64,1024]{1,0:T(8,128)(2,1)S(1)}, u32[]{:S(2)}, u32[]{:S(2)}) %collective-permute-start.12) | collective-permute-done | bytes 131104 | tf_op jit(solution)/shard_map/ppermute | solution.py:393
  169.7 1.9 all-to-all-done.2
  172.1 2.2 collective-permute-start.18
  174.3 4.5 %all-to-all-start.3 = ((bf16[8,2,64,1024]{3,2,1,0:T(8,128)(2,1)}), bf16[8,2,64,1024]{3,2,1,0:T(8,128)(2,1)}, u32[]{:S(2)}, u32[]{:S(2)}) async-start(bf16[8,2,64,1024]{3,2,1,0:T(8,128)(2,1)} %get-tuple-element.59), calls=%async_computation.3 | async-start | bytes 4194304 | tf_op jit(solution)/shard_map/all_to_all | solution.py:294
  178.7 3.3 %slice_bitcast_fusion = (bf16[8,64,1024]{2,1,0:T(8,128)(2,1)}, bf16[8,64,1024]{2,1,0:T(8,128)(2,1)}) fusion(bf16[8,2,64,1024]{3,2,1,0:T(8,128)(2,1)} %all-to-all-done.2), kind=kLoop, calls=%fused_computation.1 | loop fusion | bytes 4194304 | tf_op jit(solution)/shard_map/squeeze | solution.py:389
  182.0 1.2 collective-permute-start.16
  183.1 2.6 %collective-permute-start.15 = (bf16[8,64,1024]{2,1,0:T(8,128)(2,1)}, bf16[8,64,1024]{2,1,0:T(8,128)(2,1)}, u32[]{:S(2)}, u32[]{:S(2)}) collective-permute-start(bf16[8,64,1024]{2,1,0:T(8,128)(2,1)} %get-tuple-element.76), channel_id=1, source_target_pairs={{0,4},{4,8},{8,12},{12,16},{16,20},{20,24},{24,28},{28,0},{1,5},{5... | collective-permute-start | bytes 3145736 | tf_op jit(solution)/shard_map/ppermute | solution.py:290
  185.7 18.1 %local_part.1 = (f32[1024,512]{1,0:T(8,128)S(1)}, f32[1024,128]{1,0:T(8,128)S(1)}) custom-call(s32[1]{0:T(128)} %bitcast.1.z_ref.refs_0_.refs_1_, s32[64]{0:T(128)S(1)} %broadcast_add_fusion.refs_1_.refs_2_, s32[1]{0:T(128)} %bitcast.2.refs_2_, bf16[1024,512]{1,0:T(8,128)(2,1)S(1)} %copy-done, bf16[1152,1024]{1,0:T(8,128)(2,1)S(1)} %pad_maximum_fusion.refs_4_, ...), custom_call_target="tpu_custom_call" | custom-call | flops 24999999488 | bytes 4194304 | tf_op jit(solution)/shard_map/local_part/pallas_call | solution.py:157
  203.8 1.3 copy-done.4
  205.9 2.2 pad_maximum_fusion.1
  208.2 5.8 %all-to-all-start.4 = ((bf16[8,64,1024]{2,1,0:T(8,128)(2,1)}), bf16[8,64,1024]{2,1,0:T(8,128)(2,1)S(1)}, u32[]{:S(2)}, u32[]{:S(2)}) async-start(bf16[8,64,1024]{2,1,0:T(8,128)(2,1)} %pad_maximum_fusion.1), calls=%async_computation.4 | async-start | bytes 2097152 | tf_op jit(solution)/shard_map/all_to_all | solution.py:294
  214.0 1.6 copy-done.5
  215.6 11.1 %more_part.1 = (f32[1024,512]{1,0:T(8,128)S(1)}, f32[1024,128]{1,0:T(8,128)S(1)}) custom-call(s32[1]{0:T(128)} %bitcast.1.z_ref.refs_0_.refs_1_, s32[64]{0:T(128)S(1)} %broadcast_add_fusion.refs_1_.refs_2_, bf16[1024,512]{1,0:T(8,128)(2,1)S(1)} %copy-done.1, f32[1024,512]{1,0:T(8,128)S(1)} %copy-done.5, f32[1024,128]{1,0:T(8,128)S(1)} %copy-done.7, ...), custom_call_target="tpu_custom_call" | custom-call | flops 12000000000 | bytes 4194304 | tf_op jit(solution)/shard_map/more_part/pallas_call | solution.py:173
  226.7 1.3 copy-done.2
  228.1 1.6 copy-done.3
  229.6 2.8 %final_part.1 = (bf16[256,512]{1,0:T(8,128)(2,1)S(1)}, bf16[256,512]{1,0:T(8,128)(2,1)S(1)}, bf16[256,512]{1,0:T(8,128)(2,1)S(1)}, bf16[256,512]{1,0:T(8,128)(2,1)S(1)}) custom-call(s32[1]{0:T(128)} %bitcast.refs_0_, s32[1]{0:T(128)} %bitcast.1.z_ref.refs_0_.refs_1_, s32[64]{0:T(128)S(1)} %broadcast_add_fusion.refs_1_.refs_2_, ...), custom_call_target="tpu_custom_call" | custom-call | flops 6000000000 | bytes 4194304 | tf_op jit(solution)/shard_map/final_part/pallas_call | solution.py:190
  232.4 4.2 %collective-permute-start.21 = (bf16[256,512]{1,0:T(8,128)(2,1)S(1)}, bf16[256,512]{1,0:T(8,128)(2,1)S(1)}, u32[]{:S(2)}, u32[]{:S(2)}) collective-permute-start(bf16[256,512]{1,0:T(8,128)(2,1)S(1)} %get-tuple-element.69), channel_id=1, source_target_pairs={{0,1},{1,0},{2,3},{3,2},{4,5},{5,4},{6,7},{7,6},{8,9},{9,8},{10,11... | collective-permute-start | bytes 786440 | tf_op jit(solution)/shard_map/ppermute | solution.py:414
  237.0 1.3 collective-permute-start.20
  238.3 4.6 %project.2.refs_6_ = f32[256,4096]{1,0:T(8,128)S(1)} custom-call(bf16[256,512]{1,0:T(8,128)(2,1)S(1)} %get-tuple-element.68.refs_0_, bf16[256,512]{1,0:T(8,128)(2,1)S(1)} %collective-permute-done.21.refs_1_, bf16[256,4096]{1,0:T(8,128)(2,1)} %get-tuple-element.74.refs_2_, bf16[256,4096]{1,0:T(8,128)(2,1)} %get-tuple-element.73.refs_3_, ...), custom_call_target="tpu_custom_call" | custom-call | flops 6000000000 | bytes 4194304 | tf_op jit(solution)/shard_map/project/pallas_call | solution.py:273
  242.9 1.6 collective-permute-done.19.refs_0_
  244.5 5.8 %collective-permute-done.20.refs_1_ = bf16[256,512]{1,0:T(8,128)(2,1)S(1)} collective-permute-done((bf16[256,512]{1,0:T(8,128)(2,1)S(1)}, bf16[256,512]{1,0:T(8,128)(2,1)S(1)}, u32[]{:S(2)}, u32[]{:S(2)}) %collective-permute-start.20) | collective-permute-done | bytes 262176 | tf_op jit(solution)/shard_map/ppermute | solution.py:413
  250.3 5.8 %project.3 = bf16[256,4096]{1,0:T(8,128)(2,1)} custom-call(bf16[256,512]{1,0:T(8,128)(2,1)S(1)} %collective-permute-done.19.refs_0_, bf16[256,512]{1,0:T(8,128)(2,1)S(1)} %collective-permute-done.20.refs_1_, bf16[256,4096]{1,0:T(8,128)(2,1)} %collective-permute-done.2.refs_2_, bf16[256,4096]{1,0:T(8,128)(2,1)} %collective-permute-done.3.refs_3_, ...), custom_call_target="tpu_custom_call" | custom-call | flops 6000000000 | bytes 4194304 | tf_op jit(solution)/shard_map/project/pallas_call | solution.py:273
  (57 shorter events, 4.8 us)
Async XLA Ops:
  4.7 64.1 %collective-permute-start.2 = (bf16[256,4096]{1,0:T(8,128)(2,1)}, bf16[256,4096]{1,0:T(8,128)(2,1)}, u32[]{:S(2)}, u32[]{:S(2)}) collective-permute-start(bf16[256,4096]{1,0:T(8,128)(2,1)} %get-tuple-element.74.refs_2_), channel_id=1, source_target_pairs={{0,2},{2,32},{32,34},{34,0},{1,3},{3,33},{33,35},{35,1},{4,6},{6,3... | collective-permute-start | bytes 6291464 | tf_op jit(solution)/shard_map/ppermute | solution.py:347
  6.7 12.3 %copy-start.8 = (s32[16,2]{0,1:T(2,128)S(1)}, s32[16,2]{0,1:T(2,128)}, u32[]{:S(2)}) copy-start(s32[16,2]{0,1:T(2,128)} %param.6) | copy-start | bytes 388
  6.7 62.0 %collective-permute-start.3 = (bf16[256,4096]{1,0:T(8,128)(2,1)}, bf16[256,4096]{1,0:T(8,128)(2,1)}, u32[]{:S(2)}, u32[]{:S(2)}) collective-permute-start(bf16[256,4096]{1,0:T(8,128)(2,1)} %get-tuple-element.73.refs_3_), channel_id=1, source_target_pairs={{0,34},{2,0},{32,2},{34,32},{1,35},{3,1},{33,3},{35,33},{4,38},{6,... | collective-permute-start | bytes 6291464 | tf_op jit(solution)/shard_map/ppermute | solution.py:348
  11.2 57.5 %collective-permute-start = (bf16[16,64,1024]{2,1,0:T(8,128)(2,1)S(1)}, bf16[16,64,1024]{2,1,0:T(8,128)(2,1)}, u32[]{:S(2)}, u32[]{:S(2)}) collective-permute-start(bf16[16,64,1024]{2,1,0:T(8,128)(2,1)S(1)} %reshape.121.refs_0_), channel_id=1, source_target_pairs={{0,4},{4,8},{8,12},{12,16},{16,20},{20,24},{24,28},{28,0},{1,5},{5... | collective-permute-start | bytes 6291464 | tf_op jit(solution)/shard_map/ppermute | solution.py:290
  13.2 55.6 %collective-permute-start.1 = (bf16[16,64,1024]{2,1,0:T(8,128)(2,1)S(1)}, bf16[16,64,1024]{2,1,0:T(8,128)(2,1)}, u32[]{:S(2)}, u32[]{:S(2)}) collective-permute-start(bf16[16,64,1024]{2,1,0:T(8,128)(2,1)S(1)} %reshape.121.refs_0_), channel_id=1, source_target_pairs={{0,28},{4,0},{8,4},{12,8},{16,12},{20,16},{24,20},{28,24},{1,29},{... | collective-permute-start | bytes 6291464 | tf_op jit(solution)/shard_map/ppermute | solution.py:290
  18.3 50.4 %collective-permute-start.4 = (bf16[64,1024]{1,0:T(8,128)(2,1)S(1)}, bf16[64,1024]{1,0:T(8,128)(2,1)S(1)}, u32[]{:S(2)}, u32[]{:S(2)}) collective-permute-start(bf16[64,1024]{1,0:T(8,128)(2,1)S(1)} %bitcast.30), channel_id=1, source_target_pairs={{28,32},{60,64},{92,96},{124,128},{156,160},{188,192},{220,224},{3... | collective-permute-start | bytes 393224 | tf_op jit(solution)/shard_map/ppermute | solution.py:351
  68.8 51.3 %collective-permute-start.7 = (bf16[512,4096]{1,0:T(8,128)(2,1)}, bf16[512,4096]{1,0:T(8,128)(2,1)}, u32[]{:S(2)}, u32[]{:S(2)}) collective-permute-start(bf16[512,4096]{1,0:T(8,128)(2,1)} %param.7), channel_id=1, source_target_pairs={{0,1},{1,0},{2,3},{3,2},{4,5},{5,4},{6,7},{7,6},{8,9},{9,8},{10,11... | collective-permute-start | bytes 12582920 | tf_op jit(solution)/shard_map/ppermute | solution.py:364
  71.1 48.9 %collective-permute-start.5 = (bf16[16,64,1024]{2,1,0:T(8,128)(2,1)}, bf16[16,64,1024]{2,1,0:T(8,128)(2,1)}, u32[]{:S(2)}, u32[]{:S(2)}) collective-permute-start(bf16[16,64,1024]{2,1,0:T(8,128)(2,1)} %collective-permute-done.refs_1_), channel_id=1, source_target_pairs={{0,4},{4,8},{8,12},{12,16},{16,20},{20,24},{24,28},{28,0},{1,5},{5... | collective-permute-start | bytes 6291464 | tf_op jit(solution)/shard_map/ppermute | solution.py:290
  72.5 47.5 %collective-permute-start.6 = (bf16[16,64,1024]{2,1,0:T(8,128)(2,1)}, bf16[16,64,1024]{2,1,0:T(8,128)(2,1)}, u32[]{:S(2)}, u32[]{:S(2)}) collective-permute-start(bf16[16,64,1024]{2,1,0:T(8,128)(2,1)} %collective-permute-done.1.refs_2_), channel_id=1, source_target_pairs={{0,28},{4,0},{8,4},{12,8},{16,12},{20,16},{24,20},{28,24},{1,29},{... | collective-permute-start | bytes 6291464 | tf_op jit(solution)/shard_map/ppermute | solution.py:290
  73.9 46.1 %collective-permute-start.8 = (bf16[256,4096]{1,0:T(8,128)(2,1)}, bf16[256,4096]{1,0:T(8,128)(2,1)}, u32[]{:S(2)}, u32[]{:S(2)}) collective-permute-start(bf16[256,4096]{1,0:T(8,128)(2,1)} %collective-permute-done.2.refs_2_), channel_id=1, source_target_pairs={{0,1},{1,0},{2,3},{3,2},{4,5},{5,4},{6,7},{7,6},{8,9},{9,8},{10,11... | collective-permute-start | bytes 6291464 | tf_op jit(solution)/shard_map/ppermute | solution.py:364
  74.5 45.6 %collective-permute-start.9 = (bf16[256,4096]{1,0:T(8,128)(2,1)}, bf16[256,4096]{1,0:T(8,128)(2,1)}, u32[]{:S(2)}, u32[]{:S(2)}) collective-permute-start(bf16[256,4096]{1,0:T(8,128)(2,1)} %collective-permute-done.3.refs_3_), channel_id=1, source_target_pairs={{0,1},{1,0},{2,3},{3,2},{4,5},{5,4},{6,7},{7,6},{8,9},{9,8},{10,11... | collective-permute-start | bytes 6291464 | tf_op jit(solution)/shard_map/ppermute | solution.py:364
  84.9 55.1 %all-to-all-start.1 = ((bf16[8,4,64,1024]{3,2,1,0:T(8,128)(2,1)}), bf16[8,4,64,1024]{3,2,1,0:T(8,128)(2,1)}, u32[]{:S(2)}, u32[]{:S(2)}) async-start(bf16[8,4,64,1024]{3,2,1,0:T(8,128)(2,1)} %pick.3), calls=%async_computation.1 | async-start | bytes 8388608 | tf_op jit(solution)/shard_map/all_to_all | solution.py:294
  140.0 14.6 %copy-start.9 = (bf16[4,64,1024]{2,1,0:T(8,128)(2,1)S(1)}, bf16[4,64,1024]{2,1,0:T(8,128)(2,1)}, u32[]{:S(2)}) copy-start(bf16[4,64,1024]{2,1,0:T(8,128)(2,1)} %get-tuple-element.55) | copy-start | bytes 1572868
  140.0 31.6 %all-to-all-start.2 = ((bf16[8,2,64,1024]{3,2,1,0:T(8,128)(2,1)}), bf16[8,2,64,1024]{3,2,1,0:T(8,128)(2,1)}, u32[]{:S(2)}, u32[]{:S(2)}) async-start(bf16[8,2,64,1024]{3,2,1,0:T(8,128)(2,1)} %get-tuple-element.53), calls=%async_computation.2 | async-start | bytes 4194304 | tf_op jit(solution)/shard_map/all_to_all | solution.py:294
  145.5 6.7 %collective-permute-start.10 = (bf16[64,1024]{1,0:T(8,128)(2,1)S(1)}, bf16[64,1024]{1,0:T(8,128)(2,1)S(1)}, u32[]{:S(2)}, u32[]{:S(2)}) collective-permute-start(bf16[64,1024]{1,0:T(8,128)(2,1)S(1)} %select_bitcast_fusion), channel_id=1, source_target_pairs={{0,16},{28,12},{1,17},{29,13},{2,18},{30,14},{3,19},{31,15},{32,48... | collective-permute-start | bytes 393224 | tf_op jit(solution)/shard_map/ppermute | solution.py:384
  153.2 4.1 %collective-permute-start.11 = (bf16[64,1024]{1,0:T(8,128)(2,1)S(1)}, bf16[64,1024]{1,0:T(8,128)(2,1)S(1)}, u32[]{:S(2)}, u32[]{:S(2)}) collective-permute-start(bf16[64,1024]{1,0:T(8,128)(2,1)S(1)} %broadcast_select_fusion.1), channel_id=1, source_target_pairs={{0,8},{16,24},{28,20},{12,4},{1,9},{17,25},{29,21},{13,5},{2,10},{... | collective-permute-start | bytes 393224 | tf_op jit(solution)/shard_map/ppermute | solution.py:390
  154.6 15.1 %collective-permute-start.13 = (bf16[4,64,1024]{2,1,0:T(8,128)(2,1)}, bf16[4,64,1024]{2,1,0:T(8,128)(2,1)}, u32[]{:S(2)}, u32[]{:S(2)}) collective-permute-start(bf16[4,64,1024]{2,1,0:T(8,128)(2,1)} %get-tuple-element.54), channel_id=1, source_target_pairs={{0,4},{4,8},{8,12},{12,16},{16,20},{20,24},{24,28},{28,0},{1,5},{5... | collective-permute-start | bytes 1572872 | tf_op jit(solution)/shard_map/ppermute | solution.py:290
  154.7 15.0 %collective-permute-start.14 = (bf16[4,64,1024]{2,1,0:T(8,128)(2,1)S(1)}, bf16[4,64,1024]{2,1,0:T(8,128)(2,1)}, u32[]{:S(2)}, u32[]{:S(2)}) collective-permute-start(bf16[4,64,1024]{2,1,0:T(8,128)(2,1)S(1)} %copy-done.9), channel_id=1, source_target_pairs={{0,28},{4,0},{8,4},{12,8},{16,12},{20,16},{24,20},{28,24},{1,29},{... | collective-permute-start | bytes 1572872 | tf_op jit(solution)/shard_map/ppermute | solution.py:290
  157.3 12.3 %collective-permute-start.12 = (bf16[64,1024]{1,0:T(8,128)(2,1)S(1)}, bf16[64,1024]{1,0:T(8,128)(2,1)S(1)}, u32[]{:S(2)}, u32[]{:S(2)}) collective-permute-start(bf16[64,1024]{1,0:T(8,128)(2,1)S(1)} %broadcast_select_fusion.2), channel_id=1, source_target_pairs={{0,4},{4,0},{8,12},{12,8},{16,20},{20,16},{24,28},{28,24},{1,5},{5... | collective-permute-start | bytes 393224 | tf_op jit(solution)/shard_map/ppermute | solution.py:393
  171.6 34.4 %collective-permute-start.17 = (bf16[4,64,1024]{2,1,0:T(8,128)(2,1)}, bf16[4,64,1024]{2,1,0:T(8,128)(2,1)S(1)}, u32[]{:S(2)}, u32[]{:S(2)}) collective-permute-start(bf16[4,64,1024]{2,1,0:T(8,128)(2,1)} %collective-permute-done.13), channel_id=1, source_target_pairs={{0,4},{4,8},{8,12},{12,16},{16,20},{20,24},{24,28},{28,0},{1,5},{5... | collective-permute-start | bytes 1572872 | tf_op jit(solution)/shard_map/ppermute | solution.py:290
  172.1 33.8 %collective-permute-start.18 = (bf16[4,64,1024]{2,1,0:T(8,128)(2,1)}, bf16[4,64,1024]{2,1,0:T(8,128)(2,1)}, u32[]{:S(2)}, u32[]{:S(2)}) collective-permute-start(bf16[4,64,1024]{2,1,0:T(8,128)(2,1)} %collective-permute-done.14), channel_id=1, source_target_pairs={{0,28},{4,0},{8,4},{12,8},{16,12},{20,16},{24,20},{28,24},{1,29},{... | collective-permute-start | bytes 1572872 | tf_op jit(solution)/shard_map/ppermute | solution.py:290
  174.3 33.9 %all-to-all-start.3 = ((bf16[8,2,64,1024]{3,2,1,0:T(8,128)(2,1)}), bf16[8,2,64,1024]{3,2,1,0:T(8,128)(2,1)}, u32[]{:S(2)}, u32[]{:S(2)}) async-start(bf16[8,2,64,1024]{3,2,1,0:T(8,128)(2,1)} %get-tuple-element.59), calls=%async_computation.3 | async-start | bytes 4194304 | tf_op jit(solution)/shard_map/all_to_all | solution.py:294
  178.7 7.0 %copy-start = (bf16[1024,512]{1,0:T(8,128)(2,1)S(1)}, bf16[1024,512]{1,0:T(8,128)(2,1)}, u32[]{:S(2)}) copy-start(bf16[1024,512]{1,0:T(8,128)(2,1)} %refs_3_.3) | copy-start | bytes 3145732
  182.0 32.0 %collective-permute-start.16 = (bf16[8,64,1024]{2,1,0:T(8,128)(2,1)}, bf16[8,64,1024]{2,1,0:T(8,128)(2,1)}, u32[]{:S(2)}, u32[]{:S(2)}) collective-permute-start(bf16[8,64,1024]{2,1,0:T(8,128)(2,1)} %get-tuple-element.75), channel_id=1, source_target_pairs={{0,28},{4,0},{8,4},{12,8},{16,12},{20,16},{24,20},{28,24},{1,29},{... | collective-permute-start | bytes 3145736 | tf_op jit(solution)/shard_map/ppermute | solution.py:290
  183.1 30.9 %collective-permute-start.15 = (bf16[8,64,1024]{2,1,0:T(8,128)(2,1)}, bf16[8,64,1024]{2,1,0:T(8,128)(2,1)}, u32[]{:S(2)}, u32[]{:S(2)}) collective-permute-start(bf16[8,64,1024]{2,1,0:T(8,128)(2,1)} %get-tuple-element.76), channel_id=1, source_target_pairs={{0,4},{4,8},{8,12},{12,16},{16,20},{20,24},{24,28},{28,0},{1,5},{5... | collective-permute-start | bytes 3145736 | tf_op jit(solution)/shard_map/ppermute | solution.py:290
  203.8 1.3 copy-start.4
  205.1 0.8 copy-start.6
  205.9 8.1 %copy-start.1 = (bf16[1024,512]{1,0:T(8,128)(2,1)S(1)}, bf16[1024,512]{1,0:T(8,128)(2,1)}, u32[]{:S(2)}) copy-start(bf16[1024,512]{1,0:T(8,128)(2,1)} %refs_3_.3) | copy-start | bytes 3145732
  205.9 8.1 %copy-start.7 = (f32[1024,128]{1,0:T(8,128)S(1)}, f32[1024,128]{1,0:T(8,128)}, u32[]{:S(2)}) copy-start(f32[1024,128]{1,0:T(8,128)} %copy-done.6) | copy-start | bytes 1572868
  208.2 19.9 %all-to-all-start.4 = ((bf16[8,64,1024]{2,1,0:T(8,128)(2,1)}), bf16[8,64,1024]{2,1,0:T(8,128)(2,1)S(1)}, u32[]{:S(2)}, u32[]{:S(2)}) async-start(bf16[8,64,1024]{2,1,0:T(8,128)(2,1)} %pad_maximum_fusion.1), calls=%async_computation.4 | async-start | bytes 2097152 | tf_op jit(solution)/shard_map/all_to_all | solution.py:294
  214.0 1.6 copy-start.5
  226.7 1.3 copy-start.2
  228.0 1.6 copy-start.3
  232.4 5.9 %collective-permute-start.21 = (bf16[256,512]{1,0:T(8,128)(2,1)S(1)}, bf16[256,512]{1,0:T(8,128)(2,1)S(1)}, u32[]{:S(2)}, u32[]{:S(2)}) collective-permute-start(bf16[256,512]{1,0:T(8,128)(2,1)S(1)} %get-tuple-element.69), channel_id=1, source_target_pairs={{0,1},{1,0},{2,3},{3,2},{4,5},{5,4},{6,7},{7,6},{8,9},{9,8},{10,11... | collective-permute-start | bytes 786440 | tf_op jit(solution)/shard_map/ppermute | solution.py:414
  236.6 7.9 %collective-permute-start.19 = (bf16[256,512]{1,0:T(8,128)(2,1)S(1)}, bf16[256,512]{1,0:T(8,128)(2,1)S(1)}, u32[]{:S(2)}, u32[]{:S(2)}) collective-permute-start(bf16[256,512]{1,0:T(8,128)(2,1)S(1)} %get-tuple-element.64), channel_id=1, source_target_pairs={{0,2},{1,3},{2,0},{3,1},{4,6},{5,7},{6,4},{7,5},{8,10},{9,11},{10,... | collective-permute-start | bytes 786440 | tf_op jit(solution)/shard_map/ppermute | solution.py:413
  237.0 13.2 %collective-permute-start.20 = (bf16[256,512]{1,0:T(8,128)(2,1)S(1)}, bf16[256,512]{1,0:T(8,128)(2,1)S(1)}, u32[]{:S(2)}, u32[]{:S(2)}) collective-permute-start(bf16[256,512]{1,0:T(8,128)(2,1)S(1)} %get-tuple-element.65), channel_id=1, source_target_pairs={{0,3},{1,2},{2,1},{3,0},{4,7},{5,6},{6,5},{7,4},{8,11},{9,10},{10,... | collective-permute-start | bytes 786440 | tf_op jit(solution)/shard_map/ppermute | solution.py:413

commit v7 on v6

--- a/solution.py
+++ b/solution.py
@@ -205,11 +205,8 @@
         held, in_sems, out_sems = refs[-3:]
         loads, stores = [], []
         for n, (o, position, s, lane, plane, owner) in enumerate(plan):
-            if lane is None:
-                block = jnp.where(z_ref[0] == 0, 0, sources[s].shape[0] - 1)
-            else:
-                row = lane * NZ + lax.rem(z_ref[0] + (plane + NZ), NZ)
-                block = asked_ref[row, lax.rem(z_ref[0] + (owner + NZ), NZ)]
+            row = lane * NZ + lax.rem(z_ref[0] + (plane + NZ), NZ)
+            block = asked_ref[row, lax.rem(z_ref[0] + (owner + NZ), NZ)]
             loads.append(pltpu.make_async_copy(src[s].at[block], held.at[n], in_sems.at[n]))
             stores.append(pltpu.make_async_copy(held.at[n], out[o].at[position], out_sems.at[n]))
             loads[-1].start()
@@ -294,6 +291,24 @@
     return lax.all_to_all(x, LANE, split_axis=0, concat_axis=0, tiled=True)
 
 
+def spread_lanes(edge, z):
+    lane = lax.axis_index(LANE)
+    steps = ([(0, 4)], [(0, 2), (4, 6)], [(0, 1), (2, 3), (4, 5), (6, 7)])
+    held = edge
+    for pairs in steps:
+        other = [(LANES - 1 - a, LANES - 1 - b) for a, b in pairs]
+        moves = [(a * NZ, b * NZ) for a, b in pairs]
+        moves += [(a * NZ + NZ - 1, b * NZ + NZ - 1) for a, b in other]
+        got = lax.ppermute(held, SEQ, moves)
+        low = reduce(jnp.logical_or, [lane == b for _, b in pairs])
+        high = reduce(jnp.logical_or, [lane == b for _, b in other])
+        fresh = jnp.logical_or(
+            jnp.logical_and(z == 0, low), jnp.logical_and(z == NZ - 1, high)
+        )
+        held = jnp.where(fresh, got, held)
+    return held
+
+
 def wanted_blocks(rand_blocks, block_ids, all_blocks, blocks_dev):
     taken = [
         block_ids - 1,
@@ -341,32 +356,29 @@
     offset, where = wanted_blocks(rand_blocks, block_ids, all_blocks, blocks_dev)
     asked = jnp.broadcast_to(offset.reshape(LANES, 1, NZ), (LANES, NZ, NZ)).reshape(-1, NZ)
     asked = lax.all_to_all(asked, SEQ, split_axis=0, concat_axis=0, tiled=True)
+    edge = jnp.where(z == 0, kv[0], kv[blocks_dev - 1])
+    held = spread_lanes(edge, z)
+    w_first, held = tie(w_out, held)
     rows = w_out.shape[0] // 2
-    own = [w_out[:rows], w_out[rows:]]
+    own = [w_first[:rows], w_first[rows:]]
     ring = NXH * NXL
     low = lax.ppermute(own[0], XRING, [(i, (i + 1) % ring) for i in range(ring)])
     high = lax.ppermute(own[1], XRING, [(i, (i - 1) % ring) for i in range(ring)])
-    edge = jnp.where(z == 0, kv[0], kv[blocks_dev - 1])
     turns = [(NZ * i + NZ - 1, NZ * i + NZ) for i in range(LANES - 1)]
     crossed = lax.ppermute(edge, SEQ, turns + [(b, a) for a, b in turns])
-    up1, down1, asked, low, high, crossed, w_core = tie(
-        up1, down1, asked, low, high, crossed, w_out
-    )
+    up1, down1, asked, crossed = tie(up1, down1, asked, crossed)
 
     up2, down2 = z_shift(up1, 1), z_shift(down1, -1)
     plan = [(0, (lane, 0), 0, lane, 0, 0) for lane in lanes]
     plan += [(0, (lane, 1), 1, lane, 0, -1) for lane in lanes]
     plan += [(0, (lane, 2), 2, lane, 0, 1) for lane in lanes]
-    plan += [(0, (lane, 3), 0, None, 0, 0) for lane in lanes]
-    (c1,) = pick(zs, asked, [kv, up1, down1], plan, [(LANES, 4)])
+    (c1,) = pick(zs, asked, [kv, up1, down1], plan, [(LANES, 3)])
+    c1, crossed, kv_late = tie(c1, crossed, kv)
     r1 = lane_exchange(c1)
-    swap = [(0, 1), (1, 0)]
-    others = [lax.ppermute(x, "core", swap) for x in (w_core, low, high)]
     before = jnp.where(z == 0, crossed, up1[blocks_dev - 1])
     after = jnp.where(z == NZ - 1, crossed, down1[0])
-    kv_pad = jnp.concatenate([before, kv.reshape(tok, 2 * feat), after], axis=0)
-    up2, down2, kv_pad, *others = tie(up2, down2, kv_pad, *others)
-    weights = own + [others[0], low, high] + others[1:]
+    kv_pad = jnp.concatenate([before, kv_late.reshape(tok, 2 * feat), after], axis=0)
+    up2, down2, kv_pad, w_core, low, high = tie(up2, down2, kv_pad, w_out, low, high)
 
     plan = [(0, (lane, 0), 0, lane, 1, -2) for lane in lanes]
     plan += [(0, (lane, 1), 1, lane, -1, 2) for lane in lanes]
@@ -380,9 +392,10 @@
     c3, r1 = tie(c3, r1)
     fu, fd = z_shift(fu, 1), z_shift(fd, -1)
     c3 = lane_exchange(c3)
-    held = jnp.where(z == 0, r1[0, 3], r1[LANES - 1, 3])
     got = lax.ppermute(held, "z", [(0, 4), (7, 3)])
     held = jnp.where(jnp.logical_or(z == 4, z == 3), got, held)
+    swap = [(0, 1), (1, 0)]
+    others = [lax.ppermute(x, "core", swap) for x in (w_core, low, high)]
     c2, c3, fu, fd = tie(c2, c3, fu, fd)
     r2 = lane_exchange(c2)
     fu, fd = z_shift(fu, 1), z_shift(fd, -1)
@@ -394,7 +407,8 @@
     even = z % 2 == 0
     ends = jnp.concatenate([jnp.where(even, held, got), jnp.where(even, got, held)], axis=0)
     far = jnp.concatenate([fu, fd], axis=0)
-    far, r2 = tie(far, r2)
+    far, r2, *others = tie(far, r2, *others)
+    weights = own + [others[0], low, high] + others[1:]
     r4 = lane_exchange(far)
 
     def slots(x):

time: 260 us -> 260 us (level)
  blocking collectives: 49.1 us -> 0 us
  starting transfers between devices: 59.4 us -> 92.1 us
  waiting for transfers between devices: 60.8 us -> 80.1 us
  other arithmetic: 8.33 us -> 5.25 us
    all_to_all x1 -> x0, blocking collectives: 49.1 us -> none  [body(): asked = lax.all_to_all(asked, SEQ, split_axis=0, concat_axis=0, tiled=True)]
    all_to_all x0 -> x1, waiting for transfers between devices: none -> 18.8 us  [body(): asked = lax.all_to_all(asked, SEQ, split_axis=0, concat_axis=0, tiled=True)]
    ppermute x0 -> x3, starting transfers between devices: none -> 12.4 us  [spread_lanes(): got = lax.ppermute(held, SEQ, moves)]
    ppermute x1, waiting for transfers between devices: 0.01 us -> 11.6 us  [body(): lax.ppermute(own[0], XRING, [(i, (i + 1) % ring) for i in range(ring)])]
    ppermute x1, waiting for transfers between devices: 8.95 us -> 0.01 us  [body(): got = lax.ppermute(held, 'z', [(i, i ^ 1) for i in range(NZ)])]
    ppermute x3, starting transfers between devices: 2.91 us -> 10.5 us  [body(): others = [lax.ppermute(x, 'core', swap) for x in (w_core, low, high)]]
    all_to_all x0 -> x1, starting transfers between devices: none -> 7.52 us  [body(): asked = lax.all_to_all(asked, SEQ, split_axis=0, concat_axis=0, tiled=True)]
    all_to_all x4, waiting for transfers between devices: 14.8 us -> 8.18 us  [lane_exchange(): return lax.all_to_all(x, LANE, split_axis=0, concat_axis=0, tiled=True)]
  transfers between devices with their start and end apart: 26 -> 30, of which waited for: 7 -> 12; matrix products, arithmetic and copies ran while one was open for 7% -> 6% of each run, Pallas kernels for 19% -> 18%
where the time goes in v7:
time: 260 us; the launch traced here: 256 us
  starting transfers between devices  92.1 us (35%)
  waiting for transfers between devices  80.1 us (31%)
  Pallas kernels  54 us (21%)
  local copies, waits for them, and re-layouts  24.2 us (9%)
  other arithmetic  5.25 us (2%)
    ppermute x10, waiting for transfers between devices, z_shift(): return lax.ppermute(x, 'z', [(i, (i + by) % NZ) for i in range(NZ)])  27.6 us
    all_to_all x4, starting transfers between devices, lane_exchange(): return lax.all_to_all(x, LANE, split_axis=0, concat_axis=0, tiled=True)  22.2 us
    ppermute x10, starting transfers between devices, z_shift(): return lax.ppermute(x, 'z', [(i, (i + by) % NZ) for i in range(NZ)])  19.3 us
    all_to_all x1, waiting for transfers between devices, body(): asked = lax.all_to_all(asked, SEQ, split_axis=0, concat_axis=0, tiled=True)  18.8 us
    pallas_call x1, Pallas kernels, local_part(): pl.pallas_call(lambda *refs: local_kernel(all_blocks, deltas, *refs), out...  18.2 us
    pallas_call x2, Pallas kernels, pick(): pl.pallas_call(kernel, out_shape=tuple((pltpu.HBM(shape + block_shape, BF...  12.8 us
    ppermute x3, starting transfers between devices, spread_lanes(): got = lax.ppermute(held, SEQ, moves)  12.4 us
    unnamed x32, local copies, waits for them, and re-layouts  12 us
  transfers between devices with their start and end apart: 30, of which 12 were waited for; matrix products, arithmetic and copies ran while one was open for 6% of the time, Pallas kernels for 18%

profile of v7, /device:TPU:1, one launch (start us, length us, event | category | flops | bytes accessed | tf_op | source)
XLA Modules:
  0.0 256.3 jit_solution(2531659733877270793)
XLA Ops:
  0.0 3.2 %reshape.122.refs_0_ = bf16[16,64,1024]{2,1,0:T(8,128)(2,1)S(1)} reshape(bf16[1024,2,512]{2,1,0:T(2,128)(2,1)} %param.5) | data formatting | bytes 4194304 | tf_op jit(solution)/shard_map/reshape | solution.py:352
  3.3 2.5 collective-permute-start
  5.8 4.0 %collective-permute-start.1 = (bf16[16,64,1024]{2,1,0:T(8,128)(2,1)S(1)}, bf16[16,64,1024]{2,1,0:T(8,128)(2,1)}, u32[]{:S(2)}, u32[]{:S(2)}) collective-permute-start(bf16[16,64,1024]{2,1,0:T(8,128)(2,1)S(1)} %reshape.122.refs_0_), channel_id=1, source_target_pairs={{0,28},{4,0},{8,4},{12,8},{16,12},{20,16},{24,20},{28,24},{1,29},{... | collective-permute-start | bytes 6291464 | tf_op jit(solution)/shard_map/ppermute | solution.py:287
  11.6 9.8 %collective-permute-start.5 = (bf16[64,1024]{1,0:T(8,128)(2,1)S(1)}, bf16[64,1024]{1,0:T(8,128)(2,1)S(1)}, u32[]{:S(2)}, u32[]{:S(2)}) collective-permute-start(bf16[64,1024]{1,0:T(8,128)(2,1)S(1)} %bitcast.24), channel_id=1, source_target_pairs={{0,128},{252,124},{1,129},{253,125},{2,130},{254,126},{3,131},{255... | collective-permute-start | bytes 393224 | tf_op jit(solution)/shard_map/ppermute | solution.py:302
  21.7 1.7 collective-permute-done.5
  23.4 1.3 collective-permute-start.6
  24.7 2.0 collective-permute-done.6
  26.7 1.3 collective-permute-start.7
  29.0 7.5 %all-to-all-start = ((s32[64,1,8]{2,1,0:T(1,128)}), s32[64,1,8]{2,1,0:T(1,128)S(1)}, u32[]{:S(2)}, u32[]{:S(2)}) async-start(s32[64,1,8]{2,1,0:T(1,128)} %bitcast.3), calls=%async_computation | async-start | bytes 65536 | tf_op jit(solution)/shard_map/all_to_all | solution.py:358
  36.7 4.7 %fusion.4 = (bf16[256,4096]{1,0:T(8,128)(2,1)}, bf16[256,4096]{1,0:T(8,128)(2,1)}) fusion(bf16[512,4096]{1,0:T(8,128)(2,1)} %param.7), kind=kLoop, calls=%fused_computation.36 | loop fusion | bytes 8388608 | tf_op jit(solution)/shard_map/slice | solution.py:363
  42.6 1.9 collective-permute-start.9
  44.5 18.8 %all-to-all-done = s32[64,1,8]{2,1,0:T(1,128)S(1)} async-done(((s32[64,1,8]{2,1,0:T(1,128)}), s32[64,1,8]{2,1,0:T(1,128)S(1)}, u32[]{:S(2)}, u32[]{:S(2)}) %all-to-all-start) | async-done | bytes 2080 | tf_op jit(solution)/shard_map/all_to_all | solution.py:358
  63.3 1.3 collective-permute-start.3
  64.6 1.5 collective-permute-start.4
  66.1 6.0 %pick.2 = bf16[8,3,64,1024]{3,2,1,0:T(8,128)(2,1)} custom-call(s32[1]{0:T(128)} %bitcast.1.z_ref.refs_0_.refs_1_, s32[64,8]{1,0:T(8,128)S(1)} %bitcast.21, bf16[16,64,1024]{2,1,0:T(8,128)(2,1)S(1)} %reshape.122.refs_0_, bf16[16,64,1024]{2,1,0:T(8,128)(2,1)} %collective-permute-done.refs_1_, bf16[16,64,1024]{2,1,0:T(8,128)(2,1)} %collective-permute-done.1.refs_2_), custom_call_target="tpu_custom_call" | custom-call | flops 3000000000 | bytes 4194304 | tf_op jit(solution)/shard_map/pick/pallas_call | solution.py:220
  72.1 4.5 %all-to-all-start.1 = ((bf16[8,3,64,1024]{3,2,1,0:T(8,128)(2,1)}), bf16[8,3,64,1024]{3,2,1,0:T(8,128)(2,1)}, u32[]{:S(2)}, u32[]{:S(2)}) async-start(bf16[8,3,64,1024]{3,2,1,0:T(8,128)(2,1)} %pick.2), calls=%async_computation.1 | async-start | bytes 6291456 | tf_op jit(solution)/shard_map/all_to_all | solution.py:291
  77.6 1.7 pad_maximum_fusion.refs_4_
  79.3 11.6 %collective-permute-done.8.refs_2_ = bf16[256,4096]{1,0:T(8,128)(2,1)} collective-permute-done((bf16[256,4096]{1,0:T(8,128)(2,1)}, bf16[256,4096]{1,0:T(8,128)(2,1)}, u32[]{:S(2)}, u32[]{:S(2)}) %collective-permute-start.8) | collective-permute-done | bytes 2097184 | tf_op jit(solution)/shard_map/ppermute | solution.py:365
  90.9 19.7 %collective-permute-done.3.refs_0_ = bf16[16,64,1024]{2,1,0:T(8,128)(2,1)} collective-permute-done((bf16[16,64,1024]{2,1,0:T(8,128)(2,1)}, bf16[16,64,1024]{2,1,0:T(8,128)(2,1)}, u32[]{:S(2)}, u32[]{:S(2)}) %collective-permute-start.3) | collective-permute-done | bytes 2097184 | tf_op jit(solution)/shard_map/ppermute | solution.py:287
  110.5 6.8 %pick.3 = (bf16[8,2,64,1024]{3,2,1,0:T(8,128)(2,1)}, bf16[4,64,1024]{2,1,0:T(8,128)(2,1)}, bf16[4,64,1024]{2,1,0:T(8,128)(2,1)}, bf16[8,2,64,1024]{3,2,1,0:T(8,128)(2,1)}) custom-call(s32[1]{0:T(128)} %bitcast.1.z_ref.refs_0_.refs_1_, s32[64,8]{1,0:T(8,128)S(1)} %bitcast.22, bf16[16,64,1024]{2,1,0:T(8,128)(2,1)} %collective-permute-done.3.refs_0_, ...), custom_call_target="tpu_custom_call" | custom-call | flops 60000002048 | bytes 4194304 | tf_op jit(solution)/shard_map/pick/pallas_call | solution.py:220
  117.3 7.7 %all-to-all-done.1.refs_6_ = bf16[8,3,64,1024]{3,2,1,0:T(8,128)(2,1)} async-done(((bf16[8,3,64,1024]{3,2,1,0:T(8,128)(2,1)}), bf16[8,3,64,1024]{3,2,1,0:T(8,128)(2,1)}, u32[]{:S(2)}, u32[]{:S(2)}) %all-to-all-start.1) | async-done | bytes 3145760 | tf_op jit(solution)/shard_map/all_to_all | solution.py:291
  125.0 4.6 %all-to-all-start.2 = ((bf16[8,2,64,1024]{3,2,1,0:T(8,128)(2,1)}), bf16[8,2,64,1024]{3,2,1,0:T(8,128)(2,1)S(1)}, u32[]{:S(2)}, u32[]{:S(2)}) async-start(bf16[8,2,64,1024]{3,2,1,0:T(8,128)(2,1)} %get-tuple-element.60), calls=%async_computation.2 | async-start | bytes 4194304 | tf_op jit(solution)/shard_map/all_to_all | solution.py:291
  129.6 9.5 %collective-permute-start.19 = (bf16[512,4096]{1,0:T(8,128)(2,1)}, bf16[512,4096]{1,0:T(8,128)(2,1)}, u32[]{:S(2)}, u32[]{:S(2)}) collective-permute-start(bf16[512,4096]{1,0:T(8,128)(2,1)} %param.7), channel_id=1, source_target_pairs={{0,1},{1,0},{2,3},{3,2},{4,5},{5,4},{6,7},{7,6},{8,9},{9,8},{10,11... | collective-permute-start | bytes 12582920 | tf_op jit(solution)/shard_map/ppermute | solution.py:398
  139.1 4.2 %collective-permute-start.10 = (bf16[64,1024]{1,0:T(8,128)(2,1)S(1)}, bf16[64,1024]{1,0:T(8,128)(2,1)S(1)}, u32[]{:S(2)}, u32[]{:S(2)}) collective-permute-start(bf16[64,1024]{1,0:T(8,128)(2,1)S(1)} %broadcast_select_fusion.7), channel_id=1, source_target_pairs={{0,16},{28,12},{1,17},{29,13},{2,18},{30,14},{3,19},{31,15},{32,48... | collective-permute-start | bytes 393224 | tf_op jit(solution)/shard_map/ppermute | solution.py:395
  143.3 2.9 %collective-permute-done.10 = bf16[64,1024]{1,0:T(8,128)(2,1)S(1)} collective-permute-done((bf16[64,1024]{1,0:T(8,128)(2,1)S(1)}, bf16[64,1024]{1,0:T(8,128)(2,1)S(1)}, u32[]{:S(2)}, u32[]{:S(2)}) %collective-permute-start.10) | collective-permute-done | bytes 131104 | tf_op jit(solution)/shard_map/ppermute | solution.py:395
  146.3 1.3 collective-permute-start.11
  147.7 2.7 %collective-permute-start.14 = (bf16[4,64,1024]{2,1,0:T(8,128)(2,1)}, bf16[4,64,1024]{2,1,0:T(8,128)(2,1)}, u32[]{:S(2)}, u32[]{:S(2)}) collective-permute-start(bf16[4,64,1024]{2,1,0:T(8,128)(2,1)} %get-tuple-element.62), channel_id=1, source_target_pairs={{0,28},{4,0},{8,4},{12,8},{16,12},{20,16},{24,20},{28,24},{1,29},{... | collective-permute-start | bytes 1572872 | tf_op jit(solution)/shard_map/ppermute | solution.py:287
  150.4 4.2 %collective-permute-start.12 = (bf16[64,1024]{1,0:T(8,128)(2,1)S(1)}, bf16[64,1024]{1,0:T(8,128)(2,1)S(1)}, u32[]{:S(2)}, u32[]{:S(2)}) collective-permute-start(bf16[64,1024]{1,0:T(8,128)(2,1)S(1)} %broadcast_select_fusion.2), channel_id=1, source_target_pairs={{0,4},{4,0},{8,12},{12,8},{16,20},{20,16},{24,28},{28,24},{1,5},{5... | collective-permute-start | bytes 393224 | tf_op jit(solution)/shard_map/ppermute | solution.py:406
  154.5 7.2 %collective-permute-done.13 = bf16[4,64,1024]{2,1,0:T(8,128)(2,1)S(1)} collective-permute-done((bf16[4,64,1024]{2,1,0:T(8,128)(2,1)}, bf16[4,64,1024]{2,1,0:T(8,128)(2,1)S(1)}, u32[]{:S(2)}, u32[]{:S(2)}) %collective-permute-start.13) | collective-permute-done | bytes 524320 | tf_op jit(solution)/shard_map/ppermute | solution.py:287
  162.5 2.0 collective-permute-start.18
  164.5 2.6 collective-permute-start.17
  168.0 6.9 %all-to-all-start.3 = ((bf16[8,2,64,1024]{3,2,1,0:T(8,128)(2,1)}), bf16[8,2,64,1024]{3,2,1,0:T(8,128)(2,1)S(1)}, u32[]{:S(2)}, u32[]{:S(2)}) async-start(bf16[8,2,64,1024]{3,2,1,0:T(8,128)(2,1)} %get-tuple-element.66), calls=%async_computation.3 | async-start | bytes 4194304 | tf_op jit(solution)/shard_map/all_to_all | solution.py:291
  175.0 3.3 %slice_bitcast_fusion = (bf16[8,64,1024]{2,1,0:T(8,128)(2,1)}, bf16[8,64,1024]{2,1,0:T(8,128)(2,1)}) fusion(bf16[8,2,64,1024]{3,2,1,0:T(8,128)(2,1)} %copy-done.12), kind=kLoop, calls=%fused_computation.1 | loop fusion | bytes 4194304 | tf_op jit(solution)/shard_map/squeeze | solution.py:402
  179.0 1.3 collective-permute-start.15
  180.3 1.4 collective-permute-start.16
  181.7 18.2 %local_part.1 = (f32[1024,512]{1,0:T(8,128)S(1)}, f32[1024,128]{1,0:T(8,128)S(1)}) custom-call(s32[1]{0:T(128)} %bitcast.1.z_ref.refs_0_.refs_1_, s32[64]{0:T(128)S(1)} %broadcast_add_fusion.refs_1_.refs_2_, s32[1]{0:T(128)} %bitcast.2.refs_2_, bf16[1024,512]{1,0:T(8,128)(2,1)S(1)} %copy-done.1, bf16[1152,1024]{1,0:T(8,128)(2,1)S(1)} %copy-done, ...), custom_call_target="tpu_custom_call" | custom-call | flops 24999999488 | bytes 4194304 | tf_op jit(solution)/shard_map/local_part/pallas_call | solution.py:157
  202.8 6.3 %all-to-all-start.4 = ((bf16[8,64,1024]{2,1,0:T(8,128)(2,1)}), bf16[8,64,1024]{2,1,0:T(8,128)(2,1)S(1)}, u32[]{:S(2)}, u32[]{:S(2)}) async-start(bf16[8,64,1024]{2,1,0:T(8,128)(2,1)} %pad_maximum_fusion.1), calls=%async_computation.4 | async-start | bytes 2097152 | tf_op jit(solution)/shard_map/all_to_all | solution.py:291
  210.3 1.6 copy-done.9
  213.0 9.9 %more_part.1 = (f32[1024,512]{1,0:T(8,128)S(1)}, f32[1024,128]{1,0:T(8,128)S(1)}) custom-call(s32[1]{0:T(128)} %bitcast.1.z_ref.refs_0_.refs_1_, s32[64]{0:T(128)S(1)} %broadcast_add_fusion.refs_1_.refs_2_, bf16[1024,512]{1,0:T(8,128)(2,1)S(1)} %copy-done.2, f32[1024,512]{1,0:T(8,128)S(1)} %copy-done.9, f32[1024,128]{1,0:T(8,128)S(1)} %copy-done.11, ...), custom_call_target="tpu_custom_call" | custom-call | flops 12000000000 | bytes 4194304 | tf_op jit(solution)/shard_map/more_part/pallas_call | solution.py:173
  222.9 1.3 copy-done.4
  226.3 1.6 copy-done.5
  228.9 2.8 %final_part.1 = (bf16[256,512]{1,0:T(8,128)(2,1)S(1)}, bf16[256,512]{1,0:T(8,128)(2,1)S(1)}, bf16[256,512]{1,0:T(8,128)(2,1)S(1)}, bf16[256,512]{1,0:T(8,128)(2,1)S(1)}) custom-call(s32[1]{0:T(128)} %bitcast.refs_0_, s32[1]{0:T(128)} %bitcast.1.z_ref.refs_0_.refs_1_, s32[64]{0:T(128)S(1)} %broadcast_add_fusion.refs_1_.refs_2_, ...), custom_call_target="tpu_custom_call" | custom-call | flops 6000000000 | bytes 4194304 | tf_op jit(solution)/shard_map/final_part/pallas_call | solution.py:190
  231.6 2.3 collective-permute-start.24
  233.9 4.2 %collective-permute-start.22 = (bf16[256,512]{1,0:T(8,128)(2,1)S(1)}, bf16[256,512]{1,0:T(8,128)(2,1)S(1)}, u32[]{:S(2)}, u32[]{:S(2)}) collective-permute-start(bf16[256,512]{1,0:T(8,128)(2,1)S(1)} %get-tuple-element.74), channel_id=1, source_target_pairs={{0,2},{1,3},{2,0},{3,1},{4,6},{5,7},{6,4},{7,5},{8,10},{9,11},{10,... | collective-permute-start | bytes 786440 | tf_op jit(solution)/shard_map/ppermute | solution.py:427
  238.4 4.5 %project.2.refs_6_ = f32[256,4096]{1,0:T(8,128)S(1)} custom-call(bf16[256,512]{1,0:T(8,128)(2,1)S(1)} %get-tuple-element.78.refs_0_, bf16[256,512]{1,0:T(8,128)(2,1)S(1)} %collective-permute-done.24.refs_1_, bf16[256,4096]{1,0:T(8,128)(2,1)} %get-tuple-element.84.refs_2_, bf16[256,4096]{1,0:T(8,128)(2,1)} %get-tuple-element.83.refs_3_, ...), custom_call_target="tpu_custom_call" | custom-call | flops 6000000000 | bytes 4194304 | tf_op jit(solution)/shard_map/project/pallas_call | solution.py:270
  242.9 1.7 collective-permute-done.22.refs_0_
  244.7 5.6 %collective-permute-done.23.refs_1_ = bf16[256,512]{1,0:T(8,128)(2,1)S(1)} collective-permute-done((bf16[256,512]{1,0:T(8,128)(2,1)S(1)}, bf16[256,512]{1,0:T(8,128)(2,1)S(1)}, u32[]{:S(2)}, u32[]{:S(2)}) %collective-permute-start.23) | collective-permute-done | bytes 262176 | tf_op jit(solution)/shard_map/ppermute | solution.py:427
  250.3 5.9 %project.3 = bf16[256,4096]{1,0:T(8,128)(2,1)} custom-call(bf16[256,512]{1,0:T(8,128)(2,1)S(1)} %collective-permute-done.22.refs_0_, bf16[256,512]{1,0:T(8,128)(2,1)S(1)} %collective-permute-done.23.refs_1_, bf16[256,4096]{1,0:T(8,128)(2,1)} %collective-permute-done.8.refs_2_, bf16[256,4096]{1,0:T(8,128)(2,1)} %collective-permute-done.9.refs_3_, ...), custom_call_target="tpu_custom_call" | custom-call | flops 6000000000 | bytes 4194304 | tf_op jit(solution)/shard_map/project/pallas_call | solution.py:270
  (75 shorter events, 16.5 us)
Async XLA Ops:
  0.0 21.4 %copy-start.13 = (s32[16,2]{0,1:T(2,128)S(1)}, s32[16,2]{0,1:T(2,128)}, u32[]{:S(2)}) copy-start(s32[16,2]{0,1:T(2,128)} %param.6) | copy-start | bytes 388
  3.3 60.1 %collective-permute-start = (bf16[16,64,1024]{2,1,0:T(8,128)(2,1)S(1)}, bf16[16,64,1024]{2,1,0:T(8,128)(2,1)}, u32[]{:S(2)}, u32[]{:S(2)}) collective-permute-start(bf16[16,64,1024]{2,1,0:T(8,128)(2,1)S(1)} %reshape.122.refs_0_), channel_id=1, source_target_pairs={{0,4},{4,8},{8,12},{12,16},{16,20},{20,24},{24,28},{28,0},{1,5},{5... | collective-permute-start | bytes 6291464 | tf_op jit(solution)/shard_map/ppermute | solution.py:287
  5.8 57.5 %collective-permute-start.1 = (bf16[16,64,1024]{2,1,0:T(8,128)(2,1)S(1)}, bf16[16,64,1024]{2,1,0:T(8,128)(2,1)}, u32[]{:S(2)}, u32[]{:S(2)}) collective-permute-start(bf16[16,64,1024]{2,1,0:T(8,128)(2,1)S(1)} %reshape.122.refs_0_), channel_id=1, source_target_pairs={{0,28},{4,0},{8,4},{12,8},{16,12},{20,16},{24,20},{28,24},{1,29},{... | collective-permute-start | bytes 6291464 | tf_op jit(solution)/shard_map/ppermute | solution.py:287
  11.0 52.4 %collective-permute-start.2 = (bf16[64,1024]{1,0:T(8,128)(2,1)S(1)}, bf16[64,1024]{1,0:T(8,128)(2,1)S(1)}, u32[]{:S(2)}, u32[]{:S(2)}) collective-permute-start(bf16[64,1024]{1,0:T(8,128)(2,1)S(1)} %bitcast.23), channel_id=1, source_target_pairs={{28,32},{60,64},{92,96},{124,128},{156,160},{188,192},{220,224},{3... | collective-permute-start | bytes 393224 | tf_op jit(solution)/shard_map/ppermute | solution.py:368
  11.6 11.7 %collective-permute-start.5 = (bf16[64,1024]{1,0:T(8,128)(2,1)S(1)}, bf16[64,1024]{1,0:T(8,128)(2,1)S(1)}, u32[]{:S(2)}, u32[]{:S(2)}) collective-permute-start(bf16[64,1024]{1,0:T(8,128)(2,1)S(1)} %bitcast.24), channel_id=1, source_target_pairs={{0,128},{252,124},{1,129},{253,125},{2,130},{254,126},{3,131},{255... | collective-permute-start | bytes 393224 | tf_op jit(solution)/shard_map/ppermute | solution.py:302
  23.4 3.3 %collective-permute-start.6 = (bf16[64,1024]{1,0:T(8,128)(2,1)S(1)}, bf16[64,1024]{1,0:T(8,128)(2,1)S(1)}, u32[]{:S(2)}, u32[]{:S(2)}) collective-permute-start(bf16[64,1024]{1,0:T(8,128)(2,1)S(1)} %broadcast_select_fusion.5), channel_id=1, source_target_pairs={{0,64},{128,192},{252,188},{124,60},{1,65},{129,193},{253,189},{12... | collective-permute-start | bytes 393224 | tf_op jit(solution)/shard_map/ppermute | solution.py:302
  26.7 9.9 %collective-permute-start.7 = (bf16[64,1024]{1,0:T(8,128)(2,1)S(1)}, bf16[64,1024]{1,0:T(8,128)(2,1)S(1)}, u32[]{:S(2)}, u32[]{:S(2)}) collective-permute-start(bf16[64,1024]{1,0:T(8,128)(2,1)S(1)} %broadcast_select_fusion.6), channel_id=1, source_target_pairs={{0,32},{64,96},{128,160},{192,224},{252,220},{188,156},{124,92},{6... | collective-permute-start | bytes 393224 | tf_op jit(solution)/shard_map/ppermute | solution.py:302
  29.0 34.3 %all-to-all-start = ((s32[64,1,8]{2,1,0:T(1,128)}), s32[64,1,8]{2,1,0:T(1,128)S(1)}, u32[]{:S(2)}, u32[]{:S(2)}) async-start(s32[64,1,8]{2,1,0:T(1,128)} %bitcast.3), calls=%async_computation | async-start | bytes 65536 | tf_op jit(solution)/shard_map/all_to_all | solution.py:358
  41.3 49.5 %collective-permute-start.8 = (bf16[256,4096]{1,0:T(8,128)(2,1)}, bf16[256,4096]{1,0:T(8,128)(2,1)}, u32[]{:S(2)}, u32[]{:S(2)}) collective-permute-start(bf16[256,4096]{1,0:T(8,128)(2,1)} %get-tuple-element.84.refs_2_), channel_id=1, source_target_pairs={{0,2},{2,32},{32,34},{34,0},{1,3},{3,33},{33,35},{35,1},{4,6},{6,3... | collective-permute-start | bytes 6291464 | tf_op jit(solution)/shard_map/ppermute | solution.py:365
  42.6 48.3 %collective-permute-start.9 = (bf16[256,4096]{1,0:T(8,128)(2,1)}, bf16[256,4096]{1,0:T(8,128)(2,1)}, u32[]{:S(2)}, u32[]{:S(2)}) collective-permute-start(bf16[256,4096]{1,0:T(8,128)(2,1)} %get-tuple-element.83.refs_3_), channel_id=1, source_target_pairs={{0,34},{2,0},{32,2},{34,32},{1,35},{3,1},{33,3},{35,33},{4,38},{6,... | collective-permute-start | bytes 6291464 | tf_op jit(solution)/shard_map/ppermute | solution.py:366
  63.3 47.2 %collective-permute-start.3 = (bf16[16,64,1024]{2,1,0:T(8,128)(2,1)}, bf16[16,64,1024]{2,1,0:T(8,128)(2,1)}, u32[]{:S(2)}, u32[]{:S(2)}) collective-permute-start(bf16[16,64,1024]{2,1,0:T(8,128)(2,1)} %collective-permute-done.refs_1_), channel_id=1, source_target_pairs={{0,4},{4,8},{8,12},{12,16},{16,20},{20,24},{24,28},{28,0},{1,5},{5... | collective-permute-start | bytes 6291464 | tf_op jit(solution)/shard_map/ppermute | solution.py:287
  64.6 45.9 %collective-permute-start.4 = (bf16[16,64,1024]{2,1,0:T(8,128)(2,1)}, bf16[16,64,1024]{2,1,0:T(8,128)(2,1)}, u32[]{:S(2)}, u32[]{:S(2)}) collective-permute-start(bf16[16,64,1024]{2,1,0:T(8,128)(2,1)} %collective-permute-done.1.refs_2_), channel_id=1, source_target_pairs={{0,28},{4,0},{8,4},{12,8},{16,12},{20,16},{24,20},{28,24},{1,29},{... | collective-permute-start | bytes 6291464 | tf_op jit(solution)/shard_map/ppermute | solution.py:287
  72.1 52.9 %all-to-all-start.1 = ((bf16[8,3,64,1024]{3,2,1,0:T(8,128)(2,1)}), bf16[8,3,64,1024]{3,2,1,0:T(8,128)(2,1)}, u32[]{:S(2)}, u32[]{:S(2)}) async-start(bf16[8,3,64,1024]{3,2,1,0:T(8,128)(2,1)} %pick.2), calls=%async_computation.1 | async-start | bytes 6291456 | tf_op jit(solution)/shard_map/all_to_all | solution.py:291
  125.0 36.7 %all-to-all-start.2 = ((bf16[8,2,64,1024]{3,2,1,0:T(8,128)(2,1)}), bf16[8,2,64,1024]{3,2,1,0:T(8,128)(2,1)S(1)}, u32[]{:S(2)}, u32[]{:S(2)}) async-start(bf16[8,2,64,1024]{3,2,1,0:T(8,128)(2,1)} %get-tuple-element.60), calls=%async_computation.2 | async-start | bytes 4194304 | tf_op jit(solution)/shard_map/all_to_all | solution.py:291
  129.6 72.8 %collective-permute-start.19 = (bf16[512,4096]{1,0:T(8,128)(2,1)}, bf16[512,4096]{1,0:T(8,128)(2,1)}, u32[]{:S(2)}, u32[]{:S(2)}) collective-permute-start(bf16[512,4096]{1,0:T(8,128)(2,1)} %param.7), channel_id=1, source_target_pairs={{0,1},{1,0},{2,3},{3,2},{4,5},{5,4},{6,7},{7,6},{8,9},{9,8},{10,11... | collective-permute-start | bytes 12582920 | tf_op jit(solution)/shard_map/ppermute | solution.py:398
  139.1 7.1 %collective-permute-start.10 = (bf16[64,1024]{1,0:T(8,128)(2,1)S(1)}, bf16[64,1024]{1,0:T(8,128)(2,1)S(1)}, u32[]{:S(2)}, u32[]{:S(2)}) collective-permute-start(bf16[64,1024]{1,0:T(8,128)(2,1)S(1)} %broadcast_select_fusion.7), channel_id=1, source_target_pairs={{0,16},{28,12},{1,17},{29,13},{2,18},{30,14},{3,19},{31,15},{32,48... | collective-permute-start | bytes 393224 | tf_op jit(solution)/shard_map/ppermute | solution.py:395
  146.3 4.1 %collective-permute-start.11 = (bf16[64,1024]{1,0:T(8,128)(2,1)S(1)}, bf16[64,1024]{1,0:T(8,128)(2,1)S(1)}, u32[]{:S(2)}, u32[]{:S(2)}) collective-permute-start(bf16[64,1024]{1,0:T(8,128)(2,1)S(1)} %broadcast_select_fusion.1), channel_id=1, source_target_pairs={{0,8},{16,24},{28,20},{12,4},{1,9},{17,25},{29,21},{13,5},{2,10},{... | collective-permute-start | bytes 393224 | tf_op jit(solution)/shard_map/ppermute | solution.py:403
  147.6 14.1 %collective-permute-start.13 = (bf16[4,64,1024]{2,1,0:T(8,128)(2,1)}, bf16[4,64,1024]{2,1,0:T(8,128)(2,1)S(1)}, u32[]{:S(2)}, u32[]{:S(2)}) collective-permute-start(bf16[4,64,1024]{2,1,0:T(8,128)(2,1)} %get-tuple-element.61), channel_id=1, source_target_pairs={{0,4},{4,8},{8,12},{12,16},{16,20},{20,24},{24,28},{28,0},{1,5},{5... | collective-permute-start | bytes 1572872 | tf_op jit(solution)/shard_map/ppermute | solution.py:287
  147.7 14.1 %collective-permute-start.14 = (bf16[4,64,1024]{2,1,0:T(8,128)(2,1)}, bf16[4,64,1024]{2,1,0:T(8,128)(2,1)}, u32[]{:S(2)}, u32[]{:S(2)}) collective-permute-start(bf16[4,64,1024]{2,1,0:T(8,128)(2,1)} %get-tuple-element.62), channel_id=1, source_target_pairs={{0,28},{4,0},{8,4},{12,8},{16,12},{20,16},{24,20},{28,24},{1,29},{... | collective-permute-start | bytes 1572872 | tf_op jit(solution)/shard_map/ppermute | solution.py:287
  150.4 16.7 %collective-permute-start.12 = (bf16[64,1024]{1,0:T(8,128)(2,1)S(1)}, bf16[64,1024]{1,0:T(8,128)(2,1)S(1)}, u32[]{:S(2)}, u32[]{:S(2)}) collective-permute-start(bf16[64,1024]{1,0:T(8,128)(2,1)S(1)} %broadcast_select_fusion.2), channel_id=1, source_target_pairs={{0,4},{4,0},{8,12},{12,8},{16,20},{20,16},{24,28},{28,24},{1,5},{5... | collective-permute-start | bytes 393224 | tf_op jit(solution)/shard_map/ppermute | solution.py:406
  161.7 0.8 copy-start.14
  162.5 5.5 %copy-start.12 = (bf16[8,2,64,1024]{3,2,1,0:T(8,128)(2,1)}, bf16[8,2,64,1024]{3,2,1,0:T(8,128)(2,1)S(1)}, u32[]{:S(2)}) copy-start(bf16[8,2,64,1024]{3,2,1,0:T(8,128)(2,1)S(1)} %all-to-all-done.2) | copy-start | bytes 6291460
  162.5 16.5 %collective-permute-start.18 = (bf16[4,64,1024]{2,1,0:T(8,128)(2,1)}, bf16[4,64,1024]{2,1,0:T(8,128)(2,1)S(1)}, u32[]{:S(2)}, u32[]{:S(2)}) collective-permute-start(bf16[4,64,1024]{2,1,0:T(8,128)(2,1)} %collective-permute-done.14), channel_id=1, source_target_pairs={{0,28},{4,0},{8,4},{12,8},{16,12},{20,16},{24,20},{28,24},{1,29},{... | collective-permute-start | bytes 1572872 | tf_op jit(solution)/shard_map/ppermute | solution.py:287
  164.5 15.8 %collective-permute-start.17 = (bf16[4,64,1024]{2,1,0:T(8,128)(2,1)}, bf16[4,64,1024]{2,1,0:T(8,128)(2,1)S(1)}, u32[]{:S(2)}, u32[]{:S(2)}) collective-permute-start(bf16[4,64,1024]{2,1,0:T(8,128)(2,1)} %copy-done.14), channel_id=1, source_target_pairs={{0,4},{4,8},{8,12},{12,16},{16,20},{20,24},{24,28},{28,0},{1,5},{5... | collective-permute-start | bytes 1572872 | tf_op jit(solution)/shard_map/ppermute | solution.py:287
  167.1 34.8 %collective-permute-start.20 = (bf16[256,4096]{1,0:T(8,128)(2,1)}, bf16[256,4096]{1,0:T(8,128)(2,1)}, u32[]{:S(2)}, u32[]{:S(2)}) collective-permute-start(bf16[256,4096]{1,0:T(8,128)(2,1)} %collective-permute-done.8.refs_2_), channel_id=1, source_target_pairs={{0,1},{1,0},{2,3},{3,2},{4,5},{5,4},{6,7},{7,6},{8,9},{9,8},{10,11... | collective-permute-start | bytes 6291464 | tf_op jit(solution)/shard_map/ppermute | solution.py:398
  167.9 34.0 %collective-permute-start.21 = (bf16[256,4096]{1,0:T(8,128)(2,1)}, bf16[256,4096]{1,0:T(8,128)(2,1)}, u32[]{:S(2)}, u32[]{:S(2)}) collective-permute-start(bf16[256,4096]{1,0:T(8,128)(2,1)} %collective-permute-done.9.refs_3_), channel_id=1, source_target_pairs={{0,1},{1,0},{2,3},{3,2},{4,5},{5,4},{6,7},{7,6},{8,9},{9,8},{10,11... | collective-permute-start | bytes 6291464 | tf_op jit(solution)/shard_map/ppermute | solution.py:398
  168.0 34.8 %all-to-all-start.3 = ((bf16[8,2,64,1024]{3,2,1,0:T(8,128)(2,1)}), bf16[8,2,64,1024]{3,2,1,0:T(8,128)(2,1)S(1)}, u32[]{:S(2)}, u32[]{:S(2)}) async-start(bf16[8,2,64,1024]{3,2,1,0:T(8,128)(2,1)} %get-tuple-element.66), calls=%async_computation.3 | async-start | bytes 4194304 | tf_op jit(solution)/shard_map/all_to_all | solution.py:291
  175.0 6.7 %copy-start = (bf16[1152,1024]{1,0:T(8,128)(2,1)S(1)}, bf16[1152,1024]{1,0:T(8,128)(2,1)}, u32[]{:S(2)}) copy-start(bf16[1152,1024]{1,0:T(8,128)(2,1)} %pad_maximum_fusion.refs_4_) | copy-start | bytes 7077892
  175.0 6.7 %copy-start.1 = (bf16[1024,512]{1,0:T(8,128)(2,1)S(1)}, bf16[1024,512]{1,0:T(8,128)(2,1)}, u32[]{:S(2)}) copy-start(bf16[1024,512]{1,0:T(8,128)(2,1)} %refs_3_.3) | copy-start | bytes 3145732
  179.0 30.1 %collective-permute-start.15 = (bf16[8,64,1024]{2,1,0:T(8,128)(2,1)}, bf16[8,64,1024]{2,1,0:T(8,128)(2,1)}, u32[]{:S(2)}, u32[]{:S(2)}) collective-permute-start(bf16[8,64,1024]{2,1,0:T(8,128)(2,1)} %get-tuple-element.86), channel_id=1, source_target_pairs={{0,4},{4,8},{8,12},{12,16},{16,20},{20,24},{24,28},{28,0},{1,5},{5... | collective-permute-start | bytes 3145736 | tf_op jit(solution)/shard_map/ppermute | solution.py:287
  180.3 28.8 %collective-permute-start.16 = (bf16[8,64,1024]{2,1,0:T(8,128)(2,1)}, bf16[8,64,1024]{2,1,0:T(8,128)(2,1)}, u32[]{:S(2)}, u32[]{:S(2)}) collective-permute-start(bf16[8,64,1024]{2,1,0:T(8,128)(2,1)} %get-tuple-element.85), channel_id=1, source_target_pairs={{0,28},{4,0},{8,4},{12,8},{16,12},{20,16},{24,20},{28,24},{1,29},{... | collective-permute-start | bytes 3145736 | tf_op jit(solution)/shard_map/ppermute | solution.py:287
  199.9 0.8 copy-start.10
  200.7 1.7 copy-start.8
  202.8 22.2 %all-to-all-start.4 = ((bf16[8,64,1024]{2,1,0:T(8,128)(2,1)}), bf16[8,64,1024]{2,1,0:T(8,128)(2,1)S(1)}, u32[]{:S(2)}, u32[]{:S(2)}) async-start(bf16[8,64,1024]{2,1,0:T(8,128)(2,1)} %pad_maximum_fusion.1), calls=%async_computation.4 | async-start | bytes 2097152 | tf_op jit(solution)/shard_map/all_to_all | solution.py:291
  209.1 1.2 copy-start.2
  210.3 1.6 copy-start.9
  211.9 1.0 copy-start.11
  222.9 1.3 copy-start.4
  224.2 0.8 copy-start.6
  225.0 1.2 copy-start.3
  226.2 1.6 copy-start.5
  227.8 1.0 copy-start.7
  231.6 6.7 %collective-permute-start.24 = (bf16[256,512]{1,0:T(8,128)(2,1)S(1)}, bf16[256,512]{1,0:T(8,128)(2,1)S(1)}, u32[]{:S(2)}, u32[]{:S(2)}) collective-permute-start(bf16[256,512]{1,0:T(8,128)(2,1)S(1)} %get-tuple-element.79), channel_id=1, source_target_pairs={{0,1},{1,0},{2,3},{3,2},{4,5},{5,4},{6,7},{7,6},{8,9},{9,8},{10,11... | collective-permute-start | bytes 786440 | tf_op jit(solution)/shard_map/ppermute | solution.py:428
  233.9 10.7 %collective-permute-start.22 = (bf16[256,512]{1,0:T(8,128)(2,1)S(1)}, bf16[256,512]{1,0:T(8,128)(2,1)S(1)}, u32[]{:S(2)}, u32[]{:S(2)}) collective-permute-start(bf16[256,512]{1,0:T(8,128)(2,1)S(1)} %get-tuple-element.74), channel_id=1, source_target_pairs={{0,2},{1,3},{2,0},{3,1},{4,6},{5,7},{6,4},{7,5},{8,10},{9,11},{10,... | collective-permute-start | bytes 786440 | tf_op jit(solution)/shard_map/ppermute | solution.py:427
  238.1 12.2 %collective-permute-start.23 = (bf16[256,512]{1,0:T(8,128)(2,1)S(1)}, bf16[256,512]{1,0:T(8,128)(2,1)S(1)}, u32[]{:S(2)}, u32[]{:S(2)}) collective-permute-start(bf16[256,512]{1,0:T(8,128)(2,1)S(1)} %get-tuple-element.75), channel_id=1, source_target_pairs={{0,3},{1,2},{2,1},{3,0},{4,7},{5,6},{6,5},{7,4},{8,11},{9,10},{10,... | collective-permute-start | bytes 786440 | tf_op jit(solution)/shard_map/ppermute | solution.py:427

commit v8 on v7

--- a/solution.py
+++ b/solution.py
@@ -394,18 +394,19 @@
     c3 = lane_exchange(c3)
     got = lax.ppermute(held, "z", [(0, 4), (7, 3)])
     held = jnp.where(jnp.logical_or(z == 4, z == 3), got, held)
-    swap = [(0, 1), (1, 0)]
-    others = [lax.ppermute(x, "core", swap) for x in (w_core, low, high)]
-    c2, c3, fu, fd = tie(c2, c3, fu, fd)
-    r2 = lane_exchange(c2)
-    fu, fd = z_shift(fu, 1), z_shift(fd, -1)
-    r3u, r3d = z_shift(c3[:, 0], 1), z_shift(c3[:, 1], -1)
     got = lax.ppermute(held, "z", [(0, 2), (4, 6), (7, 5), (3, 1)])
     fresh = reduce(jnp.logical_or, [z == 2, z == 6, z == 5, z == 1])
     held = jnp.where(fresh, got, held)
     got = lax.ppermute(held, "z", [(i, i ^ 1) for i in range(NZ)])
     even = z % 2 == 0
     ends = jnp.concatenate([jnp.where(even, held, got), jnp.where(even, got, held)], axis=0)
+    c2, c3, fu, fd, ends = tie(c2, c3, fu, fd, ends)
+    low, high, w_core, ends = tie(low, high, w_core, ends)
+    swap = [(0, 1), (1, 0)]
+    others = [lax.ppermute(x, "core", swap) for x in (w_core, low, high)]
+    r2 = lane_exchange(c2)
+    fu, fd = z_shift(fu, 1), z_shift(fd, -1)
+    r3u, r3d = z_shift(c3[:, 0], 1), z_shift(c3[:, 1], -1)
     far = jnp.concatenate([fu, fd], axis=0)
     far, r2, *others = tie(far, r2, *others)
     weights = own + [others[0], low, high] + others[1:]

time: 260 us -> 252 us (0.969)
  waiting for transfers between devices: 80.1 us -> 73.1 us
    ppermute x1, waiting for transfers between devices: 11.6 us -> 3.14 us  [body(): lax.ppermute(own[0], XRING, [(i, (i + 1) % ring) for i in range(ring)])]
    all_to_all x1, waiting for transfers between devices: 18.8 us -> 26.6 us  [body(): asked = lax.all_to_all(asked, SEQ, split_axis=0, concat_axis=0, tiled=True)]
    ppermute x3, starting transfers between devices: 10.5 us -> 17.3 us  [body(): others = [lax.ppermute(x, 'core', swap) for x in (w_core, low, high)]]
    all_to_all x4, waiting for transfers between devices: 8.18 us -> 1.39 us  [lane_exchange(): return lax.all_to_all(x, LANE, split_axis=0, concat_axis=0, tiled=True)]
    ppermute x10, starting transfers between devices: 19.3 us -> 13.5 us  [z_shift(): return lax.ppermute(x, 'z', [(i, (i + by) % NZ) for i in range(NZ)])]
    ppermute x1, waiting for transfers between devices: 0.01 us -> 3.48 us  [body(): got = lax.ppermute(held, 'z', [(i, i ^ 1) for i in range(NZ)])]
    ppermute x1, starting transfers between devices: 4.2 us -> 7.03 us  [body(): got = lax.ppermute(held, 'z', [(0, 4), (7, 3)])]
    ppermute x2, starting transfers between devices: 4.44 us -> 1.73 us  [body(): lax.ppermute(away[k - 1], HEAD, [(h, h ^ k) for h in heads])]
  transfers between devices with their start and end apart: 30 -> 30, of which waited for: 12 -> 10; matrix products, arithmetic and copies ran while one was open for 6% -> 7% of each run, Pallas kernels for 18% -> 18%
where the time goes in v8:
time: 252 us; the launch traced here: 250 us
  starting transfers between devices  93.6 us (37%)
  waiting for transfers between devices  73.1 us (29%)
  Pallas kernels  54.2 us (22%)
  local copies, waits for them, and re-layouts  23.5 us (9%)
  other arithmetic  5.2 us (2%)
    all_to_all x1, waiting for transfers between devices, body(): asked = lax.all_to_all(asked, SEQ, split_axis=0, concat_axis=0, tiled=True)  26.6 us
    ppermute x10, waiting for transfers between devices, z_shift(): return lax.ppermute(x, 'z', [(i, (i + by) % NZ) for i in range(NZ)])  25.6 us
    all_to_all x4, starting transfers between devices, lane_exchange(): return lax.all_to_all(x, LANE, split_axis=0, concat_axis=0, tiled=True)  22 us
    ppermute x3, starting transfers between devices, body(): others = [lax.ppermute(x, 'core', swap) for x in (w_core, low, high)]  17.3 us
    pallas_call x1, Pallas kernels, local_part(): pl.pallas_call(lambda *refs: local_kernel(all_blocks, deltas, *refs), out...  16.4 us
    ppermute x3, starting transfers between devices, spread_lanes(): got = lax.ppermute(held, SEQ, moves)  14 us
    ppermute x10, starting transfers between devices, z_shift(): return lax.ppermute(x, 'z', [(i, (i + by) % NZ) for i in range(NZ)])  13.5 us
    pallas_call x2, Pallas kernels, pick(): pl.pallas_call(kernel, out_shape=tuple((pltpu.HBM(shape + block_shape, BF...  12.9 us
  transfers between devices with their start and end apart: 30, of which 10 were waited for; matrix products, arithmetic and copies ran while one was open for 7% of the time, Pallas kernels for 18%

profile of v8, /device:TPU:1, one launch (start us, length us, event | category | flops | bytes accessed | tf_op | source)
XLA Modules:
  0.0 250.2 jit_solution(6604097232578340026)
XLA Ops:
  1.1 5.7 %collective-permute-start.5 = (bf16[64,1024]{1,0:T(8,128)(2,1)S(1)}, bf16[64,1024]{1,0:T(8,128)(2,1)S(1)}, u32[]{:S(2)}, u32[]{:S(2)}) collective-permute-start(bf16[64,1024]{1,0:T(8,128)(2,1)S(1)} %bitcast.23), channel_id=1, source_target_pairs={{0,128},{252,124},{1,129},{253,125},{2,130},{254,126},{3,131},{255... | collective-permute-start | bytes 393224 | tf_op jit(solution)/shard_map/ppermute | solution.py:302
  7.5 3.2 %reshape.122.refs_0_ = bf16[16,64,1024]{2,1,0:T(8,128)(2,1)S(1)} reshape(bf16[1024,2,512]{2,1,0:T(2,128)(2,1)} %param.5) | data formatting | bytes 4194304 | tf_op jit(solution)/shard_map/reshape | solution.py:352
  10.7 2.7 %collective-permute-start.1 = (bf16[16,64,1024]{2,1,0:T(8,128)(2,1)S(1)}, bf16[16,64,1024]{2,1,0:T(8,128)(2,1)}, u32[]{:S(2)}, u32[]{:S(2)}) collective-permute-start(bf16[16,64,1024]{2,1,0:T(8,128)(2,1)S(1)} %reshape.122.refs_0_), channel_id=1, source_target_pairs={{0,28},{4,0},{8,4},{12,8},{16,12},{20,16},{24,20},{28,24},{1,29},{... | collective-permute-start | bytes 6291464 | tf_op jit(solution)/shard_map/ppermute | solution.py:287
  13.7 7.0 %collective-permute-start.6 = (bf16[64,1024]{1,0:T(8,128)(2,1)S(1)}, bf16[64,1024]{1,0:T(8,128)(2,1)S(1)}, u32[]{:S(2)}, u32[]{:S(2)}) collective-permute-start(bf16[64,1024]{1,0:T(8,128)(2,1)S(1)} %broadcast_select_fusion.5), channel_id=1, source_target_pairs={{0,64},{128,192},{252,188},{124,60},{1,65},{129,193},{253,189},{12... | collective-permute-start | bytes 393224 | tf_op jit(solution)/shard_map/ppermute | solution.py:302
  20.8 1.9 collective-permute-done.6
  22.7 1.3 collective-permute-start.7
  25.0 7.2 %all-to-all-start = ((s32[64,1,8]{2,1,0:T(1,128)}), s32[64,1,8]{2,1,0:T(1,128)S(1)}, u32[]{:S(2)}, u32[]{:S(2)}) async-start(s32[64,1,8]{2,1,0:T(1,128)} %bitcast.3), calls=%async_computation | async-start | bytes 65536 | tf_op jit(solution)/shard_map/all_to_all | solution.py:358
  32.3 4.7 %fusion.4 = (bf16[256,4096]{1,0:T(8,128)(2,1)}, bf16[256,4096]{1,0:T(8,128)(2,1)}) fusion(bf16[512,4096]{1,0:T(8,128)(2,1)} %param.7), kind=kLoop, calls=%fused_computation.36 | loop fusion | bytes 8388608 | tf_op jit(solution)/shard_map/slice | solution.py:363
  37.0 3.2 %collective-permute-start.9 = (bf16[256,4096]{1,0:T(8,128)(2,1)}, bf16[256,4096]{1,0:T(8,128)(2,1)}, u32[]{:S(2)}, u32[]{:S(2)}) collective-permute-start(bf16[256,4096]{1,0:T(8,128)(2,1)} %get-tuple-element.93.refs_3_), channel_id=1, source_target_pairs={{0,34},{2,0},{32,2},{34,32},{1,35},{3,1},{33,3},{35,33},{4,38},{6,... | collective-permute-start | bytes 6291464 | tf_op jit(solution)/shard_map/ppermute | solution.py:366
  40.2 26.6 %all-to-all-done = s32[64,1,8]{2,1,0:T(1,128)S(1)} async-done(((s32[64,1,8]{2,1,0:T(1,128)}), s32[64,1,8]{2,1,0:T(1,128)S(1)}, u32[]{:S(2)}, u32[]{:S(2)}) %all-to-all-start) | async-done | bytes 2080 | tf_op jit(solution)/shard_map/all_to_all | solution.py:358
  66.8 1.3 collective-permute-start.3
  68.1 1.5 collective-permute-start.4
  69.6 6.1 %pick.2 = bf16[8,3,64,1024]{3,2,1,0:T(8,128)(2,1)} custom-call(s32[1]{0:T(128)} %bitcast.1.z_ref.refs_0_.refs_1_, s32[64,8]{1,0:T(8,128)S(1)} %bitcast.21, bf16[16,64,1024]{2,1,0:T(8,128)(2,1)S(1)} %reshape.122.refs_0_, bf16[16,64,1024]{2,1,0:T(8,128)(2,1)} %collective-permute-done.refs_1_, bf16[16,64,1024]{2,1,0:T(8,128)(2,1)} %collective-permute-done.1.refs_2_), custom_call_target="tpu_custom_call" | custom-call | flops 3000000000 | bytes 4194304 | tf_op jit(solution)/shard_map/pick/pallas_call | solution.py:220
  75.6 4.5 %all-to-all-start.1 = ((bf16[8,3,64,1024]{3,2,1,0:T(8,128)(2,1)}), bf16[8,3,64,1024]{3,2,1,0:T(8,128)(2,1)}, u32[]{:S(2)}, u32[]{:S(2)}) async-start(bf16[8,3,64,1024]{3,2,1,0:T(8,128)(2,1)} %pick.2), calls=%async_computation.1 | async-start | bytes 6291456 | tf_op jit(solution)/shard_map/all_to_all | solution.py:291
  81.1 1.7 pad_maximum_fusion.refs_4_
  82.8 1.6 collective-permute-done.9.refs_3_
  84.4 3.1 %collective-permute-done.8.refs_2_ = bf16[256,4096]{1,0:T(8,128)(2,1)} collective-permute-done((bf16[256,4096]{1,0:T(8,128)(2,1)}, bf16[256,4096]{1,0:T(8,128)(2,1)}, u32[]{:S(2)}, u32[]{:S(2)}) %collective-permute-start.8) | collective-permute-done | bytes 2097184 | tf_op jit(solution)/shard_map/ppermute | solution.py:365
  87.5 25.6 %collective-permute-done.3.refs_0_ = bf16[16,64,1024]{2,1,0:T(8,128)(2,1)} collective-permute-done((bf16[16,64,1024]{2,1,0:T(8,128)(2,1)}, bf16[16,64,1024]{2,1,0:T(8,128)(2,1)}, u32[]{:S(2)}, u32[]{:S(2)}) %collective-permute-start.3) | collective-permute-done | bytes 2097184 | tf_op jit(solution)/shard_map/ppermute | solution.py:287
  113.1 6.8 %pick.3 = (bf16[8,2,64,1024]{3,2,1,0:T(8,128)(2,1)}, bf16[4,64,1024]{2,1,0:T(8,128)(2,1)}, bf16[4,64,1024]{2,1,0:T(8,128)(2,1)}, bf16[8,2,64,1024]{3,2,1,0:T(8,128)(2,1)}) custom-call(s32[1]{0:T(128)} %bitcast.1.z_ref.refs_0_.refs_1_, s32[64,8]{1,0:T(8,128)S(1)} %bitcast.22, bf16[16,64,1024]{2,1,0:T(8,128)(2,1)} %collective-permute-done.3.refs_0_, ...), custom_call_target="tpu_custom_call" | custom-call | flops 60000002048 | bytes 4194304 | tf_op jit(solution)/shard_map/pick/pallas_call | solution.py:220
  119.9 1.4 all-to-all-done.1.refs_6_
  121.3 3.6 %all-to-all-start.2 = ((bf16[8,2,64,1024]{3,2,1,0:T(8,128)(2,1)}), bf16[8,2,64,1024]{3,2,1,0:T(8,128)(2,1)S(1)}, u32[]{:S(2)}, u32[]{:S(2)}) async-start(bf16[8,2,64,1024]{3,2,1,0:T(8,128)(2,1)} %get-tuple-element.64), calls=%async_computation.2 | async-start | bytes 4194304 | tf_op jit(solution)/shard_map/all_to_all | solution.py:291
  124.9 7.0 %collective-permute-start.12 = (bf16[64,1024]{1,0:T(8,128)(2,1)S(1)}, bf16[64,1024]{1,0:T(8,128)(2,1)S(1)}, u32[]{:S(2)}, u32[]{:S(2)}) collective-permute-start(bf16[64,1024]{1,0:T(8,128)(2,1)S(1)} %broadcast_select_fusion.7), channel_id=1, source_target_pairs={{0,16},{28,12},{1,17},{29,13},{2,18},{30,14},{3,19},{31,15},{32,48... | collective-permute-start | bytes 393224 | tf_op jit(solution)/shard_map/ppermute | solution.py:395
  131.9 1.9 collective-permute-done.12
  133.9 1.3 collective-permute-start.13
  135.3 2.7 %collective-permute-start.11 = (bf16[4,64,1024]{2,1,0:T(8,128)(2,1)}, bf16[4,64,1024]{2,1,0:T(8,128)(2,1)S(1)}, u32[]{:S(2)}, u32[]{:S(2)}) collective-permute-start(bf16[4,64,1024]{2,1,0:T(8,128)(2,1)} %get-tuple-element.66), channel_id=1, source_target_pairs={{0,28},{4,0},{8,4},{12,8},{16,12},{20,16},{24,20},{28,24},{1,29},{... | collective-permute-start | bytes 1572872 | tf_op jit(solution)/shard_map/ppermute | solution.py:287
  138.0 3.9 %collective-permute-start.14 = (bf16[64,1024]{1,0:T(8,128)(2,1)S(1)}, bf16[64,1024]{1,0:T(8,128)(2,1)S(1)}, u32[]{:S(2)}, u32[]{:S(2)}) collective-permute-start(bf16[64,1024]{1,0:T(8,128)(2,1)S(1)} %broadcast_select_fusion.2), channel_id=1, source_target_pairs={{0,4},{4,0},{8,12},{12,8},{16,20},{20,16},{24,28},{28,24},{1,5},{5... | collective-permute-start | bytes 393224 | tf_op jit(solution)/shard_map/ppermute | solution.py:400
  141.8 3.5 %collective-permute-done.14 = bf16[64,1024]{1,0:T(8,128)(2,1)S(1)} collective-permute-done((bf16[64,1024]{1,0:T(8,128)(2,1)S(1)}, bf16[64,1024]{1,0:T(8,128)(2,1)S(1)}, u32[]{:S(2)}, u32[]{:S(2)}) %collective-permute-start.14) | collective-permute-done | bytes 131104 | tf_op jit(solution)/shard_map/ppermute | solution.py:400
  145.4 13.0 %collective-permute-start.19 = (bf16[512,4096]{1,0:T(8,128)(2,1)}, bf16[512,4096]{1,0:T(8,128)(2,1)}, u32[]{:S(2)}, u32[]{:S(2)}) collective-permute-start(bf16[512,4096]{1,0:T(8,128)(2,1)} %param.7), channel_id=1, source_target_pairs={{0,1},{1,0},{2,3},{3,2},{4,5},{5,4},{6,7},{7,6},{8,9},{9,8},{10,11... | collective-permute-start | bytes 12582920 | tf_op jit(solution)/shard_map/ppermute | solution.py:406
  158.5 2.1 collective-permute-start.17
  161.2 6.9 %all-to-all-start.3 = ((bf16[8,2,64,1024]{3,2,1,0:T(8,128)(2,1)}), bf16[8,2,64,1024]{3,2,1,0:T(8,128)(2,1)S(1)}, u32[]{:S(2)}, u32[]{:S(2)}) async-start(bf16[8,2,64,1024]{3,2,1,0:T(8,128)(2,1)} %get-tuple-element.76), calls=%async_computation.3 | async-start | bytes 4194304 | tf_op jit(solution)/shard_map/all_to_all | solution.py:291
  168.1 3.3 %slice_bitcast_fusion = (bf16[8,64,1024]{2,1,0:T(8,128)(2,1)}, bf16[8,64,1024]{2,1,0:T(8,128)(2,1)}) fusion(bf16[8,2,64,1024]{3,2,1,0:T(8,128)(2,1)} %copy-done.12), kind=kLoop, calls=%fused_computation.1 | loop fusion | bytes 4194304 | tf_op jit(solution)/shard_map/squeeze | solution.py:409
  172.5 1.5 collective-permute-start.15
  173.9 1.5 collective-permute-start.20
  175.5 2.8 %collective-permute-start.21 = (bf16[256,4096]{1,0:T(8,128)(2,1)}, bf16[256,4096]{1,0:T(8,128)(2,1)}, u32[]{:S(2)}, u32[]{:S(2)}) collective-permute-start(bf16[256,4096]{1,0:T(8,128)(2,1)} %collective-permute-done.9.refs_3_), channel_id=1, source_target_pairs={{0,1},{1,0},{2,3},{3,2},{4,5},{5,4},{6,7},{7,6},{8,9},{9,8},{10,11... | collective-permute-start | bytes 6291464 | tf_op jit(solution)/shard_map/ppermute | solution.py:406
  178.3 16.4 %local_part.1 = (f32[1024,512]{1,0:T(8,128)S(1)}, f32[1024,128]{1,0:T(8,128)S(1)}) custom-call(s32[1]{0:T(128)} %bitcast.1.z_ref.refs_0_.refs_1_, s32[64]{0:T(128)S(1)} %broadcast_add_fusion.refs_1_.refs_2_, s32[1]{0:T(128)} %bitcast.2.refs_2_, bf16[1024,512]{1,0:T(8,128)(2,1)S(1)} %copy-done.1, bf16[1152,1024]{1,0:T(8,128)(2,1)S(1)} %copy-done, ...), custom_call_target="tpu_custom_call" | custom-call | flops 24999999488 | bytes 4194304 | tf_op jit(solution)/shard_map/local_part/pallas_call | solution.py:157
  194.7 1.3 copy-done.8
  197.2 7.0 %all-to-all-start.4 = ((bf16[8,64,1024]{2,1,0:T(8,128)(2,1)}), bf16[8,64,1024]{2,1,0:T(8,128)(2,1)S(1)}, u32[]{:S(2)}, u32[]{:S(2)}) async-start(bf16[8,64,1024]{2,1,0:T(8,128)(2,1)} %pad_maximum_fusion.1), calls=%async_computation.4 | async-start | bytes 2097152 | tf_op jit(solution)/shard_map/all_to_all | solution.py:291
  205.5 1.6 copy-done.9
  208.1 10.4 %more_part.1 = (f32[1024,512]{1,0:T(8,128)S(1)}, f32[1024,128]{1,0:T(8,128)S(1)}) custom-call(s32[1]{0:T(128)} %bitcast.1.z_ref.refs_0_.refs_1_, s32[64]{0:T(128)S(1)} %broadcast_add_fusion.refs_1_.refs_2_, bf16[1024,512]{1,0:T(8,128)(2,1)S(1)} %copy-done.2, f32[1024,512]{1,0:T(8,128)S(1)} %copy-done.9, f32[1024,128]{1,0:T(8,128)S(1)} %copy-done.11, ...), custom_call_target="tpu_custom_call" | custom-call | flops 12000000000 | bytes 4194304 | tf_op jit(solution)/shard_map/more_part/pallas_call | solution.py:173
  218.5 1.3 copy-done.4
  221.9 1.6 copy-done.5
  224.5 4.2 %final_part.1 = (bf16[256,512]{1,0:T(8,128)(2,1)S(1)}, bf16[256,512]{1,0:T(8,128)(2,1)S(1)}, bf16[256,512]{1,0:T(8,128)(2,1)S(1)}, bf16[256,512]{1,0:T(8,128)(2,1)S(1)}) custom-call(s32[1]{0:T(128)} %bitcast.refs_0_, s32[1]{0:T(128)} %bitcast.1.z_ref.refs_0_.refs_1_, s32[64]{0:T(128)S(1)} %broadcast_add_fusion.refs_1_.refs_2_, ...), custom_call_target="tpu_custom_call" | custom-call | flops 6000000000 | bytes 4194304 | tf_op jit(solution)/shard_map/final_part/pallas_call | solution.py:190
  228.7 1.8 collective-permute-start.24
  230.5 1.7 collective-permute-start.23
  232.3 4.5 %project.2.refs_6_ = f32[256,4096]{1,0:T(8,128)S(1)} custom-call(bf16[256,512]{1,0:T(8,128)(2,1)S(1)} %get-tuple-element.88.refs_0_, bf16[256,512]{1,0:T(8,128)(2,1)S(1)} %collective-permute-done.24.refs_1_, bf16[256,4096]{1,0:T(8,128)(2,1)} %get-tuple-element.94.refs_2_, bf16[256,4096]{1,0:T(8,128)(2,1)} %get-tuple-element.93.refs_3_, ...), custom_call_target="tpu_custom_call" | custom-call | flops 6000000000 | bytes 4194304 | tf_op jit(solution)/shard_map/project/pallas_call | solution.py:270
  236.8 1.6 collective-permute-done.22.refs_0_
  238.4 5.8 %collective-permute-done.23.refs_1_ = bf16[256,512]{1,0:T(8,128)(2,1)S(1)} collective-permute-done((bf16[256,512]{1,0:T(8,128)(2,1)S(1)}, bf16[256,512]{1,0:T(8,128)(2,1)S(1)}, u32[]{:S(2)}, u32[]{:S(2)}) %collective-permute-start.23) | collective-permute-done | bytes 262176 | tf_op jit(solution)/shard_map/ppermute | solution.py:428
  244.2 5.8 %project.3 = bf16[256,4096]{1,0:T(8,128)(2,1)} custom-call(bf16[256,512]{1,0:T(8,128)(2,1)S(1)} %collective-permute-done.22.refs_0_, bf16[256,512]{1,0:T(8,128)(2,1)S(1)} %collective-permute-done.23.refs_1_, bf16[256,4096]{1,0:T(8,128)(2,1)} %collective-permute-done.8.refs_2_, bf16[256,4096]{1,0:T(8,128)(2,1)} %collective-permute-done.9.refs_3_, ...), custom_call_target="tpu_custom_call" | custom-call | flops 6000000000 | bytes 4194304 | tf_op jit(solution)/shard_map/project/pallas_call | solution.py:270
  (79 shorter events, 12.5 us)
Async XLA Ops:
  1.1 12.3 %copy-start.15 = (s32[16,2]{0,1:T(2,128)S(1)}, s32[16,2]{0,1:T(2,128)}, u32[]{:S(2)}) copy-start(s32[16,2]{0,1:T(2,128)} %param.6) | copy-start | bytes 388
  1.1 12.5 %collective-permute-start.5 = (bf16[64,1024]{1,0:T(8,128)(2,1)S(1)}, bf16[64,1024]{1,0:T(8,128)(2,1)S(1)}, u32[]{:S(2)}, u32[]{:S(2)}) collective-permute-start(bf16[64,1024]{1,0:T(8,128)(2,1)S(1)} %bitcast.23), channel_id=1, source_target_pairs={{0,128},{252,124},{1,129},{253,125},{2,130},{254,126},{3,131},{255... | collective-permute-start | bytes 393224 | tf_op jit(solution)/shard_map/ppermute | solution.py:302
  6.8 60.0 %collective-permute-start.2 = (bf16[64,1024]{1,0:T(8,128)(2,1)S(1)}, bf16[64,1024]{1,0:T(8,128)(2,1)S(1)}, u32[]{:S(2)}, u32[]{:S(2)}) collective-permute-start(bf16[64,1024]{1,0:T(8,128)(2,1)S(1)} %bitcast.24), channel_id=1, source_target_pairs={{28,32},{60,64},{92,96},{124,128},{156,160},{188,192},{220,224},{3... | collective-permute-start | bytes 393224 | tf_op jit(solution)/shard_map/ppermute | solution.py:368
  10.7 56.1 %collective-permute-start.1 = (bf16[16,64,1024]{2,1,0:T(8,128)(2,1)S(1)}, bf16[16,64,1024]{2,1,0:T(8,128)(2,1)}, u32[]{:S(2)}, u32[]{:S(2)}) collective-permute-start(bf16[16,64,1024]{2,1,0:T(8,128)(2,1)S(1)} %reshape.122.refs_0_), channel_id=1, source_target_pairs={{0,28},{4,0},{8,4},{12,8},{16,12},{20,16},{24,20},{28,24},{1,29},{... | collective-permute-start | bytes 6291464 | tf_op jit(solution)/shard_map/ppermute | solution.py:287
  13.5 53.3 %collective-permute-start = (bf16[16,64,1024]{2,1,0:T(8,128)(2,1)S(1)}, bf16[16,64,1024]{2,1,0:T(8,128)(2,1)}, u32[]{:S(2)}, u32[]{:S(2)}) collective-permute-start(bf16[16,64,1024]{2,1,0:T(8,128)(2,1)S(1)} %reshape.122.refs_0_), channel_id=1, source_target_pairs={{0,4},{4,8},{8,12},{12,16},{16,20},{20,24},{24,28},{28,0},{1,5},{5... | collective-permute-start | bytes 6291464 | tf_op jit(solution)/shard_map/ppermute | solution.py:287
  13.7 8.9 %collective-permute-start.6 = (bf16[64,1024]{1,0:T(8,128)(2,1)S(1)}, bf16[64,1024]{1,0:T(8,128)(2,1)S(1)}, u32[]{:S(2)}, u32[]{:S(2)}) collective-permute-start(bf16[64,1024]{1,0:T(8,128)(2,1)S(1)} %broadcast_select_fusion.5), channel_id=1, source_target_pairs={{0,64},{128,192},{252,188},{124,60},{1,65},{129,193},{253,189},{12... | collective-permute-start | bytes 393224 | tf_op jit(solution)/shard_map/ppermute | solution.py:302
  22.7 9.6 %collective-permute-start.7 = (bf16[64,1024]{1,0:T(8,128)(2,1)S(1)}, bf16[64,1024]{1,0:T(8,128)(2,1)S(1)}, u32[]{:S(2)}, u32[]{:S(2)}) collective-permute-start(bf16[64,1024]{1,0:T(8,128)(2,1)S(1)} %broadcast_select_fusion.6), channel_id=1, source_target_pairs={{0,32},{64,96},{128,160},{192,224},{252,220},{188,156},{124,92},{6... | collective-permute-start | bytes 393224 | tf_op jit(solution)/shard_map/ppermute | solution.py:302
  25.0 41.8 %all-to-all-start = ((s32[64,1,8]{2,1,0:T(1,128)}), s32[64,1,8]{2,1,0:T(1,128)S(1)}, u32[]{:S(2)}, u32[]{:S(2)}) async-start(s32[64,1,8]{2,1,0:T(1,128)} %bitcast.3), calls=%async_computation | async-start | bytes 65536 | tf_op jit(solution)/shard_map/all_to_all | solution.py:358
  37.0 47.3 %collective-permute-start.9 = (bf16[256,4096]{1,0:T(8,128)(2,1)}, bf16[256,4096]{1,0:T(8,128)(2,1)}, u32[]{:S(2)}, u32[]{:S(2)}) collective-permute-start(bf16[256,4096]{1,0:T(8,128)(2,1)} %get-tuple-element.93.refs_3_), channel_id=1, source_target_pairs={{0,34},{2,0},{32,2},{34,32},{1,35},{3,1},{33,3},{35,33},{4,38},{6,... | collective-permute-start | bytes 6291464 | tf_op jit(solution)/shard_map/ppermute | solution.py:366
  40.2 47.3 %collective-permute-start.8 = (bf16[256,4096]{1,0:T(8,128)(2,1)}, bf16[256,4096]{1,0:T(8,128)(2,1)}, u32[]{:S(2)}, u32[]{:S(2)}) collective-permute-start(bf16[256,4096]{1,0:T(8,128)(2,1)} %get-tuple-element.94.refs_2_), channel_id=1, source_target_pairs={{0,2},{2,32},{32,34},{34,0},{1,3},{3,33},{33,35},{35,1},{4,6},{6,3... | collective-permute-start | bytes 6291464 | tf_op jit(solution)/shard_map/ppermute | solution.py:365
  66.8 46.3 %collective-permute-start.3 = (bf16[16,64,1024]{2,1,0:T(8,128)(2,1)}, bf16[16,64,1024]{2,1,0:T(8,128)(2,1)}, u32[]{:S(2)}, u32[]{:S(2)}) collective-permute-start(bf16[16,64,1024]{2,1,0:T(8,128)(2,1)} %collective-permute-done.refs_1_), channel_id=1, source_target_pairs={{0,4},{4,8},{8,12},{12,16},{16,20},{20,24},{24,28},{28,0},{1,5},{5... | collective-permute-start | bytes 6291464 | tf_op jit(solution)/shard_map/ppermute | solution.py:287
  68.1 45.0 %collective-permute-start.4 = (bf16[16,64,1024]{2,1,0:T(8,128)(2,1)}, bf16[16,64,1024]{2,1,0:T(8,128)(2,1)}, u32[]{:S(2)}, u32[]{:S(2)}) collective-permute-start(bf16[16,64,1024]{2,1,0:T(8,128)(2,1)} %collective-permute-done.1.refs_2_), channel_id=1, source_target_pairs={{0,28},{4,0},{8,4},{12,8},{16,12},{20,16},{24,20},{28,24},{1,29},{... | collective-permute-start | bytes 6291464 | tf_op jit(solution)/shard_map/ppermute | solution.py:287
  75.6 45.7 %all-to-all-start.1 = ((bf16[8,3,64,1024]{3,2,1,0:T(8,128)(2,1)}), bf16[8,3,64,1024]{3,2,1,0:T(8,128)(2,1)}, u32[]{:S(2)}, u32[]{:S(2)}) async-start(bf16[8,3,64,1024]{3,2,1,0:T(8,128)(2,1)} %pick.2), calls=%async_computation.1 | async-start | bytes 6291456 | tf_op jit(solution)/shard_map/all_to_all | solution.py:291
  121.3 24.1 %all-to-all-start.2 = ((bf16[8,2,64,1024]{3,2,1,0:T(8,128)(2,1)}), bf16[8,2,64,1024]{3,2,1,0:T(8,128)(2,1)S(1)}, u32[]{:S(2)}, u32[]{:S(2)}) async-start(bf16[8,2,64,1024]{3,2,1,0:T(8,128)(2,1)} %get-tuple-element.64), calls=%async_computation.2 | async-start | bytes 4194304 | tf_op jit(solution)/shard_map/all_to_all | solution.py:291
  124.9 9.0 %collective-permute-start.12 = (bf16[64,1024]{1,0:T(8,128)(2,1)S(1)}, bf16[64,1024]{1,0:T(8,128)(2,1)S(1)}, u32[]{:S(2)}, u32[]{:S(2)}) collective-permute-start(bf16[64,1024]{1,0:T(8,128)(2,1)S(1)} %broadcast_select_fusion.7), channel_id=1, source_target_pairs={{0,16},{28,12},{1,17},{29,13},{2,18},{30,14},{3,19},{31,15},{32,48... | collective-permute-start | bytes 393224 | tf_op jit(solution)/shard_map/ppermute | solution.py:395
  133.9 4.1 %collective-permute-start.13 = (bf16[64,1024]{1,0:T(8,128)(2,1)S(1)}, bf16[64,1024]{1,0:T(8,128)(2,1)S(1)}, u32[]{:S(2)}, u32[]{:S(2)}) collective-permute-start(bf16[64,1024]{1,0:T(8,128)(2,1)S(1)} %broadcast_select_fusion.1), channel_id=1, source_target_pairs={{0,8},{16,24},{28,20},{12,4},{1,9},{17,25},{29,21},{13,5},{2,10},{... | collective-permute-start | bytes 393224 | tf_op jit(solution)/shard_map/ppermute | solution.py:397
  135.2 10.2 %collective-permute-start.10 = (bf16[4,64,1024]{2,1,0:T(8,128)(2,1)}, bf16[4,64,1024]{2,1,0:T(8,128)(2,1)}, u32[]{:S(2)}, u32[]{:S(2)}) collective-permute-start(bf16[4,64,1024]{2,1,0:T(8,128)(2,1)} %get-tuple-element.65), channel_id=1, source_target_pairs={{0,4},{4,8},{8,12},{12,16},{16,20},{20,24},{24,28},{28,0},{1,5},{5... | collective-permute-start | bytes 1572872 | tf_op jit(solution)/shard_map/ppermute | solution.py:287
  135.3 10.1 %collective-permute-start.11 = (bf16[4,64,1024]{2,1,0:T(8,128)(2,1)}, bf16[4,64,1024]{2,1,0:T(8,128)(2,1)S(1)}, u32[]{:S(2)}, u32[]{:S(2)}) collective-permute-start(bf16[4,64,1024]{2,1,0:T(8,128)(2,1)} %get-tuple-element.66), channel_id=1, source_target_pairs={{0,28},{4,0},{8,4},{12,8},{16,12},{20,16},{24,20},{28,24},{1,29},{... | collective-permute-start | bytes 1572872 | tf_op jit(solution)/shard_map/ppermute | solution.py:287
  138.0 7.3 %collective-permute-start.14 = (bf16[64,1024]{1,0:T(8,128)(2,1)S(1)}, bf16[64,1024]{1,0:T(8,128)(2,1)S(1)}, u32[]{:S(2)}, u32[]{:S(2)}) collective-permute-start(bf16[64,1024]{1,0:T(8,128)(2,1)S(1)} %broadcast_select_fusion.2), channel_id=1, source_target_pairs={{0,4},{4,0},{8,12},{12,8},{16,20},{20,16},{24,28},{28,24},{1,5},{5... | collective-permute-start | bytes 393224 | tf_op jit(solution)/shard_map/ppermute | solution.py:400
  145.4 13.1 %copy-start.16 = (bf16[4,64,1024]{2,1,0:T(8,128)(2,1)}, bf16[4,64,1024]{2,1,0:T(8,128)(2,1)S(1)}, u32[]{:S(2)}) copy-start(bf16[4,64,1024]{2,1,0:T(8,128)(2,1)S(1)} %collective-permute-done.11) | copy-start | bytes 1572868
  145.4 15.7 %copy-start.12 = (bf16[8,2,64,1024]{3,2,1,0:T(8,128)(2,1)}, bf16[8,2,64,1024]{3,2,1,0:T(8,128)(2,1)S(1)}, u32[]{:S(2)}) copy-start(bf16[8,2,64,1024]{3,2,1,0:T(8,128)(2,1)S(1)} %all-to-all-done.2) | copy-start | bytes 6291460
  145.4 51.8 %collective-permute-start.19 = (bf16[512,4096]{1,0:T(8,128)(2,1)}, bf16[512,4096]{1,0:T(8,128)(2,1)}, u32[]{:S(2)}, u32[]{:S(2)}) collective-permute-start(bf16[512,4096]{1,0:T(8,128)(2,1)} %param.7), channel_id=1, source_target_pairs={{0,1},{1,0},{2,3},{3,2},{4,5},{5,4},{6,7},{7,6},{8,9},{9,8},{10,11... | collective-permute-start | bytes 12582920 | tf_op jit(solution)/shard_map/ppermute | solution.py:406
  158.5 15.4 %collective-permute-start.17 = (bf16[4,64,1024]{2,1,0:T(8,128)(2,1)}, bf16[4,64,1024]{2,1,0:T(8,128)(2,1)S(1)}, u32[]{:S(2)}, u32[]{:S(2)}) collective-permute-start(bf16[4,64,1024]{2,1,0:T(8,128)(2,1)} %collective-permute-done.10), channel_id=1, source_target_pairs={{0,4},{4,8},{8,12},{12,16},{16,20},{20,24},{24,28},{28,0},{1,5},{5... | collective-permute-start | bytes 1572872 | tf_op jit(solution)/shard_map/ppermute | solution.py:287
  160.6 14.9 %collective-permute-start.18 = (bf16[4,64,1024]{2,1,0:T(8,128)(2,1)}, bf16[4,64,1024]{2,1,0:T(8,128)(2,1)S(1)}, u32[]{:S(2)}, u32[]{:S(2)}) collective-permute-start(bf16[4,64,1024]{2,1,0:T(8,128)(2,1)} %copy-done.16), channel_id=1, source_target_pairs={{0,28},{4,0},{8,4},{12,8},{16,12},{20,16},{24,20},{28,24},{1,29},{... | collective-permute-start | bytes 1572872 | tf_op jit(solution)/shard_map/ppermute | solution.py:287
  161.2 36.0 %all-to-all-start.3 = ((bf16[8,2,64,1024]{3,2,1,0:T(8,128)(2,1)}), bf16[8,2,64,1024]{3,2,1,0:T(8,128)(2,1)S(1)}, u32[]{:S(2)}, u32[]{:S(2)}) async-start(bf16[8,2,64,1024]{3,2,1,0:T(8,128)(2,1)} %get-tuple-element.76), calls=%async_computation.3 | async-start | bytes 4194304 | tf_op jit(solution)/shard_map/all_to_all | solution.py:291
  168.1 10.2 %copy-start = (bf16[1152,1024]{1,0:T(8,128)(2,1)S(1)}, bf16[1152,1024]{1,0:T(8,128)(2,1)}, u32[]{:S(2)}) copy-start(bf16[1152,1024]{1,0:T(8,128)(2,1)} %pad_maximum_fusion.refs_4_) | copy-start | bytes 7077892
  168.1 10.2 %copy-start.1 = (bf16[1024,512]{1,0:T(8,128)(2,1)S(1)}, bf16[1024,512]{1,0:T(8,128)(2,1)}, u32[]{:S(2)}) copy-start(bf16[1024,512]{1,0:T(8,128)(2,1)} %refs_3_.3) | copy-start | bytes 3145732
  171.4 32.9 %collective-permute-start.16 = (bf16[8,64,1024]{2,1,0:T(8,128)(2,1)}, bf16[8,64,1024]{2,1,0:T(8,128)(2,1)}, u32[]{:S(2)}, u32[]{:S(2)}) collective-permute-start(bf16[8,64,1024]{2,1,0:T(8,128)(2,1)} %get-tuple-element.95), channel_id=1, source_target_pairs={{0,28},{4,0},{8,4},{12,8},{16,12},{20,16},{24,20},{28,24},{1,29},{... | collective-permute-start | bytes 3145736 | tf_op jit(solution)/shard_map/ppermute | solution.py:287
  172.5 31.8 %collective-permute-start.15 = (bf16[8,64,1024]{2,1,0:T(8,128)(2,1)}, bf16[8,64,1024]{2,1,0:T(8,128)(2,1)}, u32[]{:S(2)}, u32[]{:S(2)}) collective-permute-start(bf16[8,64,1024]{2,1,0:T(8,128)(2,1)} %get-tuple-element.96), channel_id=1, source_target_pairs={{0,4},{4,8},{8,12},{12,16},{16,20},{20,24},{24,28},{28,0},{1,5},{5... | collective-permute-start | bytes 3145736 | tf_op jit(solution)/shard_map/ppermute | solution.py:287
  173.9 23.3 %collective-permute-start.20 = (bf16[256,4096]{1,0:T(8,128)(2,1)}, bf16[256,4096]{1,0:T(8,128)(2,1)}, u32[]{:S(2)}, u32[]{:S(2)}) collective-permute-start(bf16[256,4096]{1,0:T(8,128)(2,1)} %collective-permute-done.8.refs_2_), channel_id=1, source_target_pairs={{0,1},{1,0},{2,3},{3,2},{4,5},{5,4},{6,7},{7,6},{8,9},{9,8},{10,11... | collective-permute-start | bytes 6291464 | tf_op jit(solution)/shard_map/ppermute | solution.py:406
  175.5 2.8 %copy-start.13 = (bf16[4,64,1024]{2,1,0:T(8,128)(2,1)}, bf16[4,64,1024]{2,1,0:T(8,128)(2,1)S(1)}, u32[]{:S(2)}) copy-start(bf16[4,64,1024]{2,1,0:T(8,128)(2,1)S(1)} %collective-permute-done.18) | copy-start | bytes 1572868
  175.5 21.7 %collective-permute-start.21 = (bf16[256,4096]{1,0:T(8,128)(2,1)}, bf16[256,4096]{1,0:T(8,128)(2,1)}, u32[]{:S(2)}, u32[]{:S(2)}) collective-permute-start(bf16[256,4096]{1,0:T(8,128)(2,1)} %collective-permute-done.9.refs_3_), channel_id=1, source_target_pairs={{0,1},{1,0},{2,3},{3,2},{4,5},{5,4},{6,7},{7,6},{8,9},{9,8},{10,11... | collective-permute-start | bytes 6291464 | tf_op jit(solution)/shard_map/ppermute | solution.py:406
  178.3 17.7 %copy-start.14 = (bf16[4,64,1024]{2,1,0:T(8,128)(2,1)S(1)}, bf16[4,64,1024]{2,1,0:T(8,128)(2,1)}, u32[]{:S(2)}) copy-start(bf16[4,64,1024]{2,1,0:T(8,128)(2,1)} %copy-done.13) | copy-start | bytes 1572868
  194.7 1.3 copy-start.8
  196.0 1.2 copy-start.10
  197.2 23.4 %all-to-all-start.4 = ((bf16[8,64,1024]{2,1,0:T(8,128)(2,1)}), bf16[8,64,1024]{2,1,0:T(8,128)(2,1)S(1)}, u32[]{:S(2)}, u32[]{:S(2)}) async-start(bf16[8,64,1024]{2,1,0:T(8,128)(2,1)} %pad_maximum_fusion.1), calls=%async_computation.4 | async-start | bytes 2097152 | tf_op jit(solution)/shard_map/all_to_all | solution.py:291
  204.3 1.2 copy-start.2
  205.5 1.6 copy-start.9
  207.1 1.0 copy-start.11
  218.5 1.3 copy-start.4
  219.8 0.8 copy-start.6
  220.7 1.2 copy-start.3
  221.9 1.6 copy-start.5
  223.5 1.0 copy-start.7
  228.7 3.6 %collective-permute-start.24 = (bf16[256,512]{1,0:T(8,128)(2,1)S(1)}, bf16[256,512]{1,0:T(8,128)(2,1)S(1)}, u32[]{:S(2)}, u32[]{:S(2)}) collective-permute-start(bf16[256,512]{1,0:T(8,128)(2,1)S(1)} %get-tuple-element.89), channel_id=1, source_target_pairs={{0,1},{1,0},{2,3},{3,2},{4,5},{5,4},{6,7},{7,6},{8,9},{9,8},{10,11... | collective-permute-start | bytes 786440 | tf_op jit(solution)/shard_map/ppermute | solution.py:429
  230.5 7.9 %collective-permute-start.22 = (bf16[256,512]{1,0:T(8,128)(2,1)S(1)}, bf16[256,512]{1,0:T(8,128)(2,1)S(1)}, u32[]{:S(2)}, u32[]{:S(2)}) collective-permute-start(bf16[256,512]{1,0:T(8,128)(2,1)S(1)} %get-tuple-element.84), channel_id=1, source_target_pairs={{0,2},{1,3},{2,0},{3,1},{4,6},{5,7},{6,4},{7,5},{8,10},{9,11},{10,... | collective-permute-start | bytes 786440 | tf_op jit(solution)/shard_map/ppermute | solution.py:428
  230.5 13.7 %collective-permute-start.23 = (bf16[256,512]{1,0:T(8,128)(2,1)S(1)}, bf16[256,512]{1,0:T(8,128)(2,1)S(1)}, u32[]{:S(2)}, u32[]{:S(2)}) collective-permute-start(bf16[256,512]{1,0:T(8,128)(2,1)S(1)} %get-tuple-element.85), channel_id=1, source_target_pairs={{0,3},{1,2},{2,1},{3,0},{4,7},{5,6},{6,5},{7,4},{8,11},{9,10},{10,... | collective-permute-start | bytes 786440 | tf_op jit(solution)/shard_map/ppermute | solution.py:428

commit v9 on v8

--- a/solution.py
+++ b/solution.py
@@ -378,7 +378,9 @@
     before = jnp.where(z == 0, crossed, up1[blocks_dev - 1])
     after = jnp.where(z == NZ - 1, crossed, down1[0])
     kv_pad = jnp.concatenate([before, kv_late.reshape(tok, 2 * feat), after], axis=0)
-    up2, down2, kv_pad, w_core, low, high = tie(up2, down2, kv_pad, w_out, low, high)
+    swap = [(0, 1), (1, 0)]
+    w_core = lax.ppermute(w_out, "core", swap)
+    up2, down2, kv_pad, w_core, low, high = tie(up2, down2, kv_pad, w_core, low, high)
 
     plan = [(0, (lane, 0), 0, lane, 1, -2) for lane in lanes]
     plan += [(0, (lane, 1), 1, lane, -1, 2) for lane in lanes]
@@ -401,9 +403,8 @@
     even = z % 2 == 0
     ends = jnp.concatenate([jnp.where(even, held, got), jnp.where(even, got, held)], axis=0)
     c2, c3, fu, fd, ends = tie(c2, c3, fu, fd, ends)
-    low, high, w_core, ends = tie(low, high, w_core, ends)
-    swap = [(0, 1), (1, 0)]
-    others = [lax.ppermute(x, "core", swap) for x in (w_core, low, high)]
+    low, high, ends = tie(low, high, ends)
+    others = [w_core] + [lax.ppermute(x, "core", swap) for x in (low, high)]
     r2 = lane_exchange(c2)
     fu, fd = z_shift(fu, 1), z_shift(fd, -1)
     r3u, r3d = z_shift(c3[:, 0], 1), z_shift(c3[:, 1], -1)

time: 252 us -> 272 us (1.079)
  starting transfers between devices: 93.6 us -> 106 us
  waiting for transfers between devices: 73.1 us -> 83.7 us
  local copies, waits for them, and re-layouts: 23.5 us -> 18.4 us
    ppermute x1, waiting for transfers between devices: 1.6 us -> 48.3 us  [body(): lax.ppermute(own[1], XRING, [(i, (i - 1) % ring) for i in range(ring)])]
    ppermute x10, waiting for transfers between devices: 25.6 us -> 0.03 us  [z_shift(): return lax.ppermute(x, 'z', [(i, (i + by) % NZ) for i in range(NZ)])]
    all_to_all x1, waiting for transfers between devices: 26.6 us -> 1.71 us  [body(): asked = lax.all_to_all(asked, SEQ, split_axis=0, concat_axis=0, tiled=True)]
    ppermute x1, starting transfers between devices: 3.15 us -> 19.1 us  [body(): lax.ppermute(own[1], XRING, [(i, (i - 1) % ring) for i in range(ring)])]
    ppermute x1, waiting for transfers between devices: 3.14 us -> 11.9 us  [body(): lax.ppermute(own[0], XRING, [(i, (i + 1) % ring) for i in range(ring)])]
    ppermute x3, starting transfers between devices: 17.3 us -> 9.17 us  [the longest x2 7.28 us: body(): others = [w_core] + [lax.ppermute(x, 'core', swap) for x in (low, high)]]
    ppermute x10, starting transfers between devices: 13.5 us -> 21 us  [z_shift(): return lax.ppermute(x, 'z', [(i, (i + by) % NZ) for i in range(NZ)])]
    ppermute x1, starting transfers between devices: 7.03 us -> 1.3 us  [body(): got = lax.ppermute(held, 'z', [(0, 4), (7, 3)])]
  transfers between devices with their start and end apart: 30 -> 30, of which waited for: 10 -> 10; matrix products, arithmetic and copies ran while one was open for 7% -> 5% of each run, Pallas kernels for 18% -> 17%
where the time goes in v9:
time: 272 us; the launch traced here: 270 us
  starting transfers between devices  106 us (39%)
  waiting for transfers between devices  83.7 us (31%)
  Pallas kernels  54.6 us (20%)
  local copies, waits for them, and re-layouts  18.4 us (7%)
  other arithmetic  6.28 us (2%)
    ppermute x1, waiting for transfers between devices, body(): lax.ppermute(own[1], XRING, [(i, (i - 1) % ring) for i in range(ring)])  48.3 us
    ppermute x10, starting transfers between devices, z_shift(): return lax.ppermute(x, 'z', [(i, (i + by) % NZ) for i in range(NZ)])  21 us
    ppermute x1, starting transfers between devices, body(): lax.ppermute(own[1], XRING, [(i, (i - 1) % ring) for i in range(ring)])  19.1 us
    all_to_all x4, starting transfers between devices, lane_exchange(): return lax.all_to_all(x, LANE, split_axis=0, concat_axis=0, tiled=True)  18.5 us
    pallas_call x1, Pallas kernels, local_part(): pl.pallas_call(lambda *refs: local_kernel(all_blocks, deltas, *refs), out...  17.9 us
    pallas_call x2, Pallas kernels, pick(): pl.pallas_call(kernel, out_shape=tuple((pltpu.HBM(shape + block_shape, BF...  12.4 us
    ppermute x3, starting transfers between devices, spread_lanes(): got = lax.ppermute(held, SEQ, moves)  12.4 us
    ppermute x1, waiting for transfers between devices, body(): lax.ppermute(own[0], XRING, [(i, (i + 1) % ring) for i in range(ring)])  11.9 us
  transfers between devices with their start and end apart: 30, of which 10 were waited for; matrix products, arithmetic and copies ran while one was open for 5% of the time, Pallas kernels for 17%

profile of v9, /device:TPU:1, one launch (start us, length us, event | category | flops | bytes accessed | tf_op | source)
XLA Modules:
  0.0 269.8 jit_solution(10367159898953967647)
XLA Ops:
  0.0 3.2 %reshape.122.refs_0_ = bf16[16,64,1024]{2,1,0:T(8,128)(2,1)S(1)} reshape(bf16[1024,2,512]{2,1,0:T(2,128)(2,1)} %param.5) | data formatting | bytes 4194304 | tf_op jit(solution)/shard_map/reshape | solution.py:352
  3.3 2.5 collective-permute-start
  5.8 4.0 %collective-permute-start.1 = (bf16[16,64,1024]{2,1,0:T(8,128)(2,1)S(1)}, bf16[16,64,1024]{2,1,0:T(8,128)(2,1)}, u32[]{:S(2)}, u32[]{:S(2)}) collective-permute-start(bf16[16,64,1024]{2,1,0:T(8,128)(2,1)S(1)} %reshape.122.refs_0_), channel_id=1, source_target_pairs={{0,28},{4,0},{8,4},{12,8},{16,12},{20,16},{24,20},{28,24},{1,29},{... | collective-permute-start | bytes 6291464 | tf_op jit(solution)/shard_map/ppermute | solution.py:287
  11.6 9.8 %collective-permute-start.6 = (bf16[64,1024]{1,0:T(8,128)(2,1)S(1)}, bf16[64,1024]{1,0:T(8,128)(2,1)S(1)}, u32[]{:S(2)}, u32[]{:S(2)}) collective-permute-start(bf16[64,1024]{1,0:T(8,128)(2,1)S(1)} %bitcast.24), channel_id=1, source_target_pairs={{0,128},{252,124},{1,129},{253,125},{2,130},{254,126},{3,131},{255... | collective-permute-start | bytes 393224 | tf_op jit(solution)/shard_map/ppermute | solution.py:302
  21.4 1.9 collective-permute-start.5
  24.9 1.9 collective-permute-done.7
  26.8 1.3 collective-permute-start.8
  29.2 7.4 %all-to-all-start = ((s32[64,1,8]{2,1,0:T(1,128)}), s32[64,1,8]{2,1,0:T(1,128)S(1)}, u32[]{:S(2)}, u32[]{:S(2)}) async-start(s32[64,1,8]{2,1,0:T(1,128)} %bitcast.3), calls=%async_computation | async-start | bytes 65536 | tf_op jit(solution)/shard_map/all_to_all | solution.py:358
  36.7 4.7 %fusion.4 = (bf16[256,4096]{1,0:T(8,128)(2,1)}, bf16[256,4096]{1,0:T(8,128)(2,1)}) fusion(bf16[512,4096]{1,0:T(8,128)(2,1)} %param.7), kind=kLoop, calls=%fused_computation.36 | loop fusion | bytes 8388608 | tf_op jit(solution)/shard_map/slice | solution.py:363
  42.5 19.1 %collective-permute-start.10 = (bf16[256,4096]{1,0:T(8,128)(2,1)}, bf16[256,4096]{1,0:T(8,128)(2,1)}, u32[]{:S(2)}, u32[]{:S(2)}) collective-permute-start(bf16[256,4096]{1,0:T(8,128)(2,1)} %get-tuple-element.91.refs_3_), channel_id=1, source_target_pairs={{0,34},{2,0},{32,2},{34,32},{1,35},{3,1},{33,3},{35,33},{4,38},{6,... | collective-permute-start | bytes 6291464 | tf_op jit(solution)/shard_map/ppermute | solution.py:366
  61.6 1.7 all-to-all-done
  64.5 1.5 collective-permute-start.4
  66.0 5.7 %pick.2 = bf16[8,3,64,1024]{3,2,1,0:T(8,128)(2,1)} custom-call(s32[1]{0:T(128)} %bitcast.1.z_ref.refs_0_.refs_1_, s32[64,8]{1,0:T(8,128)S(1)} %bitcast.21, bf16[16,64,1024]{2,1,0:T(8,128)(2,1)S(1)} %reshape.122.refs_0_, bf16[16,64,1024]{2,1,0:T(8,128)(2,1)} %collective-permute-done.refs_1_, bf16[16,64,1024]{2,1,0:T(8,128)(2,1)} %collective-permute-done.1.refs_2_), custom_call_target="tpu_custom_call" | custom-call | flops 3000000000 | bytes 4194304 | tf_op jit(solution)/shard_map/pick/pallas_call | solution.py:220
  71.7 4.5 %all-to-all-start.1 = ((bf16[8,3,64,1024]{3,2,1,0:T(8,128)(2,1)}), bf16[8,3,64,1024]{3,2,1,0:T(8,128)(2,1)}, u32[]{:S(2)}, u32[]{:S(2)}) async-start(bf16[8,3,64,1024]{3,2,1,0:T(8,128)(2,1)} %pick.2), calls=%async_computation.1 | async-start | bytes 6291456 | tf_op jit(solution)/shard_map/all_to_all | solution.py:291
  77.2 1.7 pad_maximum_fusion.refs_4_
  78.9 11.9 %collective-permute-done.9.refs_2_ = bf16[256,4096]{1,0:T(8,128)(2,1)} collective-permute-done((bf16[256,4096]{1,0:T(8,128)(2,1)}, bf16[256,4096]{1,0:T(8,128)(2,1)}, u32[]{:S(2)}, u32[]{:S(2)}) %collective-permute-start.9) | collective-permute-done | bytes 2097184 | tf_op jit(solution)/shard_map/ppermute | solution.py:365
  90.8 48.3 %collective-permute-done.10.refs_3_ = bf16[256,4096]{1,0:T(8,128)(2,1)} collective-permute-done((bf16[256,4096]{1,0:T(8,128)(2,1)}, bf16[256,4096]{1,0:T(8,128)(2,1)}, u32[]{:S(2)}, u32[]{:S(2)}) %collective-permute-start.10) | collective-permute-done | bytes 2097184 | tf_op jit(solution)/shard_map/ppermute | solution.py:366
  139.1 6.7 %pick.3 = (bf16[8,2,64,1024]{3,2,1,0:T(8,128)(2,1)}, bf16[4,64,1024]{2,1,0:T(8,128)(2,1)}, bf16[4,64,1024]{2,1,0:T(8,128)(2,1)}, bf16[8,2,64,1024]{3,2,1,0:T(8,128)(2,1)}) custom-call(s32[1]{0:T(128)} %bitcast.1.z_ref.refs_0_.refs_1_, s32[64,8]{1,0:T(8,128)S(1)} %bitcast.22, bf16[16,64,1024]{2,1,0:T(8,128)(2,1)} %collective-permute-done.3.refs_0_, ...), custom_call_target="tpu_custom_call" | custom-call | flops 60000002048 | bytes 4194304 | tf_op jit(solution)/shard_map/pick/pallas_call | solution.py:220
  145.9 3.7 %all-to-all-start.2 = ((bf16[8,2,64,1024]{3,2,1,0:T(8,128)(2,1)}), bf16[8,2,64,1024]{3,2,1,0:T(8,128)(2,1)S(1)}, u32[]{:S(2)}, u32[]{:S(2)}) async-start(bf16[8,2,64,1024]{3,2,1,0:T(8,128)(2,1)} %get-tuple-element.62), calls=%async_computation.2 | async-start | bytes 4194304 | tf_op jit(solution)/shard_map/all_to_all | solution.py:291
  149.7 1.3 collective-permute-start.13
  151.0 1.9 collective-permute-done.13
  152.9 1.3 collective-permute-start.14
  154.3 3.7 %collective-permute-start.12 = (bf16[4,64,1024]{2,1,0:T(8,128)(2,1)S(1)}, bf16[4,64,1024]{2,1,0:T(8,128)(2,1)}, u32[]{:S(2)}, u32[]{:S(2)}) collective-permute-start(bf16[4,64,1024]{2,1,0:T(8,128)(2,1)S(1)} %copy-done.10), channel_id=1, source_target_pairs={{0,28},{4,0},{8,4},{12,8},{16,12},{20,16},{24,20},{28,24},{1,29},{... | collective-permute-start | bytes 1572872 | tf_op jit(solution)/shard_map/ppermute | solution.py:287
  158.1 6.3 %collective-permute-start.15 = (bf16[64,1024]{1,0:T(8,128)(2,1)S(1)}, bf16[64,1024]{1,0:T(8,128)(2,1)S(1)}, u32[]{:S(2)}, u32[]{:S(2)}) collective-permute-start(bf16[64,1024]{1,0:T(8,128)(2,1)S(1)} %broadcast_select_fusion.2), channel_id=1, source_target_pairs={{0,4},{4,0},{8,12},{12,8},{16,20},{20,16},{24,28},{28,24},{1,5},{5... | collective-permute-start | bytes 393224 | tf_op jit(solution)/shard_map/ppermute | solution.py:402
  164.4 4.2 %collective-permute-done.15 = bf16[64,1024]{1,0:T(8,128)(2,1)S(1)} collective-permute-done((bf16[64,1024]{1,0:T(8,128)(2,1)S(1)}, bf16[64,1024]{1,0:T(8,128)(2,1)S(1)}, u32[]{:S(2)}, u32[]{:S(2)}) %collective-permute-start.15) | collective-permute-done | bytes 131104 | tf_op jit(solution)/shard_map/ppermute | solution.py:402
  168.7 4.7 %all-to-all-done.2 = bf16[8,2,64,1024]{3,2,1,0:T(8,128)(2,1)S(1)} async-done(((bf16[8,2,64,1024]{3,2,1,0:T(8,128)(2,1)}), bf16[8,2,64,1024]{3,2,1,0:T(8,128)(2,1)S(1)}, u32[]{:S(2)}, u32[]{:S(2)}) %all-to-all-start.2) | async-done | bytes 2097184 | tf_op jit(solution)/shard_map/all_to_all | solution.py:291
  173.4 5.2 %collective-permute-start.19 = (bf16[4,64,1024]{2,1,0:T(8,128)(2,1)}, bf16[4,64,1024]{2,1,0:T(8,128)(2,1)S(1)}, u32[]{:S(2)}, u32[]{:S(2)}) collective-permute-start(bf16[4,64,1024]{2,1,0:T(8,128)(2,1)} %collective-permute-done.12), channel_id=1, source_target_pairs={{0,28},{4,0},{8,4},{12,8},{16,12},{20,16},{24,20},{28,24},{1,29},{... | collective-permute-start | bytes 1572872 | tf_op jit(solution)/shard_map/ppermute | solution.py:287
  178.6 1.6 slice_bitcast_fusion
  180.2 2.7 collective-permute-start.17
  182.9 5.6 %all-to-all-start.3 = ((bf16[8,2,64,1024]{3,2,1,0:T(8,128)(2,1)}), bf16[8,2,64,1024]{3,2,1,0:T(8,128)(2,1)}, u32[]{:S(2)}, u32[]{:S(2)}) async-start(bf16[8,2,64,1024]{3,2,1,0:T(8,128)(2,1)} %get-tuple-element.74), calls=%async_computation.3 | async-start | bytes 4194304 | tf_op jit(solution)/shard_map/all_to_all | solution.py:291
  188.4 3.9 %collective-permute-start.20 = (bf16[256,4096]{1,0:T(8,128)(2,1)}, bf16[256,4096]{1,0:T(8,128)(2,1)}, u32[]{:S(2)}, u32[]{:S(2)}) collective-permute-start(bf16[256,4096]{1,0:T(8,128)(2,1)} %collective-permute-done.9.refs_2_), channel_id=1, source_target_pairs={{0,1},{1,0},{2,3},{3,2},{4,5},{5,4},{6,7},{7,6},{8,9},{9,8},{10,11... | collective-permute-start | bytes 6291464 | tf_op jit(solution)/shard_map/ppermute | solution.py:407
  192.3 3.4 %collective-permute-start.21 = (bf16[256,4096]{1,0:T(8,128)(2,1)}, bf16[256,4096]{1,0:T(8,128)(2,1)}, u32[]{:S(2)}, u32[]{:S(2)}) collective-permute-start(bf16[256,4096]{1,0:T(8,128)(2,1)} %collective-permute-done.10.refs_3_), channel_id=1, source_target_pairs={{0,1},{1,0},{2,3},{3,2},{4,5},{5,4},{6,7},{7,6},{8,9},{9,8},{10,11... | collective-permute-start | bytes 6291464 | tf_op jit(solution)/shard_map/ppermute | solution.py:407
  196.9 17.9 %local_part.1 = (f32[1024,512]{1,0:T(8,128)S(1)}, f32[1024,128]{1,0:T(8,128)S(1)}) custom-call(s32[1]{0:T(128)} %bitcast.1.z_ref.refs_0_.refs_1_, s32[64]{0:T(128)S(1)} %broadcast_add_fusion.refs_1_.refs_2_, s32[1]{0:T(128)} %bitcast.2.refs_2_, bf16[1024,512]{1,0:T(8,128)(2,1)S(1)} %copy-done.1, bf16[1152,1024]{1,0:T(8,128)(2,1)S(1)} %copy-done, ...), custom_call_target="tpu_custom_call" | custom-call | flops 24999999488 | bytes 4194304 | tf_op jit(solution)/shard_map/local_part/pallas_call | solution.py:157
  214.9 1.3 copy-done.5
  217.0 2.2 pad_maximum_fusion.1
  219.2 4.8 %all-to-all-start.4 = ((bf16[8,64,1024]{2,1,0:T(8,128)(2,1)}), bf16[8,64,1024]{2,1,0:T(8,128)(2,1)S(1)}, u32[]{:S(2)}, u32[]{:S(2)}) async-start(bf16[8,64,1024]{2,1,0:T(8,128)(2,1)} %pad_maximum_fusion.1), calls=%async_computation.4 | async-start | bytes 2097152 | tf_op jit(solution)/shard_map/all_to_all | solution.py:291
  224.1 1.6 copy-done.6
  225.6 10.1 %more_part.1 = (f32[1024,512]{1,0:T(8,128)S(1)}, f32[1024,128]{1,0:T(8,128)S(1)}) custom-call(s32[1]{0:T(128)} %bitcast.1.z_ref.refs_0_.refs_1_, s32[64]{0:T(128)S(1)} %broadcast_add_fusion.refs_1_.refs_2_, bf16[1024,512]{1,0:T(8,128)(2,1)S(1)} %copy-done.2, f32[1024,512]{1,0:T(8,128)S(1)} %copy-done.6, f32[1024,128]{1,0:T(8,128)S(1)} %copy-done.8, ...), custom_call_target="tpu_custom_call" | custom-call | flops 12000000000 | bytes 4194304 | tf_op jit(solution)/shard_map/more_part/pallas_call | solution.py:173
  235.8 1.3 copy-done.3
  237.1 1.6 all-to-all-done.4
  238.7 1.6 copy-done.4
  240.3 3.7 %final_part.1 = (bf16[256,512]{1,0:T(8,128)(2,1)S(1)}, bf16[256,512]{1,0:T(8,128)(2,1)S(1)}, bf16[256,512]{1,0:T(8,128)(2,1)S(1)}, bf16[256,512]{1,0:T(8,128)(2,1)S(1)}) custom-call(s32[1]{0:T(128)} %bitcast.refs_0_, s32[1]{0:T(128)} %bitcast.1.z_ref.refs_0_.refs_1_, s32[64]{0:T(128)S(1)} %broadcast_add_fusion.refs_1_.refs_2_, ...), custom_call_target="tpu_custom_call" | custom-call | flops 6000000000 | bytes 4194304 | tf_op jit(solution)/shard_map/final_part/pallas_call | solution.py:190
  244.0 3.5 %collective-permute-start.24 = (bf16[256,512]{1,0:T(8,128)(2,1)S(1)}, bf16[256,512]{1,0:T(8,128)(2,1)S(1)}, u32[]{:S(2)}, u32[]{:S(2)}) collective-permute-start(bf16[256,512]{1,0:T(8,128)(2,1)S(1)} %get-tuple-element.87), channel_id=1, source_target_pairs={{0,1},{1,0},{2,3},{3,2},{4,5},{5,4},{6,7},{7,6},{8,9},{9,8},{10,11... | collective-permute-start | bytes 786440 | tf_op jit(solution)/shard_map/ppermute | solution.py:430
  247.5 4.1 %collective-permute-start.22 = (bf16[256,512]{1,0:T(8,128)(2,1)S(1)}, bf16[256,512]{1,0:T(8,128)(2,1)S(1)}, u32[]{:S(2)}, u32[]{:S(2)}) collective-permute-start(bf16[256,512]{1,0:T(8,128)(2,1)S(1)} %get-tuple-element.82), channel_id=1, source_target_pairs={{0,2},{1,3},{2,0},{3,1},{4,6},{5,7},{6,4},{7,5},{8,10},{9,11},{10,... | collective-permute-start | bytes 786440 | tf_op jit(solution)/shard_map/ppermute | solution.py:429
  251.9 4.5 %project.2.refs_6_ = f32[256,4096]{1,0:T(8,128)S(1)} custom-call(bf16[256,512]{1,0:T(8,128)(2,1)S(1)} %get-tuple-element.86.refs_0_, bf16[256,512]{1,0:T(8,128)(2,1)S(1)} %collective-permute-done.24.refs_1_, bf16[256,4096]{1,0:T(8,128)(2,1)} %get-tuple-element.92.refs_2_, bf16[256,4096]{1,0:T(8,128)(2,1)} %get-tuple-element.91.refs_3_, ...), custom_call_target="tpu_custom_call" | custom-call | flops 6000000000 | bytes 4194304 | tf_op jit(solution)/shard_map/project/pallas_call | solution.py:270
  256.4 1.7 collective-permute-done.22.refs_0_
  258.2 5.6 %collective-permute-done.23.refs_1_ = bf16[256,512]{1,0:T(8,128)(2,1)S(1)} collective-permute-done((bf16[256,512]{1,0:T(8,128)(2,1)S(1)}, bf16[256,512]{1,0:T(8,128)(2,1)S(1)}, u32[]{:S(2)}, u32[]{:S(2)}) %collective-permute-start.23) | collective-permute-done | bytes 262176 | tf_op jit(solution)/shard_map/ppermute | solution.py:429
  263.8 5.8 %project.3 = bf16[256,4096]{1,0:T(8,128)(2,1)} custom-call(bf16[256,512]{1,0:T(8,128)(2,1)S(1)} %collective-permute-done.22.refs_0_, bf16[256,512]{1,0:T(8,128)(2,1)S(1)} %collective-permute-done.23.refs_1_, bf16[256,4096]{1,0:T(8,128)(2,1)} %collective-permute-done.9.refs_2_, bf16[256,4096]{1,0:T(8,128)(2,1)} %collective-permute-done.10.refs_3_, ...), custom_call_target="tpu_custom_call" | custom-call | flops 6000000000 | bytes 4194304 | tf_op jit(solution)/shard_map/project/pallas_call | solution.py:270
  (67 shorter events, 10.3 us)
Async XLA Ops:
  0.0 23.3 %copy-start.9 = (s32[16,2]{0,1:T(2,128)S(1)}, s32[16,2]{0,1:T(2,128)}, u32[]{:S(2)}) copy-start(s32[16,2]{0,1:T(2,128)} %param.6) | copy-start | bytes 388
  3.3 60.1 %collective-permute-start = (bf16[16,64,1024]{2,1,0:T(8,128)(2,1)S(1)}, bf16[16,64,1024]{2,1,0:T(8,128)(2,1)}, u32[]{:S(2)}, u32[]{:S(2)}) collective-permute-start(bf16[16,64,1024]{2,1,0:T(8,128)(2,1)S(1)} %reshape.122.refs_0_), channel_id=1, source_target_pairs={{0,4},{4,8},{8,12},{12,16},{16,20},{20,24},{24,28},{28,0},{1,5},{5... | collective-permute-start | bytes 6291464 | tf_op jit(solution)/shard_map/ppermute | solution.py:287
  5.8 57.5 %collective-permute-start.1 = (bf16[16,64,1024]{2,1,0:T(8,128)(2,1)S(1)}, bf16[16,64,1024]{2,1,0:T(8,128)(2,1)}, u32[]{:S(2)}, u32[]{:S(2)}) collective-permute-start(bf16[16,64,1024]{2,1,0:T(8,128)(2,1)S(1)} %reshape.122.refs_0_), channel_id=1, source_target_pairs={{0,28},{4,0},{8,4},{12,8},{16,12},{20,16},{24,20},{28,24},{1,29},{... | collective-permute-start | bytes 6291464 | tf_op jit(solution)/shard_map/ppermute | solution.py:287
  11.0 31.6 %collective-permute-start.2 = (bf16[64,1024]{1,0:T(8,128)(2,1)S(1)}, bf16[64,1024]{1,0:T(8,128)(2,1)S(1)}, u32[]{:S(2)}, u32[]{:S(2)}) collective-permute-start(bf16[64,1024]{1,0:T(8,128)(2,1)S(1)} %bitcast.23), channel_id=1, source_target_pairs={{28,32},{60,64},{92,96},{124,128},{156,160},{188,192},{220,224},{3... | collective-permute-start | bytes 393224 | tf_op jit(solution)/shard_map/ppermute | solution.py:368
  11.6 11.9 %collective-permute-start.6 = (bf16[64,1024]{1,0:T(8,128)(2,1)S(1)}, bf16[64,1024]{1,0:T(8,128)(2,1)S(1)}, u32[]{:S(2)}, u32[]{:S(2)}) collective-permute-start(bf16[64,1024]{1,0:T(8,128)(2,1)S(1)} %bitcast.24), channel_id=1, source_target_pairs={{0,128},{252,124},{1,129},{253,125},{2,130},{254,126},{3,131},{255... | collective-permute-start | bytes 393224 | tf_op jit(solution)/shard_map/ppermute | solution.py:302
  21.4 117.7 %collective-permute-start.5 = (bf16[512,4096]{1,0:T(8,128)(2,1)}, bf16[512,4096]{1,0:T(8,128)(2,1)}, u32[]{:S(2)}, u32[]{:S(2)}) collective-permute-start(bf16[512,4096]{1,0:T(8,128)(2,1)} %param.7), channel_id=1, source_target_pairs={{0,1},{1,0},{2,3},{3,2},{4,5},{5,4},{6,7},{7,6},{8,9},{9,8},{10,11... | collective-permute-start | bytes 12582920 | tf_op jit(solution)/shard_map/ppermute | solution.py:382
  23.6 3.2 %collective-permute-start.7 = (bf16[64,1024]{1,0:T(8,128)(2,1)S(1)}, bf16[64,1024]{1,0:T(8,128)(2,1)S(1)}, u32[]{:S(2)}, u32[]{:S(2)}) collective-permute-start(bf16[64,1024]{1,0:T(8,128)(2,1)S(1)} %broadcast_select_fusion.5), channel_id=1, source_target_pairs={{0,64},{128,192},{252,188},{124,60},{1,65},{129,193},{253,189},{12... | collective-permute-start | bytes 393224 | tf_op jit(solution)/shard_map/ppermute | solution.py:302
  26.8 9.8 %collective-permute-start.8 = (bf16[64,1024]{1,0:T(8,128)(2,1)S(1)}, bf16[64,1024]{1,0:T(8,128)(2,1)S(1)}, u32[]{:S(2)}, u32[]{:S(2)}) collective-permute-start(bf16[64,1024]{1,0:T(8,128)(2,1)S(1)} %broadcast_select_fusion.6), channel_id=1, source_target_pairs={{0,32},{64,96},{128,160},{192,224},{252,220},{188,156},{124,92},{6... | collective-permute-start | bytes 393224 | tf_op jit(solution)/shard_map/ppermute | solution.py:302
  29.2 34.2 %all-to-all-start = ((s32[64,1,8]{2,1,0:T(1,128)}), s32[64,1,8]{2,1,0:T(1,128)S(1)}, u32[]{:S(2)}, u32[]{:S(2)}) async-start(s32[64,1,8]{2,1,0:T(1,128)} %bitcast.3), calls=%async_computation | async-start | bytes 65536 | tf_op jit(solution)/shard_map/all_to_all | solution.py:358
  41.3 49.5 %collective-permute-start.9 = (bf16[256,4096]{1,0:T(8,128)(2,1)}, bf16[256,4096]{1,0:T(8,128)(2,1)}, u32[]{:S(2)}, u32[]{:S(2)}) collective-permute-start(bf16[256,4096]{1,0:T(8,128)(2,1)} %get-tuple-element.92.refs_2_), channel_id=1, source_target_pairs={{0,2},{2,32},{32,34},{34,0},{1,3},{3,33},{33,35},{35,1},{4,6},{6,3... | collective-permute-start | bytes 6291464 | tf_op jit(solution)/shard_map/ppermute | solution.py:365
  42.5 96.6 %collective-permute-start.10 = (bf16[256,4096]{1,0:T(8,128)(2,1)}, bf16[256,4096]{1,0:T(8,128)(2,1)}, u32[]{:S(2)}, u32[]{:S(2)}) collective-permute-start(bf16[256,4096]{1,0:T(8,128)(2,1)} %get-tuple-element.91.refs_3_), channel_id=1, source_target_pairs={{0,34},{2,0},{32,2},{34,32},{1,35},{3,1},{33,3},{35,33},{4,38},{6,... | collective-permute-start | bytes 6291464 | tf_op jit(solution)/shard_map/ppermute | solution.py:366
  63.3 75.8 %collective-permute-start.3 = (bf16[16,64,1024]{2,1,0:T(8,128)(2,1)}, bf16[16,64,1024]{2,1,0:T(8,128)(2,1)}, u32[]{:S(2)}, u32[]{:S(2)}) collective-permute-start(bf16[16,64,1024]{2,1,0:T(8,128)(2,1)} %collective-permute-done.refs_1_), channel_id=1, source_target_pairs={{0,4},{4,8},{8,12},{12,16},{16,20},{20,24},{24,28},{28,0},{1,5},{5... | collective-permute-start | bytes 6291464 | tf_op jit(solution)/shard_map/ppermute | solution.py:287
  64.5 74.6 %collective-permute-start.4 = (bf16[16,64,1024]{2,1,0:T(8,128)(2,1)}, bf16[16,64,1024]{2,1,0:T(8,128)(2,1)}, u32[]{:S(2)}, u32[]{:S(2)}) collective-permute-start(bf16[16,64,1024]{2,1,0:T(8,128)(2,1)} %collective-permute-done.1.refs_2_), channel_id=1, source_target_pairs={{0,28},{4,0},{8,4},{12,8},{16,12},{20,16},{24,20},{28,24},{1,29},{... | collective-permute-start | bytes 6291464 | tf_op jit(solution)/shard_map/ppermute | solution.py:287
  71.7 74.2 %all-to-all-start.1 = ((bf16[8,3,64,1024]{3,2,1,0:T(8,128)(2,1)}), bf16[8,3,64,1024]{3,2,1,0:T(8,128)(2,1)}, u32[]{:S(2)}, u32[]{:S(2)}) async-start(bf16[8,3,64,1024]{3,2,1,0:T(8,128)(2,1)} %pick.2), calls=%async_computation.1 | async-start | bytes 6291456 | tf_op jit(solution)/shard_map/all_to_all | solution.py:291
  145.9 8.4 %copy-start.10 = (bf16[4,64,1024]{2,1,0:T(8,128)(2,1)S(1)}, bf16[4,64,1024]{2,1,0:T(8,128)(2,1)}, u32[]{:S(2)}) copy-start(bf16[4,64,1024]{2,1,0:T(8,128)(2,1)} %get-tuple-element.64) | copy-start | bytes 1572868
  145.9 27.5 %all-to-all-start.2 = ((bf16[8,2,64,1024]{3,2,1,0:T(8,128)(2,1)}), bf16[8,2,64,1024]{3,2,1,0:T(8,128)(2,1)S(1)}, u32[]{:S(2)}, u32[]{:S(2)}) async-start(bf16[8,2,64,1024]{3,2,1,0:T(8,128)(2,1)} %get-tuple-element.62), calls=%async_computation.2 | async-start | bytes 4194304 | tf_op jit(solution)/shard_map/all_to_all | solution.py:291
  149.7 3.2 %collective-permute-start.13 = (bf16[64,1024]{1,0:T(8,128)(2,1)S(1)}, bf16[64,1024]{1,0:T(8,128)(2,1)S(1)}, u32[]{:S(2)}, u32[]{:S(2)}) collective-permute-start(bf16[64,1024]{1,0:T(8,128)(2,1)S(1)} %broadcast_select_fusion.7), channel_id=1, source_target_pairs={{0,16},{28,12},{1,17},{29,13},{2,18},{30,14},{3,19},{31,15},{32,48... | collective-permute-start | bytes 393224 | tf_op jit(solution)/shard_map/ppermute | solution.py:397
  152.9 5.2 %collective-permute-start.14 = (bf16[64,1024]{1,0:T(8,128)(2,1)S(1)}, bf16[64,1024]{1,0:T(8,128)(2,1)S(1)}, u32[]{:S(2)}, u32[]{:S(2)}) collective-permute-start(bf16[64,1024]{1,0:T(8,128)(2,1)S(1)} %broadcast_select_fusion.1), channel_id=1, source_target_pairs={{0,8},{16,24},{28,20},{12,4},{1,9},{17,25},{29,21},{13,5},{2,10},{... | collective-permute-start | bytes 393224 | tf_op jit(solution)/shard_map/ppermute | solution.py:399
  154.2 14.4 %collective-permute-start.11 = (bf16[4,64,1024]{2,1,0:T(8,128)(2,1)}, bf16[4,64,1024]{2,1,0:T(8,128)(2,1)}, u32[]{:S(2)}, u32[]{:S(2)}) collective-permute-start(bf16[4,64,1024]{2,1,0:T(8,128)(2,1)} %get-tuple-element.63), channel_id=1, source_target_pairs={{0,4},{4,8},{8,12},{12,16},{16,20},{20,24},{24,28},{28,0},{1,5},{5... | collective-permute-start | bytes 1572872 | tf_op jit(solution)/shard_map/ppermute | solution.py:287
  154.3 14.3 %collective-permute-start.12 = (bf16[4,64,1024]{2,1,0:T(8,128)(2,1)S(1)}, bf16[4,64,1024]{2,1,0:T(8,128)(2,1)}, u32[]{:S(2)}, u32[]{:S(2)}) collective-permute-start(bf16[4,64,1024]{2,1,0:T(8,128)(2,1)S(1)} %copy-done.10), channel_id=1, source_target_pairs={{0,28},{4,0},{8,4},{12,8},{16,12},{20,16},{24,20},{28,24},{1,29},{... | collective-permute-start | bytes 1572872 | tf_op jit(solution)/shard_map/ppermute | solution.py:287
  158.1 10.5 %collective-permute-start.15 = (bf16[64,1024]{1,0:T(8,128)(2,1)S(1)}, bf16[64,1024]{1,0:T(8,128)(2,1)S(1)}, u32[]{:S(2)}, u32[]{:S(2)}) collective-permute-start(bf16[64,1024]{1,0:T(8,128)(2,1)S(1)} %broadcast_select_fusion.2), channel_id=1, source_target_pairs={{0,4},{4,0},{8,12},{12,8},{16,20},{20,16},{24,28},{28,24},{1,5},{5... | collective-permute-start | bytes 393224 | tf_op jit(solution)/shard_map/ppermute | solution.py:402
  173.4 18.9 %collective-permute-start.19 = (bf16[4,64,1024]{2,1,0:T(8,128)(2,1)}, bf16[4,64,1024]{2,1,0:T(8,128)(2,1)S(1)}, u32[]{:S(2)}, u32[]{:S(2)}) collective-permute-start(bf16[4,64,1024]{2,1,0:T(8,128)(2,1)} %collective-permute-done.12), channel_id=1, source_target_pairs={{0,28},{4,0},{8,4},{12,8},{16,12},{20,16},{24,20},{28,24},{1,29},{... | collective-permute-start | bytes 1572872 | tf_op jit(solution)/shard_map/ppermute | solution.py:287
  180.2 43.8 %collective-permute-start.16 = (bf16[8,64,1024]{2,1,0:T(8,128)(2,1)}, bf16[8,64,1024]{2,1,0:T(8,128)(2,1)}, u32[]{:S(2)}, u32[]{:S(2)}) collective-permute-start(bf16[8,64,1024]{2,1,0:T(8,128)(2,1)} %get-tuple-element.94), channel_id=1, source_target_pairs={{0,4},{4,8},{8,12},{12,16},{16,20},{20,24},{24,28},{28,0},{1,5},{5... | collective-permute-start | bytes 3145736 | tf_op jit(solution)/shard_map/ppermute | solution.py:287
  180.2 15.5 %copy-start = (bf16[1152,1024]{1,0:T(8,128)(2,1)S(1)}, bf16[1152,1024]{1,0:T(8,128)(2,1)}, u32[]{:S(2)}) copy-start(bf16[1152,1024]{1,0:T(8,128)(2,1)} %pad_maximum_fusion.refs_4_) | copy-start | bytes 7077892
  180.2 43.8 %collective-permute-start.17 = (bf16[8,64,1024]{2,1,0:T(8,128)(2,1)}, bf16[8,64,1024]{2,1,0:T(8,128)(2,1)}, u32[]{:S(2)}, u32[]{:S(2)}) collective-permute-start(bf16[8,64,1024]{2,1,0:T(8,128)(2,1)} %get-tuple-element.93), channel_id=1, source_target_pairs={{0,28},{4,0},{8,4},{12,8},{16,12},{20,16},{24,20},{28,24},{1,29},{... | collective-permute-start | bytes 3145736 | tf_op jit(solution)/shard_map/ppermute | solution.py:287
  182.9 34.1 %collective-permute-start.18 = (bf16[4,64,1024]{2,1,0:T(8,128)(2,1)}, bf16[4,64,1024]{2,1,0:T(8,128)(2,1)}, u32[]{:S(2)}, u32[]{:S(2)}) collective-permute-start(bf16[4,64,1024]{2,1,0:T(8,128)(2,1)} %collective-permute-done.11), channel_id=1, source_target_pairs={{0,4},{4,8},{8,12},{12,16},{16,20},{20,24},{24,28},{28,0},{1,5},{5... | collective-permute-start | bytes 1572872 | tf_op jit(solution)/shard_map/ppermute | solution.py:287
  182.9 36.3 %all-to-all-start.3 = ((bf16[8,2,64,1024]{3,2,1,0:T(8,128)(2,1)}), bf16[8,2,64,1024]{3,2,1,0:T(8,128)(2,1)}, u32[]{:S(2)}, u32[]{:S(2)}) async-start(bf16[8,2,64,1024]{3,2,1,0:T(8,128)(2,1)} %get-tuple-element.74), calls=%async_computation.3 | async-start | bytes 4194304 | tf_op jit(solution)/shard_map/all_to_all | solution.py:291
  188.4 30.8 %collective-permute-start.20 = (bf16[256,4096]{1,0:T(8,128)(2,1)}, bf16[256,4096]{1,0:T(8,128)(2,1)}, u32[]{:S(2)}, u32[]{:S(2)}) collective-permute-start(bf16[256,4096]{1,0:T(8,128)(2,1)} %collective-permute-done.9.refs_2_), channel_id=1, source_target_pairs={{0,1},{1,0},{2,3},{3,2},{4,5},{5,4},{6,7},{7,6},{8,9},{9,8},{10,11... | collective-permute-start | bytes 6291464 | tf_op jit(solution)/shard_map/ppermute | solution.py:407
  192.3 26.9 %collective-permute-start.21 = (bf16[256,4096]{1,0:T(8,128)(2,1)}, bf16[256,4096]{1,0:T(8,128)(2,1)}, u32[]{:S(2)}, u32[]{:S(2)}) collective-permute-start(bf16[256,4096]{1,0:T(8,128)(2,1)} %collective-permute-done.10.refs_3_), channel_id=1, source_target_pairs={{0,1},{1,0},{2,3},{3,2},{4,5},{5,4},{6,7},{7,6},{8,9},{9,8},{10,11... | collective-permute-start | bytes 6291464 | tf_op jit(solution)/shard_map/ppermute | solution.py:407
  195.7 1.2 copy-start.1
  214.9 1.3 copy-start.5
  216.2 0.8 copy-start.7
  217.0 7.0 %copy-start.2 = (bf16[1024,512]{1,0:T(8,128)(2,1)S(1)}, bf16[1024,512]{1,0:T(8,128)(2,1)}, u32[]{:S(2)}) copy-start(bf16[1024,512]{1,0:T(8,128)(2,1)} %refs_3_.3) | copy-start | bytes 3145732
  217.0 7.0 %copy-start.8 = (f32[1024,128]{1,0:T(8,128)S(1)}, f32[1024,128]{1,0:T(8,128)}, u32[]{:S(2)}) copy-start(f32[1024,128]{1,0:T(8,128)} %copy-done.7) | copy-start | bytes 1572868
  219.2 19.5 %all-to-all-start.4 = ((bf16[8,64,1024]{2,1,0:T(8,128)(2,1)}), bf16[8,64,1024]{2,1,0:T(8,128)(2,1)S(1)}, u32[]{:S(2)}, u32[]{:S(2)}) async-start(bf16[8,64,1024]{2,1,0:T(8,128)(2,1)} %pad_maximum_fusion.1), calls=%async_computation.4 | async-start | bytes 2097152 | tf_op jit(solution)/shard_map/all_to_all | solution.py:291
  224.0 1.6 copy-start.6
  235.8 1.3 copy-start.3
  238.7 1.6 copy-start.4
  244.0 7.9 %collective-permute-start.24 = (bf16[256,512]{1,0:T(8,128)(2,1)S(1)}, bf16[256,512]{1,0:T(8,128)(2,1)S(1)}, u32[]{:S(2)}, u32[]{:S(2)}) collective-permute-start(bf16[256,512]{1,0:T(8,128)(2,1)S(1)} %get-tuple-element.87), channel_id=1, source_target_pairs={{0,1},{1,0},{2,3},{3,2},{4,5},{5,4},{6,7},{7,6},{8,9},{9,8},{10,11... | collective-permute-start | bytes 786440 | tf_op jit(solution)/shard_map/ppermute | solution.py:430
  247.5 10.7 %collective-permute-start.22 = (bf16[256,512]{1,0:T(8,128)(2,1)S(1)}, bf16[256,512]{1,0:T(8,128)(2,1)S(1)}, u32[]{:S(2)}, u32[]{:S(2)}) collective-permute-start(bf16[256,512]{1,0:T(8,128)(2,1)S(1)} %get-tuple-element.82), channel_id=1, source_target_pairs={{0,2},{1,3},{2,0},{3,1},{4,6},{5,7},{6,4},{7,5},{8,10},{9,11},{10,... | collective-permute-start | bytes 786440 | tf_op jit(solution)/shard_map/ppermute | solution.py:429
  251.6 12.2 %collective-permute-start.23 = (bf16[256,512]{1,0:T(8,128)(2,1)S(1)}, bf16[256,512]{1,0:T(8,128)(2,1)S(1)}, u32[]{:S(2)}, u32[]{:S(2)}) collective-permute-start(bf16[256,512]{1,0:T(8,128)(2,1)S(1)} %get-tuple-element.83), channel_id=1, source_target_pairs={{0,3},{1,2},{2,1},{3,0},{4,7},{5,6},{6,5},{7,4},{8,11},{9,10},{10,... | collective-permute-start | bytes 786440 | tf_op jit(solution)/shard_map/ppermute | solution.py:429

commit v10 on v8

--- a/solution.py
+++ b/solution.py
@@ -401,15 +401,11 @@
     even = z % 2 == 0
     ends = jnp.concatenate([jnp.where(even, held, got), jnp.where(even, got, held)], axis=0)
     c2, c3, fu, fd, ends = tie(c2, c3, fu, fd, ends)
-    low, high, w_core, ends = tie(low, high, w_core, ends)
-    swap = [(0, 1), (1, 0)]
-    others = [lax.ppermute(x, "core", swap) for x in (w_core, low, high)]
     r2 = lane_exchange(c2)
     fu, fd = z_shift(fu, 1), z_shift(fd, -1)
     r3u, r3d = z_shift(c3[:, 0], 1), z_shift(c3[:, 1], -1)
     far = jnp.concatenate([fu, fd], axis=0)
-    far, r2, *others = tie(far, r2, *others)
-    weights = own + [others[0], low, high] + others[1:]
+    far, r2 = tie(far, r2)
     r4 = lane_exchange(far)
 
     def slots(x):
@@ -418,6 +414,10 @@
     o, st = local_part(
         zs, where, first_id.reshape(1), all_blocks, queries, kv_pad, ends, (0, -1, 1), r1
     )
+    low, high, w_core, st = tie(low, high, w_core, st)
+    swap = [(0, 1), (1, 0)]
+    others = [lax.ppermute(x, "core", swap) for x in (w_core, low, high)]
+    weights = own + [others[0], low, high] + others[1:]
     o, st = more_part(
         zs, where, queries, o, st, [(-3,), (3,), (-2, 2)], [slots(r3u), slots(r3d), r2]
     )

time: 252 us -> 292 us (1.16)
  waiting for transfers between devices: 73.1 us -> 112 us
    ppermute x10, waiting for transfers between devices: 25.6 us -> 57.9 us  [z_shift(): return lax.ppermute(x, 'z', [(i, (i + by) % NZ) for i in range(NZ)])]
    all_to_all x4, waiting for transfers between devices: 1.39 us -> 9.97 us  [lane_exchange(): return lax.all_to_all(x, LANE, split_axis=0, concat_axis=0, tiled=True)]
    ppermute x1, waiting for transfers between devices: 3.14 us -> 11.3 us  [body(): lax.ppermute(own[0], XRING, [(i, (i + 1) % ring) for i in range(ring)])]
    all_to_all x1, waiting for transfers between devices: 26.6 us -> 18.9 us  [body(): asked = lax.all_to_all(asked, SEQ, split_axis=0, concat_axis=0, tiled=True)]
    ppermute x3, starting transfers between devices: 17.3 us -> 13.7 us  [body(): others = [lax.ppermute(x, 'core', swap) for x in (w_core, low, high)]]
    ppermute x1, waiting for transfers between devices: 3.48 us -> 0.07 us  [body(): got = lax.ppermute(held, 'z', [(i, i ^ 1) for i in range(NZ)])]
    unnamed x36 -> x30, local copies, waits for them, and re-layouts: 11.3 us -> 12.5 us
  transfers between devices with their start and end apart: 30 -> 30, of which waited for: 10 -> 14; matrix products, arithmetic and copies ran while one was open for 7% -> 5% of each run, Pallas kernels for 18% -> 10%
where the time goes in v10:
time: 292 us
  waiting for transfers between devices  112 us (38%)
  starting transfers between devices  95.4 us (33%)
  Pallas kernels  54.2 us (19%)
  local copies, waits for them, and re-layouts  24.5 us (8%)
  other arithmetic  5.15 us (2%)
    ppermute x10, waiting for transfers between devices, z_shift(): return lax.ppermute(x, 'z', [(i, (i + by) % NZ) for i in range(NZ)])  57.9 us
    all_to_all x4, starting transfers between devices, lane_exchange(): return lax.all_to_all(x, LANE, split_axis=0, concat_axis=0, tiled=True)  23.1 us
    all_to_all x1, waiting for transfers between devices, body(): asked = lax.all_to_all(asked, SEQ, split_axis=0, concat_axis=0, tiled=True)  18.9 us
    pallas_call x1, Pallas kernels, local_part(): pl.pallas_call(lambda *refs: local_kernel(all_blocks, deltas, *refs), out...  17.9 us
    ppermute x10, starting transfers between devices, z_shift(): return lax.ppermute(x, 'z', [(i, (i + by) % NZ) for i in range(NZ)])  16.1 us
    ppermute x3, starting transfers between devices, body(): others = [lax.ppermute(x, 'core', swap) for x in (w_core, low, high)]  13.7 us
    pallas_call x2, Pallas kernels, pick(): pl.pallas_call(kernel, out_shape=tuple((pltpu.HBM(shape + block_shape, BF...  13.3 us
    unnamed x30, local copies, waits for them, and re-layouts  12.5 us
  transfers between devices with their start and end apart: 30, of which 14 were waited for; matrix products, arithmetic and copies ran while one was open for 5% of the time, Pallas kernels for 10%

profile of v10, /device:TPU:1, one launch (start us, length us, event | category | flops | bytes accessed | tf_op | source)
XLA Modules:
  0.0 291.7 jit_solution(9358456307622074155)
XLA Ops:
  0.0 3.2 %reshape.122.refs_0_ = bf16[16,64,1024]{2,1,0:T(8,128)(2,1)S(1)} reshape(bf16[1024,2,512]{2,1,0:T(2,128)(2,1)} %param.5) | data formatting | bytes 4194304 | tf_op jit(solution)/shard_map/reshape | solution.py:352
  3.3 2.5 collective-permute-start
  5.8 4.0 %collective-permute-start.1 = (bf16[16,64,1024]{2,1,0:T(8,128)(2,1)S(1)}, bf16[16,64,1024]{2,1,0:T(8,128)(2,1)}, u32[]{:S(2)}, u32[]{:S(2)}) collective-permute-start(bf16[16,64,1024]{2,1,0:T(8,128)(2,1)S(1)} %reshape.122.refs_0_), channel_id=1, source_target_pairs={{0,28},{4,0},{8,4},{12,8},{16,12},{20,16},{24,20},{28,24},{1,29},{... | collective-permute-start | bytes 6291464 | tf_op jit(solution)/shard_map/ppermute | solution.py:287
  11.6 9.8 %collective-permute-start.5 = (bf16[64,1024]{1,0:T(8,128)(2,1)S(1)}, bf16[64,1024]{1,0:T(8,128)(2,1)S(1)}, u32[]{:S(2)}, u32[]{:S(2)}) collective-permute-start(bf16[64,1024]{1,0:T(8,128)(2,1)S(1)} %bitcast.24), channel_id=1, source_target_pairs={{0,128},{252,124},{1,129},{253,125},{2,130},{254,126},{3,131},{255... | collective-permute-start | bytes 393224 | tf_op jit(solution)/shard_map/ppermute | solution.py:302
  21.7 1.7 collective-permute-done.5
  23.4 1.3 collective-permute-start.6
  24.7 2.0 collective-permute-done.6
  26.7 1.3 collective-permute-start.7
  29.0 7.5 %all-to-all-start = ((s32[64,1,8]{2,1,0:T(1,128)}), s32[64,1,8]{2,1,0:T(1,128)S(1)}, u32[]{:S(2)}, u32[]{:S(2)}) async-start(s32[64,1,8]{2,1,0:T(1,128)} %bitcast.3), calls=%async_computation | async-start | bytes 65536 | tf_op jit(solution)/shard_map/all_to_all | solution.py:358
  36.7 4.7 %fusion.4 = (bf16[256,4096]{1,0:T(8,128)(2,1)}, bf16[256,4096]{1,0:T(8,128)(2,1)}) fusion(bf16[512,4096]{1,0:T(8,128)(2,1)} %param.7), kind=kLoop, calls=%fused_computation.36 | loop fusion | bytes 8388608 | tf_op jit(solution)/shard_map/slice | solution.py:363
  42.5 1.9 collective-permute-start.9
  44.5 18.9 %all-to-all-done = s32[64,1,8]{2,1,0:T(1,128)S(1)} async-done(((s32[64,1,8]{2,1,0:T(1,128)}), s32[64,1,8]{2,1,0:T(1,128)S(1)}, u32[]{:S(2)}, u32[]{:S(2)}) %all-to-all-start) | async-done | bytes 2080 | tf_op jit(solution)/shard_map/all_to_all | solution.py:358
  64.6 1.5 collective-permute-start.4
  66.1 6.3 %pick.2 = bf16[8,3,64,1024]{3,2,1,0:T(8,128)(2,1)} custom-call(s32[1]{0:T(128)} %bitcast.1.z_ref.refs_0_.refs_1_, s32[64,8]{1,0:T(8,128)S(1)} %bitcast.21, bf16[16,64,1024]{2,1,0:T(8,128)(2,1)S(1)} %reshape.122.refs_0_, bf16[16,64,1024]{2,1,0:T(8,128)(2,1)} %collective-permute-done.refs_1_, bf16[16,64,1024]{2,1,0:T(8,128)(2,1)} %collective-permute-done.1.refs_2_), custom_call_target="tpu_custom_call" | custom-call | flops 3000000000 | bytes 4194304 | tf_op jit(solution)/shard_map/pick/pallas_call | solution.py:220
  72.4 4.5 %all-to-all-start.1 = ((bf16[8,3,64,1024]{3,2,1,0:T(8,128)(2,1)}), bf16[8,3,64,1024]{3,2,1,0:T(8,128)(2,1)}, u32[]{:S(2)}, u32[]{:S(2)}) async-start(bf16[8,3,64,1024]{3,2,1,0:T(8,128)(2,1)} %pick.2), calls=%async_computation.1 | async-start | bytes 6291456 | tf_op jit(solution)/shard_map/all_to_all | solution.py:291
  77.9 1.7 pad_maximum_fusion.refs_4_
  79.5 11.3 %collective-permute-done.8.refs_2_ = bf16[256,4096]{1,0:T(8,128)(2,1)} collective-permute-done((bf16[256,4096]{1,0:T(8,128)(2,1)}, bf16[256,4096]{1,0:T(8,128)(2,1)}, u32[]{:S(2)}, u32[]{:S(2)}) %collective-permute-start.8) | collective-permute-done | bytes 2097184 | tf_op jit(solution)/shard_map/ppermute | solution.py:365
  90.8 19.7 %collective-permute-done.3.refs_0_ = bf16[16,64,1024]{2,1,0:T(8,128)(2,1)} collective-permute-done((bf16[16,64,1024]{2,1,0:T(8,128)(2,1)}, bf16[16,64,1024]{2,1,0:T(8,128)(2,1)}, u32[]{:S(2)}, u32[]{:S(2)}) %collective-permute-start.3) | collective-permute-done | bytes 2097184 | tf_op jit(solution)/shard_map/ppermute | solution.py:287
  110.5 7.0 %pick.3 = (bf16[8,2,64,1024]{3,2,1,0:T(8,128)(2,1)}, bf16[4,64,1024]{2,1,0:T(8,128)(2,1)}, bf16[4,64,1024]{2,1,0:T(8,128)(2,1)}, bf16[8,2,64,1024]{3,2,1,0:T(8,128)(2,1)}) custom-call(s32[1]{0:T(128)} %bitcast.1.z_ref.refs_0_.refs_1_, s32[64,8]{1,0:T(8,128)S(1)} %bitcast.22, bf16[16,64,1024]{2,1,0:T(8,128)(2,1)} %collective-permute-done.3.refs_0_, ...), custom_call_target="tpu_custom_call" | custom-call | flops 60000002048 | bytes 4194304 | tf_op jit(solution)/shard_map/pick/pallas_call | solution.py:220
  117.6 7.4 %all-to-all-done.1.refs_6_ = bf16[8,3,64,1024]{3,2,1,0:T(8,128)(2,1)} async-done(((bf16[8,3,64,1024]{3,2,1,0:T(8,128)(2,1)}), bf16[8,3,64,1024]{3,2,1,0:T(8,128)(2,1)}, u32[]{:S(2)}, u32[]{:S(2)}) %all-to-all-start.1) | async-done | bytes 3145760 | tf_op jit(solution)/shard_map/all_to_all | solution.py:291
  125.0 4.8 %all-to-all-start.2 = ((bf16[8,2,64,1024]{3,2,1,0:T(8,128)(2,1)}), bf16[8,2,64,1024]{3,2,1,0:T(8,128)(2,1)}, u32[]{:S(2)}, u32[]{:S(2)}) async-start(bf16[8,2,64,1024]{3,2,1,0:T(8,128)(2,1)} %get-tuple-element.58), calls=%async_computation.2 | async-start | bytes 4194304 | tf_op jit(solution)/shard_map/all_to_all | solution.py:291
  129.8 6.9 %collective-permute-start.12 = (bf16[64,1024]{1,0:T(8,128)(2,1)S(1)}, bf16[64,1024]{1,0:T(8,128)(2,1)S(1)}, u32[]{:S(2)}, u32[]{:S(2)}) collective-permute-start(bf16[64,1024]{1,0:T(8,128)(2,1)S(1)} %broadcast_select_fusion.7), channel_id=1, source_target_pairs={{0,16},{28,12},{1,17},{29,13},{2,18},{30,14},{3,19},{31,15},{32,48... | collective-permute-start | bytes 393224 | tf_op jit(solution)/shard_map/ppermute | solution.py:395
  136.7 1.9 collective-permute-done.12
  138.6 1.3 collective-permute-start.13
  139.9 1.9 collective-permute-done.13
  141.9 4.8 %collective-permute-start.14 = (bf16[64,1024]{1,0:T(8,128)(2,1)S(1)}, bf16[64,1024]{1,0:T(8,128)(2,1)S(1)}, u32[]{:S(2)}, u32[]{:S(2)}) collective-permute-start(bf16[64,1024]{1,0:T(8,128)(2,1)S(1)} %broadcast_select_fusion.2), channel_id=1, source_target_pairs={{0,4},{4,0},{8,12},{12,8},{16,20},{20,16},{24,28},{28,24},{1,5},{5... | collective-permute-start | bytes 393224 | tf_op jit(solution)/shard_map/ppermute | solution.py:400
  146.8 2.6 collective-permute-start.11
  149.5 7.0 %collective-permute-done.10 = bf16[4,64,1024]{2,1,0:T(8,128)(2,1)} collective-permute-done((bf16[4,64,1024]{2,1,0:T(8,128)(2,1)}, bf16[4,64,1024]{2,1,0:T(8,128)(2,1)}, u32[]{:S(2)}, u32[]{:S(2)}) %collective-permute-start.10) | collective-permute-done | bytes 524320 | tf_op jit(solution)/shard_map/ppermute | solution.py:287
  157.8 17.9 %local_part.1 = (f32[1024,512]{1,0:T(8,128)S(1)}, f32[1024,128]{1,0:T(8,128)S(1)}) custom-call(s32[1]{0:T(128)} %bitcast.1.z_ref.refs_0_.refs_1_, s32[64]{0:T(128)S(1)} %broadcast_add_fusion.refs_1_.refs_2_, s32[1]{0:T(128)} %bitcast.2.refs_2_, bf16[1024,512]{1,0:T(8,128)(2,1)S(1)} %copy-done.1, bf16[1152,1024]{1,0:T(8,128)(2,1)S(1)} %copy-done, ...), custom_call_target="tpu_custom_call" | custom-call | flops 24999999488 | bytes 4194304 | tf_op jit(solution)/shard_map/local_part/pallas_call | solution.py:157
  175.7 1.3 copy-done.8
  177.0 10.8 %collective-permute-start.24 = (bf16[512,4096]{1,0:T(8,128)(2,1)}, bf16[512,4096]{1,0:T(8,128)(2,1)}, u32[]{:S(2)}, u32[]{:S(2)}) collective-permute-start(bf16[512,4096]{1,0:T(8,128)(2,1)} %param.7), channel_id=1, source_target_pairs={{0,1},{1,0},{2,3},{3,2},{4,5},{5,4},{6,7},{7,6},{8,9},{9,8},{10,11... | collective-permute-start | bytes 12582920 | tf_op jit(solution)/shard_map/ppermute | solution.py:419
  187.8 7.1 %all-to-all-start.3 = ((bf16[8,2,64,1024]{3,2,1,0:T(8,128)(2,1)}), bf16[8,2,64,1024]{3,2,1,0:T(8,128)(2,1)S(1)}, u32[]{:S(2)}, u32[]{:S(2)}) async-start(bf16[8,2,64,1024]{3,2,1,0:T(8,128)(2,1)} %get-tuple-element.73), calls=%async_computation.3 | async-start | bytes 4194304 | tf_op jit(solution)/shard_map/all_to_all | solution.py:291
  194.9 3.1 %slice_bitcast_fusion = (bf16[8,64,1024]{2,1,0:T(8,128)(2,1)}, bf16[8,64,1024]{2,1,0:T(8,128)(2,1)}) fusion(bf16[8,2,64,1024]{3,2,1,0:T(8,128)(2,1)} %all-to-all-done.2), kind=kLoop, calls=%fused_computation.1 | loop fusion | bytes 4194304 | tf_op jit(solution)/shard_map/squeeze | solution.py:406
  198.1 2.7 collective-permute-start.16
  202.2 31.1 %collective-permute-done.18 = bf16[4,64,1024]{2,1,0:T(8,128)(2,1)S(1)} collective-permute-done((bf16[4,64,1024]{2,1,0:T(8,128)(2,1)}, bf16[4,64,1024]{2,1,0:T(8,128)(2,1)S(1)}, u32[]{:S(2)}, u32[]{:S(2)}) %collective-permute-start.18) | collective-permute-done | bytes 524320 | tf_op jit(solution)/shard_map/ppermute | solution.py:287
  233.4 2.3 collective-permute-start.21
  237.4 6.6 %all-to-all-start.4 = ((bf16[8,64,1024]{2,1,0:T(8,128)(2,1)}), bf16[8,64,1024]{2,1,0:T(8,128)(2,1)S(1)}, u32[]{:S(2)}, u32[]{:S(2)}) async-start(bf16[8,64,1024]{2,1,0:T(8,128)(2,1)} %pad_maximum_fusion.1), calls=%async_computation.4 | async-start | bytes 2097152 | tf_op jit(solution)/shard_map/all_to_all | solution.py:291
  245.3 1.6 copy-done.9
  247.9 8.5 %more_part.1 = (f32[1024,512]{1,0:T(8,128)S(1)}, f32[1024,128]{1,0:T(8,128)S(1)}) custom-call(s32[1]{0:T(128)} %bitcast.1.z_ref.refs_0_.refs_1_, s32[64]{0:T(128)S(1)} %broadcast_add_fusion.refs_1_.refs_2_, bf16[1024,512]{1,0:T(8,128)(2,1)S(1)} %copy-done.2, f32[1024,512]{1,0:T(8,128)S(1)} %copy-done.9, f32[1024,128]{1,0:T(8,128)S(1)} %copy-done.11, ...), custom_call_target="tpu_custom_call" | custom-call | flops 12000000000 | bytes 4194304 | tf_op jit(solution)/shard_map/more_part/pallas_call | solution.py:173
  256.5 1.3 copy-done.4
  258.6 2.5 all-to-all-done.4
  262.3 1.6 copy-done.5
  265.0 4.2 %final_part.1 = (bf16[256,512]{1,0:T(8,128)(2,1)S(1)}, bf16[256,512]{1,0:T(8,128)(2,1)S(1)}, bf16[256,512]{1,0:T(8,128)(2,1)S(1)}, bf16[256,512]{1,0:T(8,128)(2,1)S(1)}) custom-call(s32[1]{0:T(128)} %bitcast.refs_0_, s32[1]{0:T(128)} %bitcast.1.z_ref.refs_0_.refs_1_, s32[64]{0:T(128)S(1)} %broadcast_add_fusion.refs_1_.refs_2_, ...), custom_call_target="tpu_custom_call" | custom-call | flops 6000000000 | bytes 4194304 | tf_op jit(solution)/shard_map/final_part/pallas_call | solution.py:190
  270.4 3.1 %collective-permute-start.19 = (bf16[256,512]{1,0:T(8,128)(2,1)S(1)}, bf16[256,512]{1,0:T(8,128)(2,1)S(1)}, u32[]{:S(2)}, u32[]{:S(2)}) collective-permute-start(bf16[256,512]{1,0:T(8,128)(2,1)S(1)} %get-tuple-element.78), channel_id=1, source_target_pairs={{0,2},{1,3},{2,0},{3,1},{4,6},{5,7},{6,4},{7,5},{8,10},{9,11},{10,... | collective-permute-start | bytes 786440 | tf_op jit(solution)/shard_map/ppermute | solution.py:428
  273.5 1.4 collective-permute-start.20
  274.9 4.5 %project.2.refs_6_ = f32[256,4096]{1,0:T(8,128)S(1)} custom-call(bf16[256,512]{1,0:T(8,128)(2,1)S(1)} %get-tuple-element.82.refs_0_, bf16[256,512]{1,0:T(8,128)(2,1)S(1)} %collective-permute-done.23.refs_1_, bf16[256,4096]{1,0:T(8,128)(2,1)} %get-tuple-element.88.refs_2_, bf16[256,4096]{1,0:T(8,128)(2,1)} %get-tuple-element.87.refs_3_, ...), custom_call_target="tpu_custom_call" | custom-call | flops 6000000000 | bytes 4194304 | tf_op jit(solution)/shard_map/project/pallas_call | solution.py:270
  280.0 5.6 %collective-permute-done.20.refs_1_ = bf16[256,512]{1,0:T(8,128)(2,1)S(1)} collective-permute-done((bf16[256,512]{1,0:T(8,128)(2,1)S(1)}, bf16[256,512]{1,0:T(8,128)(2,1)S(1)}, u32[]{:S(2)}, u32[]{:S(2)}) %collective-permute-start.20) | collective-permute-done | bytes 262176 | tf_op jit(solution)/shard_map/ppermute | solution.py:428
  285.7 5.9 %project.3 = bf16[256,4096]{1,0:T(8,128)(2,1)} custom-call(bf16[256,512]{1,0:T(8,128)(2,1)S(1)} %collective-permute-done.19.refs_0_, bf16[256,512]{1,0:T(8,128)(2,1)S(1)} %collective-permute-done.20.refs_1_, bf16[256,4096]{1,0:T(8,128)(2,1)} %collective-permute-done.8.refs_2_, bf16[256,4096]{1,0:T(8,128)(2,1)} %collective-permute-done.9.refs_3_, ...), custom_call_target="tpu_custom_call" | custom-call | flops 6000000000 | bytes 4194304 | tf_op jit(solution)/shard_map/project/pallas_call | solution.py:270
  (73 shorter events, 18.4 us)
Async XLA Ops:
  0.0 21.4 %copy-start.12 = (s32[16,2]{0,1:T(2,128)S(1)}, s32[16,2]{0,1:T(2,128)}, u32[]{:S(2)}) copy-start(s32[16,2]{0,1:T(2,128)} %param.6) | copy-start | bytes 388
  3.3 60.1 %collective-permute-start = (bf16[16,64,1024]{2,1,0:T(8,128)(2,1)S(1)}, bf16[16,64,1024]{2,1,0:T(8,128)(2,1)}, u32[]{:S(2)}, u32[]{:S(2)}) collective-permute-start(bf16[16,64,1024]{2,1,0:T(8,128)(2,1)S(1)} %reshape.122.refs_0_), channel_id=1, source_target_pairs={{0,4},{4,8},{8,12},{12,16},{16,20},{20,24},{24,28},{28,0},{1,5},{5... | collective-permute-start | bytes 6291464 | tf_op jit(solution)/shard_map/ppermute | solution.py:287
  5.8 57.5 %collective-permute-start.1 = (bf16[16,64,1024]{2,1,0:T(8,128)(2,1)S(1)}, bf16[16,64,1024]{2,1,0:T(8,128)(2,1)}, u32[]{:S(2)}, u32[]{:S(2)}) collective-permute-start(bf16[16,64,1024]{2,1,0:T(8,128)(2,1)S(1)} %reshape.122.refs_0_), channel_id=1, source_target_pairs={{0,28},{4,0},{8,4},{12,8},{16,12},{20,16},{24,20},{28,24},{1,29},{... | collective-permute-start | bytes 6291464 | tf_op jit(solution)/shard_map/ppermute | solution.py:287
  11.0 52.4 %collective-permute-start.2 = (bf16[64,1024]{1,0:T(8,128)(2,1)S(1)}, bf16[64,1024]{1,0:T(8,128)(2,1)S(1)}, u32[]{:S(2)}, u32[]{:S(2)}) collective-permute-start(bf16[64,1024]{1,0:T(8,128)(2,1)S(1)} %bitcast.23), channel_id=1, source_target_pairs={{28,32},{60,64},{92,96},{124,128},{156,160},{188,192},{220,224},{3... | collective-permute-start | bytes 393224 | tf_op jit(solution)/shard_map/ppermute | solution.py:368
  11.6 11.7 %collective-permute-start.5 = (bf16[64,1024]{1,0:T(8,128)(2,1)S(1)}, bf16[64,1024]{1,0:T(8,128)(2,1)S(1)}, u32[]{:S(2)}, u32[]{:S(2)}) collective-permute-start(bf16[64,1024]{1,0:T(8,128)(2,1)S(1)} %bitcast.24), channel_id=1, source_target_pairs={{0,128},{252,124},{1,129},{253,125},{2,130},{254,126},{3,131},{255... | collective-permute-start | bytes 393224 | tf_op jit(solution)/shard_map/ppermute | solution.py:302
  23.4 3.3 %collective-permute-start.6 = (bf16[64,1024]{1,0:T(8,128)(2,1)S(1)}, bf16[64,1024]{1,0:T(8,128)(2,1)S(1)}, u32[]{:S(2)}, u32[]{:S(2)}) collective-permute-start(bf16[64,1024]{1,0:T(8,128)(2,1)S(1)} %broadcast_select_fusion.5), channel_id=1, source_target_pairs={{0,64},{128,192},{252,188},{124,60},{1,65},{129,193},{253,189},{12... | collective-permute-start | bytes 393224 | tf_op jit(solution)/shard_map/ppermute | solution.py:302
  26.7 9.9 %collective-permute-start.7 = (bf16[64,1024]{1,0:T(8,128)(2,1)S(1)}, bf16[64,1024]{1,0:T(8,128)(2,1)S(1)}, u32[]{:S(2)}, u32[]{:S(2)}) collective-permute-start(bf16[64,1024]{1,0:T(8,128)(2,1)S(1)} %broadcast_select_fusion.6), channel_id=1, source_target_pairs={{0,32},{64,96},{128,160},{192,224},{252,220},{188,156},{124,92},{6... | collective-permute-start | bytes 393224 | tf_op jit(solution)/shard_map/ppermute | solution.py:302
  29.0 34.3 %all-to-all-start = ((s32[64,1,8]{2,1,0:T(1,128)}), s32[64,1,8]{2,1,0:T(1,128)S(1)}, u32[]{:S(2)}, u32[]{:S(2)}) async-start(s32[64,1,8]{2,1,0:T(1,128)} %bitcast.3), calls=%async_computation | async-start | bytes 65536 | tf_op jit(solution)/shard_map/all_to_all | solution.py:358
  41.3 49.5 %collective-permute-start.8 = (bf16[256,4096]{1,0:T(8,128)(2,1)}, bf16[256,4096]{1,0:T(8,128)(2,1)}, u32[]{:S(2)}, u32[]{:S(2)}) collective-permute-start(bf16[256,4096]{1,0:T(8,128)(2,1)} %get-tuple-element.88.refs_2_), channel_id=1, source_target_pairs={{0,2},{2,32},{32,34},{34,0},{1,3},{3,33},{33,35},{35,1},{4,6},{6,3... | collective-permute-start | bytes 6291464 | tf_op jit(solution)/shard_map/ppermute | solution.py:365
  42.5 48.3 %collective-permute-start.9 = (bf16[256,4096]{1,0:T(8,128)(2,1)}, bf16[256,4096]{1,0:T(8,128)(2,1)}, u32[]{:S(2)}, u32[]{:S(2)}) collective-permute-start(bf16[256,4096]{1,0:T(8,128)(2,1)} %get-tuple-element.87.refs_3_), channel_id=1, source_target_pairs={{0,34},{2,0},{32,2},{34,32},{1,35},{3,1},{33,3},{35,33},{4,38},{6,... | collective-permute-start | bytes 6291464 | tf_op jit(solution)/shard_map/ppermute | solution.py:366
  63.3 47.2 %collective-permute-start.3 = (bf16[16,64,1024]{2,1,0:T(8,128)(2,1)}, bf16[16,64,1024]{2,1,0:T(8,128)(2,1)}, u32[]{:S(2)}, u32[]{:S(2)}) collective-permute-start(bf16[16,64,1024]{2,1,0:T(8,128)(2,1)} %collective-permute-done.refs_1_), channel_id=1, source_target_pairs={{0,4},{4,8},{8,12},{12,16},{16,20},{20,24},{24,28},{28,0},{1,5},{5... | collective-permute-start | bytes 6291464 | tf_op jit(solution)/shard_map/ppermute | solution.py:287
  64.6 45.9 %collective-permute-start.4 = (bf16[16,64,1024]{2,1,0:T(8,128)(2,1)}, bf16[16,64,1024]{2,1,0:T(8,128)(2,1)}, u32[]{:S(2)}, u32[]{:S(2)}) collective-permute-start(bf16[16,64,1024]{2,1,0:T(8,128)(2,1)} %collective-permute-done.1.refs_2_), channel_id=1, source_target_pairs={{0,28},{4,0},{8,4},{12,8},{16,12},{20,16},{24,20},{28,24},{1,29},{... | collective-permute-start | bytes 6291464 | tf_op jit(solution)/shard_map/ppermute | solution.py:287
  72.4 52.6 %all-to-all-start.1 = ((bf16[8,3,64,1024]{3,2,1,0:T(8,128)(2,1)}), bf16[8,3,64,1024]{3,2,1,0:T(8,128)(2,1)}, u32[]{:S(2)}, u32[]{:S(2)}) async-start(bf16[8,3,64,1024]{3,2,1,0:T(8,128)(2,1)} %pick.2), calls=%async_computation.1 | async-start | bytes 6291456 | tf_op jit(solution)/shard_map/all_to_all | solution.py:291
  125.0 21.8 %copy-start.13 = (bf16[4,64,1024]{2,1,0:T(8,128)(2,1)S(1)}, bf16[4,64,1024]{2,1,0:T(8,128)(2,1)}, u32[]{:S(2)}) copy-start(bf16[4,64,1024]{2,1,0:T(8,128)(2,1)} %get-tuple-element.60) | copy-start | bytes 1572868
  125.0 31.6 %copy-start = (bf16[1152,1024]{1,0:T(8,128)(2,1)S(1)}, bf16[1152,1024]{1,0:T(8,128)(2,1)}, u32[]{:S(2)}) copy-start(bf16[1152,1024]{1,0:T(8,128)(2,1)} %pad_maximum_fusion.refs_4_) | copy-start | bytes 7077892
  125.0 31.6 %all-to-all-start.2 = ((bf16[8,2,64,1024]{3,2,1,0:T(8,128)(2,1)}), bf16[8,2,64,1024]{3,2,1,0:T(8,128)(2,1)}, u32[]{:S(2)}, u32[]{:S(2)}) async-start(bf16[8,2,64,1024]{3,2,1,0:T(8,128)(2,1)} %get-tuple-element.58), calls=%async_computation.2 | async-start | bytes 4194304 | tf_op jit(solution)/shard_map/all_to_all | solution.py:291
  129.8 8.8 %collective-permute-start.12 = (bf16[64,1024]{1,0:T(8,128)(2,1)S(1)}, bf16[64,1024]{1,0:T(8,128)(2,1)S(1)}, u32[]{:S(2)}, u32[]{:S(2)}) collective-permute-start(bf16[64,1024]{1,0:T(8,128)(2,1)S(1)} %broadcast_select_fusion.7), channel_id=1, source_target_pairs={{0,16},{28,12},{1,17},{29,13},{2,18},{30,14},{3,19},{31,15},{32,48... | collective-permute-start | bytes 393224 | tf_op jit(solution)/shard_map/ppermute | solution.py:395
  138.6 3.2 %collective-permute-start.13 = (bf16[64,1024]{1,0:T(8,128)(2,1)S(1)}, bf16[64,1024]{1,0:T(8,128)(2,1)S(1)}, u32[]{:S(2)}, u32[]{:S(2)}) collective-permute-start(bf16[64,1024]{1,0:T(8,128)(2,1)S(1)} %broadcast_select_fusion.1), channel_id=1, source_target_pairs={{0,8},{16,24},{28,20},{12,4},{1,9},{17,25},{29,21},{13,5},{2,10},{... | collective-permute-start | bytes 393224 | tf_op jit(solution)/shard_map/ppermute | solution.py:397
  141.9 7.6 %collective-permute-start.14 = (bf16[64,1024]{1,0:T(8,128)(2,1)S(1)}, bf16[64,1024]{1,0:T(8,128)(2,1)S(1)}, u32[]{:S(2)}, u32[]{:S(2)}) collective-permute-start(bf16[64,1024]{1,0:T(8,128)(2,1)S(1)} %broadcast_select_fusion.2), channel_id=1, source_target_pairs={{0,4},{4,0},{8,12},{12,8},{16,20},{20,16},{24,28},{28,24},{1,5},{5... | collective-permute-start | bytes 393224 | tf_op jit(solution)/shard_map/ppermute | solution.py:400
  146.7 9.9 %collective-permute-start.10 = (bf16[4,64,1024]{2,1,0:T(8,128)(2,1)}, bf16[4,64,1024]{2,1,0:T(8,128)(2,1)}, u32[]{:S(2)}, u32[]{:S(2)}) collective-permute-start(bf16[4,64,1024]{2,1,0:T(8,128)(2,1)} %get-tuple-element.59), channel_id=1, source_target_pairs={{0,4},{4,8},{8,12},{12,16},{16,20},{20,24},{24,28},{28,0},{1,5},{5... | collective-permute-start | bytes 1572872 | tf_op jit(solution)/shard_map/ppermute | solution.py:287
  146.8 9.8 %collective-permute-start.11 = (bf16[4,64,1024]{2,1,0:T(8,128)(2,1)S(1)}, bf16[4,64,1024]{2,1,0:T(8,128)(2,1)}, u32[]{:S(2)}, u32[]{:S(2)}) collective-permute-start(bf16[4,64,1024]{2,1,0:T(8,128)(2,1)S(1)} %copy-done.13), channel_id=1, source_target_pairs={{0,28},{4,0},{8,4},{12,8},{16,12},{20,16},{24,20},{28,24},{1,29},{... | collective-permute-start | bytes 1572872 | tf_op jit(solution)/shard_map/ppermute | solution.py:287
  156.6 1.2 copy-start.1
  175.7 1.3 copy-start.8
  177.0 10.8 %copy-start.10 = (f32[1024,128]{1,0:T(8,128)}, f32[1024,128]{1,0:T(8,128)S(1)}, u32[]{:S(2)}) copy-start(f32[1024,128]{1,0:T(8,128)S(1)} %get-tuple-element.69.refs_4_) | copy-start | bytes 1572868
  177.0 97.9 %collective-permute-start.24 = (bf16[512,4096]{1,0:T(8,128)(2,1)}, bf16[512,4096]{1,0:T(8,128)(2,1)}, u32[]{:S(2)}, u32[]{:S(2)}) collective-permute-start(bf16[512,4096]{1,0:T(8,128)(2,1)} %param.7), channel_id=1, source_target_pairs={{0,1},{1,0},{2,3},{3,2},{4,5},{5,4},{6,7},{7,6},{8,9},{9,8},{10,11... | collective-permute-start | bytes 12582920 | tf_op jit(solution)/shard_map/ppermute | solution.py:419
  187.8 49.6 %all-to-all-start.3 = ((bf16[8,2,64,1024]{3,2,1,0:T(8,128)(2,1)}), bf16[8,2,64,1024]{3,2,1,0:T(8,128)(2,1)S(1)}, u32[]{:S(2)}, u32[]{:S(2)}) async-start(bf16[8,2,64,1024]{3,2,1,0:T(8,128)(2,1)} %get-tuple-element.73), calls=%async_computation.3 | async-start | bytes 4194304 | tf_op jit(solution)/shard_map/all_to_all | solution.py:291
  198.1 46.0 %collective-permute-start.15 = (bf16[8,64,1024]{2,1,0:T(8,128)(2,1)}, bf16[8,64,1024]{2,1,0:T(8,128)(2,1)}, u32[]{:S(2)}, u32[]{:S(2)}) collective-permute-start(bf16[8,64,1024]{2,1,0:T(8,128)(2,1)} %get-tuple-element.90), channel_id=1, source_target_pairs={{0,4},{4,8},{8,12},{12,16},{16,20},{20,24},{24,28},{28,0},{1,5},{5... | collective-permute-start | bytes 3145736 | tf_op jit(solution)/shard_map/ppermute | solution.py:287
  198.1 46.0 %collective-permute-start.16 = (bf16[8,64,1024]{2,1,0:T(8,128)(2,1)}, bf16[8,64,1024]{2,1,0:T(8,128)(2,1)}, u32[]{:S(2)}, u32[]{:S(2)}) collective-permute-start(bf16[8,64,1024]{2,1,0:T(8,128)(2,1)} %get-tuple-element.89), channel_id=1, source_target_pairs={{0,28},{4,0},{8,4},{12,8},{16,12},{20,16},{24,20},{28,24},{1,29},{... | collective-permute-start | bytes 3145736 | tf_op jit(solution)/shard_map/ppermute | solution.py:287
  200.7 32.6 %collective-permute-start.18 = (bf16[4,64,1024]{2,1,0:T(8,128)(2,1)}, bf16[4,64,1024]{2,1,0:T(8,128)(2,1)S(1)}, u32[]{:S(2)}, u32[]{:S(2)}) collective-permute-start(bf16[4,64,1024]{2,1,0:T(8,128)(2,1)} %collective-permute-done.11), channel_id=1, source_target_pairs={{0,28},{4,0},{8,4},{12,8},{16,12},{20,16},{24,20},{28,24},{1,29},{... | collective-permute-start | bytes 1572872 | tf_op jit(solution)/shard_map/ppermute | solution.py:287
  201.8 33.9 %collective-permute-start.17 = (bf16[4,64,1024]{2,1,0:T(8,128)(2,1)}, bf16[4,64,1024]{2,1,0:T(8,128)(2,1)S(1)}, u32[]{:S(2)}, u32[]{:S(2)}) collective-permute-start(bf16[4,64,1024]{2,1,0:T(8,128)(2,1)} %collective-permute-done.10), channel_id=1, source_target_pairs={{0,4},{4,8},{8,12},{12,16},{16,20},{20,24},{24,28},{28,0},{1,5},{5... | collective-permute-start | bytes 1572872 | tf_op jit(solution)/shard_map/ppermute | solution.py:287
  233.4 46.1 %collective-permute-start.21 = (bf16[256,4096]{1,0:T(8,128)(2,1)}, bf16[256,4096]{1,0:T(8,128)(2,1)}, u32[]{:S(2)}, u32[]{:S(2)}) collective-permute-start(bf16[256,4096]{1,0:T(8,128)(2,1)} %collective-permute-done.8.refs_2_), channel_id=1, source_target_pairs={{0,1},{1,0},{2,3},{3,2},{4,5},{5,4},{6,7},{7,6},{8,9},{9,8},{10,11... | collective-permute-start | bytes 6291464 | tf_op jit(solution)/shard_map/ppermute | solution.py:419
  235.7 43.8 %collective-permute-start.22 = (bf16[256,4096]{1,0:T(8,128)(2,1)}, bf16[256,4096]{1,0:T(8,128)(2,1)}, u32[]{:S(2)}, u32[]{:S(2)}) collective-permute-start(bf16[256,4096]{1,0:T(8,128)(2,1)} %collective-permute-done.9.refs_3_), channel_id=1, source_target_pairs={{0,1},{1,0},{2,3},{3,2},{4,5},{5,4},{6,7},{7,6},{8,9},{9,8},{10,11... | collective-permute-start | bytes 6291464 | tf_op jit(solution)/shard_map/ppermute | solution.py:419
  237.4 23.7 %all-to-all-start.4 = ((bf16[8,64,1024]{2,1,0:T(8,128)(2,1)}), bf16[8,64,1024]{2,1,0:T(8,128)(2,1)S(1)}, u32[]{:S(2)}, u32[]{:S(2)}) async-start(bf16[8,64,1024]{2,1,0:T(8,128)(2,1)} %pad_maximum_fusion.1), calls=%async_computation.4 | async-start | bytes 2097152 | tf_op jit(solution)/shard_map/all_to_all | solution.py:291
  244.1 1.2 copy-start.2
  245.3 1.6 copy-start.9
  246.9 1.0 copy-start.11
  256.4 1.3 copy-start.4
  257.8 0.8 copy-start.6
  261.1 1.2 copy-start.3
  262.3 1.6 copy-start.5
  263.9 1.0 copy-start.7
  269.1 4.3 %collective-permute-start.23 = (bf16[256,512]{1,0:T(8,128)(2,1)S(1)}, bf16[256,512]{1,0:T(8,128)(2,1)S(1)}, u32[]{:S(2)}, u32[]{:S(2)}) collective-permute-start(bf16[256,512]{1,0:T(8,128)(2,1)S(1)} %get-tuple-element.83), channel_id=1, source_target_pairs={{0,1},{1,0},{2,3},{3,2},{4,5},{5,4},{6,7},{7,6},{8,9},{9,8},{10,11... | collective-permute-start | bytes 786440 | tf_op jit(solution)/shard_map/ppermute | solution.py:429
  270.4 9.7 %collective-permute-start.19 = (bf16[256,512]{1,0:T(8,128)(2,1)S(1)}, bf16[256,512]{1,0:T(8,128)(2,1)S(1)}, u32[]{:S(2)}, u32[]{:S(2)}) collective-permute-start(bf16[256,512]{1,0:T(8,128)(2,1)S(1)} %get-tuple-element.78), channel_id=1, source_target_pairs={{0,2},{1,3},{2,0},{3,1},{4,6},{5,7},{6,4},{7,5},{8,10},{9,11},{10,... | collective-permute-start | bytes 786440 | tf_op jit(solution)/shard_map/ppermute | solution.py:428
  273.5 12.2 %collective-permute-start.20 = (bf16[256,512]{1,0:T(8,128)(2,1)S(1)}, bf16[256,512]{1,0:T(8,128)(2,1)S(1)}, u32[]{:S(2)}, u32[]{:S(2)}) collective-permute-start(bf16[256,512]{1,0:T(8,128)(2,1)S(1)} %get-tuple-element.79), channel_id=1, source_target_pairs={{0,3},{1,2},{2,1},{3,0},{4,7},{5,6},{6,5},{7,4},{8,11},{9,10},{10,... | collective-permute-start | bytes 786440 | tf_op jit(solution)/shard_map/ppermute | solution.py:428
